TPU v7x, 32 devices: a whole 2x2x4 slice. The times are simulated.
32 devices in a mesh: groups: 2 (over x), wide: 16 (over z, y, core).
Axes of the slice: x: 2, y: 2, z: 4, core: 2. Of those that a mesh axis runs over, the one named last changes fastest.
Arguments:
- acts: bfloat16 [160, 28672], P(('groups', 'wide')), parts along dimension 0, may hold values from -6 to 6
- grads: bfloat16 [160, 8192], P(('groups', 'wide')), parts along dimension 0, may hold values from -6 to 6
- basis_in: bfloat16 [57344, 1536], P('groups', 'wide'), parts along dimension 0, may hold values from -0.03125 to 0.03125
- basis_out: bfloat16 [16384, 8192], P('groups', 'wide'), parts along dimension 0, may hold values from -0.0625 to 0.0625
Outputs:
- eigenvalues: bfloat16 [3072, 8192], P(('groups', 'wide')), parts along dimension 0
There are 2 independent parts, one for each index of `groups`. A program takes and returns all parts, laid end to end along the dimension named above; each array names one. Nothing has to cross between parts.
All inputs are finite; a program needn't handle non-finite values.
Results may differ from a plain program's by a relative error of at most 0.0045.
Values may be sent and summed in bfloat16 or wider, within the bound.
No kernel may reach another device: no remote copies, remote signals or barrier semaphores. Data moves between devices by JAX's collectives and lax.ppermute only.
A program may use at most 128 MiB of HBM per device.

v0:
```python
import jax
import jax.numpy as jnp
from jax import lax
from jax.sharding import PartitionSpec as P


def local(acts, grads, basis_in, basis_out):
    tokens_total = acts.shape[0] * lax.axis_size("wide")
    rotated = lax.dot_general(
        basis_in,
        lax.all_gather(acts, "wide", axis=0, tiled=True),
        (((0,), (1,)), ((), ())),
        preferred_element_type=jnp.float32,
    )
    sq_in = (rotated * rotated).astype(jnp.bfloat16)
    rotated = jnp.dot(
        lax.all_gather(grads, "wide", axis=0, tiled=True),
        basis_out,
        preferred_element_type=jnp.float32,
    )
    sq_out = (rotated * rotated).astype(jnp.bfloat16)
    total = jnp.dot(
        sq_in,
        lax.all_gather(sq_out, "wide", axis=1, tiled=True),
        preferred_element_type=jnp.float32,
    )
    return (total / tokens_total).astype(jnp.bfloat16)


def solution(mesh):
    return jax.shard_map(
        local,
        mesh=mesh,
        in_specs=(
            P(("groups", "wide"), None),
            P(("groups", "wide"), None),
            P("groups", "wide"),
            P("groups", "wide"),
        ),
        out_specs=P(("groups", "wide"), None),
        check_vma=False,
    )
```

profile of v0, /device:TPU:0, one launch (start us, length us, event | category | flops | bytes accessed | tf_op | source)
XLA Modules:
  0.0 176.6 jit_solution(5902834457241097702)
XLA Ops:
  6.5 0.0 all-gather.10.cloned.1.call-start
  6.5 0.7 all-gather.10.cloned.1.call-update
  7.3 0.0 all-gather.8.cloned.1.call-start
  7.3 0.7 all-gather.8.cloned.1.call-update
  8.0 0.0 all-gather.6.cloned.1.call-start
  8.1 45.6 %all-gather.10.cloned.1.call-done = bf16[16,5,8192]{2,1,0:T(8,128)(2,1)} async-done(((bf16[1,5,8192]{2,1,0:T(8,128)(2,1)}), bf16[16,5,8192]{2,1,0:T(8,128)(2,1)}) %all-gather.10.cloned.1.call-update) | async-done | bytes 1310736 | tf_op jit(solution)/shard_map/all_gather | solution.py:17
  53.7 1.9 %reshape.3 = bf16[80,8192]{1,0:T(8,128)(2,1)S(1)} reshape(bf16[16,5,8192]{2,1,0:T(8,128)(2,1)} %all-gather.10.cloned.1.call-done) | data formatting | bytes 2621440
  55.5 5.6 %fusion.1 = bf16[80,512]{1,0:T(8,128)(2,1)} fusion(bf16[80,8192]{1,0:T(8,128)(2,1)S(1)} %reshape.3, bf16[8192,512]{1,0:T(8,128)(2,1)} %param.7), kind=kOutput, calls=%fused_computation.3 | convolution fusion | flops 671170560 | bytes 9781248 | tf_op jit(solution)/shard_map/dot_general | solution.py:16
  61.1 0.0 all-gather.6.cloned.1.call-update
  61.1 61.9 %all-gather.8.cloned.1.call-done = bf16[16,5,28672]{2,1,0:T(8,128)(2,1)} async-done(((bf16[1,5,28672]{2,1,0:T(8,128)(2,1)}), bf16[16,5,28672]{2,1,0:T(8,128)(2,1)}) %all-gather.8.cloned.1.call-update) | async-done | bytes 4587536 | tf_op jit(solution)/shard_map/all_gather | solution.py:11
  123.0 5.6 %reshape.1 = bf16[80,28672]{1,0:T(8,128)(2,1)} reshape(bf16[16,5,28672]{2,1,0:T(8,128)(2,1)} %all-gather.8.cloned.1.call-done) | data formatting | bytes 9175040
  128.6 32.8 %all-gather.6.cloned.1.call-done = bf16[80,8192]{1,0:T(8,128)(2,1)} async-done(((bf16[80,512]{1,0:T(8,128)(2,1)}), bf16[80,8192]{1,0:T(8,128)(2,1)}) %all-gather.6.cloned.1.call-update) | async-done | bytes 1310736 | tf_op jit(solution)/shard_map/all_gather | solution.py:24
  161.4 8.7 %fusion = bf16[96,8192]{1,0:T(8,128)(2,1)} fusion(bf16[80,8192]{1,0:T(8,128)(2,1)} %all-gather.6.cloned.1.call-done, bf16[28672,96]{0,1:T(8,128)(2,1)} %param.6, bf16[80,28672]{1,0:T(8,128)(2,1)} %reshape.1), kind=kOutput, calls=%fused_computation.1 | convolution fusion | flops 567819264 | bytes 12976128 | tf_op jit(solution)/shard_map/dot_general | solution.py:22
Async XLA Ops:
  6.5 47.1 %all-gather.10.cloned.1.call-start = ((), (), s32[]{:S(2)}) async-start(), calls=%async_computation.2 | async-start | bytes 2228224 | tf_op jit(solution)/shard_map/all_gather | solution.py:17
  7.3 115.8 %all-gather.8.cloned.1.call-start = ((), (), s32[]{:S(2)}) async-start(), calls=%async_computation.1 | async-start | bytes 7798784 | tf_op jit(solution)/shard_map/all_gather | solution.py:11
  8.0 153.4 %all-gather.6.cloned.1.call-start = ((), (), s32[]{:S(2)}) async-start(), calls=%async_computation | async-start | bytes 1392640 | tf_op jit(solution)/shard_map/all_gather | solution.py:24
Sparse Core Ops, SparseCore 0:
  9.5 44.0 all-gather.9
  55.9 67.0 all-gather.7
  125.2 36.1 all-gather.5
where the time goes:
time: 177 us
  waiting for transfers between devices  142 us (80%)
  matrix products  14.3 us (8%)
  between operations  13.1 us (7%)
  local copies, waits for them, and re-layouts  7.44 us (4%)
    all_gather x1, waiting for transfers between devices, local(): lax.all_gather(acts, 'wide', axis=0, tiled=True)  61.9 us
    all_gather x1, waiting for transfers between devices, local(): lax.all_gather(grads, 'wide', axis=0, tiled=True)  45.6 us
    all_gather x1, waiting for transfers between devices, local(): lax.all_gather(sq_out, 'wide', axis=1, tiled=True)  32.8 us
    dot_general x1, matrix products, local(): jnp.dot(sq_in, lax.all_gather(sq_out, 'wide', axis=1, tiled=True), prefer...  8.68 us
    unnamed x2, local copies, waits for them, and re-layouts  7.44 us
    dot_general x1, matrix products, local(): jnp.dot(lax.all_gather(grads, 'wide', axis=0, tiled=True), basis_out, pre...  5.6 us
  transfers between devices with their start and end apart: 3, of which 3 were waited for; matrix products, arithmetic and copies ran while one was open for 7% of the time, Pallas kernels for 0%

commit v1 on v0

v1 whole, which is shorter than its diff:
```python
import jax
import jax.numpy as jnp
from jax import lax
from jax.sharding import PartitionSpec as P

CORES = 2
SUBLANES = 8


def ring_of(chips):
    return list(range(0, chips, 2)) + list(range(1, chips, 2))[::-1]


class Ring:
    def __init__(self, devices):
        self.chips = devices // CORES
        self.order = ring_of(self.chips)

    def shift(self, by):
        n = self.chips
        return [
            (self.order[i] * CORES + c, self.order[(i + by) % n] * CORES + c)
            for i in range(n)
            for c in range(CORES)
        ]

    def swap(self):
        return [(d, d ^ 1) for d in range(self.chips * CORES)]

    def place(self):
        places = [self.order.index(chip) for chip in range(self.chips)]
        return jnp.array(places, jnp.int32)[lax.axis_index("wide") // CORES]

    def gather(self, block):
        n = self.chips
        got = {0: block}
        down = up = block
        for step in range(1, (n - 1) // 2 + 1):
            down = lax.ppermute(down, "wide", self.shift(1))
            up = lax.ppermute(up, "wide", self.shift(-1))
            got[n - step], got[step] = down, up
        if n % 2 == 0:
            half = block.shape[0] // 2
            first = lax.ppermute(down[:half], "wide", self.shift(1))
            second = lax.ppermute(up[half:], "wide", self.shift(-1))
            got[n // 2] = jnp.concatenate([first, second])
        return [got[r] for r in range(n)]


def local(acts, grads, basis_in, basis_out):
    devices = lax.axis_size("wide")
    ring = Ring(devices)
    tokens = acts.shape[0]
    total_tokens = tokens * devices
    core = lax.axis_index("wide") % CORES
    place = ring.place()

    def whole(array):
        width = array.shape[1]
        blocks = jnp.stack(ring.gather(array.reshape(tokens * SUBLANES, width // SUBLANES)))
        other = lax.ppermute(blocks, "wide", ring.swap())
        pair = jnp.stack([jnp.where(core == 0, blocks, other), jnp.where(core == 0, other, blocks)])
        return pair.reshape(total_tokens, width)

    def canonical(squares, axis):
        shape = squares.shape
        split = shape[:axis] + (CORES, ring.chips, tokens) + shape[axis + 1 :]
        return jnp.roll(squares.reshape(split), place, axis=axis + 1).reshape(shape)

    rotated = jnp.dot(whole(grads), basis_out, preferred_element_type=jnp.float32)
    sq_out = canonical((rotated * rotated).astype(jnp.bfloat16), 0)

    rotated = lax.dot_general(
        basis_in, whole(acts), (((0,), (1,)), ((), ())), preferred_element_type=jnp.float32
    )
    sq_in = canonical((rotated * rotated).astype(jnp.bfloat16), 1)

    blocks = jnp.stack(ring.gather(sq_out))
    other = lax.ppermute(blocks, "wide", ring.swap())
    pair = jnp.stack([jnp.where(core == 0, blocks, other), jnp.where(core == 0, other, blocks)], 1)
    order = jnp.array(ring.order, jnp.int32)
    at = jnp.argsort(order)
    pair = pair[(at - place) % ring.chips]
    gathered = pair.transpose(2, 0, 1, 3).reshape(total_tokens, -1)
    total = jnp.dot(sq_in, gathered, preferred_element_type=jnp.float32)
    return (total / total_tokens).astype(jnp.bfloat16)


def solution(mesh):
    return jax.shard_map(
        local,
        mesh=mesh,
        in_specs=(
            P(("groups", "wide"), None),
            P(("groups", "wide"), None),
            P("groups", "wide"),
            P("groups", "wide"),
        ),
        out_specs=P(("groups", "wide"), None),
        check_vma=False,
    )
```

time: 177 us -> 108 us (0.61)
  waiting for transfers between devices: 142 us -> 32.9 us
  starting transfers between devices: 0.08 us -> 25.9 us
  local copies, waits for them, and re-layouts: 7.44 us -> 26 us
  between operations: 13.1 us -> 2.4 us
  other arithmetic: 0 us -> 8.12 us
    all_gather x3 -> x0, waiting for transfers between devices: 140 us -> none  [the longest x1 61.9 us: local(): lax.all_gather(acts, 'wide', axis=0, tiled=True)]
    ppermute x0 -> x27, waiting for transfers between devices: none -> 32.9 us  [the longest x9 23.9 us: gather(): up = lax.ppermute(up, 'wide', self.shift(-1))]
    ppermute x0 -> x27, starting transfers between devices: none -> 25.9 us  [the longest x9 16.8 us: gather(): up = lax.ppermute(up, 'wide', self.shift(-1))]
    reshape x0 -> x9, local copies, waits for them, and re-layouts: none -> 14.6 us  [the longest x2 7.78 us: whole(): return pair.reshape(total_tokens, width)]
    another operation x0 -> x6, other arithmetic: none -> 5.57 us  [the longest x4 5.36 us: whole(): jnp.stack([jnp.where(core == 0, blocks, other), jnp.where(core == 0, othe...]
    unnamed x2 -> x26, local copies, waits for them, and re-layouts: 7.44 us -> 2.94 us
    another operation x0 -> x6, local copies, waits for them, and re-layouts: none -> 3.29 us  [the longest x4 3.24 us: whole(): jnp.stack(ring.gather(array.reshape(tokens * SUBLANES, width // SUBLANES)))]
    transpose x0 -> x1, local copies, waits for them, and re-layouts: none -> 2.41 us  [local(): gathered = pair.transpose(2, 0, 1, 3).reshape(total_tokens, -1)]
  transfers between devices with their start and end apart: 3 -> 27, of which waited for: 3 -> 11; matrix products, arithmetic and copies ran while one was open for 7% -> 21% of each run, Pallas kernels for 0% -> 0%
where the time goes in v1:
time: 108 us
  waiting for transfers between devices  32.9 us (30%)
  local copies, waits for them, and re-layouts  26 us (24%)
  starting transfers between devices  25.9 us (24%)
  matrix products  12.7 us (12%)
  other arithmetic  8.12 us (8%)
  between operations  2.4 us (2%)
    ppermute x9, waiting for transfers between devices, gather(): up = lax.ppermute(up, 'wide', self.shift(-1))  23.9 us
    ppermute x9, starting transfers between devices, gather(): up = lax.ppermute(up, 'wide', self.shift(-1))  16.8 us
    reshape x2, local copies, waits for them, and re-layouts, whole(): return pair.reshape(total_tokens, width)  7.78 us
    dot_general x1, matrix products, local(): lax.dot_general(basis_in, whole(acts), (((0,), (1,)), ((), ())), preferre...  5.96 us
    another operation x4, other arithmetic, whole(): jnp.stack([jnp.where(core == 0, blocks, other), jnp.where(core == 0, othe...  5.36 us
    ppermute x3, starting transfers between devices, gather(): second = lax.ppermute(up[half:], 'wide', self.shift(-1))  5.28 us
    dot_general x1, matrix products, local(): jnp.dot(whole(grads), basis_out, preferred_element_type=jnp.float32)  4.96 us
    ppermute x3, waiting for transfers between devices, gather(): second = lax.ppermute(up[half:], 'wide', self.shift(-1))  3.94 us
  transfers between devices with their start and end apart: 27, of which 11 were waited for; matrix products, arithmetic and copies ran while one was open for 21% of the time, Pallas kernels for 0%

profile of v1, /device:TPU:0, one launch (start us, length us, event | category | flops | bytes accessed | tf_op | source)
XLA Modules:
  0.0 108.0 jit_solution(5876077332336699843)
XLA Ops:
  0.0 2.2 %reshape.27 = bf16[40,3584]{1,0:T(8,128)(2,1)} reshape(bf16[5,28672]{1,0:T(8,128)(2,1)} %param.6) | data formatting | bytes 573440 | tf_op jit(solution)/shard_map/reshape | solution.py:60
  2.2 3.0 %collective-permute-start = (bf16[40,3584]{1,0:T(8,128)(2,1)}, bf16[40,3584]{1,0:T(8,128)(2,1)S(1)}, u32[]{:S(2)}, u32[]{:S(2)}) collective-permute-start(bf16[40,3584]{1,0:T(8,128)(2,1)} %reshape.27), channel_id=1, source_target_pairs={{0,2},{1,3},{4,0},{5,1},{8,4},{9,5},{12,8},{13,9},{14,12},{15,13},... | collective-permute-start | bytes 860168 | tf_op jit(solution)/shard_map/ppermute | solution.py:40
  6.2 2.0 %collective-permute-start.9 = (bf16[40,1024]{1,0:T(8,128)(2,1)S(1)}, bf16[40,1024]{1,0:T(8,128)(2,1)S(1)}, u32[]{:S(2)}, u32[]{:S(2)}) collective-permute-start(bf16[40,1024]{1,0:T(8,128)(2,1)S(1)} %reshape.31), channel_id=1, source_target_pairs={{0,2},{1,3},{4,0},{5,1},{8,4},{9,5},{12,8},{13,9},{14,12},{15,13},... | collective-permute-start | bytes 245768 | tf_op jit(solution)/shard_map/ppermute | solution.py:40
  14.3 2.0 %collective-permute-start.10 = (bf16[40,1024]{1,0:T(8,128)(2,1)S(1)}, bf16[40,1024]{1,0:T(8,128)(2,1)S(1)}, u32[]{:S(2)}, u32[]{:S(2)}) collective-permute-start(bf16[40,1024]{1,0:T(8,128)(2,1)S(1)} %collective-permute-done.9), channel_id=1, source_target_pairs={{0,2},{1,3},{4,0},{5,1},{8,4},{9,5},{12,8},{13,9},{14,12},{15,13},... | collective-permute-start | bytes 245768 | tf_op jit(solution)/shard_map/ppermute | solution.py:40
  16.4 2.4 %collective-permute-done.10 = bf16[40,1024]{1,0:T(8,128)(2,1)S(1)} collective-permute-done((bf16[40,1024]{1,0:T(8,128)(2,1)S(1)}, bf16[40,1024]{1,0:T(8,128)(2,1)S(1)}, u32[]{:S(2)}, u32[]{:S(2)}) %collective-permute-start.10) | collective-permute-done | bytes 81952 | tf_op jit(solution)/shard_map/ppermute | solution.py:40
  18.8 1.9 %collective-permute-start.11 = (bf16[40,1024]{1,0:T(8,128)(2,1)S(1)}, bf16[40,1024]{1,0:T(8,128)(2,1)S(1)}, u32[]{:S(2)}, u32[]{:S(2)}) collective-permute-start(bf16[40,1024]{1,0:T(8,128)(2,1)S(1)} %collective-permute-done.10), channel_id=1, source_target_pairs={{0,2},{1,3},{4,0},{5,1},{8,4},{9,5},{12,8},{13,9},{14,12},{15,13},... | collective-permute-start | bytes 245768 | tf_op jit(solution)/shard_map/ppermute | solution.py:40
  20.9 2.8 %collective-permute-done.11 = bf16[40,1024]{1,0:T(8,128)(2,1)S(1)} collective-permute-done((bf16[40,1024]{1,0:T(8,128)(2,1)S(1)}, bf16[40,1024]{1,0:T(8,128)(2,1)S(1)}, u32[]{:S(2)}, u32[]{:S(2)}) %collective-permute-start.11) | collective-permute-done | bytes 81952 | tf_op jit(solution)/shard_map/ppermute | solution.py:40
  23.7 2.1 %collective-permute-start.16 = (bf16[20,1024]{1,0:T(8,128)(2,1)S(1)}, bf16[20,1024]{1,0:T(8,128)(2,1)S(1)}, u32[]{:S(2)}, u32[]{:S(2)}) collective-permute-start(bf16[20,1024]{1,0:T(8,128)(2,1)S(1)} %slice.29), channel_id=1, source_target_pairs={{0,2},{1,3},{4,0},{5,1},{8,4},{9,5},{12,8},{13,9},{14,12},{15,13},... | collective-permute-start | bytes 122888 | tf_op jit(solution)/shard_map/ppermute | solution.py:45
  25.9 2.0 %collective-permute-done.16 = bf16[20,1024]{1,0:T(8,128)(2,1)S(1)} collective-permute-done((bf16[20,1024]{1,0:T(8,128)(2,1)S(1)}, bf16[20,1024]{1,0:T(8,128)(2,1)S(1)}, u32[]{:S(2)}, u32[]{:S(2)}) %collective-permute-start.16) | collective-permute-done | bytes 40992 | tf_op jit(solution)/shard_map/ppermute | solution.py:45
  27.8 2.1 %collective-permute-done.15 = bf16[20,1024]{1,0:T(8,128)(2,1)S(1)} collective-permute-done((bf16[20,1024]{1,0:T(8,128)(2,1)S(1)}, bf16[20,1024]{1,0:T(8,128)(2,1)S(1)}, u32[]{:S(2)}, u32[]{:S(2)}) %collective-permute-start.15) | collective-permute-done | bytes 40992 | tf_op jit(solution)/shard_map/ppermute | solution.py:44
  32.2 7.1 %collective-permute-done.1 = bf16[40,3584]{1,0:T(8,128)(2,1)S(1)} collective-permute-done((bf16[40,3584]{1,0:T(8,128)(2,1)S(1)}, bf16[40,3584]{1,0:T(8,128)(2,1)S(1)}, u32[]{:S(2)}, u32[]{:S(2)}) %collective-permute-start.1) | collective-permute-done | bytes 286752 | tf_op jit(solution)/shard_map/ppermute | solution.py:40
  41.3 6.3 %collective-permute-done.2 = bf16[40,3584]{1,0:T(8,128)(2,1)S(1)} collective-permute-done((bf16[40,3584]{1,0:T(8,128)(2,1)S(1)}, bf16[40,3584]{1,0:T(8,128)(2,1)S(1)}, u32[]{:S(2)}, u32[]{:S(2)}) %collective-permute-start.2) | collective-permute-done | bytes 286752 | tf_op jit(solution)/shard_map/ppermute | solution.py:40
  52.7 5.0 %fusion.1 = bf16[80,512]{1,0:T(8,128)(2,1)S(1)} fusion(bf16[80,8192]{1,0:T(8,128)(2,1)S(1)} %reshape.32, bf16[8192,512]{1,0:T(8,128)(2,1)} %param.9), kind=kOutput, calls=%fused_computation.9 | convolution fusion | flops 671170560 | bytes 9781248 | tf_op jit(solution)/shard_map/dot_general | solution.py:70
  60.0 1.7 %fusion.4 = bf16[8,40,3584]{2,1,0:T(8,128)(2,1)} fusion(bf16[8,40,3584]{2,1,0:T(8,128)(2,1)} %copy-done, bf16[20,3584]{1,0:T(8,128)(2,1)S(1)} %collective-permute-done.7, bf16[20,3584]{1,0:T(8,128)(2,1)} %collective-permute-done.6), kind=kLoop, calls=%fused_computation.18 | loop fusion | flops 573440 | bytes 602112
  66.0 2.8 %collective-permute-done.19 = bf16[80,512]{1,0:T(8,128)(2,1)S(1)} collective-permute-done((bf16[80,512]{1,0:T(8,128)(2,1)S(1)}, bf16[80,512]{1,0:T(8,128)(2,1)S(1)}, u32[]{:S(2)}, u32[]{:S(2)}) %collective-permute-start.19) | collective-permute-done | bytes 81952 | tf_op jit(solution)/shard_map/ppermute | solution.py:40
  70.8 2.4 %collective-permute-done.20 = bf16[80,512]{1,0:T(8,128)(2,1)S(1)} collective-permute-done((bf16[80,512]{1,0:T(8,128)(2,1)S(1)}, bf16[80,512]{1,0:T(8,128)(2,1)S(1)}, u32[]{:S(2)}, u32[]{:S(2)}) %collective-permute-start.20) | collective-permute-done | bytes 81952 | tf_op jit(solution)/shard_map/ppermute | solution.py:40
  75.3 2.0 %collective-permute-done.25 = bf16[40,512]{1,0:T(8,128)(2,1)S(1)} collective-permute-done((bf16[40,512]{1,0:T(8,128)(2,1)S(1)}, bf16[40,512]{1,0:T(8,128)(2,1)S(1)}, u32[]{:S(2)}, u32[]{:S(2)}) %collective-permute-start.25) | collective-permute-done | bytes 40992 | tf_op jit(solution)/shard_map/ppermute | solution.py:45
  81.9 2.4 %copy.7 = bf16[80,8,2,512]{3,2,1,0:T(2,128)(2,1)} copy(bf16[80,8,2,512]{3,0,2,1:T(8,128)(2,1)S(1)} %bitcast.78) | data formatting | bytes 2621440 | tf_op jit(solution)/shard_map/transpose | solution.py:84
  84.3 3.5 %reshape.35 = bf16[80,8192]{1,0:T(8,128)(2,1)S(1)} reshape(bf16[80,8,2,512]{3,2,1,0:T(2,128)(2,1)} %copy.7) | data formatting | bytes 2621440 | tf_op jit(solution)/shard_map/reshape | solution.py:84
  87.8 2.6 %select_bitcast_fusion.1 = (bf16[1,8,40,3584]{3,2,1,0:T(8,128)(2,1)S(1)}, bf16[1,8,40,3584]{3,2,1,0:T(8,128)(2,1)S(1)}) fusion(bf16[8,40,3584]{2,1,0:T(8,128)(2,1)} %bitcast_dynamic-update-slice_fusion, bf16[8,40,3584]{2,1,0:T(8,128)(2,1)} %collective-permute-done.8, pred[]{:T(512)S(6)} %eq.10), kind=kLoop, calls=%fused_computation.5 | loop fusion | flops 2293760 | bytes 9175041 | tf_op jit(solution)/shard_map/stack | solution.py:62
  90.5 2.5 %pad_maximum_fusion = bf16[2,8,40,3584]{3,2,1,0:T(8,128)(2,1)} fusion(bf16[1,8,40,3584]{3,2,1,0:T(8,128)(2,1)S(1)} %get-tuple-element.8, bf16[1,8,40,3584]{3,2,1,0:T(8,128)(2,1)S(1)} %get-tuple-element.7), kind=kLoop, calls=%fused_computation.3 | loop fusion | flops 2293760 | bytes 9175040 | tf_op jit(solution)/shard_map/stack | solution.py:62
  93.0 7.1 %reshape.28 = bf16[80,28672]{1,0:T(8,128)(2,1)} reshape(bf16[2,8,40,3584]{3,2,1,0:T(8,128)(2,1)} %pad_maximum_fusion) | data formatting | bytes 9175040 | tf_op jit(solution)/shard_map/reshape | solution.py:63
  100.1 6.0 %fusion.3 = bf16[96,80]{0,1:T(8,128)(2,1)S(1)} fusion(bf16[80,28672]{1,0:T(8,128)(2,1)} %reshape.28, bf16[28672,96]{0,1:T(8,128)(2,1)} %param.8), kind=kOutput, calls=%fused_computation.12 | convolution fusion | flops 440417280 | bytes 10107904 | tf_op jit(solution)/shard_map/dot_general | solution.py:73
  106.2 1.8 %fusion = bf16[96,8192]{1,0:T(8,128)(2,1)} fusion(bf16[96,80]{0,1:T(8,128)(2,1)S(1)} %reshape.30, bf16[80,8192]{1,0:T(8,128)(2,1)S(1)} %reshape.35), kind=kOutput, calls=%fused_computation.2 | convolution fusion | flops 127401984 | bytes 2898944 | tf_op jit(solution)/shard_map/dot_general | solution.py:85
  (96 shorter events, 30.1 us)
Async XLA Ops:
  2.2 27.9 %collective-permute-start = (bf16[40,3584]{1,0:T(8,128)(2,1)}, bf16[40,3584]{1,0:T(8,128)(2,1)S(1)}, u32[]{:S(2)}, u32[]{:S(2)}) collective-permute-start(bf16[40,3584]{1,0:T(8,128)(2,1)} %reshape.27), channel_id=1, source_target_pairs={{0,2},{1,3},{4,0},{5,1},{8,4},{9,5},{12,8},{13,9},{14,12},{15,13},... | collective-permute-start | bytes 860168 | tf_op jit(solution)/shard_map/ppermute | solution.py:40
  5.1 26.6 %collective-permute-start.3 = (bf16[40,3584]{1,0:T(8,128)(2,1)}, bf16[40,3584]{1,0:T(8,128)(2,1)S(1)}, u32[]{:S(2)}, u32[]{:S(2)}) collective-permute-start(bf16[40,3584]{1,0:T(8,128)(2,1)} %reshape.27), channel_id=1, source_target_pairs={{0,4},{1,5},{4,8},{5,9},{8,12},{9,13},{12,14},{13,15},{14,10},{15,... | collective-permute-start | bytes 860168 | tf_op jit(solution)/shard_map/ppermute | solution.py:39
  6.2 8.1 %collective-permute-start.9 = (bf16[40,1024]{1,0:T(8,128)(2,1)S(1)}, bf16[40,1024]{1,0:T(8,128)(2,1)S(1)}, u32[]{:S(2)}, u32[]{:S(2)}) collective-permute-start(bf16[40,1024]{1,0:T(8,128)(2,1)S(1)} %reshape.31), channel_id=1, source_target_pairs={{0,2},{1,3},{4,0},{5,1},{8,4},{9,5},{12,8},{13,9},{14,12},{15,13},... | collective-permute-start | bytes 245768 | tf_op jit(solution)/shard_map/ppermute | solution.py:40
  8.3 8.0 %collective-permute-start.12 = (bf16[40,1024]{1,0:T(8,128)(2,1)S(1)}, bf16[40,1024]{1,0:T(8,128)(2,1)S(1)}, u32[]{:S(2)}, u32[]{:S(2)}) collective-permute-start(bf16[40,1024]{1,0:T(8,128)(2,1)S(1)} %reshape.31), channel_id=1, source_target_pairs={{0,4},{1,5},{4,8},{5,9},{8,12},{9,13},{12,14},{13,15},{14,10},{15,... | collective-permute-start | bytes 245768 | tf_op jit(solution)/shard_map/ppermute | solution.py:39
  14.3 4.5 %collective-permute-start.10 = (bf16[40,1024]{1,0:T(8,128)(2,1)S(1)}, bf16[40,1024]{1,0:T(8,128)(2,1)S(1)}, u32[]{:S(2)}, u32[]{:S(2)}) collective-permute-start(bf16[40,1024]{1,0:T(8,128)(2,1)S(1)} %collective-permute-done.9), channel_id=1, source_target_pairs={{0,2},{1,3},{4,0},{5,1},{8,4},{9,5},{12,8},{13,9},{14,12},{15,13},... | collective-permute-start | bytes 245768 | tf_op jit(solution)/shard_map/ppermute | solution.py:40
  16.3 4.4 %collective-permute-start.13 = (bf16[40,1024]{1,0:T(8,128)(2,1)S(1)}, bf16[40,1024]{1,0:T(8,128)(2,1)S(1)}, u32[]{:S(2)}, u32[]{:S(2)}) collective-permute-start(bf16[40,1024]{1,0:T(8,128)(2,1)S(1)} %collective-permute-done.12), channel_id=1, source_target_pairs={{0,4},{1,5},{4,8},{5,9},{8,12},{9,13},{12,14},{13,15},{14,10},{15,... | collective-permute-start | bytes 245768 | tf_op jit(solution)/shard_map/ppermute | solution.py:39
  18.8 4.8 %collective-permute-start.11 = (bf16[40,1024]{1,0:T(8,128)(2,1)S(1)}, bf16[40,1024]{1,0:T(8,128)(2,1)S(1)}, u32[]{:S(2)}, u32[]{:S(2)}) collective-permute-start(bf16[40,1024]{1,0:T(8,128)(2,1)S(1)} %collective-permute-done.10), channel_id=1, source_target_pairs={{0,2},{1,3},{4,0},{5,1},{8,4},{9,5},{12,8},{13,9},{14,12},{15,13},... | collective-permute-start | bytes 245768 | tf_op jit(solution)/shard_map/ppermute | solution.py:40
  20.7 5.0 %collective-permute-start.14 = (bf16[40,1024]{1,0:T(8,128)(2,1)S(1)}, bf16[40,1024]{1,0:T(8,128)(2,1)S(1)}, u32[]{:S(2)}, u32[]{:S(2)}) collective-permute-start(bf16[40,1024]{1,0:T(8,128)(2,1)S(1)} %collective-permute-done.13), channel_id=1, source_target_pairs={{0,4},{1,5},{4,8},{5,9},{8,12},{9,13},{12,14},{13,15},{14,10},{15,... | collective-permute-start | bytes 245768 | tf_op jit(solution)/shard_map/ppermute | solution.py:39
  23.7 4.2 %collective-permute-start.16 = (bf16[20,1024]{1,0:T(8,128)(2,1)S(1)}, bf16[20,1024]{1,0:T(8,128)(2,1)S(1)}, u32[]{:S(2)}, u32[]{:S(2)}) collective-permute-start(bf16[20,1024]{1,0:T(8,128)(2,1)S(1)} %slice.29), channel_id=1, source_target_pairs={{0,2},{1,3},{4,0},{5,1},{8,4},{9,5},{12,8},{13,9},{14,12},{15,13},... | collective-permute-start | bytes 122888 | tf_op jit(solution)/shard_map/ppermute | solution.py:45
  25.8 4.1 %collective-permute-start.15 = (bf16[20,1024]{1,0:T(8,128)(2,1)S(1)}, bf16[20,1024]{1,0:T(8,128)(2,1)S(1)}, u32[]{:S(2)}, u32[]{:S(2)}) collective-permute-start(bf16[20,1024]{1,0:T(8,128)(2,1)S(1)} %slice.28), channel_id=1, source_target_pairs={{0,4},{1,5},{4,8},{5,9},{8,12},{9,13},{12,14},{13,15},{14,10},{15,... | collective-permute-start | bytes 122888 | tf_op jit(solution)/shard_map/ppermute | solution.py:44
  30.0 20.6 %collective-permute-start.17 = (bf16[8,40,1024]{2,1,0:T(8,128)(2,1)S(1)}, bf16[8,40,1024]{2,1,0:T(8,128)(2,1)S(1)}, u32[]{:S(2)}, u32[]{:S(2)}) collective-permute-start(bf16[8,40,1024]{2,1,0:T(8,128)(2,1)S(1)} %bitcast_dynamic-update-slice_fusion.12), channel_id=1, source_target_pairs={{0,1},{1,0},{2,3},{3,2},{4,5},{5,4},{6,7},{7,6},{8,9},{9,8},{10,11... | collective-permute-start | bytes 1966088 | tf_op jit(solution)/shard_map/ppermute | solution.py:61
  30.1 9.2 %collective-permute-start.1 = (bf16[40,3584]{1,0:T(8,128)(2,1)S(1)}, bf16[40,3584]{1,0:T(8,128)(2,1)S(1)}, u32[]{:S(2)}, u32[]{:S(2)}) collective-permute-start(bf16[40,3584]{1,0:T(8,128)(2,1)S(1)} %collective-permute-done), channel_id=1, source_target_pairs={{0,2},{1,3},{4,0},{5,1},{8,4},{9,5},{12,8},{13,9},{14,12},{15,13},... | collective-permute-start | bytes 860168 | tf_op jit(solution)/shard_map/ppermute | solution.py:40
  31.7 9.2 %collective-permute-start.4 = (bf16[40,3584]{1,0:T(8,128)(2,1)S(1)}, bf16[40,3584]{1,0:T(8,128)(2,1)S(1)}, u32[]{:S(2)}, u32[]{:S(2)}) collective-permute-start(bf16[40,3584]{1,0:T(8,128)(2,1)S(1)} %collective-permute-done.3), channel_id=1, source_target_pairs={{0,4},{1,5},{4,8},{5,9},{8,12},{9,13},{12,14},{13,15},{14,10},{15,... | collective-permute-start | bytes 860168 | tf_op jit(solution)/shard_map/ppermute | solution.py:39
  39.3 8.4 %collective-permute-start.2 = (bf16[40,3584]{1,0:T(8,128)(2,1)S(1)}, bf16[40,3584]{1,0:T(8,128)(2,1)S(1)}, u32[]{:S(2)}, u32[]{:S(2)}) collective-permute-start(bf16[40,3584]{1,0:T(8,128)(2,1)S(1)} %collective-permute-done.1), channel_id=1, source_target_pairs={{0,2},{1,3},{4,0},{5,1},{8,4},{9,5},{12,8},{13,9},{14,12},{15,13},... | collective-permute-start | bytes 860168 | tf_op jit(solution)/shard_map/ppermute | solution.py:40
  40.9 8.5 %collective-permute-start.5 = (bf16[40,3584]{1,0:T(8,128)(2,1)S(1)}, bf16[40,3584]{1,0:T(8,128)(2,1)S(1)}, u32[]{:S(2)}, u32[]{:S(2)}) collective-permute-start(bf16[40,3584]{1,0:T(8,128)(2,1)S(1)} %collective-permute-done.4), channel_id=1, source_target_pairs={{0,4},{1,5},{4,8},{5,9},{8,12},{9,13},{12,14},{13,15},{14,10},{15,... | collective-permute-start | bytes 860168 | tf_op jit(solution)/shard_map/ppermute | solution.py:39
  47.7 12.3 %collective-permute-start.7 = (bf16[20,3584]{1,0:T(8,128)(2,1)S(1)}, bf16[20,3584]{1,0:T(8,128)(2,1)S(1)}, u32[]{:S(2)}, u32[]{:S(2)}) collective-permute-start(bf16[20,3584]{1,0:T(8,128)(2,1)S(1)} %slice.27), channel_id=1, source_target_pairs={{0,2},{1,3},{4,0},{5,1},{8,4},{9,5},{12,8},{13,9},{14,12},{15,13},... | collective-permute-start | bytes 430088 | tf_op jit(solution)/shard_map/ppermute | solution.py:45
  50.0 10.0 %collective-permute-start.6 = (bf16[20,3584]{1,0:T(8,128)(2,1)}, bf16[20,3584]{1,0:T(8,128)(2,1)}, u32[]{:S(2)}, u32[]{:S(2)}) collective-permute-start(bf16[20,3584]{1,0:T(8,128)(2,1)} %slice.26), channel_id=1, source_target_pairs={{0,4},{1,5},{4,8},{5,9},{8,12},{9,13},{12,14},{13,15},{14,10},{15,... | collective-permute-start | bytes 430088 | tf_op jit(solution)/shard_map/ppermute | solution.py:44
  57.9 6.0 %collective-permute-start.18 = (bf16[80,512]{1,0:T(8,128)(2,1)S(1)}, bf16[80,512]{1,0:T(8,128)(2,1)S(1)}, u32[]{:S(2)}, u32[]{:S(2)}) collective-permute-start(bf16[80,512]{1,0:T(8,128)(2,1)S(1)} %reshape.34), channel_id=1, source_target_pairs={{0,2},{1,3},{4,0},{5,1},{8,4},{9,5},{12,8},{13,9},{14,12},{15,13},... | collective-permute-start | bytes 245768 | tf_op jit(solution)/shard_map/ppermute | solution.py:40
  59.6 5.9 %collective-permute-start.21 = (bf16[80,512]{1,0:T(8,128)(2,1)S(1)}, bf16[80,512]{1,0:T(8,128)(2,1)S(1)}, u32[]{:S(2)}, u32[]{:S(2)}) collective-permute-start(bf16[80,512]{1,0:T(8,128)(2,1)S(1)} %reshape.34), channel_id=1, source_target_pairs={{0,4},{1,5},{4,8},{5,9},{8,12},{9,13},{12,14},{13,15},{14,10},{15,... | collective-permute-start | bytes 245768 | tf_op jit(solution)/shard_map/ppermute | solution.py:39
  63.9 23.9 %collective-permute-start.8 = (bf16[8,40,3584]{2,1,0:T(8,128)(2,1)}, bf16[8,40,3584]{2,1,0:T(8,128)(2,1)}, u32[]{:S(2)}, u32[]{:S(2)}) collective-permute-start(bf16[8,40,3584]{2,1,0:T(8,128)(2,1)} %bitcast_dynamic-update-slice_fusion), channel_id=1, source_target_pairs={{0,1},{1,0},{2,3},{3,2},{4,5},{5,4},{6,7},{7,6},{8,9},{9,8},{10,11... | collective-permute-start | bytes 6881288 | tf_op jit(solution)/shard_map/ppermute | solution.py:61
  63.9 4.9 %collective-permute-start.19 = (bf16[80,512]{1,0:T(8,128)(2,1)S(1)}, bf16[80,512]{1,0:T(8,128)(2,1)S(1)}, u32[]{:S(2)}, u32[]{:S(2)}) collective-permute-start(bf16[80,512]{1,0:T(8,128)(2,1)S(1)} %collective-permute-done.18), channel_id=1, source_target_pairs={{0,2},{1,3},{4,0},{5,1},{8,4},{9,5},{12,8},{13,9},{14,12},{15,13},... | collective-permute-start | bytes 245768 | tf_op jit(solution)/shard_map/ppermute | solution.py:40
  65.5 4.9 %collective-permute-start.22 = (bf16[80,512]{1,0:T(8,128)(2,1)S(1)}, bf16[80,512]{1,0:T(8,128)(2,1)S(1)}, u32[]{:S(2)}, u32[]{:S(2)}) collective-permute-start(bf16[80,512]{1,0:T(8,128)(2,1)S(1)} %collective-permute-done.21), channel_id=1, source_target_pairs={{0,4},{1,5},{4,8},{5,9},{8,12},{9,13},{12,14},{13,15},{14,10},{15,... | collective-permute-start | bytes 245768 | tf_op jit(solution)/shard_map/ppermute | solution.py:39
  68.8 4.4 %collective-permute-start.20 = (bf16[80,512]{1,0:T(8,128)(2,1)S(1)}, bf16[80,512]{1,0:T(8,128)(2,1)S(1)}, u32[]{:S(2)}, u32[]{:S(2)}) collective-permute-start(bf16[80,512]{1,0:T(8,128)(2,1)S(1)} %collective-permute-done.19), channel_id=1, source_target_pairs={{0,2},{1,3},{4,0},{5,1},{8,4},{9,5},{12,8},{13,9},{14,12},{15,13},... | collective-permute-start | bytes 245768 | tf_op jit(solution)/shard_map/ppermute | solution.py:40
  70.4 4.4 %collective-permute-start.23 = (bf16[80,512]{1,0:T(8,128)(2,1)S(1)}, bf16[80,512]{1,0:T(8,128)(2,1)S(1)}, u32[]{:S(2)}, u32[]{:S(2)}) collective-permute-start(bf16[80,512]{1,0:T(8,128)(2,1)S(1)} %collective-permute-done.22), channel_id=1, source_target_pairs={{0,4},{1,5},{4,8},{5,9},{8,12},{9,13},{12,14},{13,15},{14,10},{15,... | collective-permute-start | bytes 245768 | tf_op jit(solution)/shard_map/ppermute | solution.py:39
  (7 other events, 47.2 us)

commit v2 on v0

v2 whole, which is shorter than its diff:
```python
import functools

import jax
import jax.numpy as jnp
from jax import lax
from jax.experimental import pallas as pl
from jax.experimental.pallas import tpu as pltpu
from jax.sharding import PartitionSpec as P

CORES = 2
PAIR = 2
SUBLANES = 8
CHUNKS = 2
VMEM = pl.BlockSpec(memory_space=pltpu.VMEM)
SMEM = pl.BlockSpec(memory_space=pltpu.SMEM)


def along(devices, by):
    each = CORES * PAIR
    return [(d, (d + by * each) % devices) for d in range(devices)]


def across(devices):
    return [(d, d ^ CORES) for d in range(devices)]


def swap(devices):
    return [(d, d ^ 1) for d in range(devices)]


def send(block, pairs):
    return lax.ppermute(block, "wide", pairs)


def origin(me, devices, step, other_chip, other_core):
    each = CORES * PAIR
    pair = lax.rem(me // each + devices // each - step, devices // each)
    chip = lax.rem(me // CORES, PAIR)
    core = lax.rem(me, CORES)
    if other_chip:
        chip = 1 - chip
    if other_core:
        core = 1 - core
    return pair * PAIR + chip, core


def repeat(times, body, carry=None, loop=False):
    if loop or times > SUBLANES:
        return lax.fori_loop(0, times, body, carry)
    for step in range(times):
        carry = body(step, carry)
    return carry


def unfold_store(rows, slot, block):
    height = block.shape[0]
    at = pl.ds(pl.multiple_of(slot * height, SUBLANES), height)
    for tile in range(rows.shape[0]):
        rows[tile, at, :] = block[:, tile * 128 : (tile + 1) * 128].astype(jnp.float32)


def unfold_load(rows, fold, tokens):
    tiles = [rows[tile, pl.ds(fold, tokens, stride=SUBLANES), :] for tile in range(rows.shape[0])]
    return jnp.concatenate([tile.astype(jnp.bfloat16) for tile in tiles], 1)


def rotate_out_kernel(tokens, me_ref, z_ref, y_ref, cz_ref, cy_ref, basis_ref, sq_ref, rows):
    steps, height, width = z_ref.shape
    devices = steps * CORES * PAIR
    me = me_ref[0]
    for ref, chip_bit, core_bit in ((z_ref, 0, 0), (y_ref, 1, 0), (cz_ref, 0, 1), (cy_ref, 1, 1)):

        def put(step, _, ref=ref, chip_bit=chip_bit, core_bit=core_bit):
            chip, core = origin(me, devices, step, chip_bit, core_bit)
            unfold_store(rows, core * (devices // CORES) + chip, ref[step])

        repeat(steps, put)

    def add(fold, total):
        left = unfold_load(rows, fold, devices * tokens)
        right = basis_ref[pl.ds(pl.multiple_of(fold * width, 128), width), :]
        return total + jnp.dot(left, right, preferred_element_type=jnp.float32)

    total = repeat(SUBLANES, add, jnp.zeros(sq_ref.shape, jnp.float32), steps > SUBLANES)
    sq_ref[...] = (total * total).astype(sq_ref.dtype)


def rotate_out(tokens, me, z, y, cz, cy, basis):
    steps, height, width = z.shape
    total = steps * CORES * PAIR * tokens
    return pl.pallas_call(
        functools.partial(rotate_out_kernel, tokens),
        out_shape=jax.ShapeDtypeStruct((total, basis.shape[1]), jnp.bfloat16),
        in_specs=[SMEM] + [VMEM] * 5,
        out_specs=VMEM,
        scratch_shapes=[pltpu.VMEM((width // 128, total * SUBLANES, 128), jnp.float32)],
        compiler_params=pltpu.CompilerParams(vmem_limit_bytes=48 * 2**20),
        cost_estimate=pl.CostEstimate(
            flops=2 * total * basis.shape[0] * basis.shape[1], bytes_accessed=2 * basis.size, transcendentals=0
        ),
        name="rotate_out",
    )(me, z, y, cz, cy, basis)


def rotate_in_kernel(tokens, steps, me_ref, *refs):
    devices = steps * CORES * PAIR
    chips = devices // CORES
    blocks = refs[: CHUNKS * chips]
    mine_ref, theirs_ref, sq_mine_ref, sq_theirs_ref, rows = refs[CHUNKS * chips :]
    height, width = blocks[0].shape
    me = me_ref[0]
    total = jnp.zeros((2 * mine_ref.shape[0], chips * tokens), jnp.float32)
    for chunk in range(CHUNKS):
        for step in range(steps):
            for bit in range(PAIR):
                chip, _ = origin(me, devices, step, bit, 0)
                unfold_store(rows, chip, blocks[(chunk * steps + step) * PAIR + bit][...])

        def add(fold, total, chunk=chunk):
            at = pl.ds(pl.multiple_of((chunk * SUBLANES + fold) * width, 128), width)
            right = unfold_load(rows, fold, chips * tokens)
            left = jnp.concatenate([mine_ref[:, at], theirs_ref[:, at]])
            return total + lax.dot_general(
                left, right, (((1,), (1,)), ((), ())), preferred_element_type=jnp.float32
            )

        total = repeat(SUBLANES, add, total, steps > SUBLANES)
    squares = (total * total).astype(jnp.bfloat16)
    sq_mine_ref[...] = squares[: mine_ref.shape[0]]
    sq_theirs_ref[...] = squares[mine_ref.shape[0] :]


def rotate_in(tokens, steps, me, blocks, mine, theirs):
    chips = steps * PAIR
    height, width = blocks[0].shape
    out = jax.ShapeDtypeStruct((mine.shape[0], chips * tokens), jnp.bfloat16)
    return pl.pallas_call(
        functools.partial(rotate_in_kernel, tokens, steps),
        out_shape=(out, out),
        in_specs=[SMEM] + [VMEM] * (len(blocks) + 2),
        out_specs=(VMEM, VMEM),
        scratch_shapes=[pltpu.VMEM((width // 128, chips * height, 128), jnp.float32)],
        compiler_params=pltpu.CompilerParams(vmem_limit_bytes=48 * 2**20),
        cost_estimate=pl.CostEstimate(
            flops=4 * chips * tokens * mine.size, bytes_accessed=4 * mine.size, transcendentals=0
        ),
        name="rotate_in",
    )(me, *blocks, mine, theirs)


def combine_kernel(me_ref, own_ref, other_ref, z_ref, y_ref, cz_ref, cy_ref, out_ref):
    steps, total_tokens, width = z_ref.shape
    devices = steps * CORES * PAIR
    me = me_ref[0]
    own, other = own_ref[...].astype(jnp.float32), other_ref[...].astype(jnp.float32)
    first = lax.rem(me, CORES) == 0
    left = jnp.concatenate([jnp.where(first, own, other), jnp.where(first, other, own)], 1).astype(jnp.bfloat16)
    for ref, chip_bit, core_bit in ((z_ref, 0, 0), (y_ref, 1, 0), (cz_ref, 0, 1), (cy_ref, 1, 1)):

        def put(step, _, ref=ref, chip_bit=chip_bit, core_bit=core_bit):
            chip, core = origin(me, devices, step, chip_bit, core_bit)
            at = pl.multiple_of((chip * CORES + core) * width, 128)
            total = jnp.dot(left, ref[step], preferred_element_type=jnp.float32)
            out_ref[:, pl.ds(at, width)] = (total / total_tokens).astype(out_ref.dtype)

        repeat(steps, put)


def combine(me, own, other, z, y, cz, cy):
    steps, total_tokens, width = z.shape
    features = steps * CORES * PAIR * width
    return pl.pallas_call(
        combine_kernel,
        out_shape=jax.ShapeDtypeStruct((own.shape[0], features), jnp.bfloat16),
        in_specs=[SMEM] + [VMEM] * 6,
        out_specs=VMEM,
        compiler_params=pltpu.CompilerParams(vmem_limit_bytes=48 * 2**20),
        cost_estimate=pl.CostEstimate(
            flops=2 * own.shape[0] * total_tokens * features, bytes_accessed=4 * own.shape[0] * features, transcendentals=0
        ),
        name="combine",
    )(me, own, other, z, y, cz, cy)


def local(acts, grads, basis_in, basis_out):
    devices = lax.axis_size("wide")
    steps = devices // (CORES * PAIR)
    tokens = acts.shape[0]
    me = lax.axis_index("wide").astype(jnp.int32).reshape(1)

    def everywhere(block):
        z = jnp.stack([block] + [send(block, along(devices, step)) for step in range(1, steps)])
        y = send(z, across(devices))
        return z, y, send(z, swap(devices)), send(y, swap(devices))

    block = grads.reshape(tokens * SUBLANES, -1)
    block, acts, basis_in = lax.optimization_barrier((block, acts, basis_in))
    sq_out = rotate_out(tokens, me, *everywhere(block), basis_out)

    mine = basis_in.T
    theirs = send(mine, swap(devices))
    blocks = []
    width = acts.shape[1] // CHUNKS
    for chunk in range(CHUNKS):
        block = acts[:, chunk * width : (chunk + 1) * width].reshape(tokens * SUBLANES, -1)
        for step in range(steps):
            came = send(block, along(devices, step)) if step else block
            blocks += [came, send(came, across(devices))]
    own, given = rotate_in(tokens, steps, me, blocks, mine, theirs)
    other = send(given, swap(devices))
    return combine(me, own, other, *everywhere(sq_out))


def solution(mesh):
    return jax.shard_map(
        local,
        mesh=mesh,
        in_specs=(
            P(("groups", "wide"), None),
            P(("groups", "wide"), None),
            P("groups", "wide"),
            P("groups", "wide"),
        ),
        out_specs=P(("groups", "wide"), None),
        check_vma=False,
    )
```

time: 177 us -> 94.7 us (0.54)
  waiting for transfers between devices: 142 us -> 47.4 us
  starting transfers between devices: 0.08 us -> 30.4 us
  Pallas kernels: 0 us -> 14.9 us
  matrix products: 14.3 us -> 0 us
  between operations: 13.1 us -> 0.11 us
  local copies, waits for them, and re-layouts: 7.44 us -> 1.61 us
    all_gather x3 -> x0, waiting for transfers between devices: 140 us -> none  [the longest x1 61.9 us: local(): lax.all_gather(acts, 'wide', axis=0, tiled=True)]
    ppermute x0 -> x28, waiting for transfers between devices: none -> 47.4 us  [send(): return lax.ppermute(block, 'wide', pairs)]
    ppermute x0 -> x28, starting transfers between devices: none -> 30.4 us  [send(): return lax.ppermute(block, 'wide', pairs)]
    pallas_call x0 -> x3, Pallas kernels: none -> 14.9 us  [the longest x1 8.07 us: rotate_in(): pl.pallas_call(functools.partial(rotate_in_kernel, tokens, steps), out_sh...]
    dot_general x2 -> x0, matrix products: 14.3 us -> none  [the longest x1 8.68 us: local(): jnp.dot(sq_in, lax.all_gather(sq_out, 'wide', axis=1, tiled=True), prefer...]
    unnamed x2, local copies, waits for them, and re-layouts: 7.44 us -> 0.01 us
  transfers between devices with their start and end apart: 3 -> 28, of which waited for: 3 -> 15; matrix products, arithmetic and copies ran while one was open for 7% -> 1% of each run, Pallas kernels for 0% -> 14%
where the time goes in v2:
time: 94.7 us; the launch traced here: 94.5 us
  waiting for transfers between devices  47.4 us (50%)
  starting transfers between devices  30.4 us (32%)
  Pallas kernels  14.9 us (16%)
  local copies, waits for them, and re-layouts  1.61 us (2%)
    ppermute x28, waiting for transfers between devices, send(): return lax.ppermute(block, 'wide', pairs)  47.4 us
    ppermute x28, starting transfers between devices, send(): return lax.ppermute(block, 'wide', pairs)  30.4 us
    pallas_call x1, Pallas kernels, rotate_in(): pl.pallas_call(functools.partial(rotate_in_kernel, tokens, steps), out_sh...  8.07 us
    pallas_call x1, Pallas kernels, rotate_out(): pl.pallas_call(functools.partial(rotate_out_kernel, tokens), out_shape=ja...  5.09 us
  transfers between devices with their start and end apart: 28, of which 15 were waited for; matrix products, arithmetic and copies ran while one was open for 1% of the time, Pallas kernels for 14%

profile of v2, /device:TPU:0, one launch (start us, length us, event | category | flops | bytes accessed | tf_op | source)
XLA Modules:
  0.0 94.5 jit_solution(8889511484777901118)
XLA Ops:
  1.6 4.7 %collective-permute-start.18 = (bf16[40,1024]{1,0:T(8,128)(2,1)S(1)}, bf16[40,1024]{1,0:T(8,128)(2,1)S(1)}, u32[]{:S(2)}, u32[]{:S(2)}) collective-permute-start(bf16[40,1024]{1,0:T(8,128)(2,1)S(1)} %reshape.13), channel_id=1, source_target_pairs={{0,12},{1,13},{2,14},{3,15},{4,0},{5,1},{6,2},{7,3},{8,4},{9,5},{1... | collective-permute-start | bytes 245768 | tf_op jit(solution)/shard_map/ppermute | solution.py:32
  7.3 1.8 %collective-permute-done.18 = bf16[40,1024]{1,0:T(8,128)(2,1)S(1)} collective-permute-done((bf16[40,1024]{1,0:T(8,128)(2,1)S(1)}, bf16[40,1024]{1,0:T(8,128)(2,1)S(1)}, u32[]{:S(2)}, u32[]{:S(2)}) %collective-permute-start.18) | collective-permute-done | bytes 81952 | tf_op jit(solution)/shard_map/ppermute | solution.py:32
  9.1 5.7 %collective-permute-done.17 = bf16[40,1024]{1,0:T(8,128)(2,1)S(1)} collective-permute-done((bf16[40,1024]{1,0:T(8,128)(2,1)S(1)}, bf16[40,1024]{1,0:T(8,128)(2,1)S(1)}, u32[]{:S(2)}, u32[]{:S(2)}) %collective-permute-start.17) | collective-permute-done | bytes 81952 | tf_op jit(solution)/shard_map/ppermute | solution.py:32
  14.8 1.6 %collective-permute-start.19 = (bf16[4,40,1024]{2,1,0:T(8,128)(2,1)S(1)}, bf16[4,40,1024]{2,1,0:T(8,128)(2,1)S(1)}, u32[]{:S(2)}, u32[]{:S(2)}) collective-permute-start(bf16[4,40,1024]{2,1,0:T(8,128)(2,1)S(1)} %pad_maximum_fusion.z_ref), channel_id=1, source_target_pairs={{0,2},{1,3},{2,0},{3,1},{4,6},{5,7},{6,4},{7,5},{8,10},{9,11},{10,... | collective-permute-start | bytes 983048 | tf_op jit(solution)/shard_map/ppermute | solution.py:32
  16.4 8.1 %collective-permute-done.19.y_ref = bf16[4,40,1024]{2,1,0:T(8,128)(2,1)S(1)} collective-permute-done((bf16[4,40,1024]{2,1,0:T(8,128)(2,1)S(1)}, bf16[4,40,1024]{2,1,0:T(8,128)(2,1)S(1)}, u32[]{:S(2)}, u32[]{:S(2)}) %collective-permute-start.19) | collective-permute-done | bytes 327712 | tf_op jit(solution)/shard_map/ppermute | solution.py:32
  24.5 1.6 %collective-permute-done.21.cy_ref = bf16[4,40,1024]{2,1,0:T(8,128)(2,1)S(1)} collective-permute-done((bf16[4,40,1024]{2,1,0:T(8,128)(2,1)S(1)}, bf16[4,40,1024]{2,1,0:T(8,128)(2,1)S(1)}, u32[]{:S(2)}, u32[]{:S(2)}) %collective-permute-start.21) | collective-permute-done | bytes 327712 | tf_op jit(solution)/shard_map/ppermute | solution.py:32
  26.1 5.1 %rotate_out.1 = bf16[80,512]{1,0:T(8,128)(2,1)S(1)} custom-call(s32[1]{0:T(128)} %bitcast.me_ref, bf16[4,40,1024]{2,1,0:T(8,128)(2,1)S(1)} %pad_maximum_fusion.z_ref, bf16[4,40,1024]{2,1,0:T(8,128)(2,1)S(1)} %collective-permute-done.19.y_ref, bf16[4,40,1024]{2,1,0:T(8,128)(2,1)S(1)} %collective-permute-done.20.cz_ref, ...), custom_call_target="tpu_custom_call" | custom-call | flops 671088640 | bytes 8388608 | tf_op jit(solution)/shard_map/rotate_out/pallas_call | solution.py:91
  32.4 1.9 %collective-permute-start.22 = (bf16[80,512]{1,0:T(8,128)(2,1)S(1)}, bf16[80,512]{1,0:T(8,128)(2,1)S(1)}, u32[]{:S(2)}, u32[]{:S(2)}) collective-permute-start(bf16[80,512]{1,0:T(8,128)(2,1)S(1)} %rotate_out.1), channel_id=1, source_target_pairs={{0,4},{1,5},{2,6},{3,7},{4,8},{5,9},{6,10},{7,11},{8,12},{9,13},{1... | collective-permute-start | bytes 245768 | tf_op jit(solution)/shard_map/ppermute | solution.py:32
  34.7 1.6 %collective-permute-start = (bf16[40,1792]{1,0:T(8,128)(2,1)S(1)}, bf16[40,1792]{1,0:T(8,128)(2,1)S(1)}, u32[]{:S(2)}, u32[]{:S(2)}) collective-permute-start(bf16[40,1792]{1,0:T(8,128)(2,1)S(1)} %reshape.14.refs_0_), channel_id=1, source_target_pairs={{0,2},{1,3},{2,0},{3,1},{4,6},{5,7},{6,4},{7,5},{8,10},{9,11},{10,... | collective-permute-start | bytes 430088 | tf_op jit(solution)/shard_map/ppermute | solution.py:32
  36.9 8.8 %collective-permute-done.23 = bf16[80,512]{1,0:T(8,128)(2,1)S(1)} collective-permute-done((bf16[80,512]{1,0:T(8,128)(2,1)S(1)}, bf16[80,512]{1,0:T(8,128)(2,1)S(1)}, u32[]{:S(2)}, u32[]{:S(2)}) %collective-permute-start.23) | collective-permute-done | bytes 81952 | tf_op jit(solution)/shard_map/ppermute | solution.py:32
  45.8 1.6 %collective-permute-start.25 = (bf16[4,80,512]{2,1,0:T(8,128)(2,1)S(1)}, bf16[4,80,512]{2,1,0:T(8,128)(2,1)S(1)}, u32[]{:S(2)}, u32[]{:S(2)}) collective-permute-start(bf16[4,80,512]{2,1,0:T(8,128)(2,1)S(1)} %pad_maximum_fusion.1.z_ref), channel_id=1, source_target_pairs={{0,2},{1,3},{2,0},{3,1},{4,6},{5,7},{6,4},{7,5},{8,10},{9,11},{10,... | collective-permute-start | bytes 983048 | tf_op jit(solution)/shard_map/ppermute | solution.py:32
  48.2 3.6 %collective-permute-done.3.refs_4_ = bf16[40,1792]{1,0:T(8,128)(2,1)S(1)} collective-permute-done((bf16[40,1792]{1,0:T(8,128)(2,1)S(1)}, bf16[40,1792]{1,0:T(8,128)(2,1)S(1)}, u32[]{:S(2)}, u32[]{:S(2)}) %collective-permute-start.3) | collective-permute-done | bytes 143392 | tf_op jit(solution)/shard_map/ppermute | solution.py:32
  52.6 3.4 %collective-permute-start.10 = (bf16[40,1792]{1,0:T(8,128)(2,1)S(1)}, bf16[40,1792]{1,0:T(8,128)(2,1)S(1)}, u32[]{:S(2)}, u32[]{:S(2)}) collective-permute-start(bf16[40,1792]{1,0:T(8,128)(2,1)S(1)} %reshape.15.refs_8_), channel_id=1, source_target_pairs={{0,8},{1,9},{2,10},{3,11},{4,12},{5,13},{6,14},{7,15},{8,0},{9,1},... | collective-permute-start | bytes 430088 | tf_op jit(solution)/shard_map/ppermute | solution.py:32
  56.0 2.9 %collective-permute-start.12 = (bf16[40,1792]{1,0:T(8,128)(2,1)S(1)}, bf16[40,1792]{1,0:T(8,128)(2,1)S(1)}, u32[]{:S(2)}, u32[]{:S(2)}) collective-permute-start(bf16[40,1792]{1,0:T(8,128)(2,1)S(1)} %reshape.15.refs_8_), channel_id=1, source_target_pairs={{0,12},{1,13},{2,14},{3,15},{4,0},{5,1},{6,2},{7,3},{8,4},{9,5},{1... | collective-permute-start | bytes 430088 | tf_op jit(solution)/shard_map/ppermute | solution.py:32
  61.8 3.7 %collective-permute-done.10.refs_12_ = bf16[40,1792]{1,0:T(8,128)(2,1)S(1)} collective-permute-done((bf16[40,1792]{1,0:T(8,128)(2,1)S(1)}, bf16[40,1792]{1,0:T(8,128)(2,1)S(1)}, u32[]{:S(2)}, u32[]{:S(2)}) %collective-permute-start.10) | collective-permute-done | bytes 143392 | tf_op jit(solution)/shard_map/ppermute | solution.py:32
  67.6 1.5 %collective-permute-start.9 = (bf16[40,1792]{1,0:T(8,128)(2,1)S(1)}, bf16[40,1792]{1,0:T(8,128)(2,1)S(1)}, u32[]{:S(2)}, u32[]{:S(2)}) collective-permute-start(bf16[40,1792]{1,0:T(8,128)(2,1)S(1)} %collective-permute-done.8.refs_10_), channel_id=1, source_target_pairs={{0,2},{1,3},{2,0},{3,1},{4,6},{5,7},{6,4},{7,5},{8,10},{9,11},{10,... | collective-permute-start | bytes 430088 | tf_op jit(solution)/shard_map/ppermute | solution.py:32
  69.1 3.1 %collective-permute-done.4.refs_5_ = bf16[40,1792]{1,0:T(8,128)(2,1)S(1)} collective-permute-done((bf16[40,1792]{1,0:T(8,128)(2,1)S(1)}, bf16[40,1792]{1,0:T(8,128)(2,1)S(1)}, u32[]{:S(2)}, u32[]{:S(2)}) %collective-permute-start.4) | collective-permute-done | bytes 143392 | tf_op jit(solution)/shard_map/ppermute | solution.py:32
  72.7 2.6 %collective-permute-done.6.refs_7_ = bf16[40,1792]{1,0:T(8,128)(2,1)S(1)} collective-permute-done((bf16[40,1792]{1,0:T(8,128)(2,1)S(1)}, bf16[40,1792]{1,0:T(8,128)(2,1)S(1)}, u32[]{:S(2)}, u32[]{:S(2)}) %collective-permute-start.6) | collective-permute-done | bytes 143392 | tf_op jit(solution)/shard_map/ppermute | solution.py:32
  75.3 1.5 %collective-permute-start.11 = (bf16[40,1792]{1,0:T(8,128)(2,1)S(1)}, bf16[40,1792]{1,0:T(8,128)(2,1)S(1)}, u32[]{:S(2)}, u32[]{:S(2)}) collective-permute-start(bf16[40,1792]{1,0:T(8,128)(2,1)S(1)} %collective-permute-done.10.refs_12_), channel_id=1, source_target_pairs={{0,2},{1,3},{2,0},{3,1},{4,6},{5,7},{6,4},{7,5},{8,10},{9,11},{10,... | collective-permute-start | bytes 430088 | tf_op jit(solution)/shard_map/ppermute | solution.py:32
  76.8 1.6 %collective-permute-done.9.refs_11_ = bf16[40,1792]{1,0:T(8,128)(2,1)S(1)} collective-permute-done((bf16[40,1792]{1,0:T(8,128)(2,1)S(1)}, bf16[40,1792]{1,0:T(8,128)(2,1)S(1)}, u32[]{:S(2)}, u32[]{:S(2)}) %collective-permute-start.9) | collective-permute-done | bytes 143392 | tf_op jit(solution)/shard_map/ppermute | solution.py:32
  79.9 1.9 %collective-permute-done.11.refs_13_ = bf16[40,1792]{1,0:T(8,128)(2,1)S(1)} collective-permute-done((bf16[40,1792]{1,0:T(8,128)(2,1)S(1)}, bf16[40,1792]{1,0:T(8,128)(2,1)S(1)}, u32[]{:S(2)}, u32[]{:S(2)}) %collective-permute-start.11) | collective-permute-done | bytes 143392 | tf_op jit(solution)/shard_map/ppermute | solution.py:32
  81.8 1.7 %collective-permute-done.13.refs_15_ = bf16[40,1792]{1,0:T(8,128)(2,1)S(1)} collective-permute-done((bf16[40,1792]{1,0:T(8,128)(2,1)S(1)}, bf16[40,1792]{1,0:T(8,128)(2,1)S(1)}, u32[]{:S(2)}, u32[]{:S(2)}) %collective-permute-start.13) | collective-permute-done | bytes 143392 | tf_op jit(solution)/shard_map/ppermute | solution.py:32
  83.5 8.1 %rotate_in.1 = (bf16[96,40]{1,0:T(8,128)(2,1)S(1)}, bf16[96,40]{1,0:T(8,128)(2,1)S(1)}) custom-call(s32[1]{0:T(128)} %bitcast.me_ref, bf16[40,1792]{1,0:T(8,128)(2,1)S(1)} %reshape.14.refs_0_, bf16[40,1792]{1,0:T(8,128)(2,1)S(1)} %collective-permute-done.refs_1_, bf16[40,1792]{1,0:T(8,128)(2,1)S(1)} %collective-permute-done.1.refs_2_, ...), custom_call_target="tpu_custom_call" | custom-call | flops 440401920 | bytes 11010048 | tf_op jit(solution)/shard_map/rotate_in/pallas_call | solution.py:137
  92.8 1.8 %combine.1 = bf16[96,8192]{1,0:T(8,128)(2,1)} custom-call(s32[1]{0:T(128)} %bitcast.me_ref, bf16[96,40]{1,0:T(8,128)(2,1)S(1)} %get-tuple-element.12.own_ref, bf16[96,40]{1,0:T(8,128)(2,1)S(1)} %collective-permute-done.15.other_ref, bf16[4,80,512]{2,1,0:T(8,128)(2,1)S(1)} %pad_maximum_fusion.1.z_ref, bf16[4,80,512]{2,1,0:T(8,128)(2,1)S(1)} %collective-permute-done.25.y_ref, ...), custom_call_target="tpu_custom_call" | custom-call | flops 125829120 | bytes 3145728 | tf_op jit(solution)/shard_map/combine/pallas_call | solution.py:172
  (43 shorter events, 14.8 us)
Async XLA Ops:
  1.1 82.3 %collective-permute-start.14 = (bf16[96,28672]{1,0:T(8,128)(2,1)}, bf16[96,28672]{1,0:T(8,128)(2,1)}, u32[]{:S(2)}, u32[]{:S(2)}) collective-permute-start(bf16[96,28672]{1,0:T(8,128)(2,1)} %bitcast.11), channel_id=1, source_target_pairs={{0,1},{1,0},{2,3},{3,2},{4,5},{5,4},{6,7},{7,6},{8,9},{9,8},{10,11... | collective-permute-start | bytes 16515080 | tf_op jit(solution)/shard_map/ppermute | solution.py:32
  1.6 7.5 %collective-permute-start.18 = (bf16[40,1024]{1,0:T(8,128)(2,1)S(1)}, bf16[40,1024]{1,0:T(8,128)(2,1)S(1)}, u32[]{:S(2)}, u32[]{:S(2)}) collective-permute-start(bf16[40,1024]{1,0:T(8,128)(2,1)S(1)} %reshape.13), channel_id=1, source_target_pairs={{0,12},{1,13},{2,14},{3,15},{4,0},{5,1},{6,2},{7,3},{8,4},{9,5},{1... | collective-permute-start | bytes 245768 | tf_op jit(solution)/shard_map/ppermute | solution.py:32
  6.3 8.5 %collective-permute-start.17 = (bf16[40,1024]{1,0:T(8,128)(2,1)S(1)}, bf16[40,1024]{1,0:T(8,128)(2,1)S(1)}, u32[]{:S(2)}, u32[]{:S(2)}) collective-permute-start(bf16[40,1024]{1,0:T(8,128)(2,1)S(1)} %reshape.13), channel_id=1, source_target_pairs={{0,8},{1,9},{2,10},{3,11},{4,12},{5,13},{6,14},{7,15},{8,0},{9,1},... | collective-permute-start | bytes 245768 | tf_op jit(solution)/shard_map/ppermute | solution.py:32
  6.3 8.5 %collective-permute-start.16 = (bf16[40,1024]{1,0:T(8,128)(2,1)S(1)}, bf16[40,1024]{1,0:T(8,128)(2,1)S(1)}, u32[]{:S(2)}, u32[]{:S(2)}) collective-permute-start(bf16[40,1024]{1,0:T(8,128)(2,1)S(1)} %reshape.13), channel_id=1, source_target_pairs={{0,4},{1,5},{2,6},{3,7},{4,8},{5,9},{6,10},{7,11},{8,12},{9,13},{1... | collective-permute-start | bytes 245768 | tf_op jit(solution)/shard_map/ppermute | solution.py:32
  14.8 9.7 %collective-permute-start.19 = (bf16[4,40,1024]{2,1,0:T(8,128)(2,1)S(1)}, bf16[4,40,1024]{2,1,0:T(8,128)(2,1)S(1)}, u32[]{:S(2)}, u32[]{:S(2)}) collective-permute-start(bf16[4,40,1024]{2,1,0:T(8,128)(2,1)S(1)} %pad_maximum_fusion.z_ref), channel_id=1, source_target_pairs={{0,2},{1,3},{2,0},{3,1},{4,6},{5,7},{6,4},{7,5},{8,10},{9,11},{10,... | collective-permute-start | bytes 983048 | tf_op jit(solution)/shard_map/ppermute | solution.py:32
  16.4 8.1 %collective-permute-start.20 = (bf16[4,40,1024]{2,1,0:T(8,128)(2,1)S(1)}, bf16[4,40,1024]{2,1,0:T(8,128)(2,1)S(1)}, u32[]{:S(2)}, u32[]{:S(2)}) collective-permute-start(bf16[4,40,1024]{2,1,0:T(8,128)(2,1)S(1)} %pad_maximum_fusion.z_ref), channel_id=1, source_target_pairs={{0,1},{1,0},{2,3},{3,2},{4,5},{5,4},{6,7},{7,6},{8,9},{9,8},{10,11... | collective-permute-start | bytes 983048 | tf_op jit(solution)/shard_map/ppermute | solution.py:32
  31.5 14.2 %collective-permute-start.23 = (bf16[80,512]{1,0:T(8,128)(2,1)S(1)}, bf16[80,512]{1,0:T(8,128)(2,1)S(1)}, u32[]{:S(2)}, u32[]{:S(2)}) collective-permute-start(bf16[80,512]{1,0:T(8,128)(2,1)S(1)} %rotate_out.1), channel_id=1, source_target_pairs={{0,8},{1,9},{2,10},{3,11},{4,12},{5,13},{6,14},{7,15},{8,0},{9,1},... | collective-permute-start | bytes 245768 | tf_op jit(solution)/shard_map/ppermute | solution.py:32
  32.4 13.3 %collective-permute-start.22 = (bf16[80,512]{1,0:T(8,128)(2,1)S(1)}, bf16[80,512]{1,0:T(8,128)(2,1)S(1)}, u32[]{:S(2)}, u32[]{:S(2)}) collective-permute-start(bf16[80,512]{1,0:T(8,128)(2,1)S(1)} %rotate_out.1), channel_id=1, source_target_pairs={{0,4},{1,5},{2,6},{3,7},{4,8},{5,9},{6,10},{7,11},{8,12},{9,13},{1... | collective-permute-start | bytes 245768 | tf_op jit(solution)/shard_map/ppermute | solution.py:32
  34.7 11.1 %collective-permute-start = (bf16[40,1792]{1,0:T(8,128)(2,1)S(1)}, bf16[40,1792]{1,0:T(8,128)(2,1)S(1)}, u32[]{:S(2)}, u32[]{:S(2)}) collective-permute-start(bf16[40,1792]{1,0:T(8,128)(2,1)S(1)} %reshape.14.refs_0_), channel_id=1, source_target_pairs={{0,2},{1,3},{2,0},{3,1},{4,6},{5,7},{6,4},{7,5},{8,10},{9,11},{10,... | collective-permute-start | bytes 430088 | tf_op jit(solution)/shard_map/ppermute | solution.py:32
  36.9 10.7 %collective-permute-start.1 = (bf16[40,1792]{1,0:T(8,128)(2,1)S(1)}, bf16[40,1792]{1,0:T(8,128)(2,1)S(1)}, u32[]{:S(2)}, u32[]{:S(2)}) collective-permute-start(bf16[40,1792]{1,0:T(8,128)(2,1)S(1)} %reshape.14.refs_0_), channel_id=1, source_target_pairs={{0,4},{1,5},{2,6},{3,7},{4,8},{5,9},{6,10},{7,11},{8,12},{9,13},{1... | collective-permute-start | bytes 430088 | tf_op jit(solution)/shard_map/ppermute | solution.py:32
  45.7 6.1 %collective-permute-start.3 = (bf16[40,1792]{1,0:T(8,128)(2,1)S(1)}, bf16[40,1792]{1,0:T(8,128)(2,1)S(1)}, u32[]{:S(2)}, u32[]{:S(2)}) collective-permute-start(bf16[40,1792]{1,0:T(8,128)(2,1)S(1)} %reshape.14.refs_0_), channel_id=1, source_target_pairs={{0,8},{1,9},{2,10},{3,11},{4,12},{5,13},{6,14},{7,15},{8,0},{9,1},... | collective-permute-start | bytes 430088 | tf_op jit(solution)/shard_map/ppermute | solution.py:32
  45.7 6.9 %collective-permute-start.5 = (bf16[40,1792]{1,0:T(8,128)(2,1)S(1)}, bf16[40,1792]{1,0:T(8,128)(2,1)S(1)}, u32[]{:S(2)}, u32[]{:S(2)}) collective-permute-start(bf16[40,1792]{1,0:T(8,128)(2,1)S(1)} %reshape.14.refs_0_), channel_id=1, source_target_pairs={{0,12},{1,13},{2,14},{3,15},{4,0},{5,1},{6,2},{7,3},{8,4},{9,5},{1... | collective-permute-start | bytes 430088 | tf_op jit(solution)/shard_map/ppermute | solution.py:32
  45.8 26.4 %collective-permute-start.25 = (bf16[4,80,512]{2,1,0:T(8,128)(2,1)S(1)}, bf16[4,80,512]{2,1,0:T(8,128)(2,1)S(1)}, u32[]{:S(2)}, u32[]{:S(2)}) collective-permute-start(bf16[4,80,512]{2,1,0:T(8,128)(2,1)S(1)} %pad_maximum_fusion.1.z_ref), channel_id=1, source_target_pairs={{0,2},{1,3},{2,0},{3,1},{4,6},{5,7},{6,4},{7,5},{8,10},{9,11},{10,... | collective-permute-start | bytes 983048 | tf_op jit(solution)/shard_map/ppermute | solution.py:32
  47.6 8.4 %collective-permute-start.7 = (bf16[40,1792]{1,0:T(8,128)(2,1)S(1)}, bf16[40,1792]{1,0:T(8,128)(2,1)S(1)}, u32[]{:S(2)}, u32[]{:S(2)}) collective-permute-start(bf16[40,1792]{1,0:T(8,128)(2,1)S(1)} %reshape.15.refs_8_), channel_id=1, source_target_pairs={{0,2},{1,3},{2,0},{3,1},{4,6},{5,7},{6,4},{7,5},{8,10},{9,11},{10,... | collective-permute-start | bytes 430088 | tf_op jit(solution)/shard_map/ppermute | solution.py:32
  51.8 8.5 %collective-permute-start.8 = (bf16[40,1792]{1,0:T(8,128)(2,1)S(1)}, bf16[40,1792]{1,0:T(8,128)(2,1)S(1)}, u32[]{:S(2)}, u32[]{:S(2)}) collective-permute-start(bf16[40,1792]{1,0:T(8,128)(2,1)S(1)} %reshape.15.refs_8_), channel_id=1, source_target_pairs={{0,4},{1,5},{2,6},{3,7},{4,8},{5,9},{6,10},{7,11},{8,12},{9,13},{1... | collective-permute-start | bytes 430088 | tf_op jit(solution)/shard_map/ppermute | solution.py:32
  52.6 13.0 %collective-permute-start.10 = (bf16[40,1792]{1,0:T(8,128)(2,1)S(1)}, bf16[40,1792]{1,0:T(8,128)(2,1)S(1)}, u32[]{:S(2)}, u32[]{:S(2)}) collective-permute-start(bf16[40,1792]{1,0:T(8,128)(2,1)S(1)} %reshape.15.refs_8_), channel_id=1, source_target_pairs={{0,8},{1,9},{2,10},{3,11},{4,12},{5,13},{6,14},{7,15},{8,0},{9,1},... | collective-permute-start | bytes 430088 | tf_op jit(solution)/shard_map/ppermute | solution.py:32
  56.0 11.1 %collective-permute-start.12 = (bf16[40,1792]{1,0:T(8,128)(2,1)S(1)}, bf16[40,1792]{1,0:T(8,128)(2,1)S(1)}, u32[]{:S(2)}, u32[]{:S(2)}) collective-permute-start(bf16[40,1792]{1,0:T(8,128)(2,1)S(1)} %reshape.15.refs_8_), channel_id=1, source_target_pairs={{0,12},{1,13},{2,14},{3,15},{4,0},{5,1},{6,2},{7,3},{8,4},{9,5},{1... | collective-permute-start | bytes 430088 | tf_op jit(solution)/shard_map/ppermute | solution.py:32
  60.3 7.3 %collective-permute-start.2 = (bf16[40,1792]{1,0:T(8,128)(2,1)S(1)}, bf16[40,1792]{1,0:T(8,128)(2,1)S(1)}, u32[]{:S(2)}, u32[]{:S(2)}) collective-permute-start(bf16[40,1792]{1,0:T(8,128)(2,1)S(1)} %collective-permute-done.1.refs_2_), channel_id=1, source_target_pairs={{0,2},{1,3},{2,0},{3,1},{4,6},{5,7},{6,4},{7,5},{8,10},{9,11},{10,... | collective-permute-start | bytes 430088 | tf_op jit(solution)/shard_map/ppermute | solution.py:32
  65.6 6.6 %collective-permute-start.4 = (bf16[40,1792]{1,0:T(8,128)(2,1)S(1)}, bf16[40,1792]{1,0:T(8,128)(2,1)S(1)}, u32[]{:S(2)}, u32[]{:S(2)}) collective-permute-start(bf16[40,1792]{1,0:T(8,128)(2,1)S(1)} %collective-permute-done.3.refs_4_), channel_id=1, source_target_pairs={{0,2},{1,3},{2,0},{3,1},{4,6},{5,7},{6,4},{7,5},{8,10},{9,11},{10,... | collective-permute-start | bytes 430088 | tf_op jit(solution)/shard_map/ppermute | solution.py:32
  67.1 8.2 %collective-permute-start.6 = (bf16[40,1792]{1,0:T(8,128)(2,1)S(1)}, bf16[40,1792]{1,0:T(8,128)(2,1)S(1)}, u32[]{:S(2)}, u32[]{:S(2)}) collective-permute-start(bf16[40,1792]{1,0:T(8,128)(2,1)S(1)} %collective-permute-done.5.refs_6_), channel_id=1, source_target_pairs={{0,2},{1,3},{2,0},{3,1},{4,6},{5,7},{6,4},{7,5},{8,10},{9,11},{10,... | collective-permute-start | bytes 430088 | tf_op jit(solution)/shard_map/ppermute | solution.py:32
  67.6 10.7 %collective-permute-start.9 = (bf16[40,1792]{1,0:T(8,128)(2,1)S(1)}, bf16[40,1792]{1,0:T(8,128)(2,1)S(1)}, u32[]{:S(2)}, u32[]{:S(2)}) collective-permute-start(bf16[40,1792]{1,0:T(8,128)(2,1)S(1)} %collective-permute-done.8.refs_10_), channel_id=1, source_target_pairs={{0,2},{1,3},{2,0},{3,1},{4,6},{5,7},{6,4},{7,5},{8,10},{9,11},{10,... | collective-permute-start | bytes 430088 | tf_op jit(solution)/shard_map/ppermute | solution.py:32
  72.2 19.4 %collective-permute-start.26 = (bf16[4,80,512]{2,1,0:T(8,128)(2,1)S(1)}, bf16[4,80,512]{2,1,0:T(8,128)(2,1)S(1)}, u32[]{:S(2)}, u32[]{:S(2)}) collective-permute-start(bf16[4,80,512]{2,1,0:T(8,128)(2,1)S(1)} %pad_maximum_fusion.1.z_ref), channel_id=1, source_target_pairs={{0,1},{1,0},{2,3},{3,2},{4,5},{5,4},{6,7},{7,6},{8,9},{9,8},{10,11... | collective-permute-start | bytes 983048 | tf_op jit(solution)/shard_map/ppermute | solution.py:32
  72.2 19.4 %collective-permute-start.27 = (bf16[4,80,512]{2,1,0:T(8,128)(2,1)S(1)}, bf16[4,80,512]{2,1,0:T(8,128)(2,1)S(1)}, u32[]{:S(2)}, u32[]{:S(2)}) collective-permute-start(bf16[4,80,512]{2,1,0:T(8,128)(2,1)S(1)} %collective-permute-done.25.y_ref), channel_id=1, source_target_pairs={{0,1},{1,0},{2,3},{3,2},{4,5},{5,4},{6,7},{7,6},{8,9},{9,8},{10,11... | collective-permute-start | bytes 983048 | tf_op jit(solution)/shard_map/ppermute | solution.py:32
  75.3 6.5 %collective-permute-start.11 = (bf16[40,1792]{1,0:T(8,128)(2,1)S(1)}, bf16[40,1792]{1,0:T(8,128)(2,1)S(1)}, u32[]{:S(2)}, u32[]{:S(2)}) collective-permute-start(bf16[40,1792]{1,0:T(8,128)(2,1)S(1)} %collective-permute-done.10.refs_12_), channel_id=1, source_target_pairs={{0,2},{1,3},{2,0},{3,1},{4,6},{5,7},{6,4},{7,5},{8,10},{9,11},{10,... | collective-permute-start | bytes 430088 | tf_op jit(solution)/shard_map/ppermute | solution.py:32
  (5 other events, 48.1 us)

commit v3 on v2

v3 whole, which is shorter than its diff:
```python
import functools

import jax
import jax.numpy as jnp
from jax import lax
from jax.experimental import pallas as pl
from jax.experimental.pallas import tpu as pltpu
from jax.sharding import PartitionSpec as P

CORES = 2
PAIR = 2
SUBLANES = 8
FOLDS = 2
CHUNKS = 2
VMEM = pl.BlockSpec(memory_space=pltpu.VMEM)
ANY = pl.BlockSpec(memory_space=pl.ANY)
SMEM = pl.BlockSpec(memory_space=pltpu.SMEM)


def along(devices, by):
    each = CORES * PAIR
    return [(d, (d + by * each) % devices) for d in range(devices)]


def across(devices):
    return [(d, d ^ CORES) for d in range(devices)]


def swap(devices):
    return [(d, d ^ 1) for d in range(devices)]


def send(block, pairs):
    return lax.ppermute(block, "wide", pairs)


def origin(me, devices, step, other_chip, other_core):
    each = CORES * PAIR
    pair = lax.rem(me // each + devices // each - step, devices // each)
    chip = lax.rem(me // CORES, PAIR)
    core = lax.rem(me, CORES)
    if other_chip:
        chip = 1 - chip
    if other_core:
        core = 1 - core
    return pair * PAIR + chip, core


def repeat(times, body, carry=None, loop=False):
    if loop or times > SUBLANES:
        return lax.fori_loop(0, times, body, carry)
    for step in range(times):
        carry = body(step, carry)
    return carry


def unfold_store(rows, slot, block):
    height = block.shape[0]
    at = pl.ds(pl.multiple_of(slot * height, SUBLANES), height)
    for tile in range(rows.shape[0]):
        rows[tile, at, :] = block[:, tile * 128 : (tile + 1) * 128].astype(jnp.float32)


def unfold_load(rows, fold, tokens):
    tiles = [rows[tile, pl.ds(fold, tokens, stride=SUBLANES), :] for tile in range(rows.shape[0])]
    return jnp.concatenate([tile.astype(jnp.bfloat16) for tile in tiles], 1)


def rotate_out_kernel(tokens, waits, me_ref, z_ref, y_ref, cz_ref, cy_ref, basis_ref, *refs):
    sq_ref, rows, total = refs[waits:]
    steps, height, width = z_ref.shape
    devices = steps * CORES * PAIR
    me = me_ref[0]

    @pl.when(pl.program_id(0) == 0)
    def _():
        for ref, chip_bit, core_bit in ((z_ref, 0, 0), (y_ref, 1, 0), (cz_ref, 0, 1), (cy_ref, 1, 1)):

            def put(step, _, ref=ref, chip_bit=chip_bit, core_bit=core_bit):
                chip, core = origin(me, devices, step, chip_bit, core_bit)
                unfold_store(rows, core * (devices // CORES) + chip, ref[step])

            repeat(steps, put)
        total[...] = jnp.zeros_like(total)

    def add(fold, _):
        left = unfold_load(rows, pl.program_id(0) * FOLDS + fold, devices * tokens)
        right = basis_ref[pl.ds(pl.multiple_of(fold * width, 128), width), :]
        total[...] += jnp.dot(left, right, preferred_element_type=jnp.float32)

    repeat(FOLDS, add, None, steps > SUBLANES)

    @pl.when(pl.program_id(0) == pl.num_programs(0) - 1)
    def _():
        sq_ref[...] = (total[...] * total[...]).astype(sq_ref.dtype)


def rotate_out(tokens, me, z, y, cz, cy, basis, waits):
    steps, height, width = z.shape
    total = steps * CORES * PAIR * tokens
    columns = basis.shape[1]
    return pl.pallas_call(
        functools.partial(rotate_out_kernel, tokens, len(waits)),
        grid=(SUBLANES // FOLDS,),
        out_shape=jax.ShapeDtypeStruct((total, columns), jnp.bfloat16),
        in_specs=[SMEM] + [VMEM] * 4 + [pl.BlockSpec((FOLDS * width, columns), lambda i: (i, 0))] + [ANY] * len(waits),
        out_specs=VMEM,
        scratch_shapes=[
            pltpu.VMEM((width // 128, total * SUBLANES, 128), jnp.float32),
            pltpu.VMEM((total, columns), jnp.float32),
        ],
        compiler_params=pltpu.CompilerParams(vmem_limit_bytes=48 * 2**20),
        cost_estimate=pl.CostEstimate(
            flops=2 * total * basis.shape[0] * columns, bytes_accessed=2 * basis.size, transcendentals=0
        ),
        name="rotate_out",
    )(me, z, y, cz, cy, basis, *waits)


def rotate_in_kernel(tokens, before, me_ref, own_ref, across_ref, z_ref, y_ref, mine_ref, theirs_ref, *refs):
    total_ref, rows = refs[before:]
    height, width = own_ref.shape
    steps = z_ref.shape[0] + 1
    devices = steps * CORES * PAIR
    chips = devices // CORES
    me = me_ref[0]

    @pl.when(pl.program_id(0) == 0)
    def _():
        unfold_store(rows, origin(me, devices, 0, 0, 0)[0], own_ref[...])
        unfold_store(rows, origin(me, devices, 0, 1, 0)[0], across_ref[...])
        for ref, chip_bit in ((z_ref, 0), (y_ref, 1)):

            def put(step, _, ref=ref, chip_bit=chip_bit):
                unfold_store(rows, origin(me, devices, step + 1, chip_bit, 0)[0], ref[step])

            repeat(steps - 1, put)
        total_ref[...] = refs[0][...] if before else jnp.zeros_like(total_ref)

    def add(fold, _):
        at = pl.ds(pl.multiple_of(fold * width, 128), width)
        right = unfold_load(rows, pl.program_id(0) * FOLDS + fold, chips * tokens)
        left = jnp.concatenate([mine_ref[:, at], theirs_ref[:, at]])
        total_ref[...] += lax.dot_general(left, right, (((1,), (1,)), ((), ())), preferred_element_type=jnp.float32)

    repeat(FOLDS, add, None, steps > SUBLANES)


def rotate_in(tokens, chunk, me, own, across, z, y, mine, theirs, before):
    height, width = own.shape
    chips = (z.shape[0] + 1) * PAIR
    basis = pl.BlockSpec((mine.shape[0], FOLDS * width), lambda i: (0, chunk * (SUBLANES // FOLDS) + i))
    return pl.pallas_call(
        functools.partial(rotate_in_kernel, tokens, len(before)),
        grid=(SUBLANES // FOLDS,),
        out_shape=jax.ShapeDtypeStruct((2 * mine.shape[0], chips * tokens), jnp.float32),
        in_specs=[SMEM] + [VMEM] * 4 + [basis] * 2 + [VMEM] * len(before),
        out_specs=VMEM,
        scratch_shapes=[pltpu.VMEM((width // 128, chips * height, 128), jnp.float32)],
        compiler_params=pltpu.CompilerParams(vmem_limit_bytes=48 * 2**20),
        cost_estimate=pl.CostEstimate(
            flops=4 * chips * tokens * mine.shape[0] * SUBLANES * width,
            bytes_accessed=4 * mine.shape[0] * SUBLANES * width,
            transcendentals=0,
        ),
        name="rotate_in",
    )(me, own, across, z, y, mine, theirs, *before)


def pile_kernel(blocks, *refs):
    for step in range(blocks):
        refs[-1][step] = refs[step][...]


def pile(blocks, waits):
    return pl.pallas_call(
        functools.partial(pile_kernel, len(blocks)),
        out_shape=jax.ShapeDtypeStruct((len(blocks), *blocks[0].shape), blocks[0].dtype),
        in_specs=[VMEM] * len(blocks) + [ANY] * len(waits),
        out_specs=VMEM,
        compiler_params=pltpu.CompilerParams(vmem_limit_bytes=48 * 2**20),
        cost_estimate=pl.CostEstimate(flops=0, bytes_accessed=2 * len(blocks) * blocks[0].size, transcendentals=0),
        name="pile",
    )(*blocks, *waits)


def combine_kernel(me_ref, own_ref, other_ref, z_ref, y_ref, cz_ref, cy_ref, out_ref):
    steps, total_tokens, width = z_ref.shape
    devices = steps * CORES * PAIR
    me = me_ref[0]
    own, other = own_ref[...].astype(jnp.float32), other_ref[...].astype(jnp.float32)
    first = lax.rem(me, CORES) == 0
    left = jnp.concatenate([jnp.where(first, own, other), jnp.where(first, other, own)], 1).astype(jnp.bfloat16)
    for ref, chip_bit, core_bit in ((z_ref, 0, 0), (y_ref, 1, 0), (cz_ref, 0, 1), (cy_ref, 1, 1)):

        def put(step, _, ref=ref, chip_bit=chip_bit, core_bit=core_bit):
            chip, core = origin(me, devices, step, chip_bit, core_bit)
            at = pl.multiple_of((chip * CORES + core) * width, 128)
            total = jnp.dot(left, ref[step], preferred_element_type=jnp.float32)
            out_ref[:, pl.ds(at, width)] = (total / total_tokens).astype(out_ref.dtype)

        repeat(steps, put)


def combine(me, own, other, z, y, cz, cy):
    steps, total_tokens, width = z.shape
    features = steps * CORES * PAIR * width
    return pl.pallas_call(
        combine_kernel,
        out_shape=jax.ShapeDtypeStruct((own.shape[0], features), jnp.bfloat16),
        in_specs=[SMEM] + [VMEM] * 6,
        out_specs=VMEM,
        compiler_params=pltpu.CompilerParams(vmem_limit_bytes=48 * 2**20),
        cost_estimate=pl.CostEstimate(
            flops=2 * own.shape[0] * total_tokens * features, bytes_accessed=4 * own.shape[0] * features, transcendentals=0
        ),
        name="combine",
    )(me, own, other, z, y, cz, cy)


def local(acts, grads, basis_in, basis_out):
    devices = lax.axis_size("wide")
    steps = devices // (CORES * PAIR)
    tokens = acts.shape[0]
    me = lax.axis_index("wide").astype(jnp.int32).reshape(1)

    def along_all(block):
        return [send(block, along(devices, step)) for step in range(1, steps)]

    def others(z):
        y = send(z, across(devices))
        return z, y, send(z, swap(devices)), send(y, swap(devices))

    mine = basis_in.T
    theirs = send(mine, swap(devices))
    width = acts.shape[1] // (CHUNKS * SUBLANES)
    folded = acts.reshape(tokens, CHUNKS, SUBLANES, width).transpose(1, 0, 2, 3).reshape(CHUNKS, -1, width)
    folded_across = send(folded, across(devices))
    block = grads.reshape(tokens * SUBLANES, -1)
    grads_z = others(jnp.stack([block] + along_all(block)))

    acts_z = []
    acts_y = []
    for chunk in range(CHUNKS):
        acts_z.append(jnp.stack(along_all(folded[chunk])))
        acts_y.append(send(acts_z[chunk], across(devices)))

    sq_out = rotate_out(tokens, me, *grads_z, basis_out, [acts_y[0]])
    came = along_all(sq_out)

    def part(chunk, before):
        return rotate_in(
            tokens, chunk, me, folded[chunk], folded_across[chunk], acts_z[chunk], acts_y[chunk], mine, theirs, before
        )

    total = part(0, [])
    z = pile([sq_out] + came, [total, acts_z[-1]])
    for chunk in range(1, CHUNKS):
        total = part(chunk, [total])
    squares = (total * total).astype(jnp.bfloat16)
    own, given = squares[: mine.shape[0]], squares[mine.shape[0] :]
    other = send(given, swap(devices))
    return combine(me, own, other, *others(z))


def solution(mesh):
    return jax.shard_map(
        local,
        mesh=mesh,
        in_specs=(
            P(("groups", "wide"), None),
            P(("groups", "wide"), None),
            P("groups", "wide"),
            P("groups", "wide"),
        ),
        out_specs=P(("groups", "wide"), None),
        check_vma=False,
    )
```

time: 94.7 us -> 75 us (0.79)
  waiting for transfers between devices: 47.4 us -> 16.7 us
  starting transfers between devices: 30.4 us -> 38.4 us
  local copies, waits for them, and re-layouts: 1.61 us -> 3.21 us
  Pallas kernels: 14.9 us -> 16.1 us
    ppermute x28 -> x23, waiting for transfers between devices: 47.4 us -> 16.7 us  [send(): return lax.ppermute(block, 'wide', pairs)]
    ppermute x28 -> x23, starting transfers between devices: 30.4 us -> 38.4 us  [send(): return lax.ppermute(block, 'wide', pairs)]
    pallas_call x2 -> x4, Pallas kernels: 13.2 us -> 14.3 us  [the longest x2 9.12 us: rotate_in(): pl.pallas_call(functools.partial(rotate_in_kernel, tokens, len(before)),...]
    another operation x0 -> x1, local copies, waits for them, and re-layouts: none -> 1.04 us  [local(): grads_z = others(jnp.stack([block] + along_all(block)))]
  transfers between devices with their start and end apart: 28 -> 23, of which waited for: 15 -> 6; matrix products, arithmetic and copies ran while one was open for 1% -> 5% of each run, Pallas kernels for 14% -> 19%
where the time goes in v3:
time: 75 us; the launch traced here: 74.6 us
  starting transfers between devices  38.4 us (51%)
  waiting for transfers between devices  16.7 us (22%)
  Pallas kernels  16.1 us (21%)
  local copies, waits for them, and re-layouts  3.21 us (4%)
    ppermute x23, starting transfers between devices, send(): return lax.ppermute(block, 'wide', pairs)  38.4 us
    ppermute x23, waiting for transfers between devices, send(): return lax.ppermute(block, 'wide', pairs)  16.7 us
    pallas_call x2, Pallas kernels, rotate_in(): pl.pallas_call(functools.partial(rotate_in_kernel, tokens, len(before)),...  9.12 us
    pallas_call x1, Pallas kernels, rotate_out(): pl.pallas_call(functools.partial(rotate_out_kernel, tokens, len(waits)),...  5.18 us
    pallas_call x1, Pallas kernels, combine(): pl.pallas_call(combine_kernel, out_shape=jax.ShapeDtypeStruct((own.shape[...  1.76 us
  transfers between devices with their start and end apart: 23, of which 6 were waited for; matrix products, arithmetic and copies ran while one was open for 5% of the time, Pallas kernels for 19%

profile of v3, /device:TPU:0, one launch (start us, length us, event | category | flops | bytes accessed | tf_op | source)
XLA Modules:
  0.0 74.6 jit_solution(14141204730381809543)
XLA Ops:
  0.5 1.0 %reshape.19 = bf16[40,1024]{1,0:T(8,128)(2,1)S(1)} reshape(bf16[5,8192]{1,0:T(8,128)(2,1)} %param.5) | data formatting | bytes 163840 | tf_op jit(solution)/shard_map/reshape | solution.py:239
  1.5 4.7 %collective-permute-start.13 = (bf16[40,1024]{1,0:T(8,128)(2,1)S(1)}, bf16[40,1024]{1,0:T(8,128)(2,1)S(1)}, u32[]{:S(2)}, u32[]{:S(2)}) collective-permute-start(bf16[40,1024]{1,0:T(8,128)(2,1)S(1)} %reshape.19), channel_id=1, source_target_pairs={{0,12},{1,13},{2,14},{3,15},{4,0},{5,1},{6,2},{7,3},{8,4},{9,5},{1... | collective-permute-start | bytes 245768 | tf_op jit(solution)/shard_map/ppermute | solution.py:34
  7.2 1.1 %copy_bitcast_fusion.1 = (bf16[2,40,1792]{2,1,0:T(8,128)(2,1)S(1)}, bf16[2,5,8,1792]{3,2,1,0:T(8,128)(2,1)S(1)}) fusion(bf16[1,5,16,1792]{3,1,2,0:T(8,128)(2,1)} %bitcast.32), kind=kLoop, calls=%fused_computation.4 | loop fusion | bytes 860160 | tf_op jit(solution)/shard_map/reshape | solution.py:237
  8.3 2.9 %collective-permute-start.8 = (bf16[40,1792]{1,0:T(8,128)(2,1)S(1)}, bf16[40,1792]{1,0:T(8,128)(2,1)S(1)}, u32[]{:S(2)}, u32[]{:S(2)}) collective-permute-start(bf16[40,1792]{1,0:T(8,128)(2,1)S(1)} %get-tuple-element.7.own_ref), channel_id=1, source_target_pairs={{0,12},{1,13},{2,14},{3,15},{4,0},{5,1},{6,2},{7,3},{8,4},{9,5},{1... | collective-permute-start | bytes 430088 | tf_op jit(solution)/shard_map/ppermute | solution.py:34
  11.1 1.1 %collective-permute-start.7 = (bf16[40,1792]{1,0:T(8,128)(2,1)S(1)}, bf16[40,1792]{1,0:T(8,128)(2,1)S(1)}, u32[]{:S(2)}, u32[]{:S(2)}) collective-permute-start(bf16[40,1792]{1,0:T(8,128)(2,1)S(1)} %get-tuple-element.7.own_ref), channel_id=1, source_target_pairs={{0,8},{1,9},{2,10},{3,11},{4,12},{5,13},{6,14},{7,15},{8,0},{9,1},... | collective-permute-start | bytes 430088 | tf_op jit(solution)/shard_map/ppermute | solution.py:34
  12.3 2.5 %collective-permute-done.12 = bf16[40,1024]{1,0:T(8,128)(2,1)S(1)} collective-permute-done((bf16[40,1024]{1,0:T(8,128)(2,1)S(1)}, bf16[40,1024]{1,0:T(8,128)(2,1)S(1)}, u32[]{:S(2)}, u32[]{:S(2)}) %collective-permute-start.12) | collective-permute-done | bytes 81952 | tf_op jit(solution)/shard_map/ppermute | solution.py:34
  14.8 1.0 %stack_reshape.3 = bf16[1,40,1024]{2,1,0:T(8,128)(2,1)S(1)} reshape(bf16[5,8192]{1,0:T(8,128)(2,1)} %param.5) | data formatting | bytes 163840 | tf_op jit(solution)/shard_map/stack;reshape | solution.py:240
  15.9 3.9 %collective-permute-start.3 = (bf16[40,1792]{1,0:T(8,128)(2,1)S(1)}, bf16[40,1792]{1,0:T(8,128)(2,1)S(1)}, u32[]{:S(2)}, u32[]{:S(2)}) collective-permute-start(bf16[40,1792]{1,0:T(8,128)(2,1)S(1)} %get-tuple-element.8.own_ref), channel_id=1, source_target_pairs={{0,12},{1,13},{2,14},{3,15},{4,0},{5,1},{6,2},{7,3},{8,4},{9,5},{1... | collective-permute-start | bytes 430088 | tf_op jit(solution)/shard_map/ppermute | solution.py:34
  19.8 3.8 %collective-permute-start.2 = (bf16[40,1792]{1,0:T(8,128)(2,1)S(1)}, bf16[40,1792]{1,0:T(8,128)(2,1)S(1)}, u32[]{:S(2)}, u32[]{:S(2)}) collective-permute-start(bf16[40,1792]{1,0:T(8,128)(2,1)S(1)} %get-tuple-element.8.own_ref), channel_id=1, source_target_pairs={{0,8},{1,9},{2,10},{3,11},{4,12},{5,13},{6,14},{7,15},{8,0},{9,1},... | collective-permute-start | bytes 430088 | tf_op jit(solution)/shard_map/ppermute | solution.py:34
  23.6 3.6 %collective-permute-done.7 = bf16[40,1792]{1,0:T(8,128)(2,1)S(1)} collective-permute-done((bf16[40,1792]{1,0:T(8,128)(2,1)S(1)}, bf16[40,1792]{1,0:T(8,128)(2,1)S(1)}, u32[]{:S(2)}, u32[]{:S(2)}) %collective-permute-start.7) | collective-permute-done | bytes 143392 | tf_op jit(solution)/shard_map/ppermute | solution.py:34
  27.1 1.5 %collective-permute-start.14 = (bf16[4,40,1024]{2,1,0:T(8,128)(2,1)S(1)}, bf16[4,40,1024]{2,1,0:T(8,128)(2,1)S(1)}, u32[]{:S(2)}, u32[]{:S(2)}) collective-permute-start(bf16[4,40,1024]{2,1,0:T(8,128)(2,1)S(1)} %pad_maximum_fusion.2.z_ref), channel_id=1, source_target_pairs={{0,2},{1,3},{2,0},{3,1},{4,6},{5,7},{6,4},{7,5},{8,10},{9,11},{10,... | collective-permute-start | bytes 983048 | tf_op jit(solution)/shard_map/ppermute | solution.py:34
  29.3 6.0 %collective-permute-start.1 = (bf16[40,1792]{1,0:T(8,128)(2,1)S(1)}, bf16[40,1792]{1,0:T(8,128)(2,1)S(1)}, u32[]{:S(2)}, u32[]{:S(2)}) collective-permute-start(bf16[40,1792]{1,0:T(8,128)(2,1)S(1)} %get-tuple-element.8.own_ref), channel_id=1, source_target_pairs={{0,4},{1,5},{2,6},{3,7},{4,8},{5,9},{6,10},{7,11},{8,12},{9,13},{1... | collective-permute-start | bytes 430088 | tf_op jit(solution)/shard_map/ppermute | solution.py:34
  35.3 4.1 %collective-permute-done.2 = bf16[40,1792]{1,0:T(8,128)(2,1)S(1)} collective-permute-done((bf16[40,1792]{1,0:T(8,128)(2,1)S(1)}, bf16[40,1792]{1,0:T(8,128)(2,1)S(1)}, u32[]{:S(2)}, u32[]{:S(2)}) %collective-permute-start.2) | collective-permute-done | bytes 143392 | tf_op jit(solution)/shard_map/ppermute | solution.py:34
  39.9 1.5 %collective-permute-start = (bf16[2,40,1792]{2,1,0:T(8,128)(2,1)S(1)}, bf16[2,40,1792]{2,1,0:T(8,128)(2,1)S(1)}, u32[]{:S(2)}, u32[]{:S(2)}) collective-permute-start(bf16[2,40,1792]{2,1,0:T(8,128)(2,1)S(1)} %get-tuple-element.9), channel_id=1, source_target_pairs={{0,2},{1,3},{2,0},{3,1},{4,6},{5,7},{6,4},{7,5},{8,10},{9,11},{10,... | collective-permute-start | bytes 860168 | tf_op jit(solution)/shard_map/ppermute | solution.py:34
  41.5 1.0 %collective-permute-start.4 = (bf16[3,40,1792]{2,1,0:T(8,128)(2,1)S(1)}, bf16[3,40,1792]{2,1,0:T(8,128)(2,1)S(1)}, u32[]{:S(2)}, u32[]{:S(2)}) collective-permute-start(bf16[3,40,1792]{2,1,0:T(8,128)(2,1)S(1)} %pad_maximum_fusion.z_ref.refs_5_), channel_id=1, source_target_pairs={{0,2},{1,3},{2,0},{3,1},{4,6},{5,7},{6,4},{7,5},{8,10},{9,11},{10,... | collective-permute-start | bytes 1290248 | tf_op jit(solution)/shard_map/ppermute | solution.py:34
  42.5 4.4 %collective-permute-done.9.y_ref.refs_0_ = bf16[3,40,1792]{2,1,0:T(8,128)(2,1)S(1)} collective-permute-done((bf16[3,40,1792]{2,1,0:T(8,128)(2,1)S(1)}, bf16[3,40,1792]{2,1,0:T(8,128)(2,1)S(1)}, u32[]{:S(2)}, u32[]{:S(2)}) %collective-permute-start.9) | collective-permute-done | bytes 430112 | tf_op jit(solution)/shard_map/ppermute | solution.py:34
  46.9 5.2 %rotate_out.1.refs_0_ = bf16[80,512]{1,0:T(8,128)(2,1)S(1)} custom-call(s32[1]{0:T(128)} %bitcast.me_ref, bf16[4,40,1024]{2,1,0:T(8,128)(2,1)S(1)} %pad_maximum_fusion.2.z_ref, bf16[4,40,1024]{2,1,0:T(8,128)(2,1)S(1)} %collective-permute-done.14.y_ref, bf16[4,40,1024]{2,1,0:T(8,128)(2,1)S(1)} %collective-permute-done.15.cz_ref, ...), custom_call_target="tpu_custom_call" | custom-call | flops 671088640 | bytes 8388608 | tf_op jit(solution)/shard_map/rotate_out/pallas_call | solution.py:102
  52.1 2.6 %collective-permute-start.17 = (bf16[80,512]{1,0:T(8,128)(2,1)S(1)}, bf16[80,512]{1,0:T(8,128)(2,1)S(1)}, u32[]{:S(2)}, u32[]{:S(2)}) collective-permute-start(bf16[80,512]{1,0:T(8,128)(2,1)S(1)} %rotate_out.1.refs_0_), channel_id=1, source_target_pairs={{0,4},{1,5},{2,6},{3,7},{4,8},{5,9},{6,10},{7,11},{8,12},{9,13},{1... | collective-permute-start | bytes 245768 | tf_op jit(solution)/shard_map/ppermute | solution.py:34
  54.7 4.4 %collective-permute-start.18 = (bf16[80,512]{1,0:T(8,128)(2,1)S(1)}, bf16[80,512]{1,0:T(8,128)(2,1)S(1)}, u32[]{:S(2)}, u32[]{:S(2)}) collective-permute-start(bf16[80,512]{1,0:T(8,128)(2,1)S(1)} %rotate_out.1.refs_0_), channel_id=1, source_target_pairs={{0,8},{1,9},{2,10},{3,11},{4,12},{5,13},{6,14},{7,15},{8,0},{9,1},... | collective-permute-start | bytes 245768 | tf_op jit(solution)/shard_map/ppermute | solution.py:34
  59.4 4.6 %rotate_in.2.refs_0_.refs_4_ = f32[192,40]{1,0:T(8,128)S(1)} custom-call(s32[1]{0:T(128)} %bitcast.me_ref, bf16[40,1792]{1,0:T(8,128)(2,1)S(1)} %get-tuple-element.7.own_ref, bf16[40,1792]{1,0:T(8,128)(2,1)S(1)} %get-tuple-element.5.across_ref, bf16[3,40,1792]{2,1,0:T(8,128)(2,1)S(1)} %pad_maximum_fusion.1.z_ref, ...), custom_call_target="tpu_custom_call" | custom-call | flops 220200960 | bytes 5505024 | tf_op jit(solution)/shard_map/rotate_in/pallas_call | solution.py:153
  64.1 1.6 %collective-permute-start.20 = (bf16[4,80,512]{2,1,0:T(8,128)(2,1)S(1)}, bf16[4,80,512]{2,1,0:T(8,128)(2,1)S(1)}, u32[]{:S(2)}, u32[]{:S(2)}) collective-permute-start(bf16[4,80,512]{2,1,0:T(8,128)(2,1)S(1)} %pile.1.z_ref), channel_id=1, source_target_pairs={{0,2},{1,3},{2,0},{3,1},{4,6},{5,7},{6,4},{7,5},{8,10},{9,11},{10,... | collective-permute-start | bytes 983048 | tf_op jit(solution)/shard_map/ppermute | solution.py:34
  65.7 4.6 %rotate_in.3 = f32[192,40]{1,0:T(8,128)S(1)} custom-call(s32[1]{0:T(128)} %bitcast.me_ref, bf16[40,1792]{1,0:T(8,128)(2,1)S(1)} %get-tuple-element.8.own_ref, bf16[40,1792]{1,0:T(8,128)(2,1)S(1)} %get-tuple-element.6.across_ref, bf16[3,40,1792]{2,1,0:T(8,128)(2,1)S(1)} %pad_maximum_fusion.z_ref.refs_5_, ...), custom_call_target="tpu_custom_call" | custom-call | flops 220200960 | bytes 5505024 | tf_op jit(solution)/shard_map/rotate_in/pallas_call | solution.py:153
  71.8 1.1 %collective-permute-done.10.other_ref = bf16[96,40]{1,0:T(8,128)(2,1)S(1)} collective-permute-done((bf16[96,40]{1,0:T(8,128)(2,1)S(1)}, bf16[96,40]{1,0:T(8,128)(2,1)S(1)}, u32[]{:S(2)}, u32[]{:S(2)}) %collective-permute-start.10) | collective-permute-done | bytes 7712 | tf_op jit(solution)/shard_map/ppermute | solution.py:34
  72.9 1.8 %combine.1 = bf16[96,8192]{1,0:T(8,128)(2,1)} custom-call(s32[1]{0:T(128)} %bitcast.me_ref, bf16[96,40]{1,0:T(8,128)(2,1)S(1)} %get-tuple-element.12.own_ref, bf16[96,40]{1,0:T(8,128)(2,1)S(1)} %collective-permute-done.10.other_ref, bf16[4,80,512]{2,1,0:T(8,128)(2,1)S(1)} %pile.1.z_ref, bf16[4,80,512]{2,1,0:T(8,128)(2,1)S(1)} %collective-permute-done.20.y_ref, ...), custom_call_target="tpu_custom_call" | custom-call | flops 125829120 | bytes 3145728 | tf_op jit(solution)/shard_map/combine/pallas_call | solution.py:208
  (37 shorter events, 4.7 us)
Async XLA Ops:
  0.0 59.4 %collective-permute-start.5 = (bf16[96,28672]{1,0:T(8,128)(2,1)}, bf16[96,28672]{1,0:T(8,128)(2,1)}, u32[]{:S(2)}, u32[]{:S(2)}) collective-permute-start(bf16[96,28672]{1,0:T(8,128)(2,1)} %bitcast.29), channel_id=1, source_target_pairs={{0,1},{1,0},{2,3},{3,2},{4,5},{5,4},{6,7},{7,6},{8,9},{9,8},{10,11... | collective-permute-start | bytes 16515080 | tf_op jit(solution)/shard_map/ppermute | solution.py:34
  1.5 9.7 %collective-permute-start.13 = (bf16[40,1024]{1,0:T(8,128)(2,1)S(1)}, bf16[40,1024]{1,0:T(8,128)(2,1)S(1)}, u32[]{:S(2)}, u32[]{:S(2)}) collective-permute-start(bf16[40,1024]{1,0:T(8,128)(2,1)S(1)} %reshape.19), channel_id=1, source_target_pairs={{0,12},{1,13},{2,14},{3,15},{4,0},{5,1},{6,2},{7,3},{8,4},{9,5},{1... | collective-permute-start | bytes 245768 | tf_op jit(solution)/shard_map/ppermute | solution.py:34
  6.2 8.7 %collective-permute-start.12 = (bf16[40,1024]{1,0:T(8,128)(2,1)S(1)}, bf16[40,1024]{1,0:T(8,128)(2,1)S(1)}, u32[]{:S(2)}, u32[]{:S(2)}) collective-permute-start(bf16[40,1024]{1,0:T(8,128)(2,1)S(1)} %reshape.19), channel_id=1, source_target_pairs={{0,8},{1,9},{2,10},{3,11},{4,12},{5,13},{6,14},{7,15},{8,0},{9,1},... | collective-permute-start | bytes 245768 | tf_op jit(solution)/shard_map/ppermute | solution.py:34
  6.2 9.7 %collective-permute-start.11 = (bf16[40,1024]{1,0:T(8,128)(2,1)S(1)}, bf16[40,1024]{1,0:T(8,128)(2,1)S(1)}, u32[]{:S(2)}, u32[]{:S(2)}) collective-permute-start(bf16[40,1024]{1,0:T(8,128)(2,1)S(1)} %reshape.19), channel_id=1, source_target_pairs={{0,4},{1,5},{2,6},{3,7},{4,8},{5,9},{6,10},{7,11},{8,12},{9,13},{1... | collective-permute-start | bytes 245768 | tf_op jit(solution)/shard_map/ppermute | solution.py:34
  8.3 11.5 %collective-permute-start.8 = (bf16[40,1792]{1,0:T(8,128)(2,1)S(1)}, bf16[40,1792]{1,0:T(8,128)(2,1)S(1)}, u32[]{:S(2)}, u32[]{:S(2)}) collective-permute-start(bf16[40,1792]{1,0:T(8,128)(2,1)S(1)} %get-tuple-element.7.own_ref), channel_id=1, source_target_pairs={{0,12},{1,13},{2,14},{3,15},{4,0},{5,1},{6,2},{7,3},{8,4},{9,5},{1... | collective-permute-start | bytes 430088 | tf_op jit(solution)/shard_map/ppermute | solution.py:34
  11.1 16.0 %collective-permute-start.7 = (bf16[40,1792]{1,0:T(8,128)(2,1)S(1)}, bf16[40,1792]{1,0:T(8,128)(2,1)S(1)}, u32[]{:S(2)}, u32[]{:S(2)}) collective-permute-start(bf16[40,1792]{1,0:T(8,128)(2,1)S(1)} %get-tuple-element.7.own_ref), channel_id=1, source_target_pairs={{0,8},{1,9},{2,10},{3,11},{4,12},{5,13},{6,14},{7,15},{8,0},{9,1},... | collective-permute-start | bytes 430088 | tf_op jit(solution)/shard_map/ppermute | solution.py:34
  14.8 13.9 %collective-permute-start.6 = (bf16[40,1792]{1,0:T(8,128)(2,1)S(1)}, bf16[40,1792]{1,0:T(8,128)(2,1)S(1)}, u32[]{:S(2)}, u32[]{:S(2)}) collective-permute-start(bf16[40,1792]{1,0:T(8,128)(2,1)S(1)} %get-tuple-element.7.own_ref), channel_id=1, source_target_pairs={{0,4},{1,5},{2,6},{3,7},{4,8},{5,9},{6,10},{7,11},{8,12},{9,13},{1... | collective-permute-start | bytes 430088 | tf_op jit(solution)/shard_map/ppermute | solution.py:34
  15.9 13.4 %collective-permute-start.3 = (bf16[40,1792]{1,0:T(8,128)(2,1)S(1)}, bf16[40,1792]{1,0:T(8,128)(2,1)S(1)}, u32[]{:S(2)}, u32[]{:S(2)}) collective-permute-start(bf16[40,1792]{1,0:T(8,128)(2,1)S(1)} %get-tuple-element.8.own_ref), channel_id=1, source_target_pairs={{0,12},{1,13},{2,14},{3,15},{4,0},{5,1},{6,2},{7,3},{8,4},{9,5},{1... | collective-permute-start | bytes 430088 | tf_op jit(solution)/shard_map/ppermute | solution.py:34
  19.8 19.6 %collective-permute-start.2 = (bf16[40,1792]{1,0:T(8,128)(2,1)S(1)}, bf16[40,1792]{1,0:T(8,128)(2,1)S(1)}, u32[]{:S(2)}, u32[]{:S(2)}) collective-permute-start(bf16[40,1792]{1,0:T(8,128)(2,1)S(1)} %get-tuple-element.8.own_ref), channel_id=1, source_target_pairs={{0,8},{1,9},{2,10},{3,11},{4,12},{5,13},{6,14},{7,15},{8,0},{9,1},... | collective-permute-start | bytes 430088 | tf_op jit(solution)/shard_map/ppermute | solution.py:34
  27.1 12.3 %collective-permute-start.14 = (bf16[4,40,1024]{2,1,0:T(8,128)(2,1)S(1)}, bf16[4,40,1024]{2,1,0:T(8,128)(2,1)S(1)}, u32[]{:S(2)}, u32[]{:S(2)}) collective-permute-start(bf16[4,40,1024]{2,1,0:T(8,128)(2,1)S(1)} %pad_maximum_fusion.2.z_ref), channel_id=1, source_target_pairs={{0,2},{1,3},{2,0},{3,1},{4,6},{5,7},{6,4},{7,5},{8,10},{9,11},{10,... | collective-permute-start | bytes 983048 | tf_op jit(solution)/shard_map/ppermute | solution.py:34
  28.7 18.2 %collective-permute-start.9 = (bf16[3,40,1792]{2,1,0:T(8,128)(2,1)S(1)}, bf16[3,40,1792]{2,1,0:T(8,128)(2,1)S(1)}, u32[]{:S(2)}, u32[]{:S(2)}) collective-permute-start(bf16[3,40,1792]{2,1,0:T(8,128)(2,1)S(1)} %pad_maximum_fusion.1.z_ref), channel_id=1, source_target_pairs={{0,2},{1,3},{2,0},{3,1},{4,6},{5,7},{6,4},{7,5},{8,10},{9,11},{10,... | collective-permute-start | bytes 1290248 | tf_op jit(solution)/shard_map/ppermute | solution.py:34
  29.3 10.6 %collective-permute-start.1 = (bf16[40,1792]{1,0:T(8,128)(2,1)S(1)}, bf16[40,1792]{1,0:T(8,128)(2,1)S(1)}, u32[]{:S(2)}, u32[]{:S(2)}) collective-permute-start(bf16[40,1792]{1,0:T(8,128)(2,1)S(1)} %get-tuple-element.8.own_ref), channel_id=1, source_target_pairs={{0,4},{1,5},{2,6},{3,7},{4,8},{5,9},{6,10},{7,11},{8,12},{9,13},{1... | collective-permute-start | bytes 430088 | tf_op jit(solution)/shard_map/ppermute | solution.py:34
  39.4 2.1 %collective-permute-start.15 = (bf16[4,40,1024]{2,1,0:T(8,128)(2,1)S(1)}, bf16[4,40,1024]{2,1,0:T(8,128)(2,1)S(1)}, u32[]{:S(2)}, u32[]{:S(2)}) collective-permute-start(bf16[4,40,1024]{2,1,0:T(8,128)(2,1)S(1)} %pad_maximum_fusion.2.z_ref), channel_id=1, source_target_pairs={{0,1},{1,0},{2,3},{3,2},{4,5},{5,4},{6,7},{7,6},{8,9},{9,8},{10,11... | collective-permute-start | bytes 983048 | tf_op jit(solution)/shard_map/ppermute | solution.py:34
  39.4 7.5 %collective-permute-start.16 = (bf16[4,40,1024]{2,1,0:T(8,128)(2,1)S(1)}, bf16[4,40,1024]{2,1,0:T(8,128)(2,1)S(1)}, u32[]{:S(2)}, u32[]{:S(2)}) collective-permute-start(bf16[4,40,1024]{2,1,0:T(8,128)(2,1)S(1)} %collective-permute-done.14.y_ref), channel_id=1, source_target_pairs={{0,1},{1,0},{2,3},{3,2},{4,5},{5,4},{6,7},{7,6},{8,9},{9,8},{10,11... | collective-permute-start | bytes 983048 | tf_op jit(solution)/shard_map/ppermute | solution.py:34
  39.9 19.2 %collective-permute-start = (bf16[2,40,1792]{2,1,0:T(8,128)(2,1)S(1)}, bf16[2,40,1792]{2,1,0:T(8,128)(2,1)S(1)}, u32[]{:S(2)}, u32[]{:S(2)}) collective-permute-start(bf16[2,40,1792]{2,1,0:T(8,128)(2,1)S(1)} %get-tuple-element.9), channel_id=1, source_target_pairs={{0,2},{1,3},{2,0},{3,1},{4,6},{5,7},{6,4},{7,5},{8,10},{9,11},{10,... | collective-permute-start | bytes 860168 | tf_op jit(solution)/shard_map/ppermute | solution.py:34
  41.5 24.2 %collective-permute-start.4 = (bf16[3,40,1792]{2,1,0:T(8,128)(2,1)S(1)}, bf16[3,40,1792]{2,1,0:T(8,128)(2,1)S(1)}, u32[]{:S(2)}, u32[]{:S(2)}) collective-permute-start(bf16[3,40,1792]{2,1,0:T(8,128)(2,1)S(1)} %pad_maximum_fusion.z_ref.refs_5_), channel_id=1, source_target_pairs={{0,2},{1,3},{2,0},{3,1},{4,6},{5,7},{6,4},{7,5},{8,10},{9,11},{10,... | collective-permute-start | bytes 1290248 | tf_op jit(solution)/shard_map/ppermute | solution.py:34
  52.1 11.9 %collective-permute-start.17 = (bf16[80,512]{1,0:T(8,128)(2,1)S(1)}, bf16[80,512]{1,0:T(8,128)(2,1)S(1)}, u32[]{:S(2)}, u32[]{:S(2)}) collective-permute-start(bf16[80,512]{1,0:T(8,128)(2,1)S(1)} %rotate_out.1.refs_0_), channel_id=1, source_target_pairs={{0,4},{1,5},{2,6},{3,7},{4,8},{5,9},{6,10},{7,11},{8,12},{9,13},{1... | collective-permute-start | bytes 245768 | tf_op jit(solution)/shard_map/ppermute | solution.py:34
  54.7 9.3 %collective-permute-start.18 = (bf16[80,512]{1,0:T(8,128)(2,1)S(1)}, bf16[80,512]{1,0:T(8,128)(2,1)S(1)}, u32[]{:S(2)}, u32[]{:S(2)}) collective-permute-start(bf16[80,512]{1,0:T(8,128)(2,1)S(1)} %rotate_out.1.refs_0_), channel_id=1, source_target_pairs={{0,8},{1,9},{2,10},{3,11},{4,12},{5,13},{6,14},{7,15},{8,0},{9,1},... | collective-permute-start | bytes 245768 | tf_op jit(solution)/shard_map/ppermute | solution.py:34
  59.1 4.9 %collective-permute-start.19 = (bf16[80,512]{1,0:T(8,128)(2,1)S(1)}, bf16[80,512]{1,0:T(8,128)(2,1)S(1)}, u32[]{:S(2)}, u32[]{:S(2)}) collective-permute-start(bf16[80,512]{1,0:T(8,128)(2,1)S(1)} %rotate_out.1.refs_0_), channel_id=1, source_target_pairs={{0,12},{1,13},{2,14},{3,15},{4,0},{5,1},{6,2},{7,3},{8,4},{9,5},{1... | collective-permute-start | bytes 245768 | tf_op jit(solution)/shard_map/ppermute | solution.py:34
  64.1 7.1 %collective-permute-start.20 = (bf16[4,80,512]{2,1,0:T(8,128)(2,1)S(1)}, bf16[4,80,512]{2,1,0:T(8,128)(2,1)S(1)}, u32[]{:S(2)}, u32[]{:S(2)}) collective-permute-start(bf16[4,80,512]{2,1,0:T(8,128)(2,1)S(1)} %pile.1.z_ref), channel_id=1, source_target_pairs={{0,2},{1,3},{2,0},{3,1},{4,6},{5,7},{6,4},{7,5},{8,10},{9,11},{10,... | collective-permute-start | bytes 983048 | tf_op jit(solution)/shard_map/ppermute | solution.py:34
  65.6 7.2 %collective-permute-start.21 = (bf16[4,80,512]{2,1,0:T(8,128)(2,1)S(1)}, bf16[4,80,512]{2,1,0:T(8,128)(2,1)S(1)}, u32[]{:S(2)}, u32[]{:S(2)}) collective-permute-start(bf16[4,80,512]{2,1,0:T(8,128)(2,1)S(1)} %pile.1.z_ref), channel_id=1, source_target_pairs={{0,1},{1,0},{2,3},{3,2},{4,5},{5,4},{6,7},{7,6},{8,9},{9,8},{10,11... | collective-permute-start | bytes 983048 | tf_op jit(solution)/shard_map/ppermute | solution.py:34
  71.2 1.7 %collective-permute-start.22 = (bf16[4,80,512]{2,1,0:T(8,128)(2,1)S(1)}, bf16[4,80,512]{2,1,0:T(8,128)(2,1)S(1)}, u32[]{:S(2)}, u32[]{:S(2)}) collective-permute-start(bf16[4,80,512]{2,1,0:T(8,128)(2,1)S(1)} %collective-permute-done.20.y_ref), channel_id=1, source_target_pairs={{0,1},{1,0},{2,3},{3,2},{4,5},{5,4},{6,7},{7,6},{8,9},{9,8},{10,11... | collective-permute-start | bytes 983048 | tf_op jit(solution)/shard_map/ppermute | solution.py:34
  71.2 1.6 %collective-permute-start.10 = (bf16[96,40]{1,0:T(8,128)(2,1)S(1)}, bf16[96,40]{1,0:T(8,128)(2,1)S(1)}, u32[]{:S(2)}, u32[]{:S(2)}) collective-permute-start(bf16[96,40]{1,0:T(8,128)(2,1)S(1)} %get-tuple-element.11), channel_id=1, source_target_pairs={{0,1},{1,0},{2,3},{3,2},{4,5},{5,4},{6,7},{7,6},{8,9},{9,8},{10,11... | collective-permute-start | bytes 23048 | tf_op jit(solution)/shard_map/ppermute | solution.py:34

commit v4 on v3

--- a/solution.py
+++ b/solution.py
@@ -237,15 +237,15 @@
     folded = acts.reshape(tokens, CHUNKS, SUBLANES, width).transpose(1, 0, 2, 3).reshape(CHUNKS, -1, width)
     folded_across = send(folded, across(devices))
     block = grads.reshape(tokens * SUBLANES, -1)
-    grads_z = others(jnp.stack([block] + along_all(block)))
+    grads_z = others(pile([block] + along_all(block), [folded_across]))
 
     acts_z = []
     acts_y = []
     for chunk in range(CHUNKS):
-        acts_z.append(jnp.stack(along_all(folded[chunk])))
+        acts_z.append(pile(along_all(folded[chunk]), [] if chunk else [grads_z[1]]))
         acts_y.append(send(acts_z[chunk], across(devices)))
 
-    sq_out = rotate_out(tokens, me, *grads_z, basis_out, [acts_y[0]])
+    sq_out = rotate_out(tokens, me, *grads_z, basis_out, [acts_z[0]])
     came = along_all(sq_out)
 
     def part(chunk, before):

time: 75 us -> 77.7 us (1.036)
  waiting for transfers between devices: 16.7 us -> 23.7 us
  starting transfers between devices: 38.4 us -> 35.2 us
  local copies, waits for them, and re-layouts: 3.21 us -> 2.17 us
    ppermute x23, waiting for transfers between devices: 16.7 us -> 23.7 us  [send(): return lax.ppermute(block, 'wide', pairs)]
    ppermute x23, starting transfers between devices: 38.4 us -> 35.2 us  [send(): return lax.ppermute(block, 'wide', pairs)]
    another operation x1 -> x0, local copies, waits for them, and re-layouts: 1.04 us -> none  [local(): grads_z = others(jnp.stack([block] + along_all(block)))]
  transfers between devices with their start and end apart: 23 -> 23, of which waited for: 6 -> 10; matrix products, arithmetic and copies ran while one was open for 5% -> 3% of each run, Pallas kernels for 19% -> 19%
where the time goes in v4:
time: 77.7 us; the launch traced here: 77.4 us
  starting transfers between devices  35.2 us (45%)
  waiting for transfers between devices  23.7 us (31%)
  Pallas kernels  16.2 us (21%)
  local copies, waits for them, and re-layouts  2.17 us (3%)
    ppermute x23, starting transfers between devices, send(): return lax.ppermute(block, 'wide', pairs)  35.2 us
    ppermute x23, waiting for transfers between devices, send(): return lax.ppermute(block, 'wide', pairs)  23.7 us
    pallas_call x2, Pallas kernels, rotate_in(): pl.pallas_call(functools.partial(rotate_in_kernel, tokens, len(before)),...  9.11 us
    pallas_call x1, Pallas kernels, rotate_out(): pl.pallas_call(functools.partial(rotate_out_kernel, tokens, len(waits)),...  5.19 us
    pallas_call x1, Pallas kernels, combine(): pl.pallas_call(combine_kernel, out_shape=jax.ShapeDtypeStruct((own.shape[...  1.76 us
  transfers between devices with their start and end apart: 23, of which 10 were waited for; matrix products, arithmetic and copies ran while one was open for 3% of the time, Pallas kernels for 19%

profile of v4, /device:TPU:0, one launch (start us, length us, event | category | flops | bytes accessed | tf_op | source)
XLA Modules:
  0.0 77.4 jit_solution(910228890278042505)
XLA Ops:
  0.5 1.1 %copy_bitcast_fusion.1 = (bf16[2,40,1792]{2,1,0:T(8,128)(2,1)S(1)}, bf16[2,5,8,1792]{3,2,1,0:T(8,128)(2,1)S(1)}) fusion(bf16[1,5,16,1792]{3,1,2,0:T(8,128)(2,1)} %bitcast.23), kind=kLoop, calls=%fused_computation.1 | loop fusion | bytes 860160 | tf_op jit(solution)/shard_map/reshape | solution.py:237
  1.5 2.6 %collective-permute-start = (bf16[2,40,1792]{2,1,0:T(8,128)(2,1)S(1)}, bf16[2,40,1792]{2,1,0:T(8,128)(2,1)S(1)}, u32[]{:S(2)}, u32[]{:S(2)}) collective-permute-start(bf16[2,40,1792]{2,1,0:T(8,128)(2,1)S(1)} %get-tuple-element.9), channel_id=1, source_target_pairs={{0,2},{1,3},{2,0},{3,1},{4,6},{5,7},{6,4},{7,5},{8,10},{9,11},{10,... | collective-permute-start | bytes 860168 | tf_op jit(solution)/shard_map/ppermute | solution.py:34
  5.2 2.7 %collective-permute-start.10 = (bf16[40,1024]{1,0:T(8,128)(2,1)S(1)}, bf16[40,1024]{1,0:T(8,128)(2,1)S(1)}, u32[]{:S(2)}, u32[]{:S(2)}) collective-permute-start(bf16[40,1024]{1,0:T(8,128)(2,1)S(1)} %reshape.19.refs_0_), channel_id=1, source_target_pairs={{0,8},{1,9},{2,10},{3,11},{4,12},{5,13},{6,14},{7,15},{8,0},{9,1},... | collective-permute-start | bytes 245768 | tf_op jit(solution)/shard_map/ppermute | solution.py:34
  7.8 1.3 %collective-permute-start.11 = (bf16[40,1024]{1,0:T(8,128)(2,1)S(1)}, bf16[40,1024]{1,0:T(8,128)(2,1)S(1)}, u32[]{:S(2)}, u32[]{:S(2)}) collective-permute-start(bf16[40,1024]{1,0:T(8,128)(2,1)S(1)} %reshape.19.refs_0_), channel_id=1, source_target_pairs={{0,12},{1,13},{2,14},{3,15},{4,0},{5,1},{6,2},{7,3},{8,4},{9,5},{1... | collective-permute-start | bytes 245768 | tf_op jit(solution)/shard_map/ppermute | solution.py:34
  9.8 3.2 %collective-permute-done.10.refs_2_ = bf16[40,1024]{1,0:T(8,128)(2,1)S(1)} collective-permute-done((bf16[40,1024]{1,0:T(8,128)(2,1)S(1)}, bf16[40,1024]{1,0:T(8,128)(2,1)S(1)}, u32[]{:S(2)}, u32[]{:S(2)}) %collective-permute-start.10) | collective-permute-done | bytes 81952 | tf_op jit(solution)/shard_map/ppermute | solution.py:34
  13.0 2.5 %collective-permute-done.9.refs_1_ = bf16[40,1024]{1,0:T(8,128)(2,1)S(1)} collective-permute-done((bf16[40,1024]{1,0:T(8,128)(2,1)S(1)}, bf16[40,1024]{1,0:T(8,128)(2,1)S(1)}, u32[]{:S(2)}, u32[]{:S(2)}) %collective-permute-start.9) | collective-permute-done | bytes 81952 | tf_op jit(solution)/shard_map/ppermute | solution.py:34
  16.1 1.3 %collective-permute-start.6 = (bf16[40,1792]{1,0:T(8,128)(2,1)S(1)}, bf16[40,1792]{1,0:T(8,128)(2,1)S(1)}, u32[]{:S(2)}, u32[]{:S(2)}) collective-permute-start(bf16[40,1792]{1,0:T(8,128)(2,1)S(1)} %get-tuple-element.7.own_ref), channel_id=1, source_target_pairs={{0,4},{1,5},{2,6},{3,7},{4,8},{5,9},{6,10},{7,11},{8,12},{9,13},{1... | collective-permute-start | bytes 430088 | tf_op jit(solution)/shard_map/ppermute | solution.py:34
  17.4 2.0 %collective-permute-start.7 = (bf16[40,1792]{1,0:T(8,128)(2,1)S(1)}, bf16[40,1792]{1,0:T(8,128)(2,1)S(1)}, u32[]{:S(2)}, u32[]{:S(2)}) collective-permute-start(bf16[40,1792]{1,0:T(8,128)(2,1)S(1)} %get-tuple-element.7.own_ref), channel_id=1, source_target_pairs={{0,8},{1,9},{2,10},{3,11},{4,12},{5,13},{6,14},{7,15},{8,0},{9,1},... | collective-permute-start | bytes 430088 | tf_op jit(solution)/shard_map/ppermute | solution.py:34
  19.4 2.8 %collective-permute-start.8 = (bf16[40,1792]{1,0:T(8,128)(2,1)S(1)}, bf16[40,1792]{1,0:T(8,128)(2,1)S(1)}, u32[]{:S(2)}, u32[]{:S(2)}) collective-permute-start(bf16[40,1792]{1,0:T(8,128)(2,1)S(1)} %get-tuple-element.7.own_ref), channel_id=1, source_target_pairs={{0,12},{1,13},{2,14},{3,15},{4,0},{5,1},{6,2},{7,3},{8,4},{9,5},{1... | collective-permute-start | bytes 430088 | tf_op jit(solution)/shard_map/ppermute | solution.py:34
  22.2 1.8 %collective-permute-done.6.refs_0_ = bf16[40,1792]{1,0:T(8,128)(2,1)S(1)} collective-permute-done((bf16[40,1792]{1,0:T(8,128)(2,1)S(1)}, bf16[40,1792]{1,0:T(8,128)(2,1)S(1)}, u32[]{:S(2)}, u32[]{:S(2)}) %collective-permute-start.6) | collective-permute-done | bytes 143392 | tf_op jit(solution)/shard_map/ppermute | solution.py:34
  24.0 6.1 %collective-permute-start.1 = (bf16[40,1792]{1,0:T(8,128)(2,1)S(1)}, bf16[40,1792]{1,0:T(8,128)(2,1)S(1)}, u32[]{:S(2)}, u32[]{:S(2)}) collective-permute-start(bf16[40,1792]{1,0:T(8,128)(2,1)S(1)} %get-tuple-element.8.own_ref), channel_id=1, source_target_pairs={{0,4},{1,5},{2,6},{3,7},{4,8},{5,9},{6,10},{7,11},{8,12},{9,13},{1... | collective-permute-start | bytes 430088 | tf_op jit(solution)/shard_map/ppermute | solution.py:34
  30.1 2.4 %collective-permute-done.7.refs_1_ = bf16[40,1792]{1,0:T(8,128)(2,1)S(1)} collective-permute-done((bf16[40,1792]{1,0:T(8,128)(2,1)S(1)}, bf16[40,1792]{1,0:T(8,128)(2,1)S(1)}, u32[]{:S(2)}, u32[]{:S(2)}) %collective-permute-start.7) | collective-permute-done | bytes 143392 | tf_op jit(solution)/shard_map/ppermute | solution.py:34
  32.5 1.6 %collective-permute-start.13 = (bf16[3,40,1792]{2,1,0:T(8,128)(2,1)S(1)}, bf16[3,40,1792]{2,1,0:T(8,128)(2,1)S(1)}, u32[]{:S(2)}, u32[]{:S(2)}) collective-permute-start(bf16[3,40,1792]{2,1,0:T(8,128)(2,1)S(1)} %pile.6.z_ref.refs_0_), channel_id=1, source_target_pairs={{0,2},{1,3},{2,0},{3,1},{4,6},{5,7},{6,4},{7,5},{8,10},{9,11},{10,... | collective-permute-start | bytes 1290248 | tf_op jit(solution)/shard_map/ppermute | solution.py:34
  34.6 2.5 %collective-permute-start.2 = (bf16[40,1792]{1,0:T(8,128)(2,1)S(1)}, bf16[40,1792]{1,0:T(8,128)(2,1)S(1)}, u32[]{:S(2)}, u32[]{:S(2)}) collective-permute-start(bf16[40,1792]{1,0:T(8,128)(2,1)S(1)} %get-tuple-element.8.own_ref), channel_id=1, source_target_pairs={{0,8},{1,9},{2,10},{3,11},{4,12},{5,13},{6,14},{7,15},{8,0},{9,1},... | collective-permute-start | bytes 430088 | tf_op jit(solution)/shard_map/ppermute | solution.py:34
  37.1 7.1 %collective-permute-done.2.refs_1_ = bf16[40,1792]{1,0:T(8,128)(2,1)S(1)} collective-permute-done((bf16[40,1792]{1,0:T(8,128)(2,1)S(1)}, bf16[40,1792]{1,0:T(8,128)(2,1)S(1)}, u32[]{:S(2)}, u32[]{:S(2)}) %collective-permute-start.2) | collective-permute-done | bytes 143392 | tf_op jit(solution)/shard_map/ppermute | solution.py:34
  44.2 2.5 %collective-permute-start.3 = (bf16[40,1792]{1,0:T(8,128)(2,1)S(1)}, bf16[40,1792]{1,0:T(8,128)(2,1)S(1)}, u32[]{:S(2)}, u32[]{:S(2)}) collective-permute-start(bf16[40,1792]{1,0:T(8,128)(2,1)S(1)} %get-tuple-element.8.own_ref), channel_id=1, source_target_pairs={{0,12},{1,13},{2,14},{3,15},{4,0},{5,1},{6,2},{7,3},{8,4},{9,5},{1... | collective-permute-start | bytes 430088 | tf_op jit(solution)/shard_map/ppermute | solution.py:34
  46.7 3.0 %collective-permute-done.3.refs_2_ = bf16[40,1792]{1,0:T(8,128)(2,1)S(1)} collective-permute-done((bf16[40,1792]{1,0:T(8,128)(2,1)S(1)}, bf16[40,1792]{1,0:T(8,128)(2,1)S(1)}, u32[]{:S(2)}, u32[]{:S(2)}) %collective-permute-start.3) | collective-permute-done | bytes 143392 | tf_op jit(solution)/shard_map/ppermute | solution.py:34
  50.4 5.2 %rotate_out.1.refs_0_ = bf16[80,512]{1,0:T(8,128)(2,1)S(1)} custom-call(s32[1]{0:T(128)} %bitcast.me_ref, bf16[4,40,1024]{2,1,0:T(8,128)(2,1)S(1)} %pile.5.z_ref, bf16[4,40,1024]{2,1,0:T(8,128)(2,1)S(1)} %collective-permute-done.12.refs_3_.y_ref, bf16[4,40,1024]{2,1,0:T(8,128)(2,1)S(1)} %collective-permute-done.15.cz_ref, ...), custom_call_target="tpu_custom_call" | custom-call | flops 671088640 | bytes 8388608 | tf_op jit(solution)/shard_map/rotate_out/pallas_call | solution.py:102
  55.7 4.8 %collective-permute-start.18 = (bf16[80,512]{1,0:T(8,128)(2,1)S(1)}, bf16[80,512]{1,0:T(8,128)(2,1)S(1)}, u32[]{:S(2)}, u32[]{:S(2)}) collective-permute-start(bf16[80,512]{1,0:T(8,128)(2,1)S(1)} %rotate_out.1.refs_0_), channel_id=1, source_target_pairs={{0,8},{1,9},{2,10},{3,11},{4,12},{5,13},{6,14},{7,15},{8,0},{9,1},... | collective-permute-start | bytes 245768 | tf_op jit(solution)/shard_map/ppermute | solution.py:34
  60.6 4.6 %rotate_in.2.refs_0_.refs_4_ = f32[192,40]{1,0:T(8,128)S(1)} custom-call(s32[1]{0:T(128)} %bitcast.me_ref, bf16[40,1792]{1,0:T(8,128)(2,1)S(1)} %get-tuple-element.7.own_ref, bf16[40,1792]{1,0:T(8,128)(2,1)S(1)} %get-tuple-element.5.across_ref, bf16[3,40,1792]{2,1,0:T(8,128)(2,1)S(1)} %pile.6.z_ref.refs_0_, ...), custom_call_target="tpu_custom_call" | custom-call | flops 220200960 | bytes 5505024 | tf_op jit(solution)/shard_map/rotate_in/pallas_call | solution.py:153
  65.7 1.4 %collective-permute-start.20 = (bf16[4,80,512]{2,1,0:T(8,128)(2,1)S(1)}, bf16[4,80,512]{2,1,0:T(8,128)(2,1)S(1)}, u32[]{:S(2)}, u32[]{:S(2)}) collective-permute-start(bf16[4,80,512]{2,1,0:T(8,128)(2,1)S(1)} %pile.7.z_ref), channel_id=1, source_target_pairs={{0,2},{1,3},{2,0},{3,1},{4,6},{5,7},{6,4},{7,5},{8,10},{9,11},{10,... | collective-permute-start | bytes 983048 | tf_op jit(solution)/shard_map/ppermute | solution.py:34
  67.1 4.6 %rotate_in.3 = f32[192,40]{1,0:T(8,128)S(1)} custom-call(s32[1]{0:T(128)} %bitcast.me_ref, bf16[40,1792]{1,0:T(8,128)(2,1)S(1)} %get-tuple-element.8.own_ref, bf16[40,1792]{1,0:T(8,128)(2,1)S(1)} %get-tuple-element.6.across_ref, bf16[3,40,1792]{2,1,0:T(8,128)(2,1)S(1)} %pile.4.z_ref.refs_5_, bf16[3,40,1792]{2,1,0:T(8,128)(2,1)S(1)} %collective-permute-done.4.y_ref, ...), custom_call_target="tpu_custom_call" | custom-call | flops 220200960 | bytes 5505024 | tf_op jit(solution)/shard_map/rotate_in/pallas_call | solution.py:153
  71.7 2.3 %collective-permute-done.20.y_ref = bf16[4,80,512]{2,1,0:T(8,128)(2,1)S(1)} collective-permute-done((bf16[4,80,512]{2,1,0:T(8,128)(2,1)S(1)}, bf16[4,80,512]{2,1,0:T(8,128)(2,1)S(1)}, u32[]{:S(2)}, u32[]{:S(2)}) %collective-permute-start.20) | collective-permute-done | bytes 327712 | tf_op jit(solution)/shard_map/ppermute | solution.py:34
  75.6 1.8 %combine.1 = bf16[96,8192]{1,0:T(8,128)(2,1)} custom-call(s32[1]{0:T(128)} %bitcast.me_ref, bf16[96,40]{1,0:T(8,128)(2,1)S(1)} %get-tuple-element.12.own_ref, bf16[96,40]{1,0:T(8,128)(2,1)S(1)} %collective-permute-done.14.other_ref, bf16[4,80,512]{2,1,0:T(8,128)(2,1)S(1)} %pile.7.z_ref, bf16[4,80,512]{2,1,0:T(8,128)(2,1)S(1)} %collective-permute-done.20.y_ref, ...), custom_call_target="tpu_custom_call" | custom-call | flops 125829120 | bytes 3145728 | tf_op jit(solution)/shard_map/combine/pallas_call | solution.py:208
  (36 shorter events, 6.4 us)
Async XLA Ops:
  0.0 60.6 %collective-permute-start.5 = (bf16[96,28672]{1,0:T(8,128)(2,1)}, bf16[96,28672]{1,0:T(8,128)(2,1)}, u32[]{:S(2)}, u32[]{:S(2)}) collective-permute-start(bf16[96,28672]{1,0:T(8,128)(2,1)} %bitcast.20), channel_id=1, source_target_pairs={{0,1},{1,0},{2,3},{3,2},{4,5},{5,4},{6,7},{7,6},{8,9},{9,8},{10,11... | collective-permute-start | bytes 16515080 | tf_op jit(solution)/shard_map/ppermute | solution.py:34
  1.5 13.9 %collective-permute-start = (bf16[2,40,1792]{2,1,0:T(8,128)(2,1)S(1)}, bf16[2,40,1792]{2,1,0:T(8,128)(2,1)S(1)}, u32[]{:S(2)}, u32[]{:S(2)}) collective-permute-start(bf16[2,40,1792]{2,1,0:T(8,128)(2,1)S(1)} %get-tuple-element.9), channel_id=1, source_target_pairs={{0,2},{1,3},{2,0},{3,1},{4,6},{5,7},{6,4},{7,5},{8,10},{9,11},{10,... | collective-permute-start | bytes 860168 | tf_op jit(solution)/shard_map/ppermute | solution.py:34
  5.2 7.8 %collective-permute-start.10 = (bf16[40,1024]{1,0:T(8,128)(2,1)S(1)}, bf16[40,1024]{1,0:T(8,128)(2,1)S(1)}, u32[]{:S(2)}, u32[]{:S(2)}) collective-permute-start(bf16[40,1024]{1,0:T(8,128)(2,1)S(1)} %reshape.19.refs_0_), channel_id=1, source_target_pairs={{0,8},{1,9},{2,10},{3,11},{4,12},{5,13},{6,14},{7,15},{8,0},{9,1},... | collective-permute-start | bytes 245768 | tf_op jit(solution)/shard_map/ppermute | solution.py:34
  7.8 5.2 %collective-permute-start.11 = (bf16[40,1024]{1,0:T(8,128)(2,1)S(1)}, bf16[40,1024]{1,0:T(8,128)(2,1)S(1)}, u32[]{:S(2)}, u32[]{:S(2)}) collective-permute-start(bf16[40,1024]{1,0:T(8,128)(2,1)S(1)} %reshape.19.refs_0_), channel_id=1, source_target_pairs={{0,12},{1,13},{2,14},{3,15},{4,0},{5,1},{6,2},{7,3},{8,4},{9,5},{1... | collective-permute-start | bytes 245768 | tf_op jit(solution)/shard_map/ppermute | solution.py:34
  9.2 6.3 %collective-permute-start.9 = (bf16[40,1024]{1,0:T(8,128)(2,1)S(1)}, bf16[40,1024]{1,0:T(8,128)(2,1)S(1)}, u32[]{:S(2)}, u32[]{:S(2)}) collective-permute-start(bf16[40,1024]{1,0:T(8,128)(2,1)S(1)} %reshape.19.refs_0_), channel_id=1, source_target_pairs={{0,4},{1,5},{2,6},{3,7},{4,8},{5,9},{6,10},{7,11},{8,12},{9,13},{1... | collective-permute-start | bytes 245768 | tf_op jit(solution)/shard_map/ppermute | solution.py:34
  15.5 16.9 %collective-permute-start.12 = (bf16[4,40,1024]{2,1,0:T(8,128)(2,1)S(1)}, bf16[4,40,1024]{2,1,0:T(8,128)(2,1)S(1)}, u32[]{:S(2)}, u32[]{:S(2)}) collective-permute-start(bf16[4,40,1024]{2,1,0:T(8,128)(2,1)S(1)} %pile.5.z_ref), channel_id=1, source_target_pairs={{0,2},{1,3},{2,0},{3,1},{4,6},{5,7},{6,4},{7,5},{8,10},{9,11},{10,... | collective-permute-start | bytes 983048 | tf_op jit(solution)/shard_map/ppermute | solution.py:34
  16.1 7.9 %collective-permute-start.6 = (bf16[40,1792]{1,0:T(8,128)(2,1)S(1)}, bf16[40,1792]{1,0:T(8,128)(2,1)S(1)}, u32[]{:S(2)}, u32[]{:S(2)}) collective-permute-start(bf16[40,1792]{1,0:T(8,128)(2,1)S(1)} %get-tuple-element.7.own_ref), channel_id=1, source_target_pairs={{0,4},{1,5},{2,6},{3,7},{4,8},{5,9},{6,10},{7,11},{8,12},{9,13},{1... | collective-permute-start | bytes 430088 | tf_op jit(solution)/shard_map/ppermute | solution.py:34
  17.4 15.1 %collective-permute-start.7 = (bf16[40,1792]{1,0:T(8,128)(2,1)S(1)}, bf16[40,1792]{1,0:T(8,128)(2,1)S(1)}, u32[]{:S(2)}, u32[]{:S(2)}) collective-permute-start(bf16[40,1792]{1,0:T(8,128)(2,1)S(1)} %get-tuple-element.7.own_ref), channel_id=1, source_target_pairs={{0,8},{1,9},{2,10},{3,11},{4,12},{5,13},{6,14},{7,15},{8,0},{9,1},... | collective-permute-start | bytes 430088 | tf_op jit(solution)/shard_map/ppermute | solution.py:34
  19.4 13.1 %collective-permute-start.8 = (bf16[40,1792]{1,0:T(8,128)(2,1)S(1)}, bf16[40,1792]{1,0:T(8,128)(2,1)S(1)}, u32[]{:S(2)}, u32[]{:S(2)}) collective-permute-start(bf16[40,1792]{1,0:T(8,128)(2,1)S(1)} %get-tuple-element.7.own_ref), channel_id=1, source_target_pairs={{0,12},{1,13},{2,14},{3,15},{4,0},{5,1},{6,2},{7,3},{8,4},{9,5},{1... | collective-permute-start | bytes 430088 | tf_op jit(solution)/shard_map/ppermute | solution.py:34
  24.0 10.6 %collective-permute-start.1 = (bf16[40,1792]{1,0:T(8,128)(2,1)S(1)}, bf16[40,1792]{1,0:T(8,128)(2,1)S(1)}, u32[]{:S(2)}, u32[]{:S(2)}) collective-permute-start(bf16[40,1792]{1,0:T(8,128)(2,1)S(1)} %get-tuple-element.8.own_ref), channel_id=1, source_target_pairs={{0,4},{1,5},{2,6},{3,7},{4,8},{5,9},{6,10},{7,11},{8,12},{9,13},{1... | collective-permute-start | bytes 430088 | tf_op jit(solution)/shard_map/ppermute | solution.py:34
  32.5 28.1 %collective-permute-start.13 = (bf16[3,40,1792]{2,1,0:T(8,128)(2,1)S(1)}, bf16[3,40,1792]{2,1,0:T(8,128)(2,1)S(1)}, u32[]{:S(2)}, u32[]{:S(2)}) collective-permute-start(bf16[3,40,1792]{2,1,0:T(8,128)(2,1)S(1)} %pile.6.z_ref.refs_0_), channel_id=1, source_target_pairs={{0,2},{1,3},{2,0},{3,1},{4,6},{5,7},{6,4},{7,5},{8,10},{9,11},{10,... | collective-permute-start | bytes 1290248 | tf_op jit(solution)/shard_map/ppermute | solution.py:34
  34.0 16.4 %collective-permute-start.15 = (bf16[4,40,1024]{2,1,0:T(8,128)(2,1)S(1)}, bf16[4,40,1024]{2,1,0:T(8,128)(2,1)S(1)}, u32[]{:S(2)}, u32[]{:S(2)}) collective-permute-start(bf16[4,40,1024]{2,1,0:T(8,128)(2,1)S(1)} %pile.5.z_ref), channel_id=1, source_target_pairs={{0,1},{1,0},{2,3},{3,2},{4,5},{5,4},{6,7},{7,6},{8,9},{9,8},{10,11... | collective-permute-start | bytes 983048 | tf_op jit(solution)/shard_map/ppermute | solution.py:34
  34.1 16.4 %collective-permute-start.16 = (bf16[4,40,1024]{2,1,0:T(8,128)(2,1)S(1)}, bf16[4,40,1024]{2,1,0:T(8,128)(2,1)S(1)}, u32[]{:S(2)}, u32[]{:S(2)}) collective-permute-start(bf16[4,40,1024]{2,1,0:T(8,128)(2,1)S(1)} %collective-permute-done.12.refs_3_.y_ref), channel_id=1, source_target_pairs={{0,1},{1,0},{2,3},{3,2},{4,5},{5,4},{6,7},{7,6},{8,9},{9,8},{10,11... | collective-permute-start | bytes 983048 | tf_op jit(solution)/shard_map/ppermute | solution.py:34
  34.6 9.6 %collective-permute-start.2 = (bf16[40,1792]{1,0:T(8,128)(2,1)S(1)}, bf16[40,1792]{1,0:T(8,128)(2,1)S(1)}, u32[]{:S(2)}, u32[]{:S(2)}) collective-permute-start(bf16[40,1792]{1,0:T(8,128)(2,1)S(1)} %get-tuple-element.8.own_ref), channel_id=1, source_target_pairs={{0,8},{1,9},{2,10},{3,11},{4,12},{5,13},{6,14},{7,15},{8,0},{9,1},... | collective-permute-start | bytes 430088 | tf_op jit(solution)/shard_map/ppermute | solution.py:34
  44.2 5.4 %collective-permute-start.3 = (bf16[40,1792]{1,0:T(8,128)(2,1)S(1)}, bf16[40,1792]{1,0:T(8,128)(2,1)S(1)}, u32[]{:S(2)}, u32[]{:S(2)}) collective-permute-start(bf16[40,1792]{1,0:T(8,128)(2,1)S(1)} %get-tuple-element.8.own_ref), channel_id=1, source_target_pairs={{0,12},{1,13},{2,14},{3,15},{4,0},{5,1},{6,2},{7,3},{8,4},{9,5},{1... | collective-permute-start | bytes 430088 | tf_op jit(solution)/shard_map/ppermute | solution.py:34
  49.7 17.4 %collective-permute-start.4 = (bf16[3,40,1792]{2,1,0:T(8,128)(2,1)S(1)}, bf16[3,40,1792]{2,1,0:T(8,128)(2,1)S(1)}, u32[]{:S(2)}, u32[]{:S(2)}) collective-permute-start(bf16[3,40,1792]{2,1,0:T(8,128)(2,1)S(1)} %pile.4.z_ref.refs_5_), channel_id=1, source_target_pairs={{0,2},{1,3},{2,0},{3,1},{4,6},{5,7},{6,4},{7,5},{8,10},{9,11},{10,... | collective-permute-start | bytes 1290248 | tf_op jit(solution)/shard_map/ppermute | solution.py:34
  55.6 9.5 %collective-permute-start.17 = (bf16[80,512]{1,0:T(8,128)(2,1)S(1)}, bf16[80,512]{1,0:T(8,128)(2,1)S(1)}, u32[]{:S(2)}, u32[]{:S(2)}) collective-permute-start(bf16[80,512]{1,0:T(8,128)(2,1)S(1)} %rotate_out.1.refs_0_), channel_id=1, source_target_pairs={{0,4},{1,5},{2,6},{3,7},{4,8},{5,9},{6,10},{7,11},{8,12},{9,13},{1... | collective-permute-start | bytes 245768 | tf_op jit(solution)/shard_map/ppermute | solution.py:34
  55.7 9.7 %collective-permute-start.18 = (bf16[80,512]{1,0:T(8,128)(2,1)S(1)}, bf16[80,512]{1,0:T(8,128)(2,1)S(1)}, u32[]{:S(2)}, u32[]{:S(2)}) collective-permute-start(bf16[80,512]{1,0:T(8,128)(2,1)S(1)} %rotate_out.1.refs_0_), channel_id=1, source_target_pairs={{0,8},{1,9},{2,10},{3,11},{4,12},{5,13},{6,14},{7,15},{8,0},{9,1},... | collective-permute-start | bytes 245768 | tf_op jit(solution)/shard_map/ppermute | solution.py:34
  60.5 5.1 %collective-permute-start.19 = (bf16[80,512]{1,0:T(8,128)(2,1)S(1)}, bf16[80,512]{1,0:T(8,128)(2,1)S(1)}, u32[]{:S(2)}, u32[]{:S(2)}) collective-permute-start(bf16[80,512]{1,0:T(8,128)(2,1)S(1)} %rotate_out.1.refs_0_), channel_id=1, source_target_pairs={{0,12},{1,13},{2,14},{3,15},{4,0},{5,1},{6,2},{7,3},{8,4},{9,5},{1... | collective-permute-start | bytes 245768 | tf_op jit(solution)/shard_map/ppermute | solution.py:34
  65.7 8.2 %collective-permute-start.20 = (bf16[4,80,512]{2,1,0:T(8,128)(2,1)S(1)}, bf16[4,80,512]{2,1,0:T(8,128)(2,1)S(1)}, u32[]{:S(2)}, u32[]{:S(2)}) collective-permute-start(bf16[4,80,512]{2,1,0:T(8,128)(2,1)S(1)} %pile.7.z_ref), channel_id=1, source_target_pairs={{0,2},{1,3},{2,0},{3,1},{4,6},{5,7},{6,4},{7,5},{8,10},{9,11},{10,... | collective-permute-start | bytes 983048 | tf_op jit(solution)/shard_map/ppermute | solution.py:34
  67.1 8.5 %collective-permute-start.21 = (bf16[4,80,512]{2,1,0:T(8,128)(2,1)S(1)}, bf16[4,80,512]{2,1,0:T(8,128)(2,1)S(1)}, u32[]{:S(2)}, u32[]{:S(2)}) collective-permute-start(bf16[4,80,512]{2,1,0:T(8,128)(2,1)S(1)} %pile.7.z_ref), channel_id=1, source_target_pairs={{0,1},{1,0},{2,3},{3,2},{4,5},{5,4},{6,7},{7,6},{8,9},{9,8},{10,11... | collective-permute-start | bytes 983048 | tf_op jit(solution)/shard_map/ppermute | solution.py:34
  73.9 1.7 %collective-permute-start.22 = (bf16[4,80,512]{2,1,0:T(8,128)(2,1)S(1)}, bf16[4,80,512]{2,1,0:T(8,128)(2,1)S(1)}, u32[]{:S(2)}, u32[]{:S(2)}) collective-permute-start(bf16[4,80,512]{2,1,0:T(8,128)(2,1)S(1)} %collective-permute-done.20.y_ref), channel_id=1, source_target_pairs={{0,1},{1,0},{2,3},{3,2},{4,5},{5,4},{6,7},{7,6},{8,9},{9,8},{10,11... | collective-permute-start | bytes 983048 | tf_op jit(solution)/shard_map/ppermute | solution.py:34
  73.9 1.6 %collective-permute-start.14 = (bf16[96,40]{1,0:T(8,128)(2,1)S(1)}, bf16[96,40]{1,0:T(8,128)(2,1)S(1)}, u32[]{:S(2)}, u32[]{:S(2)}) collective-permute-start(bf16[96,40]{1,0:T(8,128)(2,1)S(1)} %get-tuple-element.11), channel_id=1, source_target_pairs={{0,1},{1,0},{2,3},{3,2},{4,5},{5,4},{6,7},{7,6},{8,9},{9,8},{10,11... | collective-permute-start | bytes 23048 | tf_op jit(solution)/shard_map/ppermute | solution.py:34

commit v5 on v4

--- a/solution.py
+++ b/solution.py
@@ -17,9 +17,12 @@
 SMEM = pl.BlockSpec(memory_space=pltpu.SMEM)
 
 
-def along(devices, by):
+def row(block, devices):
     each = CORES * PAIR
-    return [(d, (d + by * each) % devices) for d in range(devices)]
+    steps = devices // each
+    rows = [[first + each * step for step in range(steps)] for first in range(each)]
+    copies = jnp.broadcast_to(block, (steps, *block.shape))
+    return lax.all_to_all(copies, "wide", 0, 0, axis_index_groups=rows)
 
 
 def across(devices):
@@ -34,16 +37,14 @@
     return lax.ppermute(block, "wide", pairs)
 
 
-def origin(me, devices, step, other_chip, other_core):
-    each = CORES * PAIR
-    pair = lax.rem(me // each + devices // each - step, devices // each)
+def origin(me, step, other_chip, other_core):
     chip = lax.rem(me // CORES, PAIR)
     core = lax.rem(me, CORES)
     if other_chip:
         chip = 1 - chip
     if other_core:
         core = 1 - core
-    return pair * PAIR + chip, core
+    return step * PAIR + chip, core
 
 
 def repeat(times, body, carry=None, loop=False):
@@ -77,7 +78,7 @@
         for ref, chip_bit, core_bit in ((z_ref, 0, 0), (y_ref, 1, 0), (cz_ref, 0, 1), (cy_ref, 1, 1)):
 
             def put(step, _, ref=ref, chip_bit=chip_bit, core_bit=core_bit):
-                chip, core = origin(me, devices, step, chip_bit, core_bit)
+                chip, core = origin(me, step, chip_bit, core_bit)
                 unfold_store(rows, core * (devices // CORES) + chip, ref[step])
 
             repeat(steps, put)
@@ -117,24 +118,21 @@
     )(me, z, y, cz, cy, basis, *waits)
 
 
-def rotate_in_kernel(tokens, before, me_ref, own_ref, across_ref, z_ref, y_ref, mine_ref, theirs_ref, *refs):
+def rotate_in_kernel(tokens, before, me_ref, z_ref, y_ref, mine_ref, theirs_ref, *refs):
     total_ref, rows = refs[before:]
-    height, width = own_ref.shape
-    steps = z_ref.shape[0] + 1
+    steps, _, width = z_ref.shape
     devices = steps * CORES * PAIR
     chips = devices // CORES
     me = me_ref[0]
 
     @pl.when(pl.program_id(0) == 0)
     def _():
-        unfold_store(rows, origin(me, devices, 0, 0, 0)[0], own_ref[...])
-        unfold_store(rows, origin(me, devices, 0, 1, 0)[0], across_ref[...])
         for ref, chip_bit in ((z_ref, 0), (y_ref, 1)):
 
             def put(step, _, ref=ref, chip_bit=chip_bit):
-                unfold_store(rows, origin(me, devices, step + 1, chip_bit, 0)[0], ref[step])
-
-            repeat(steps - 1, put)
+                unfold_store(rows, origin(me, step, chip_bit, 0)[0], ref[step])
+
+            repeat(steps, put)
         total_ref[...] = refs[0][...] if before else jnp.zeros_like(total_ref)
 
     def add(fold, _):
@@ -146,15 +144,15 @@
     repeat(FOLDS, add, None, steps > SUBLANES)
 
 
-def rotate_in(tokens, chunk, me, own, across, z, y, mine, theirs, before):
-    height, width = own.shape
-    chips = (z.shape[0] + 1) * PAIR
+def rotate_in(tokens, chunk, me, z, y, mine, theirs, before):
+    steps, height, width = z.shape
+    chips = steps * PAIR
     basis = pl.BlockSpec((mine.shape[0], FOLDS * width), lambda i: (0, chunk * (SUBLANES // FOLDS) + i))
     return pl.pallas_call(
         functools.partial(rotate_in_kernel, tokens, len(before)),
         grid=(SUBLANES // FOLDS,),
         out_shape=jax.ShapeDtypeStruct((2 * mine.shape[0], chips * tokens), jnp.float32),
-        in_specs=[SMEM] + [VMEM] * 4 + [basis] * 2 + [VMEM] * len(before),
+        in_specs=[SMEM] + [VMEM] * 2 + [basis] * 2 + [VMEM] * len(before),
         out_specs=VMEM,
         scratch_shapes=[pltpu.VMEM((width // 128, chips * height, 128), jnp.float32)],
         compiler_params=pltpu.CompilerParams(vmem_limit_bytes=48 * 2**20),
@@ -164,24 +162,7 @@
             transcendentals=0,
         ),
         name="rotate_in",
-    )(me, own, across, z, y, mine, theirs, *before)
-
-
-def pile_kernel(blocks, *refs):
-    for step in range(blocks):
-        refs[-1][step] = refs[step][...]
-
-
-def pile(blocks, waits):
-    return pl.pallas_call(
-        functools.partial(pile_kernel, len(blocks)),
-        out_shape=jax.ShapeDtypeStruct((len(blocks), *blocks[0].shape), blocks[0].dtype),
-        in_specs=[VMEM] * len(blocks) + [ANY] * len(waits),
-        out_specs=VMEM,
-        compiler_params=pltpu.CompilerParams(vmem_limit_bytes=48 * 2**20),
-        cost_estimate=pl.CostEstimate(flops=0, bytes_accessed=2 * len(blocks) * blocks[0].size, transcendentals=0),
-        name="pile",
-    )(*blocks, *waits)
+    )(me, z, y, mine, theirs, *before)
 
 
 def combine_kernel(me_ref, own_ref, other_ref, z_ref, y_ref, cz_ref, cy_ref, out_ref):
@@ -194,7 +175,7 @@
     for ref, chip_bit, core_bit in ((z_ref, 0, 0), (y_ref, 1, 0), (cz_ref, 0, 1), (cy_ref, 1, 1)):
 
         def put(step, _, ref=ref, chip_bit=chip_bit, core_bit=core_bit):
-            chip, core = origin(me, devices, step, chip_bit, core_bit)
+            chip, core = origin(me, step, chip_bit, core_bit)
             at = pl.multiple_of((chip * CORES + core) * width, 128)
             total = jnp.dot(left, ref[step], preferred_element_type=jnp.float32)
             out_ref[:, pl.ds(at, width)] = (total / total_tokens).astype(out_ref.dtype)
@@ -220,12 +201,8 @@
 
 def local(acts, grads, basis_in, basis_out):
     devices = lax.axis_size("wide")
-    steps = devices // (CORES * PAIR)
     tokens = acts.shape[0]
     me = lax.axis_index("wide").astype(jnp.int32).reshape(1)
-
-    def along_all(block):
-        return [send(block, along(devices, step)) for step in range(1, steps)]
 
     def others(z):
         y = send(z, across(devices))
@@ -235,32 +212,19 @@
     theirs = send(mine, swap(devices))
     width = acts.shape[1] // (CHUNKS * SUBLANES)
     folded = acts.reshape(tokens, CHUNKS, SUBLANES, width).transpose(1, 0, 2, 3).reshape(CHUNKS, -1, width)
-    folded_across = send(folded, across(devices))
-    block = grads.reshape(tokens * SUBLANES, -1)
-    grads_z = others(pile([block] + along_all(block), [folded_across]))
-
-    acts_z = []
-    acts_y = []
+    grads_all = others(row(grads.reshape(tokens * SUBLANES, -1), devices))
+    acts_z = [row(folded[chunk], devices) for chunk in range(CHUNKS)]
+    acts_y = [send(z, across(devices)) for z in acts_z]
+
+    sq_out = rotate_out(tokens, me, *grads_all, basis_out, [acts_z[0]])
+
+    total = []
     for chunk in range(CHUNKS):
-        acts_z.append(pile(along_all(folded[chunk]), [] if chunk else [grads_z[1]]))
-        acts_y.append(send(acts_z[chunk], across(devices)))
-
-    sq_out = rotate_out(tokens, me, *grads_z, basis_out, [acts_z[0]])
-    came = along_all(sq_out)
-
-    def part(chunk, before):
-        return rotate_in(
-            tokens, chunk, me, folded[chunk], folded_across[chunk], acts_z[chunk], acts_y[chunk], mine, theirs, before
-        )
-
-    total = part(0, [])
-    z = pile([sq_out] + came, [total, acts_z[-1]])
-    for chunk in range(1, CHUNKS):
-        total = part(chunk, [total])
-    squares = (total * total).astype(jnp.bfloat16)
+        total = [rotate_in(tokens, chunk, me, acts_z[chunk], acts_y[chunk], mine, theirs, total)]
+    squares = (total[0] * total[0]).astype(jnp.bfloat16)
     own, given = squares[: mine.shape[0]], squares[mine.shape[0] :]
     other = send(given, swap(devices))
-    return combine(me, own, other, *others(z))
+    return combine(me, own, other, *others(row(sq_out, devices)))
 
 
 def solution(mesh):

time: 77.7 us -> 109 us (1.40)
  waiting for transfers between devices: 23.7 us -> 49.4 us
  blocking collectives: 0 us -> 17.8 us
  starting transfers between devices: 35.2 us -> 20.2 us
  local copies, waits for them, and re-layouts: 2.17 us -> 4.54 us
    ppermute x23 -> x10, starting transfers between devices: 35.2 us -> 6.15 us  [send(): return lax.ppermute(block, 'wide', pairs)]
    all_to_all x0 -> x3, waiting for transfers between devices: none -> 18.4 us  [row(): return lax.all_to_all(copies, 'wide', 0, 0, axis_index_groups=rows)]
    all_to_all x0 -> x1, blocking collectives: none -> 17.8 us  [row(): return lax.all_to_all(copies, 'wide', 0, 0, axis_index_groups=rows)]
    all_to_all x0 -> x3, starting transfers between devices: none -> 14.1 us  [row(): return lax.all_to_all(copies, 'wide', 0, 0, axis_index_groups=rows)]
    ppermute x23 -> x10, waiting for transfers between devices: 23.7 us -> 31 us  [send(): return lax.ppermute(block, 'wide', pairs)]
    broadcast_in_dim x0 -> x4, local copies, waits for them, and re-layouts: none -> 2.39 us  [row(): copies = jnp.broadcast_to(block, (steps, *block.shape))]
  transfers between devices with their start and end apart: 23 -> 13, of which waited for: 10 -> 6; matrix products, arithmetic and copies ran while one was open for 3% -> 4% of each run, Pallas kernels for 19% -> 13%
where the time goes in v5:
time: 109 us; the launch traced here: 108 us
  waiting for transfers between devices  49.4 us (45%)
  starting transfers between devices  20.2 us (19%)
  blocking collectives  17.8 us (16%)
  Pallas kernels  16 us (15%)
  local copies, waits for them, and re-layouts  4.54 us (4%)
    ppermute x10, waiting for transfers between devices, send(): return lax.ppermute(block, 'wide', pairs)  31 us
    all_to_all x3, waiting for transfers between devices, row(): return lax.all_to_all(copies, 'wide', 0, 0, axis_index_groups=rows)  18.4 us
    all_to_all x1, blocking collectives, row(): return lax.all_to_all(copies, 'wide', 0, 0, axis_index_groups=rows)  17.8 us
    all_to_all x3, starting transfers between devices, row(): return lax.all_to_all(copies, 'wide', 0, 0, axis_index_groups=rows)  14.1 us
    pallas_call x2, Pallas kernels, rotate_in(): pl.pallas_call(functools.partial(rotate_in_kernel, tokens, len(before)),...  9.1 us
    ppermute x10, starting transfers between devices, send(): return lax.ppermute(block, 'wide', pairs)  6.15 us
    pallas_call x1, Pallas kernels, rotate_out(): pl.pallas_call(functools.partial(rotate_out_kernel, tokens, len(waits)),...  5.18 us
    broadcast_in_dim x4, local copies, waits for them, and re-layouts, row(): copies = jnp.broadcast_to(block, (steps, *block.shape))  2.39 us
  transfers between devices with their start and end apart: 13, of which 6 were waited for; matrix products, arithmetic and copies ran while one was open for 4% of the time, Pallas kernels for 13%

profile of v5, /device:TPU:0, one launch (start us, length us, event | category | flops | bytes accessed | tf_op | source)
XLA Modules:
  0.0 108.1 jit_solution(8593270180525718010)
XLA Ops:
  0.5 1.0 reshape.16
  1.5 0.8 broadcast_in_dim.14
  2.3 5.9 %all-to-all-start.2 = ((bf16[4,40,1024]{2,1,0:T(8,128)(2,1)}), bf16[4,40,1024]{2,1,0:T(8,128)(2,1)S(1)}, u32[]{:S(2)}, u32[]{:S(2)}) async-start(bf16[4,40,1024]{2,1,0:T(8,128)(2,1)} %broadcast_in_dim.14), calls=%async_computation.2 | async-start | bytes 655360 | tf_op jit(solution)/shard_map/all_to_all | solution.py:25
  8.1 1.1 copy.7
  9.2 9.8 %all-to-all-done.2.z_ref = bf16[4,40,1024]{2,1,0:T(8,128)(2,1)S(1)} async-done(((bf16[4,40,1024]{2,1,0:T(8,128)(2,1)}), bf16[4,40,1024]{2,1,0:T(8,128)(2,1)S(1)}, u32[]{:S(2)}, u32[]{:S(2)}) %all-to-all-start.2) | async-done | bytes 327712 | tf_op jit(solution)/shard_map/all_to_all | solution.py:25
  19.1 17.8 %all_to_all.20.z_ref.refs_0_ = bf16[4,40,1792]{2,1,0:T(8,128)(2,1)S(1)} all-to-all(bf16[4,40,1792]{2,1,0:T(8,128)(2,1)S(1)} %broadcast_in_dim.13), channel_id=1, replica_groups={{0,4,8,12},{1,5,9,13},{2,6,10,14},{3,7,11,15},{16,20,24,28},{17,21,25,2..., dimensions={0} | all-to-all | bytes 1146880 | tf_op jit(solution)/shard_map/all_to_all | solution.py:25
  36.9 0.8 broadcast_in_dim.12
  37.7 3.5 %all-to-all-start = ((bf16[4,40,1792]{2,1,0:T(8,128)(2,1)}), bf16[4,40,1792]{2,1,0:T(8,128)(2,1)S(1)}, u32[]{:S(2)}, u32[]{:S(2)}) async-start(bf16[4,40,1792]{2,1,0:T(8,128)(2,1)} %broadcast_in_dim.12), calls=%async_computation | async-start | bytes 1146880 | tf_op jit(solution)/shard_map/all_to_all | solution.py:25
  41.2 1.6 %collective-permute-start.4 = (bf16[4,40,1024]{2,1,0:T(8,128)(2,1)S(1)}, bf16[4,40,1024]{2,1,0:T(8,128)(2,1)S(1)}, u32[]{:S(2)}, u32[]{:S(2)}) collective-permute-start(bf16[4,40,1024]{2,1,0:T(8,128)(2,1)S(1)} %all-to-all-done.2.z_ref), channel_id=1, source_target_pairs={{0,2},{1,3},{2,0},{3,1},{4,6},{5,7},{6,4},{7,5},{8,10},{9,11},{10,... | collective-permute-start | bytes 983048 | tf_op jit(solution)/shard_map/ppermute | solution.py:37
  42.8 6.6 %collective-permute-done.4.y_ref = bf16[4,40,1024]{2,1,0:T(8,128)(2,1)S(1)} collective-permute-done((bf16[4,40,1024]{2,1,0:T(8,128)(2,1)S(1)}, bf16[4,40,1024]{2,1,0:T(8,128)(2,1)S(1)}, u32[]{:S(2)}, u32[]{:S(2)}) %collective-permute-start.4) | collective-permute-done | bytes 327712 | tf_op jit(solution)/shard_map/ppermute | solution.py:37
  49.4 1.6 %collective-permute-done.6.cy_ref = bf16[4,40,1024]{2,1,0:T(8,128)(2,1)S(1)} collective-permute-done((bf16[4,40,1024]{2,1,0:T(8,128)(2,1)S(1)}, bf16[4,40,1024]{2,1,0:T(8,128)(2,1)S(1)}, u32[]{:S(2)}, u32[]{:S(2)}) %collective-permute-start.6) | collective-permute-done | bytes 327712 | tf_op jit(solution)/shard_map/ppermute | solution.py:37
  51.0 5.2 %rotate_out.1 = bf16[80,512]{1,0:T(8,128)(2,1)S(1)} custom-call(s32[1]{0:T(128)} %bitcast.me_ref, bf16[4,40,1024]{2,1,0:T(8,128)(2,1)S(1)} %all-to-all-done.2.z_ref, bf16[4,40,1024]{2,1,0:T(8,128)(2,1)S(1)} %collective-permute-done.4.y_ref, bf16[4,40,1024]{2,1,0:T(8,128)(2,1)S(1)} %collective-permute-done.5.cz_ref, ...), custom_call_target="tpu_custom_call" | custom-call | flops 671088640 | bytes 8388608 | tf_op jit(solution)/shard_map/rotate_out/pallas_call | solution.py:103
  56.2 0.7 broadcast_in_dim.15
  57.0 4.7 %all-to-all-start.3 = ((bf16[4,80,512]{2,1,0:T(8,128)(2,1)}), bf16[4,80,512]{2,1,0:T(8,128)(2,1)S(1)}, u32[]{:S(2)}, u32[]{:S(2)}) async-start(bf16[4,80,512]{2,1,0:T(8,128)(2,1)} %broadcast_in_dim.15), calls=%async_computation.3 | async-start | bytes 655360 | tf_op jit(solution)/shard_map/all_to_all | solution.py:25
  61.7 1.5 %collective-permute-start.2 = (bf16[4,40,1792]{2,1,0:T(8,128)(2,1)S(1)}, bf16[4,40,1792]{2,1,0:T(8,128)(2,1)S(1)}, u32[]{:S(2)}, u32[]{:S(2)}) collective-permute-start(bf16[4,40,1792]{2,1,0:T(8,128)(2,1)S(1)} %all_to_all.20.z_ref.refs_0_), channel_id=1, source_target_pairs={{0,2},{1,3},{2,0},{3,1},{4,6},{5,7},{6,4},{7,5},{8,10},{9,11},{10,... | collective-permute-start | bytes 1720328 | tf_op jit(solution)/shard_map/ppermute | solution.py:37
  63.2 0.5 collective-permute-start
  63.7 8.6 %all-to-all-done.3.z_ref = bf16[4,80,512]{2,1,0:T(8,128)(2,1)S(1)} async-done(((bf16[4,80,512]{2,1,0:T(8,128)(2,1)}), bf16[4,80,512]{2,1,0:T(8,128)(2,1)S(1)}, u32[]{:S(2)}, u32[]{:S(2)}) %all-to-all-start.3) | async-done | bytes 327712 | tf_op jit(solution)/shard_map/all_to_all | solution.py:25
  72.3 1.5 %collective-permute-start.7 = (bf16[4,80,512]{2,1,0:T(8,128)(2,1)S(1)}, bf16[4,80,512]{2,1,0:T(8,128)(2,1)S(1)}, u32[]{:S(2)}, u32[]{:S(2)}) collective-permute-start(bf16[4,80,512]{2,1,0:T(8,128)(2,1)S(1)} %all-to-all-done.3.z_ref), channel_id=1, source_target_pairs={{0,2},{1,3},{2,0},{3,1},{4,6},{5,7},{6,4},{7,5},{8,10},{9,11},{10,... | collective-permute-start | bytes 983048 | tf_op jit(solution)/shard_map/ppermute | solution.py:37
  73.8 21.9 %collective-permute-done.7.y_ref = bf16[4,80,512]{2,1,0:T(8,128)(2,1)S(1)} collective-permute-done((bf16[4,80,512]{2,1,0:T(8,128)(2,1)S(1)}, bf16[4,80,512]{2,1,0:T(8,128)(2,1)S(1)}, u32[]{:S(2)}, u32[]{:S(2)}) %collective-permute-start.7) | collective-permute-done | bytes 327712 | tf_op jit(solution)/shard_map/ppermute | solution.py:37
  95.8 4.5 %rotate_in.2.refs_0_ = f32[192,40]{1,0:T(8,128)S(1)} custom-call(s32[1]{0:T(128)} %bitcast.me_ref, bf16[4,40,1792]{2,1,0:T(8,128)(2,1)S(1)} %all_to_all.20.z_ref.refs_0_, bf16[4,40,1792]{2,1,0:T(8,128)(2,1)S(1)} %collective-permute-done.2.y_ref, bf16[96,28672]{1,0:T(8,128)(2,1)} %bitcast.15, bf16[96,28672]{1,0:T(8,128)(2,1)} %collective-permute-done.1.theirs_ref), custom_call_target="tpu_custom_call" | custom-call | flops 220200960 | bytes 5505024 | tf_op jit(solution)/shard_map/rotate_in/pallas_call | solution.py:151
  100.3 4.6 %rotate_in.3 = f32[192,40]{1,0:T(8,128)S(1)} custom-call(s32[1]{0:T(128)} %bitcast.me_ref, bf16[4,40,1792]{2,1,0:T(8,128)(2,1)S(1)} %all-to-all-done.z_ref, bf16[4,40,1792]{2,1,0:T(8,128)(2,1)S(1)} %collective-permute-done.y_ref, bf16[96,28672]{1,0:T(8,128)(2,1)} %bitcast.16, bf16[96,28672]{1,0:T(8,128)(2,1)} %collective-permute-done.1.theirs_ref, ...), custom_call_target="tpu_custom_call" | custom-call | flops 220200960 | bytes 5505024 | tf_op jit(solution)/shard_map/rotate_in/pallas_call | solution.py:151
  104.9 0.6 collective-permute-start.3
  105.5 0.8 collective-permute-done.3.other_ref
  106.3 1.8 %combine.1 = bf16[96,8192]{1,0:T(8,128)(2,1)} custom-call(s32[1]{0:T(128)} %bitcast.me_ref, bf16[96,40]{1,0:T(8,128)(2,1)S(1)} %get-tuple-element.8.own_ref, bf16[96,40]{1,0:T(8,128)(2,1)S(1)} %collective-permute-done.3.other_ref, bf16[4,80,512]{2,1,0:T(8,128)(2,1)S(1)} %all-to-all-done.3.z_ref, bf16[4,80,512]{2,1,0:T(8,128)(2,1)S(1)} %collective-permute-done.7.y_ref, ...), custom_call_target="tpu_custom_call" | custom-call | flops 125829120 | bytes 3145728 | tf_op jit(solution)/shard_map/combine/pallas_call | solution.py:189
  (16 shorter events, 0.6 us)
Async XLA Ops:
  0.0 95.7 %collective-permute-start.1 = (bf16[96,28672]{1,0:T(8,128)(2,1)}, bf16[96,28672]{1,0:T(8,128)(2,1)}, u32[]{:S(2)}, u32[]{:S(2)}) collective-permute-start(bf16[96,28672]{1,0:T(8,128)(2,1)} %bitcast.14), channel_id=1, source_target_pairs={{0,1},{1,0},{2,3},{3,2},{4,5},{5,4},{6,7},{7,6},{8,9},{9,8},{10,11... | collective-permute-start | bytes 16515080 | tf_op jit(solution)/shard_map/ppermute | solution.py:37
  2.3 16.8 %all-to-all-start.2 = ((bf16[4,40,1024]{2,1,0:T(8,128)(2,1)}), bf16[4,40,1024]{2,1,0:T(8,128)(2,1)S(1)}, u32[]{:S(2)}, u32[]{:S(2)}) async-start(bf16[4,40,1024]{2,1,0:T(8,128)(2,1)} %broadcast_in_dim.14), calls=%async_computation.2 | async-start | bytes 655360 | tf_op jit(solution)/shard_map/all_to_all | solution.py:25
  37.7 18.5 %all-to-all-start = ((bf16[4,40,1792]{2,1,0:T(8,128)(2,1)}), bf16[4,40,1792]{2,1,0:T(8,128)(2,1)S(1)}, u32[]{:S(2)}, u32[]{:S(2)}) async-start(bf16[4,40,1792]{2,1,0:T(8,128)(2,1)} %broadcast_in_dim.12), calls=%async_computation | async-start | bytes 1146880 | tf_op jit(solution)/shard_map/all_to_all | solution.py:25
  41.2 8.2 %collective-permute-start.4 = (bf16[4,40,1024]{2,1,0:T(8,128)(2,1)S(1)}, bf16[4,40,1024]{2,1,0:T(8,128)(2,1)S(1)}, u32[]{:S(2)}, u32[]{:S(2)}) collective-permute-start(bf16[4,40,1024]{2,1,0:T(8,128)(2,1)S(1)} %all-to-all-done.2.z_ref), channel_id=1, source_target_pairs={{0,2},{1,3},{2,0},{3,1},{4,6},{5,7},{6,4},{7,5},{8,10},{9,11},{10,... | collective-permute-start | bytes 983048 | tf_op jit(solution)/shard_map/ppermute | solution.py:37
  42.8 6.6 %collective-permute-start.5 = (bf16[4,40,1024]{2,1,0:T(8,128)(2,1)S(1)}, bf16[4,40,1024]{2,1,0:T(8,128)(2,1)S(1)}, u32[]{:S(2)}, u32[]{:S(2)}) collective-permute-start(bf16[4,40,1024]{2,1,0:T(8,128)(2,1)S(1)} %all-to-all-done.2.z_ref), channel_id=1, source_target_pairs={{0,1},{1,0},{2,3},{3,2},{4,5},{5,4},{6,7},{7,6},{8,9},{9,8},{10,11... | collective-permute-start | bytes 983048 | tf_op jit(solution)/shard_map/ppermute | solution.py:37
  49.4 1.6 %collective-permute-start.6 = (bf16[4,40,1024]{2,1,0:T(8,128)(2,1)S(1)}, bf16[4,40,1024]{2,1,0:T(8,128)(2,1)S(1)}, u32[]{:S(2)}, u32[]{:S(2)}) collective-permute-start(bf16[4,40,1024]{2,1,0:T(8,128)(2,1)S(1)} %collective-permute-done.4.y_ref), channel_id=1, source_target_pairs={{0,1},{1,0},{2,3},{3,2},{4,5},{5,4},{6,7},{7,6},{8,9},{9,8},{10,11... | collective-permute-start | bytes 983048 | tf_op jit(solution)/shard_map/ppermute | solution.py:37
  57.0 15.3 %all-to-all-start.3 = ((bf16[4,80,512]{2,1,0:T(8,128)(2,1)}), bf16[4,80,512]{2,1,0:T(8,128)(2,1)S(1)}, u32[]{:S(2)}, u32[]{:S(2)}) async-start(bf16[4,80,512]{2,1,0:T(8,128)(2,1)} %broadcast_in_dim.15), calls=%async_computation.3 | async-start | bytes 655360 | tf_op jit(solution)/shard_map/all_to_all | solution.py:25
  61.7 34.1 %collective-permute-start.2 = (bf16[4,40,1792]{2,1,0:T(8,128)(2,1)S(1)}, bf16[4,40,1792]{2,1,0:T(8,128)(2,1)S(1)}, u32[]{:S(2)}, u32[]{:S(2)}) collective-permute-start(bf16[4,40,1792]{2,1,0:T(8,128)(2,1)S(1)} %all_to_all.20.z_ref.refs_0_), channel_id=1, source_target_pairs={{0,2},{1,3},{2,0},{3,1},{4,6},{5,7},{6,4},{7,5},{8,10},{9,11},{10,... | collective-permute-start | bytes 1720328 | tf_op jit(solution)/shard_map/ppermute | solution.py:37
  63.2 37.1 %collective-permute-start = (bf16[4,40,1792]{2,1,0:T(8,128)(2,1)S(1)}, bf16[4,40,1792]{2,1,0:T(8,128)(2,1)S(1)}, u32[]{:S(2)}, u32[]{:S(2)}) collective-permute-start(bf16[4,40,1792]{2,1,0:T(8,128)(2,1)S(1)} %all-to-all-done.z_ref), channel_id=1, source_target_pairs={{0,2},{1,3},{2,0},{3,1},{4,6},{5,7},{6,4},{7,5},{8,10},{9,11},{10,... | collective-permute-start | bytes 1720328 | tf_op jit(solution)/shard_map/ppermute | solution.py:37
  72.3 23.4 %collective-permute-start.7 = (bf16[4,80,512]{2,1,0:T(8,128)(2,1)S(1)}, bf16[4,80,512]{2,1,0:T(8,128)(2,1)S(1)}, u32[]{:S(2)}, u32[]{:S(2)}) collective-permute-start(bf16[4,80,512]{2,1,0:T(8,128)(2,1)S(1)} %all-to-all-done.3.z_ref), channel_id=1, source_target_pairs={{0,2},{1,3},{2,0},{3,1},{4,6},{5,7},{6,4},{7,5},{8,10},{9,11},{10,... | collective-permute-start | bytes 983048 | tf_op jit(solution)/shard_map/ppermute | solution.py:37
  73.8 31.6 %collective-permute-start.8 = (bf16[4,80,512]{2,1,0:T(8,128)(2,1)S(1)}, bf16[4,80,512]{2,1,0:T(8,128)(2,1)S(1)}, u32[]{:S(2)}, u32[]{:S(2)}) collective-permute-start(bf16[4,80,512]{2,1,0:T(8,128)(2,1)S(1)} %all-to-all-done.3.z_ref), channel_id=1, source_target_pairs={{0,1},{1,0},{2,3},{3,2},{4,5},{5,4},{6,7},{7,6},{8,9},{9,8},{10,11... | collective-permute-start | bytes 983048 | tf_op jit(solution)/shard_map/ppermute | solution.py:37
  95.7 9.7 %collective-permute-start.9 = (bf16[4,80,512]{2,1,0:T(8,128)(2,1)S(1)}, bf16[4,80,512]{2,1,0:T(8,128)(2,1)S(1)}, u32[]{:S(2)}, u32[]{:S(2)}) collective-permute-start(bf16[4,80,512]{2,1,0:T(8,128)(2,1)S(1)} %collective-permute-done.7.y_ref), channel_id=1, source_target_pairs={{0,1},{1,0},{2,3},{3,2},{4,5},{5,4},{6,7},{7,6},{8,9},{9,8},{10,11... | collective-permute-start | bytes 983048 | tf_op jit(solution)/shard_map/ppermute | solution.py:37
  104.9 1.4 %collective-permute-start.3 = (bf16[96,40]{1,0:T(8,128)(2,1)S(1)}, bf16[96,40]{1,0:T(8,128)(2,1)S(1)}, u32[]{:S(2)}, u32[]{:S(2)}) collective-permute-start(bf16[96,40]{1,0:T(8,128)(2,1)S(1)} %get-tuple-element.7), channel_id=1, source_target_pairs={{0,1},{1,0},{2,3},{3,2},{4,5},{5,4},{6,7},{7,6},{8,9},{9,8},{10,11... | collective-permute-start | bytes 23048 | tf_op jit(solution)/shard_map/ppermute | solution.py:37

commit v6 on v4

--- a/solution.py
+++ b/solution.py
@@ -237,16 +237,14 @@
     folded = acts.reshape(tokens, CHUNKS, SUBLANES, width).transpose(1, 0, 2, 3).reshape(CHUNKS, -1, width)
     folded_across = send(folded, across(devices))
     block = grads.reshape(tokens * SUBLANES, -1)
-    grads_z = others(pile([block] + along_all(block), [folded_across]))
-
-    acts_z = []
-    acts_y = []
-    for chunk in range(CHUNKS):
-        acts_z.append(pile(along_all(folded[chunk]), [] if chunk else [grads_z[1]]))
-        acts_y.append(send(acts_z[chunk], across(devices)))
-
+    grads_z = others(pile([block] + along_all(block), []))
+
+    acts_z = [pile(along_all(folded[0]), [])]
+    acts_y = [send(acts_z[0], across(devices))]
     sq_out = rotate_out(tokens, me, *grads_z, basis_out, [acts_z[0]])
     came = along_all(sq_out)
+    acts_z.append(pile(along_all(folded[1]), [sq_out]))
+    acts_y.append(send(acts_z[1], across(devices)))
 
     def part(chunk, before):
         return rotate_in(

time: 77.7 us -> 70.7 us (0.910)
  starting transfers between devices: 35.2 us -> 26.8 us
  waiting for transfers between devices: 23.7 us -> 25.2 us
    ppermute x23, starting transfers between devices: 35.2 us -> 26.8 us  [send(): return lax.ppermute(block, 'wide', pairs)]
    ppermute x23, waiting for transfers between devices: 23.7 us -> 25.2 us  [send(): return lax.ppermute(block, 'wide', pairs)]
  transfers between devices with their start and end apart: 23 -> 23, of which waited for: 10 -> 8; matrix products, arithmetic and copies ran while one was open for 3% -> 3% of each run, Pallas kernels for 19% -> 20%
where the time goes in v6:
time: 70.7 us; the launch traced here: 70.4 us
  starting transfers between devices  26.8 us (38%)
  waiting for transfers between devices  25.2 us (36%)
  Pallas kernels  16.2 us (23%)
  local copies, waits for them, and re-layouts  2.17 us (3%)
    ppermute x23, starting transfers between devices, send(): return lax.ppermute(block, 'wide', pairs)  26.8 us
    ppermute x23, waiting for transfers between devices, send(): return lax.ppermute(block, 'wide', pairs)  25.2 us
    pallas_call x2, Pallas kernels, rotate_in(): pl.pallas_call(functools.partial(rotate_in_kernel, tokens, len(before)),...  9.11 us
    pallas_call x1, Pallas kernels, rotate_out(): pl.pallas_call(functools.partial(rotate_out_kernel, tokens, len(waits)),...  5.18 us
    pallas_call x1, Pallas kernels, combine(): pl.pallas_call(combine_kernel, out_shape=jax.ShapeDtypeStruct((own.shape[...  1.76 us
  transfers between devices with their start and end apart: 23, of which 8 were waited for; matrix products, arithmetic and copies ran while one was open for 3% of the time, Pallas kernels for 20%

profile of v6, /device:TPU:0, one launch (start us, length us, event | category | flops | bytes accessed | tf_op | source)
XLA Modules:
  0.0 70.4 jit_solution(12763695732984262640)
XLA Ops:
  0.5 1.0 %reshape.19.refs_0_ = bf16[40,1024]{1,0:T(8,128)(2,1)S(1)} reshape(bf16[5,8192]{1,0:T(8,128)(2,1)} %param.5) | data formatting | bytes 163840 | tf_op jit(solution)/shard_map/reshape | solution.py:239
  1.5 2.6 %collective-permute-start.4 = (bf16[40,1024]{1,0:T(8,128)(2,1)S(1)}, bf16[40,1024]{1,0:T(8,128)(2,1)S(1)}, u32[]{:S(2)}, u32[]{:S(2)}) collective-permute-start(bf16[40,1024]{1,0:T(8,128)(2,1)S(1)} %reshape.19.refs_0_), channel_id=1, source_target_pairs={{0,4},{1,5},{2,6},{3,7},{4,8},{5,9},{6,10},{7,11},{8,12},{9,13},{1... | collective-permute-start | bytes 245768 | tf_op jit(solution)/shard_map/ppermute | solution.py:34
  4.1 2.6 %collective-permute-start.5 = (bf16[40,1024]{1,0:T(8,128)(2,1)S(1)}, bf16[40,1024]{1,0:T(8,128)(2,1)S(1)}, u32[]{:S(2)}, u32[]{:S(2)}) collective-permute-start(bf16[40,1024]{1,0:T(8,128)(2,1)S(1)} %reshape.19.refs_0_), channel_id=1, source_target_pairs={{0,8},{1,9},{2,10},{3,11},{4,12},{5,13},{6,14},{7,15},{8,0},{9,1},... | collective-permute-start | bytes 245768 | tf_op jit(solution)/shard_map/ppermute | solution.py:34
  6.7 1.3 %collective-permute-start.6 = (bf16[40,1024]{1,0:T(8,128)(2,1)S(1)}, bf16[40,1024]{1,0:T(8,128)(2,1)S(1)}, u32[]{:S(2)}, u32[]{:S(2)}) collective-permute-start(bf16[40,1024]{1,0:T(8,128)(2,1)S(1)} %reshape.19.refs_0_), channel_id=1, source_target_pairs={{0,12},{1,13},{2,14},{3,15},{4,0},{5,1},{6,2},{7,3},{8,4},{9,5},{1... | collective-permute-start | bytes 245768 | tf_op jit(solution)/shard_map/ppermute | solution.py:34
  8.1 1.1 %copy_bitcast_fusion.1 = (bf16[2,40,1792]{2,1,0:T(8,128)(2,1)S(1)}, bf16[2,5,8,1792]{3,2,1,0:T(8,128)(2,1)S(1)}) fusion(bf16[1,5,16,1792]{3,1,2,0:T(8,128)(2,1)} %bitcast.23), kind=kLoop, calls=%fused_computation.1 | loop fusion | bytes 860160 | tf_op jit(solution)/shard_map/reshape | solution.py:237
  9.5 3.3 %collective-permute-done.5.refs_2_ = bf16[40,1024]{1,0:T(8,128)(2,1)S(1)} collective-permute-done((bf16[40,1024]{1,0:T(8,128)(2,1)S(1)}, bf16[40,1024]{1,0:T(8,128)(2,1)S(1)}, u32[]{:S(2)}, u32[]{:S(2)}) %collective-permute-start.5) | collective-permute-done | bytes 81952 | tf_op jit(solution)/shard_map/ppermute | solution.py:34
  12.9 1.6 %collective-permute-start.7 = (bf16[4,40,1024]{2,1,0:T(8,128)(2,1)S(1)}, bf16[4,40,1024]{2,1,0:T(8,128)(2,1)S(1)}, u32[]{:S(2)}, u32[]{:S(2)}) collective-permute-start(bf16[4,40,1024]{2,1,0:T(8,128)(2,1)S(1)} %pile.4.z_ref), channel_id=1, source_target_pairs={{0,2},{1,3},{2,0},{3,1},{4,6},{5,7},{6,4},{7,5},{8,10},{9,11},{10,... | collective-permute-start | bytes 983048 | tf_op jit(solution)/shard_map/ppermute | solution.py:34
  14.5 2.3 %collective-permute-start.10 = (bf16[40,1792]{1,0:T(8,128)(2,1)S(1)}, bf16[40,1792]{1,0:T(8,128)(2,1)S(1)}, u32[]{:S(2)}, u32[]{:S(2)}) collective-permute-start(bf16[40,1792]{1,0:T(8,128)(2,1)S(1)} %get-tuple-element.7.own_ref), channel_id=1, source_target_pairs={{0,4},{1,5},{2,6},{3,7},{4,8},{5,9},{6,10},{7,11},{8,12},{9,13},{1... | collective-permute-start | bytes 430088 | tf_op jit(solution)/shard_map/ppermute | solution.py:34
  16.8 1.6 %collective-permute-start.11 = (bf16[40,1792]{1,0:T(8,128)(2,1)S(1)}, bf16[40,1792]{1,0:T(8,128)(2,1)S(1)}, u32[]{:S(2)}, u32[]{:S(2)}) collective-permute-start(bf16[40,1792]{1,0:T(8,128)(2,1)S(1)} %get-tuple-element.7.own_ref), channel_id=1, source_target_pairs={{0,8},{1,9},{2,10},{3,11},{4,12},{5,13},{6,14},{7,15},{8,0},{9,1},... | collective-permute-start | bytes 430088 | tf_op jit(solution)/shard_map/ppermute | solution.py:34
  19.3 3.9 %collective-permute-done.10.refs_0_ = bf16[40,1792]{1,0:T(8,128)(2,1)S(1)} collective-permute-done((bf16[40,1792]{1,0:T(8,128)(2,1)S(1)}, bf16[40,1792]{1,0:T(8,128)(2,1)S(1)}, u32[]{:S(2)}, u32[]{:S(2)}) %collective-permute-start.10) | collective-permute-done | bytes 143392 | tf_op jit(solution)/shard_map/ppermute | solution.py:34
  23.7 4.3 %collective-permute-done.11.refs_1_ = bf16[40,1792]{1,0:T(8,128)(2,1)S(1)} collective-permute-done((bf16[40,1792]{1,0:T(8,128)(2,1)S(1)}, bf16[40,1792]{1,0:T(8,128)(2,1)S(1)}, u32[]{:S(2)}, u32[]{:S(2)}) %collective-permute-start.11) | collective-permute-done | bytes 143392 | tf_op jit(solution)/shard_map/ppermute | solution.py:34
  28.0 1.6 %collective-permute-start.1 = (bf16[40,1792]{1,0:T(8,128)(2,1)S(1)}, bf16[40,1792]{1,0:T(8,128)(2,1)S(1)}, u32[]{:S(2)}, u32[]{:S(2)}) collective-permute-start(bf16[40,1792]{1,0:T(8,128)(2,1)S(1)} %get-tuple-element.8.own_ref), channel_id=1, source_target_pairs={{0,4},{1,5},{2,6},{3,7},{4,8},{5,9},{6,10},{7,11},{8,12},{9,13},{1... | collective-permute-start | bytes 430088 | tf_op jit(solution)/shard_map/ppermute | solution.py:34
  30.2 5.3 %collective-permute-done.1.refs_0_ = bf16[40,1792]{1,0:T(8,128)(2,1)S(1)} collective-permute-done((bf16[40,1792]{1,0:T(8,128)(2,1)S(1)}, bf16[40,1792]{1,0:T(8,128)(2,1)S(1)}, u32[]{:S(2)}, u32[]{:S(2)}) %collective-permute-start.1) | collective-permute-done | bytes 143392 | tf_op jit(solution)/shard_map/ppermute | solution.py:34
  36.1 2.0 %collective-permute-start.3 = (bf16[40,1792]{1,0:T(8,128)(2,1)S(1)}, bf16[40,1792]{1,0:T(8,128)(2,1)S(1)}, u32[]{:S(2)}, u32[]{:S(2)}) collective-permute-start(bf16[40,1792]{1,0:T(8,128)(2,1)S(1)} %get-tuple-element.8.own_ref), channel_id=1, source_target_pairs={{0,12},{1,13},{2,14},{3,15},{4,0},{5,1},{6,2},{7,3},{8,4},{9,5},{1... | collective-permute-start | bytes 430088 | tf_op jit(solution)/shard_map/ppermute | solution.py:34
  38.1 5.2 %rotate_out.1.refs_3_.refs_0_ = bf16[80,512]{1,0:T(8,128)(2,1)S(1)} custom-call(s32[1]{0:T(128)} %bitcast.me_ref, bf16[4,40,1024]{2,1,0:T(8,128)(2,1)S(1)} %pile.4.z_ref, bf16[4,40,1024]{2,1,0:T(8,128)(2,1)S(1)} %collective-permute-done.7.y_ref, bf16[4,40,1024]{2,1,0:T(8,128)(2,1)S(1)} %collective-permute-done.8.cz_ref, ...), custom_call_target="tpu_custom_call" | custom-call | flops 671088640 | bytes 8388608 | tf_op jit(solution)/shard_map/rotate_out/pallas_call | solution.py:102
  44.0 0.9 %collective-permute-start.17 = (bf16[80,512]{1,0:T(8,128)(2,1)S(1)}, bf16[80,512]{1,0:T(8,128)(2,1)S(1)}, u32[]{:S(2)}, u32[]{:S(2)}) collective-permute-start(bf16[80,512]{1,0:T(8,128)(2,1)S(1)} %rotate_out.1.refs_3_.refs_0_), channel_id=1, source_target_pairs={{0,4},{1,5},{2,6},{3,7},{4,8},{5,9},{6,10},{7,11},{8,12},{9,13},{1... | collective-permute-start | bytes 245768 | tf_op jit(solution)/shard_map/ppermute | solution.py:34
  44.9 3.4 %collective-permute-start.18 = (bf16[80,512]{1,0:T(8,128)(2,1)S(1)}, bf16[80,512]{1,0:T(8,128)(2,1)S(1)}, u32[]{:S(2)}, u32[]{:S(2)}) collective-permute-start(bf16[80,512]{1,0:T(8,128)(2,1)S(1)} %rotate_out.1.refs_3_.refs_0_), channel_id=1, source_target_pairs={{0,8},{1,9},{2,10},{3,11},{4,12},{5,13},{6,14},{7,15},{8,0},{9,1},... | collective-permute-start | bytes 245768 | tf_op jit(solution)/shard_map/ppermute | solution.py:34
  48.3 1.2 %collective-permute-start.19 = (bf16[80,512]{1,0:T(8,128)(2,1)S(1)}, bf16[80,512]{1,0:T(8,128)(2,1)S(1)}, u32[]{:S(2)}, u32[]{:S(2)}) collective-permute-start(bf16[80,512]{1,0:T(8,128)(2,1)S(1)} %rotate_out.1.refs_3_.refs_0_), channel_id=1, source_target_pairs={{0,12},{1,13},{2,14},{3,15},{4,0},{5,1},{6,2},{7,3},{8,4},{9,5},{1... | collective-permute-start | bytes 245768 | tf_op jit(solution)/shard_map/ppermute | solution.py:34
  50.2 4.6 %rotate_in.2.refs_0_.refs_4_ = f32[192,40]{1,0:T(8,128)S(1)} custom-call(s32[1]{0:T(128)} %bitcast.me_ref, bf16[40,1792]{1,0:T(8,128)(2,1)S(1)} %get-tuple-element.7.own_ref, bf16[40,1792]{1,0:T(8,128)(2,1)S(1)} %get-tuple-element.5.across_ref, bf16[3,40,1792]{2,1,0:T(8,128)(2,1)S(1)} %pile.5.refs_0_.z_ref, ...), custom_call_target="tpu_custom_call" | custom-call | flops 220200960 | bytes 5505024 | tf_op jit(solution)/shard_map/rotate_in/pallas_call | solution.py:153
  54.8 1.5 %collective-permute-start.20 = (bf16[4,80,512]{2,1,0:T(8,128)(2,1)S(1)}, bf16[4,80,512]{2,1,0:T(8,128)(2,1)S(1)}, u32[]{:S(2)}, u32[]{:S(2)}) collective-permute-start(bf16[4,80,512]{2,1,0:T(8,128)(2,1)S(1)} %pile.7.z_ref), channel_id=1, source_target_pairs={{0,2},{1,3},{2,0},{3,1},{4,6},{5,7},{6,4},{7,5},{8,10},{9,11},{10,... | collective-permute-start | bytes 983048 | tf_op jit(solution)/shard_map/ppermute | solution.py:34
  56.3 6.1 %collective-permute-done.13.y_ref = bf16[3,40,1792]{2,1,0:T(8,128)(2,1)S(1)} collective-permute-done((bf16[3,40,1792]{2,1,0:T(8,128)(2,1)S(1)}, bf16[3,40,1792]{2,1,0:T(8,128)(2,1)S(1)}, u32[]{:S(2)}, u32[]{:S(2)}) %collective-permute-start.13) | collective-permute-done | bytes 430112 | tf_op jit(solution)/shard_map/ppermute | solution.py:34
  62.3 4.6 %rotate_in.3 = f32[192,40]{1,0:T(8,128)S(1)} custom-call(s32[1]{0:T(128)} %bitcast.me_ref, bf16[40,1792]{1,0:T(8,128)(2,1)S(1)} %get-tuple-element.8.own_ref, bf16[40,1792]{1,0:T(8,128)(2,1)S(1)} %get-tuple-element.6.across_ref, bf16[3,40,1792]{2,1,0:T(8,128)(2,1)S(1)} %pile.6.z_ref.refs_5_, bf16[3,40,1792]{2,1,0:T(8,128)(2,1)S(1)} %collective-permute-done.13.y_ref, ...), custom_call_target="tpu_custom_call" | custom-call | flops 220200960 | bytes 5505024 | tf_op jit(solution)/shard_map/rotate_in/pallas_call | solution.py:153
  67.6 1.1 %collective-permute-done.16.other_ref = bf16[96,40]{1,0:T(8,128)(2,1)S(1)} collective-permute-done((bf16[96,40]{1,0:T(8,128)(2,1)S(1)}, bf16[96,40]{1,0:T(8,128)(2,1)S(1)}, u32[]{:S(2)}, u32[]{:S(2)}) %collective-permute-start.16) | collective-permute-done | bytes 7712 | tf_op jit(solution)/shard_map/ppermute | solution.py:34
  68.7 1.8 %combine.1 = bf16[96,8192]{1,0:T(8,128)(2,1)} custom-call(s32[1]{0:T(128)} %bitcast.me_ref, bf16[96,40]{1,0:T(8,128)(2,1)S(1)} %get-tuple-element.12.own_ref, bf16[96,40]{1,0:T(8,128)(2,1)S(1)} %collective-permute-done.16.other_ref, bf16[4,80,512]{2,1,0:T(8,128)(2,1)S(1)} %pile.7.z_ref, bf16[4,80,512]{2,1,0:T(8,128)(2,1)S(1)} %collective-permute-done.20.y_ref, ...), custom_call_target="tpu_custom_call" | custom-call | flops 125829120 | bytes 3145728 | tf_op jit(solution)/shard_map/combine/pallas_call | solution.py:208
  (36 shorter events, 5.5 us)
Async XLA Ops:
  0.0 50.2 %collective-permute-start.14 = (bf16[96,28672]{1,0:T(8,128)(2,1)}, bf16[96,28672]{1,0:T(8,128)(2,1)}, u32[]{:S(2)}, u32[]{:S(2)}) collective-permute-start(bf16[96,28672]{1,0:T(8,128)(2,1)} %bitcast.20), channel_id=1, source_target_pairs={{0,1},{1,0},{2,3},{3,2},{4,5},{5,4},{6,7},{7,6},{8,9},{9,8},{10,11... | collective-permute-start | bytes 16515080 | tf_op jit(solution)/shard_map/ppermute | solution.py:34
  1.5 8.0 %collective-permute-start.4 = (bf16[40,1024]{1,0:T(8,128)(2,1)S(1)}, bf16[40,1024]{1,0:T(8,128)(2,1)S(1)}, u32[]{:S(2)}, u32[]{:S(2)}) collective-permute-start(bf16[40,1024]{1,0:T(8,128)(2,1)S(1)} %reshape.19.refs_0_), channel_id=1, source_target_pairs={{0,4},{1,5},{2,6},{3,7},{4,8},{5,9},{6,10},{7,11},{8,12},{9,13},{1... | collective-permute-start | bytes 245768 | tf_op jit(solution)/shard_map/ppermute | solution.py:34
  4.1 8.7 %collective-permute-start.5 = (bf16[40,1024]{1,0:T(8,128)(2,1)S(1)}, bf16[40,1024]{1,0:T(8,128)(2,1)S(1)}, u32[]{:S(2)}, u32[]{:S(2)}) collective-permute-start(bf16[40,1024]{1,0:T(8,128)(2,1)S(1)} %reshape.19.refs_0_), channel_id=1, source_target_pairs={{0,8},{1,9},{2,10},{3,11},{4,12},{5,13},{6,14},{7,15},{8,0},{9,1},... | collective-permute-start | bytes 245768 | tf_op jit(solution)/shard_map/ppermute | solution.py:34
  6.7 6.1 %collective-permute-start.6 = (bf16[40,1024]{1,0:T(8,128)(2,1)S(1)}, bf16[40,1024]{1,0:T(8,128)(2,1)S(1)}, u32[]{:S(2)}, u32[]{:S(2)}) collective-permute-start(bf16[40,1024]{1,0:T(8,128)(2,1)S(1)} %reshape.19.refs_0_), channel_id=1, source_target_pairs={{0,12},{1,13},{2,14},{3,15},{4,0},{5,1},{6,2},{7,3},{8,4},{9,5},{1... | collective-permute-start | bytes 245768 | tf_op jit(solution)/shard_map/ppermute | solution.py:34
  12.9 10.3 %collective-permute-start.7 = (bf16[4,40,1024]{2,1,0:T(8,128)(2,1)S(1)}, bf16[4,40,1024]{2,1,0:T(8,128)(2,1)S(1)}, u32[]{:S(2)}, u32[]{:S(2)}) collective-permute-start(bf16[4,40,1024]{2,1,0:T(8,128)(2,1)S(1)} %pile.4.z_ref), channel_id=1, source_target_pairs={{0,2},{1,3},{2,0},{3,1},{4,6},{5,7},{6,4},{7,5},{8,10},{9,11},{10,... | collective-permute-start | bytes 983048 | tf_op jit(solution)/shard_map/ppermute | solution.py:34
  14.5 8.6 %collective-permute-start.10 = (bf16[40,1792]{1,0:T(8,128)(2,1)S(1)}, bf16[40,1792]{1,0:T(8,128)(2,1)S(1)}, u32[]{:S(2)}, u32[]{:S(2)}) collective-permute-start(bf16[40,1792]{1,0:T(8,128)(2,1)S(1)} %get-tuple-element.7.own_ref), channel_id=1, source_target_pairs={{0,4},{1,5},{2,6},{3,7},{4,8},{5,9},{6,10},{7,11},{8,12},{9,13},{1... | collective-permute-start | bytes 430088 | tf_op jit(solution)/shard_map/ppermute | solution.py:34
  16.8 11.1 %collective-permute-start.11 = (bf16[40,1792]{1,0:T(8,128)(2,1)S(1)}, bf16[40,1792]{1,0:T(8,128)(2,1)S(1)}, u32[]{:S(2)}, u32[]{:S(2)}) collective-permute-start(bf16[40,1792]{1,0:T(8,128)(2,1)S(1)} %get-tuple-element.7.own_ref), channel_id=1, source_target_pairs={{0,8},{1,9},{2,10},{3,11},{4,12},{5,13},{6,14},{7,15},{8,0},{9,1},... | collective-permute-start | bytes 430088 | tf_op jit(solution)/shard_map/ppermute | solution.py:34
  18.4 11.2 %collective-permute-start.12 = (bf16[40,1792]{1,0:T(8,128)(2,1)S(1)}, bf16[40,1792]{1,0:T(8,128)(2,1)S(1)}, u32[]{:S(2)}, u32[]{:S(2)}) collective-permute-start(bf16[40,1792]{1,0:T(8,128)(2,1)S(1)} %get-tuple-element.7.own_ref), channel_id=1, source_target_pairs={{0,12},{1,13},{2,14},{3,15},{4,0},{5,1},{6,2},{7,3},{8,4},{9,5},{1... | collective-permute-start | bytes 430088 | tf_op jit(solution)/shard_map/ppermute | solution.py:34
  23.1 12.8 %collective-permute-start.8 = (bf16[4,40,1024]{2,1,0:T(8,128)(2,1)S(1)}, bf16[4,40,1024]{2,1,0:T(8,128)(2,1)S(1)}, u32[]{:S(2)}, u32[]{:S(2)}) collective-permute-start(bf16[4,40,1024]{2,1,0:T(8,128)(2,1)S(1)} %pile.4.z_ref), channel_id=1, source_target_pairs={{0,1},{1,0},{2,3},{3,2},{4,5},{5,4},{6,7},{7,6},{8,9},{9,8},{10,11... | collective-permute-start | bytes 983048 | tf_op jit(solution)/shard_map/ppermute | solution.py:34
  23.1 13.0 %collective-permute-start.9 = (bf16[4,40,1024]{2,1,0:T(8,128)(2,1)S(1)}, bf16[4,40,1024]{2,1,0:T(8,128)(2,1)S(1)}, u32[]{:S(2)}, u32[]{:S(2)}) collective-permute-start(bf16[4,40,1024]{2,1,0:T(8,128)(2,1)S(1)} %collective-permute-done.7.y_ref), channel_id=1, source_target_pairs={{0,1},{1,0},{2,3},{3,2},{4,5},{5,4},{6,7},{7,6},{8,9},{9,8},{10,11... | collective-permute-start | bytes 983048 | tf_op jit(solution)/shard_map/ppermute | solution.py:34
  28.0 7.5 %collective-permute-start.1 = (bf16[40,1792]{1,0:T(8,128)(2,1)S(1)}, bf16[40,1792]{1,0:T(8,128)(2,1)S(1)}, u32[]{:S(2)}, u32[]{:S(2)}) collective-permute-start(bf16[40,1792]{1,0:T(8,128)(2,1)S(1)} %get-tuple-element.8.own_ref), channel_id=1, source_target_pairs={{0,4},{1,5},{2,6},{3,7},{4,8},{5,9},{6,10},{7,11},{8,12},{9,13},{1... | collective-permute-start | bytes 430088 | tf_op jit(solution)/shard_map/ppermute | solution.py:34
  29.6 19.9 %collective-permute-start.15 = (bf16[3,40,1792]{2,1,0:T(8,128)(2,1)S(1)}, bf16[3,40,1792]{2,1,0:T(8,128)(2,1)S(1)}, u32[]{:S(2)}, u32[]{:S(2)}) collective-permute-start(bf16[3,40,1792]{2,1,0:T(8,128)(2,1)S(1)} %pile.5.refs_0_.z_ref), channel_id=1, source_target_pairs={{0,2},{1,3},{2,0},{3,1},{4,6},{5,7},{6,4},{7,5},{8,10},{9,11},{10,... | collective-permute-start | bytes 1290248 | tf_op jit(solution)/shard_map/ppermute | solution.py:34
  35.5 12.8 %collective-permute-start = (bf16[2,40,1792]{2,1,0:T(8,128)(2,1)S(1)}, bf16[2,40,1792]{2,1,0:T(8,128)(2,1)S(1)}, u32[]{:S(2)}, u32[]{:S(2)}) collective-permute-start(bf16[2,40,1792]{2,1,0:T(8,128)(2,1)S(1)} %get-tuple-element.9), channel_id=1, source_target_pairs={{0,2},{1,3},{2,0},{3,1},{4,6},{5,7},{6,4},{7,5},{8,10},{9,11},{10,... | collective-permute-start | bytes 860168 | tf_op jit(solution)/shard_map/ppermute | solution.py:34
  36.0 8.0 %collective-permute-start.2 = (bf16[40,1792]{1,0:T(8,128)(2,1)S(1)}, bf16[40,1792]{1,0:T(8,128)(2,1)S(1)}, u32[]{:S(2)}, u32[]{:S(2)}) collective-permute-start(bf16[40,1792]{1,0:T(8,128)(2,1)S(1)} %get-tuple-element.8.own_ref), channel_id=1, source_target_pairs={{0,8},{1,9},{2,10},{3,11},{4,12},{5,13},{6,14},{7,15},{8,0},{9,1},... | collective-permute-start | bytes 430088 | tf_op jit(solution)/shard_map/ppermute | solution.py:34
  36.1 8.8 %collective-permute-start.3 = (bf16[40,1792]{1,0:T(8,128)(2,1)S(1)}, bf16[40,1792]{1,0:T(8,128)(2,1)S(1)}, u32[]{:S(2)}, u32[]{:S(2)}) collective-permute-start(bf16[40,1792]{1,0:T(8,128)(2,1)S(1)} %get-tuple-element.8.own_ref), channel_id=1, source_target_pairs={{0,12},{1,13},{2,14},{3,15},{4,0},{5,1},{6,2},{7,3},{8,4},{9,5},{1... | collective-permute-start | bytes 430088 | tf_op jit(solution)/shard_map/ppermute | solution.py:34
  44.0 10.7 %collective-permute-start.17 = (bf16[80,512]{1,0:T(8,128)(2,1)S(1)}, bf16[80,512]{1,0:T(8,128)(2,1)S(1)}, u32[]{:S(2)}, u32[]{:S(2)}) collective-permute-start(bf16[80,512]{1,0:T(8,128)(2,1)S(1)} %rotate_out.1.refs_3_.refs_0_), channel_id=1, source_target_pairs={{0,4},{1,5},{2,6},{3,7},{4,8},{5,9},{6,10},{7,11},{8,12},{9,13},{1... | collective-permute-start | bytes 245768 | tf_op jit(solution)/shard_map/ppermute | solution.py:34
  44.9 9.8 %collective-permute-start.18 = (bf16[80,512]{1,0:T(8,128)(2,1)S(1)}, bf16[80,512]{1,0:T(8,128)(2,1)S(1)}, u32[]{:S(2)}, u32[]{:S(2)}) collective-permute-start(bf16[80,512]{1,0:T(8,128)(2,1)S(1)} %rotate_out.1.refs_3_.refs_0_), channel_id=1, source_target_pairs={{0,8},{1,9},{2,10},{3,11},{4,12},{5,13},{6,14},{7,15},{8,0},{9,1},... | collective-permute-start | bytes 245768 | tf_op jit(solution)/shard_map/ppermute | solution.py:34
  48.3 6.4 %collective-permute-start.19 = (bf16[80,512]{1,0:T(8,128)(2,1)S(1)}, bf16[80,512]{1,0:T(8,128)(2,1)S(1)}, u32[]{:S(2)}, u32[]{:S(2)}) collective-permute-start(bf16[80,512]{1,0:T(8,128)(2,1)S(1)} %rotate_out.1.refs_3_.refs_0_), channel_id=1, source_target_pairs={{0,12},{1,13},{2,14},{3,15},{4,0},{5,1},{6,2},{7,3},{8,4},{9,5},{1... | collective-permute-start | bytes 245768 | tf_op jit(solution)/shard_map/ppermute | solution.py:34
  49.5 12.8 %collective-permute-start.13 = (bf16[3,40,1792]{2,1,0:T(8,128)(2,1)S(1)}, bf16[3,40,1792]{2,1,0:T(8,128)(2,1)S(1)}, u32[]{:S(2)}, u32[]{:S(2)}) collective-permute-start(bf16[3,40,1792]{2,1,0:T(8,128)(2,1)S(1)} %pile.6.z_ref.refs_5_), channel_id=1, source_target_pairs={{0,2},{1,3},{2,0},{3,1},{4,6},{5,7},{6,4},{7,5},{8,10},{9,11},{10,... | collective-permute-start | bytes 1290248 | tf_op jit(solution)/shard_map/ppermute | solution.py:34
  54.8 12.1 %collective-permute-start.20 = (bf16[4,80,512]{2,1,0:T(8,128)(2,1)S(1)}, bf16[4,80,512]{2,1,0:T(8,128)(2,1)S(1)}, u32[]{:S(2)}, u32[]{:S(2)}) collective-permute-start(bf16[4,80,512]{2,1,0:T(8,128)(2,1)S(1)} %pile.7.z_ref), channel_id=1, source_target_pairs={{0,2},{1,3},{2,0},{3,1},{4,6},{5,7},{6,4},{7,5},{8,10},{9,11},{10,... | collective-permute-start | bytes 983048 | tf_op jit(solution)/shard_map/ppermute | solution.py:34
  56.3 12.4 %collective-permute-start.21 = (bf16[4,80,512]{2,1,0:T(8,128)(2,1)S(1)}, bf16[4,80,512]{2,1,0:T(8,128)(2,1)S(1)}, u32[]{:S(2)}, u32[]{:S(2)}) collective-permute-start(bf16[4,80,512]{2,1,0:T(8,128)(2,1)S(1)} %pile.7.z_ref), channel_id=1, source_target_pairs={{0,1},{1,0},{2,3},{3,2},{4,5},{5,4},{6,7},{7,6},{8,9},{9,8},{10,11... | collective-permute-start | bytes 983048 | tf_op jit(solution)/shard_map/ppermute | solution.py:34
  66.9 1.7 %collective-permute-start.22 = (bf16[4,80,512]{2,1,0:T(8,128)(2,1)S(1)}, bf16[4,80,512]{2,1,0:T(8,128)(2,1)S(1)}, u32[]{:S(2)}, u32[]{:S(2)}) collective-permute-start(bf16[4,80,512]{2,1,0:T(8,128)(2,1)S(1)} %collective-permute-done.20.y_ref), channel_id=1, source_target_pairs={{0,1},{1,0},{2,3},{3,2},{4,5},{5,4},{6,7},{7,6},{8,9},{9,8},{10,11... | collective-permute-start | bytes 983048 | tf_op jit(solution)/shard_map/ppermute | solution.py:34
  67.0 1.6 %collective-permute-start.16 = (bf16[96,40]{1,0:T(8,128)(2,1)S(1)}, bf16[96,40]{1,0:T(8,128)(2,1)S(1)}, u32[]{:S(2)}, u32[]{:S(2)}) collective-permute-start(bf16[96,40]{1,0:T(8,128)(2,1)S(1)} %get-tuple-element.11), channel_id=1, source_target_pairs={{0,1},{1,0},{2,3},{3,2},{4,5},{5,4},{6,7},{7,6},{8,9},{9,8},{10,11... | collective-permute-start | bytes 23048 | tf_op jit(solution)/shard_map/ppermute | solution.py:34

commit v7 on v6

v7 whole, which is shorter than its diff:
```python
import functools

import jax
import jax.numpy as jnp
from jax import lax
from jax.experimental import pallas as pl
from jax.experimental.pallas import tpu as pltpu
from jax.sharding import PartitionSpec as P

CORES = 2
PAIR = 2
SUBLANES = 8
FOLDS = 2
SHARES = (14, 14)
VMEM = pl.BlockSpec(memory_space=pltpu.VMEM)
ANY = pl.BlockSpec(memory_space=pl.ANY)
SMEM = pl.BlockSpec(memory_space=pltpu.SMEM)


def along(devices, by):
    each = CORES * PAIR
    return [(d, (d + by * each) % devices) for d in range(devices)]


def across(devices):
    return [(d, d ^ CORES) for d in range(devices)]


def swap(devices):
    return [(d, d ^ 1) for d in range(devices)]


def send(block, pairs):
    return lax.ppermute(block, "wide", pairs)


def origin(me, devices, step, other_chip, other_core):
    each = CORES * PAIR
    pair = lax.rem(me // each + devices // each - step, devices // each)
    chip = lax.rem(me // CORES, PAIR)
    core = lax.rem(me, CORES)
    if other_chip:
        chip = 1 - chip
    if other_core:
        core = 1 - core
    return pair * PAIR + chip, core


def repeat(times, body, carry=None, loop=False):
    if loop or times > SUBLANES:
        return lax.fori_loop(0, times, body, carry)
    for step in range(times):
        carry = body(step, carry)
    return carry


def unfold_store(rows, first, block):
    at = pl.ds(pl.multiple_of(first, SUBLANES), block.shape[0])
    for tile in range(rows.shape[0]):
        rows[tile, at, :] = block[:, tile * 128 : (tile + 1) * 128].astype(jnp.float32)


def unfold_load(rows, fold, tokens):
    tiles = [rows[tile, pl.ds(fold, tokens, stride=SUBLANES), :] for tile in range(rows.shape[0])]
    return jnp.concatenate([tile.astype(jnp.bfloat16) for tile in tiles], 1)


def rotate_out_kernel(tokens, waits, me_ref, z_ref, y_ref, cz_ref, cy_ref, basis_ref, *refs):
    sq_ref, rows, total = refs[waits:]
    steps, height, width = z_ref.shape
    devices = steps * CORES * PAIR
    me = me_ref[0]

    @pl.when(pl.program_id(0) == 0)
    def _():
        for ref, chip_bit, core_bit in ((z_ref, 0, 0), (y_ref, 1, 0), (cz_ref, 0, 1), (cy_ref, 1, 1)):

            def put(step, _, ref=ref, chip_bit=chip_bit, core_bit=core_bit):
                chip, core = origin(me, devices, step, chip_bit, core_bit)
                unfold_store(rows, (core * (devices // CORES) + chip) * height, ref[step])

            repeat(steps, put)
        total[...] = jnp.zeros_like(total)

    def add(fold, _):
        left = unfold_load(rows, pl.program_id(0) * FOLDS + fold, devices * tokens)
        right = basis_ref[pl.ds(pl.multiple_of(fold * width, 128), width), :]
        total[...] += jnp.dot(left, right, preferred_element_type=jnp.float32)

    repeat(FOLDS, add, None, steps > SUBLANES)

    @pl.when(pl.program_id(0) == pl.num_programs(0) - 1)
    def _():
        sq_ref[...] = (total[...] * total[...]).astype(sq_ref.dtype)


def rotate_out(tokens, me, z, y, cz, cy, basis, waits):
    steps, height, width = z.shape
    total = steps * CORES * PAIR * tokens
    columns = basis.shape[1]
    return pl.pallas_call(
        functools.partial(rotate_out_kernel, tokens, len(waits)),
        grid=(SUBLANES // FOLDS,),
        out_shape=jax.ShapeDtypeStruct((total, columns), jnp.bfloat16),
        in_specs=[SMEM] + [VMEM] * 4 + [pl.BlockSpec((FOLDS * width, columns), lambda i: (i, 0))] + [ANY] * len(waits),
        out_specs=VMEM,
        scratch_shapes=[
            pltpu.VMEM((width // 128, total * SUBLANES, 128), jnp.float32),
            pltpu.VMEM((total, columns), jnp.float32),
        ],
        compiler_params=pltpu.CompilerParams(vmem_limit_bytes=24 * 2**20),
        cost_estimate=pl.CostEstimate(
            flops=2 * total * basis.shape[0] * columns, bytes_accessed=2 * basis.size, transcendentals=0
        ),
        name="rotate_out",
    )(me, z, y, cz, cy, basis, *waits)


def rotate_in_kernel(tokens, start, before, me_ref, own_ref, across_ref, z_ref, y_ref, mine_ref, theirs_ref, *refs):
    total_ref, rows = refs[before:]
    height, whole = own_ref.shape
    width = z_ref.shape[2]
    steps = z_ref.shape[0] + 1
    devices = steps * CORES * PAIR
    chips = devices // CORES
    me = me_ref[0]
    unfold_store(rows, origin(me, devices, 0, 0, 0)[0] * height, own_ref[:, start : start + width])
    unfold_store(rows, origin(me, devices, 0, 1, 0)[0] * height, across_ref[:, start : start + width])
    for ref, chip_bit in ((z_ref, 0), (y_ref, 1)):

        def put(step, _, ref=ref, chip_bit=chip_bit):
            unfold_store(rows, origin(me, devices, step + 1, chip_bit, 0)[0] * height, ref[step])

        repeat(steps - 1, put)

    def add(fold, total):
        at = pl.ds(pl.multiple_of(fold * whole + start, 128), width)
        right = unfold_load(rows, fold, chips * tokens)
        left = jnp.concatenate([mine_ref[:, at], theirs_ref[:, at]])
        return total + lax.dot_general(left, right, (((1,), (1,)), ((), ())), preferred_element_type=jnp.float32)

    total = refs[0][...] if before else jnp.zeros(total_ref.shape, jnp.float32)
    total_ref[...] = repeat(SUBLANES, add, total, steps > SUBLANES)


def rotate_in(tokens, start, me, own, across, z, y, mine, theirs, before):
    height, width = z.shape[1:]
    chips = (z.shape[0] + 1) * PAIR
    return pl.pallas_call(
        functools.partial(rotate_in_kernel, tokens, start, len(before)),
        out_shape=jax.ShapeDtypeStruct((2 * mine.shape[0], chips * tokens), jnp.float32),
        in_specs=[SMEM] + [VMEM] * (6 + len(before)),
        out_specs=VMEM,
        scratch_shapes=[pltpu.VMEM((width // 128, chips * height, 128), jnp.float32)],
        compiler_params=pltpu.CompilerParams(vmem_limit_bytes=(28 if chips <= SUBLANES else 48) * 2**20),
        cost_estimate=pl.CostEstimate(
            flops=4 * chips * tokens * mine.shape[0] * SUBLANES * width,
            bytes_accessed=4 * mine.shape[0] * SUBLANES * width,
            transcendentals=0,
        ),
        name="rotate_in",
    )(me, own, across, z, y, mine, theirs, *before)


def pile_kernel(blocks, *refs):
    for step in range(blocks):
        refs[-1][step] = refs[step][...]


def pile(blocks, waits):
    return pl.pallas_call(
        functools.partial(pile_kernel, len(blocks)),
        out_shape=jax.ShapeDtypeStruct((len(blocks), *blocks[0].shape), blocks[0].dtype),
        in_specs=[VMEM] * len(blocks) + [ANY] * len(waits),
        out_specs=VMEM,
        compiler_params=pltpu.CompilerParams(vmem_limit_bytes=24 * 2**20),
        cost_estimate=pl.CostEstimate(flops=0, bytes_accessed=2 * len(blocks) * blocks[0].size, transcendentals=0),
        name="pile",
    )(*blocks, *waits)


def fetch_kernel(from_ref, *refs):
    to_ref, done = refs[-2:]
    copy = pltpu.make_async_copy(from_ref, to_ref, done)
    copy.start()
    copy.wait()


def fetch(array, waits):
    return pl.pallas_call(
        fetch_kernel,
        out_shape=jax.ShapeDtypeStruct(array.shape, array.dtype),
        in_specs=[ANY] * (1 + len(waits)),
        out_specs=VMEM,
        scratch_shapes=[pltpu.SemaphoreType.DMA],
        compiler_params=pltpu.CompilerParams(vmem_limit_bytes=16 * 2**20),
        cost_estimate=pl.CostEstimate(flops=0, bytes_accessed=2 * array.size, transcendentals=0),
        name="fetch",
    )(array, *waits)


def after(arrays, waits):
    return pl.pallas_call(
        lambda *refs: None,
        out_shape=[jax.ShapeDtypeStruct(array.shape, array.dtype) for array in arrays],
        in_specs=[ANY] * (len(arrays) + len(waits)),
        out_specs=[ANY] * len(arrays),
        input_output_aliases={i: i for i in range(len(arrays))},
        compiler_params=pltpu.CompilerParams(vmem_limit_bytes=2**20),
        cost_estimate=pl.CostEstimate(flops=0, bytes_accessed=0, transcendentals=0),
        name="after",
    )(*arrays, *waits)


def pile_kernel(blocks, *refs):
    for step in range(blocks):
        refs[-1][step] = refs[step][...]


def pile(blocks, waits):
    return pl.pallas_call(
        functools.partial(pile_kernel, len(blocks)),
        out_shape=jax.ShapeDtypeStruct((len(blocks), *blocks[0].shape), blocks[0].dtype),
        in_specs=[VMEM] * len(blocks) + [ANY] * len(waits),
        out_specs=VMEM,
        compiler_params=pltpu.CompilerParams(vmem_limit_bytes=24 * 2**20),
        cost_estimate=pl.CostEstimate(flops=0, bytes_accessed=2 * len(blocks) * blocks[0].size, transcendentals=0),
        name="pile",
    )(*blocks, *waits)


def combine_kernel(steps, me_ref, own_ref, other_ref, *refs):
    blocks, out_ref = refs[:-1], refs[-1]
    _, total_tokens, width = blocks[0].shape
    devices = steps * CORES * PAIR
    me = me_ref[0]
    own, other = own_ref[...].astype(jnp.float32), other_ref[...].astype(jnp.float32)
    first = lax.rem(me, CORES) == 0
    left = jnp.concatenate([jnp.where(first, own, other), jnp.where(first, other, own)], 1).astype(jnp.bfloat16)
    for i, block in enumerate(blocks):
        for bit in range(PAIR):
            chip, core = origin(me, devices, i % steps, bit, i // steps)
            at = pl.multiple_of((chip * CORES + core) * width, 128)
            total = jnp.dot(left, block[bit], preferred_element_type=jnp.float32)
            out_ref[:, pl.ds(at, width)] = (total / total_tokens).astype(out_ref.dtype)


def combine(me, own, other, blocks):
    steps = len(blocks) // CORES
    _, total_tokens, width = blocks[0].shape
    features = steps * PAIR * CORES * width
    return pl.pallas_call(
        functools.partial(combine_kernel, steps),
        out_shape=jax.ShapeDtypeStruct((own.shape[0], features), jnp.bfloat16),
        in_specs=[SMEM] + [VMEM] * (2 + len(blocks)),
        out_specs=VMEM,
        compiler_params=pltpu.CompilerParams(vmem_limit_bytes=24 * 2**20),
        cost_estimate=pl.CostEstimate(
            flops=2 * own.shape[0] * total_tokens * features, bytes_accessed=4 * own.shape[0] * features, transcendentals=0
        ),
        name="combine",
    )(me, own, other, *blocks)


def local(acts, grads, basis_in, basis_out):
    devices = lax.axis_size("wide")
    steps = devices // (CORES * PAIR)
    tokens = acts.shape[0]
    me = lax.axis_index("wide").astype(jnp.int32).reshape(1)

    def along_all(block):
        return [send(block, along(devices, step)) for step in range(1, steps)]

    folded = acts.reshape(tokens * SUBLANES, -1)
    folded_across = send(folded, across(devices))
    unit = folded.shape[1] // sum(SHARES)
    starts = [sum(SHARES[:chunk]) * unit for chunk in range(len(SHARES))]

    def chunk_along(chunk, waits):
        acts_s.append(along_all(folded[:, starts[chunk] : starts[chunk] + SHARES[chunk] * unit]))
        z = pile(acts_s[-1], waits)
        acts_z.append(z)
        acts_y.append(send(z, across(devices)))

    def part(chunk, before):
        return rotate_in(
            tokens, starts[chunk], me, folded, folded_across, acts_z[chunk], acts_y[chunk], mine, theirs, before
        )

    acts_s, acts_z, acts_y = [], [], []
    mine = basis_in.T
    theirs = send(mine, swap(devices))
    block = grads.reshape(tokens * SUBLANES, -1)
    grads_z = pile([block] + along_all(block), [folded_across])
    grads_y = send(grads_z, across(devices))
    chunk_along(0, [theirs])
    [grads_y] = after([grads_y], [acts_z[0]])
    grads_cz, grads_cy = send(grads_z, swap(devices)), send(grads_y, swap(devices))
    sq_out = rotate_out(tokens, me, grads_z, grads_y, grads_cz, grads_cy, basis_out, [acts_z[0]])
    sq_pair = pile([sq_out, send(sq_out, across(devices))], [acts_y[0]])
    came = [sq_pair] + along_all(sq_pair)
    chunk_along(1, [sq_pair])
    total = None
    for chunk in range(len(SHARES)):
        total = part(chunk, [total] if chunk else [])
    came[-1:] = after(came[-1:], [total])
    swapped = [send(pair, swap(devices)) for pair in came]
    squares = (total * total).astype(jnp.bfloat16)
    own, given = squares[: mine.shape[0]], squares[mine.shape[0] :]
    other = send(given, swap(devices))
    return combine(me, own, other, came + swapped)


def solution(mesh):
    return jax.shard_map(
        local,
        mesh=mesh,
        in_specs=(
            P(("groups", "wide"), None),
            P(("groups", "wide"), None),
            P("groups", "wide"),
            P("groups", "wide"),
        ),
        out_specs=P(("groups", "wide"), None),
        check_vma=False,
    )
```

time: 70.7 us -> 71.7 us (1.014); the launches traced: 70.4 us -> 70.6 us
  local copies, waits for them, and re-layouts: 2.17 us -> 6.07 us
  Pallas kernels: 16.2 us -> 12.8 us
  starting transfers between devices: 26.8 us -> 25.8 us
    unnamed x0 -> x6, local copies, waits for them, and re-layouts: none -> 3.54 us
    pallas_call x1, Pallas kernels: 5.18 us -> 2.28 us  [rotate_out(): pl.pallas_call(functools.partial(rotate_out_kernel, tokens, len(waits)),...]
    ppermute x23 -> x25, starting transfers between devices: 26.8 us -> 25.8 us  [send(): return lax.ppermute(block, 'wide', pairs)]
    ppermute x23 -> x25, waiting for transfers between devices: 25.2 us -> 25.9 us  [send(): return lax.ppermute(block, 'wide', pairs)]
    pallas_call x3 -> x5, Pallas kernels: 10.9 us -> 10.4 us  [the longest x2 8.63 us: rotate_in(): pl.pallas_call(functools.partial(rotate_in_kernel, tokens, start, len(bef...]
  transfers between devices with their start and end apart: 23 -> 25, of which waited for: 8 -> 9; matrix products, arithmetic and copies ran while one was open for 3% -> 4% of each run, Pallas kernels for 20% -> 16%
where the time goes in v7:
time: 71.7 us; the launch traced here: 70.6 us
  waiting for transfers between devices  25.9 us (36%)
  starting transfers between devices  25.8 us (36%)
  Pallas kernels  12.8 us (18%)
  local copies, waits for them, and re-layouts  6.07 us (8%)
    ppermute x25, waiting for transfers between devices, send(): return lax.ppermute(block, 'wide', pairs)  25.9 us
    ppermute x25, starting transfers between devices, send(): return lax.ppermute(block, 'wide', pairs)  25.8 us
    pallas_call x2, Pallas kernels, rotate_in(): pl.pallas_call(functools.partial(rotate_in_kernel, tokens, start, len(bef...  8.63 us
    unnamed x6, local copies, waits for them, and re-layouts  3.54 us
    pallas_call x1, Pallas kernels, rotate_out(): pl.pallas_call(functools.partial(rotate_out_kernel, tokens, len(waits)),...  2.28 us
    pallas_call x1, Pallas kernels, combine(): pl.pallas_call(functools.partial(combine_kernel, steps), out_shape=jax.Sh...  1.76 us
    reshape x1, local copies, waits for them, and re-layouts, local(): folded = acts.reshape(tokens * SUBLANES, -1)  1.46 us
  transfers between devices with their start and end apart: 25, of which 9 were waited for; matrix products, arithmetic and copies ran while one was open for 4% of the time, Pallas kernels for 16%

profile of v7, /device:TPU:0, one launch (start us, length us, event | category | flops | bytes accessed | tf_op | source)
XLA Modules:
  0.0 70.6 jit_solution(16591066948453605986)
XLA Ops:
  0.5 1.5 %reshape.10.own_ref = bf16[40,3584]{1,0:T(8,128)(2,1)S(1)} reshape(bf16[5,28672]{1,0:T(8,128)(2,1)} %param.4) | data formatting | bytes 573440 | tf_op jit(solution)/shard_map/reshape | solution.py:274
  1.9 2.6 %collective-permute-start = (bf16[40,3584]{1,0:T(8,128)(2,1)S(1)}, bf16[40,3584]{1,0:T(8,128)(2,1)S(1)}, u32[]{:S(2)}, u32[]{:S(2)}) collective-permute-start(bf16[40,3584]{1,0:T(8,128)(2,1)S(1)} %reshape.10.own_ref), channel_id=1, source_target_pairs={{0,2},{1,3},{2,0},{3,1},{4,6},{5,7},{6,4},{7,5},{8,10},{9,11},{10,... | collective-permute-start | bytes 860168 | tf_op jit(solution)/shard_map/ppermute | solution.py:34
  4.5 1.0 %reshape.11.refs_0_ = bf16[40,1024]{1,0:T(8,128)(2,1)S(1)} reshape(bf16[5,8192]{1,0:T(8,128)(2,1)} %param.5) | data formatting | bytes 163840 | tf_op jit(solution)/shard_map/reshape | solution.py:293
  5.5 1.6 %collective-permute-start.4 = (bf16[40,1024]{1,0:T(8,128)(2,1)S(1)}, bf16[40,1024]{1,0:T(8,128)(2,1)S(1)}, u32[]{:S(2)}, u32[]{:S(2)}) collective-permute-start(bf16[40,1024]{1,0:T(8,128)(2,1)S(1)} %reshape.11.refs_0_), channel_id=1, source_target_pairs={{0,4},{1,5},{2,6},{3,7},{4,8},{5,9},{6,10},{7,11},{8,12},{9,13},{1... | collective-permute-start | bytes 245768 | tf_op jit(solution)/shard_map/ppermute | solution.py:34
  7.2 2.6 %collective-permute-start.5 = (bf16[40,1024]{1,0:T(8,128)(2,1)S(1)}, bf16[40,1024]{1,0:T(8,128)(2,1)S(1)}, u32[]{:S(2)}, u32[]{:S(2)}) collective-permute-start(bf16[40,1024]{1,0:T(8,128)(2,1)S(1)} %reshape.11.refs_0_), channel_id=1, source_target_pairs={{0,8},{1,9},{2,10},{3,11},{4,12},{5,13},{6,14},{7,15},{8,0},{9,1},... | collective-permute-start | bytes 245768 | tf_op jit(solution)/shard_map/ppermute | solution.py:34
  9.8 1.3 %collective-permute-start.6 = (bf16[40,1024]{1,0:T(8,128)(2,1)S(1)}, bf16[40,1024]{1,0:T(8,128)(2,1)S(1)}, u32[]{:S(2)}, u32[]{:S(2)}) collective-permute-start(bf16[40,1024]{1,0:T(8,128)(2,1)S(1)} %reshape.11.refs_0_), channel_id=1, source_target_pairs={{0,12},{1,13},{2,14},{3,15},{4,0},{5,1},{6,2},{7,3},{8,4},{9,5},{1... | collective-permute-start | bytes 245768 | tf_op jit(solution)/shard_map/ppermute | solution.py:34
  11.1 1.5 %collective-permute-done.4.refs_1_ = bf16[40,1024]{1,0:T(8,128)(2,1)S(1)} collective-permute-done((bf16[40,1024]{1,0:T(8,128)(2,1)S(1)}, bf16[40,1024]{1,0:T(8,128)(2,1)S(1)}, u32[]{:S(2)}, u32[]{:S(2)}) %collective-permute-start.4) | collective-permute-done | bytes 81952 | tf_op jit(solution)/shard_map/ppermute | solution.py:34
  12.6 3.1 %collective-permute-done.5.refs_2_ = bf16[40,1024]{1,0:T(8,128)(2,1)S(1)} collective-permute-done((bf16[40,1024]{1,0:T(8,128)(2,1)S(1)}, bf16[40,1024]{1,0:T(8,128)(2,1)S(1)}, u32[]{:S(2)}, u32[]{:S(2)}) %collective-permute-start.5) | collective-permute-done | bytes 81952 | tf_op jit(solution)/shard_map/ppermute | solution.py:34
  16.5 3.1 %collective-permute-start.10 = (bf16[40,1792]{1,0:T(8,128)(2,1)S(1)}, bf16[40,1792]{1,0:T(8,128)(2,1)S(1)}, u32[]{:S(2)}, u32[]{:S(2)}) collective-permute-start(bf16[40,1792]{1,0:T(8,128)(2,1)S(1)} %get-tuple-element.5), channel_id=1, source_target_pairs={{0,12},{1,13},{2,14},{3,15},{4,0},{5,1},{6,2},{7,3},{8,4},{9,5},{1... | collective-permute-start | bytes 430088 | tf_op jit(solution)/shard_map/ppermute | solution.py:34
  20.2 3.6 %collective-permute-done.10.refs_2_ = bf16[40,1792]{1,0:T(8,128)(2,1)S(1)} collective-permute-done((bf16[40,1792]{1,0:T(8,128)(2,1)S(1)}, bf16[40,1792]{1,0:T(8,128)(2,1)S(1)}, u32[]{:S(2)}, u32[]{:S(2)}) %collective-permute-start.10) | collective-permute-done | bytes 143392 | tf_op jit(solution)/shard_map/ppermute | solution.py:34
  23.8 3.8 %collective-permute-done.8.refs_0_ = bf16[40,1792]{1,0:T(8,128)(2,1)S(1)} collective-permute-done((bf16[40,1792]{1,0:T(8,128)(2,1)S(1)}, bf16[40,1792]{1,0:T(8,128)(2,1)S(1)}, u32[]{:S(2)}, u32[]{:S(2)}) %collective-permute-start.8) | collective-permute-done | bytes 143392 | tf_op jit(solution)/shard_map/ppermute | solution.py:34
  27.6 5.0 %collective-permute-done.9.refs_1_ = bf16[40,1792]{1,0:T(8,128)(2,1)S(1)} collective-permute-done((bf16[40,1792]{1,0:T(8,128)(2,1)S(1)}, bf16[40,1792]{1,0:T(8,128)(2,1)S(1)}, u32[]{:S(2)}, u32[]{:S(2)}) %collective-permute-start.9) | collective-permute-done | bytes 143392 | tf_op jit(solution)/shard_map/ppermute | solution.py:34
  32.8 1.6 %collective-permute-start.15 = (bf16[3,40,1792]{2,1,0:T(8,128)(2,1)S(1)}, bf16[3,40,1792]{2,1,0:T(8,128)(2,1)S(1)}, u32[]{:S(2)}, u32[]{:S(2)}) collective-permute-start(bf16[3,40,1792]{2,1,0:T(8,128)(2,1)S(1)} %pile.5.refs_1_.refs_0_.z_ref), channel_id=1, source_target_pairs={{0,2},{1,3},{2,0},{3,1},{4,6},{5,7},{6,4},{7,5},{8,10},{9,11},{10,... | collective-permute-start | bytes 1290248 | tf_op jit(solution)/shard_map/ppermute | solution.py:34
  34.4 3.2 %collective-permute-start.2 = (bf16[40,1792]{1,0:T(8,128)(2,1)S(1)}, bf16[40,1792]{1,0:T(8,128)(2,1)S(1)}, u32[]{:S(2)}, u32[]{:S(2)}) collective-permute-start(bf16[40,1792]{1,0:T(8,128)(2,1)S(1)} %get-tuple-element.6), channel_id=1, source_target_pairs={{0,8},{1,9},{2,10},{3,11},{4,12},{5,13},{6,14},{7,15},{8,0},{9,1},... | collective-permute-start | bytes 430088 | tf_op jit(solution)/shard_map/ppermute | solution.py:34
  38.2 3.5 %copy-done = bf16[8192,512]{1,0:T(8,128)(2,1)S(1)} copy-done((bf16[8192,512]{1,0:T(8,128)(2,1)S(1)}, bf16[8192,512]{1,0:T(8,128)(2,1)}, u32[]{:S(2)}) %copy-start) | copy-done | bytes 8388632
  41.7 2.3 %rotate_out.1.refs_0_ = bf16[80,512]{1,0:T(8,128)(2,1)S(1)} custom-call(s32[1]{0:T(128)} %bitcast.me_ref, bf16[4,40,1024]{2,1,0:T(8,128)(2,1)S(1)} %pile.4.z_ref, bf16[4,40,1024]{2,1,0:T(8,128)(2,1)S(1)} %after.2.y_ref, bf16[4,40,1024]{2,1,0:T(8,128)(2,1)S(1)} %collective-permute-done.12.cz_ref, bf16[4,40,1024]{2,1,0:T(8,128)(2,1)S(1)} %collective-permute-done.13.cy_ref, ...), custom_call_target="tpu_custom_call" | custom-call | flops 671088640 | bytes 8388608 | tf_op jit(solution)/shard_map/rotate_out/pallas_call | solution.py:101
  44.6 3.9 %collective-permute-done.14.refs_1_ = bf16[80,512]{1,0:T(8,128)(2,1)S(1)} collective-permute-done((bf16[80,512]{1,0:T(8,128)(2,1)S(1)}, bf16[80,512]{1,0:T(8,128)(2,1)S(1)}, u32[]{:S(2)}, u32[]{:S(2)}) %collective-permute-start.14) | collective-permute-done | bytes 81952 | tf_op jit(solution)/shard_map/ppermute | solution.py:34
  49.2 2.6 %collective-permute-start.18 = (bf16[2,80,512]{2,1,0:T(8,128)(2,1)S(1)}, bf16[2,80,512]{2,1,0:T(8,128)(2,1)S(1)}, u32[]{:S(2)}, u32[]{:S(2)}) collective-permute-start(bf16[2,80,512]{2,1,0:T(8,128)(2,1)S(1)} %pile.6.refs_3_.refs_0_), channel_id=1, source_target_pairs={{0,4},{1,5},{2,6},{3,7},{4,8},{5,9},{6,10},{7,11},{8,12},{9,13},{1... | collective-permute-start | bytes 491528 | tf_op jit(solution)/shard_map/ppermute | solution.py:34
  52.0 2.2 %collective-permute-start.20 = (bf16[2,80,512]{2,1,0:T(8,128)(2,1)S(1)}, bf16[2,80,512]{2,1,0:T(8,128)(2,1)S(1)}, u32[]{:S(2)}, u32[]{:S(2)}) collective-permute-start(bf16[2,80,512]{2,1,0:T(8,128)(2,1)S(1)} %pile.6.refs_3_.refs_0_), channel_id=1, source_target_pairs={{0,12},{1,13},{2,14},{3,15},{4,0},{5,1},{6,2},{7,3},{8,4},{9,5},{1... | collective-permute-start | bytes 491528 | tf_op jit(solution)/shard_map/ppermute | solution.py:34
  54.2 4.3 %rotate_in.2.refs_0_ = f32[192,40]{1,0:T(8,128)S(1)} custom-call(s32[1]{0:T(128)} %bitcast.me_ref, bf16[40,3584]{1,0:T(8,128)(2,1)S(1)} %reshape.10.own_ref, bf16[40,3584]{1,0:T(8,128)(2,1)S(1)} %collective-permute-done.refs_4_.across_ref, bf16[3,40,1792]{2,1,0:T(8,128)(2,1)S(1)} %pile.5.refs_1_.refs_0_.z_ref, ...), custom_call_target="tpu_custom_call" | custom-call | flops 220200960 | bytes 5505024 | tf_op jit(solution)/shard_map/rotate_in/pallas_call | solution.py:149
  59.1 3.7 %collective-permute-done.19.refs_2_ = bf16[2,80,512]{2,1,0:T(8,128)(2,1)S(1)} collective-permute-done((bf16[2,80,512]{2,1,0:T(8,128)(2,1)S(1)}, bf16[2,80,512]{2,1,0:T(8,128)(2,1)S(1)}, u32[]{:S(2)}, u32[]{:S(2)}) %collective-permute-start.19) | collective-permute-done | bytes 163872 | tf_op jit(solution)/shard_map/ppermute | solution.py:34
  62.7 4.3 %rotate_in.3.refs_1_ = f32[192,40]{1,0:T(8,128)S(1)} custom-call(s32[1]{0:T(128)} %bitcast.me_ref, bf16[40,3584]{1,0:T(8,128)(2,1)S(1)} %reshape.10.own_ref, bf16[40,3584]{1,0:T(8,128)(2,1)S(1)} %collective-permute-done.refs_4_.across_ref, bf16[3,40,1792]{2,1,0:T(8,128)(2,1)S(1)} %pile.7.z_ref, bf16[3,40,1792]{2,1,0:T(8,128)(2,1)S(1)} %collective-permute-done.16.y_ref, ...), custom_call_target="tpu_custom_call" | custom-call | flops 220200960 | bytes 5505024 | tf_op jit(solution)/shard_map/rotate_in/pallas_call | solution.py:149
  67.8 1.1 %collective-permute-done.17.other_ref = bf16[96,40]{1,0:T(8,128)(2,1)S(1)} collective-permute-done((bf16[96,40]{1,0:T(8,128)(2,1)S(1)}, bf16[96,40]{1,0:T(8,128)(2,1)S(1)}, u32[]{:S(2)}, u32[]{:S(2)}) %collective-permute-start.17) | collective-permute-done | bytes 7712 | tf_op jit(solution)/shard_map/ppermute | solution.py:34
  68.9 1.8 %combine.1 = bf16[96,8192]{1,0:T(8,128)(2,1)} custom-call(s32[1]{0:T(128)} %bitcast.me_ref, bf16[96,40]{1,0:T(8,128)(2,1)S(1)} %get-tuple-element.8.own_ref, bf16[96,40]{1,0:T(8,128)(2,1)S(1)} %collective-permute-done.17.other_ref, bf16[2,80,512]{2,1,0:T(8,128)(2,1)S(1)} %pile.6.refs_3_.refs_0_, bf16[2,80,512]{2,1,0:T(8,128)(2,1)S(1)} %collective-permute-done.18.refs_1_, ...), custom_call_target="tpu_custom_call" | custom-call | flops 125829120 | bytes 3145728 | tf_op jit(solution)/shard_map/combine/pallas_call | solution.py:252
  (48 shorter events, 5.3 us)
Async XLA Ops:
  0.0 32.6 %collective-permute-start.11 = (bf16[96,28672]{1,0:T(8,128)(2,1)}, bf16[96,28672]{1,0:T(8,128)(2,1)}, u32[]{:S(2)}, u32[]{:S(2)}) collective-permute-start(bf16[96,28672]{1,0:T(8,128)(2,1)} %bitcast.2), channel_id=1, source_target_pairs={{0,1},{1,0},{2,3},{3,2},{4,5},{5,4},{6,7},{7,6},{8,9},{9,8},{10,11... | collective-permute-start | bytes 16515080 | tf_op jit(solution)/shard_map/ppermute | solution.py:34
  1.9 13.9 %collective-permute-start = (bf16[40,3584]{1,0:T(8,128)(2,1)S(1)}, bf16[40,3584]{1,0:T(8,128)(2,1)S(1)}, u32[]{:S(2)}, u32[]{:S(2)}) collective-permute-start(bf16[40,3584]{1,0:T(8,128)(2,1)S(1)} %reshape.10.own_ref), channel_id=1, source_target_pairs={{0,2},{1,3},{2,0},{3,1},{4,6},{5,7},{6,4},{7,5},{8,10},{9,11},{10,... | collective-permute-start | bytes 860168 | tf_op jit(solution)/shard_map/ppermute | solution.py:34
  5.5 7.0 %collective-permute-start.4 = (bf16[40,1024]{1,0:T(8,128)(2,1)S(1)}, bf16[40,1024]{1,0:T(8,128)(2,1)S(1)}, u32[]{:S(2)}, u32[]{:S(2)}) collective-permute-start(bf16[40,1024]{1,0:T(8,128)(2,1)S(1)} %reshape.11.refs_0_), channel_id=1, source_target_pairs={{0,4},{1,5},{2,6},{3,7},{4,8},{5,9},{6,10},{7,11},{8,12},{9,13},{1... | collective-permute-start | bytes 245768 | tf_op jit(solution)/shard_map/ppermute | solution.py:34
  7.2 8.5 %collective-permute-start.5 = (bf16[40,1024]{1,0:T(8,128)(2,1)S(1)}, bf16[40,1024]{1,0:T(8,128)(2,1)S(1)}, u32[]{:S(2)}, u32[]{:S(2)}) collective-permute-start(bf16[40,1024]{1,0:T(8,128)(2,1)S(1)} %reshape.11.refs_0_), channel_id=1, source_target_pairs={{0,8},{1,9},{2,10},{3,11},{4,12},{5,13},{6,14},{7,15},{8,0},{9,1},... | collective-permute-start | bytes 245768 | tf_op jit(solution)/shard_map/ppermute | solution.py:34
  9.8 6.1 %collective-permute-start.6 = (bf16[40,1024]{1,0:T(8,128)(2,1)S(1)}, bf16[40,1024]{1,0:T(8,128)(2,1)S(1)}, u32[]{:S(2)}, u32[]{:S(2)}) collective-permute-start(bf16[40,1024]{1,0:T(8,128)(2,1)S(1)} %reshape.11.refs_0_), channel_id=1, source_target_pairs={{0,12},{1,13},{2,14},{3,15},{4,0},{5,1},{6,2},{7,3},{8,4},{9,5},{1... | collective-permute-start | bytes 245768 | tf_op jit(solution)/shard_map/ppermute | solution.py:34
  15.9 16.8 %collective-permute-start.7 = (bf16[4,40,1024]{2,1,0:T(8,128)(2,1)S(1)}, bf16[4,40,1024]{2,1,0:T(8,128)(2,1)S(1)}, u32[]{:S(2)}, u32[]{:S(2)}) collective-permute-start(bf16[4,40,1024]{2,1,0:T(8,128)(2,1)S(1)} %pile.4.z_ref), channel_id=1, source_target_pairs={{0,2},{1,3},{2,0},{3,1},{4,6},{5,7},{6,4},{7,5},{8,10},{9,11},{10,... | collective-permute-start | bytes 983048 | tf_op jit(solution)/shard_map/ppermute | solution.py:34
  16.5 7.4 %collective-permute-start.10 = (bf16[40,1792]{1,0:T(8,128)(2,1)S(1)}, bf16[40,1792]{1,0:T(8,128)(2,1)S(1)}, u32[]{:S(2)}, u32[]{:S(2)}) collective-permute-start(bf16[40,1792]{1,0:T(8,128)(2,1)S(1)} %get-tuple-element.5), channel_id=1, source_target_pairs={{0,12},{1,13},{2,14},{3,15},{4,0},{5,1},{6,2},{7,3},{8,4},{9,5},{1... | collective-permute-start | bytes 430088 | tf_op jit(solution)/shard_map/ppermute | solution.py:34
  19.6 8.0 %collective-permute-start.8 = (bf16[40,1792]{1,0:T(8,128)(2,1)S(1)}, bf16[40,1792]{1,0:T(8,128)(2,1)S(1)}, u32[]{:S(2)}, u32[]{:S(2)}) collective-permute-start(bf16[40,1792]{1,0:T(8,128)(2,1)S(1)} %get-tuple-element.5), channel_id=1, source_target_pairs={{0,4},{1,5},{2,6},{3,7},{4,8},{5,9},{6,10},{7,11},{8,12},{9,13},{1... | collective-permute-start | bytes 430088 | tf_op jit(solution)/shard_map/ppermute | solution.py:34
  19.6 13.0 %collective-permute-start.9 = (bf16[40,1792]{1,0:T(8,128)(2,1)S(1)}, bf16[40,1792]{1,0:T(8,128)(2,1)S(1)}, u32[]{:S(2)}, u32[]{:S(2)}) collective-permute-start(bf16[40,1792]{1,0:T(8,128)(2,1)S(1)} %get-tuple-element.5), channel_id=1, source_target_pairs={{0,8},{1,9},{2,10},{3,11},{4,12},{5,13},{6,14},{7,15},{8,0},{9,1},... | collective-permute-start | bytes 430088 | tf_op jit(solution)/shard_map/ppermute | solution.py:34
  23.8 13.8 %collective-permute-start.12 = (bf16[4,40,1024]{2,1,0:T(8,128)(2,1)S(1)}, bf16[4,40,1024]{2,1,0:T(8,128)(2,1)S(1)}, u32[]{:S(2)}, u32[]{:S(2)}) collective-permute-start(bf16[4,40,1024]{2,1,0:T(8,128)(2,1)S(1)} %pile.4.z_ref), channel_id=1, source_target_pairs={{0,1},{1,0},{2,3},{3,2},{4,5},{5,4},{6,7},{7,6},{8,9},{9,8},{10,11... | collective-permute-start | bytes 983048 | tf_op jit(solution)/shard_map/ppermute | solution.py:34
  32.7 5.5 %collective-permute-start.13 = (bf16[4,40,1024]{2,1,0:T(8,128)(2,1)S(1)}, bf16[4,40,1024]{2,1,0:T(8,128)(2,1)S(1)}, u32[]{:S(2)}, u32[]{:S(2)}) collective-permute-start(bf16[4,40,1024]{2,1,0:T(8,128)(2,1)S(1)} %after.2.y_ref), channel_id=1, source_target_pairs={{0,1},{1,0},{2,3},{3,2},{4,5},{5,4},{6,7},{7,6},{8,9},{9,8},{10,11... | collective-permute-start | bytes 983048 | tf_op jit(solution)/shard_map/ppermute | solution.py:34
  32.8 15.8 %collective-permute-start.15 = (bf16[3,40,1792]{2,1,0:T(8,128)(2,1)S(1)}, bf16[3,40,1792]{2,1,0:T(8,128)(2,1)S(1)}, u32[]{:S(2)}, u32[]{:S(2)}) collective-permute-start(bf16[3,40,1792]{2,1,0:T(8,128)(2,1)S(1)} %pile.5.refs_1_.refs_0_.z_ref), channel_id=1, source_target_pairs={{0,2},{1,3},{2,0},{3,1},{4,6},{5,7},{6,4},{7,5},{8,10},{9,11},{10,... | collective-permute-start | bytes 1290248 | tf_op jit(solution)/shard_map/ppermute | solution.py:34
  34.4 14.2 %collective-permute-start.1 = (bf16[40,1792]{1,0:T(8,128)(2,1)S(1)}, bf16[40,1792]{1,0:T(8,128)(2,1)S(1)}, u32[]{:S(2)}, u32[]{:S(2)}) collective-permute-start(bf16[40,1792]{1,0:T(8,128)(2,1)S(1)} %get-tuple-element.6), channel_id=1, source_target_pairs={{0,4},{1,5},{2,6},{3,7},{4,8},{5,9},{6,10},{7,11},{8,12},{9,13},{1... | collective-permute-start | bytes 430088 | tf_op jit(solution)/shard_map/ppermute | solution.py:34
  34.4 14.2 %collective-permute-start.2 = (bf16[40,1792]{1,0:T(8,128)(2,1)S(1)}, bf16[40,1792]{1,0:T(8,128)(2,1)S(1)}, u32[]{:S(2)}, u32[]{:S(2)}) collective-permute-start(bf16[40,1792]{1,0:T(8,128)(2,1)S(1)} %get-tuple-element.6), channel_id=1, source_target_pairs={{0,8},{1,9},{2,10},{3,11},{4,12},{5,13},{6,14},{7,15},{8,0},{9,1},... | collective-permute-start | bytes 430088 | tf_op jit(solution)/shard_map/ppermute | solution.py:34
  37.6 11.0 %collective-permute-start.3 = (bf16[40,1792]{1,0:T(8,128)(2,1)S(1)}, bf16[40,1792]{1,0:T(8,128)(2,1)S(1)}, u32[]{:S(2)}, u32[]{:S(2)}) collective-permute-start(bf16[40,1792]{1,0:T(8,128)(2,1)S(1)} %get-tuple-element.6), channel_id=1, source_target_pairs={{0,12},{1,13},{2,14},{3,15},{4,0},{5,1},{6,2},{7,3},{8,4},{9,5},{1... | collective-permute-start | bytes 430088 | tf_op jit(solution)/shard_map/ppermute | solution.py:34
  44.0 4.5 %collective-permute-start.14 = (bf16[80,512]{1,0:T(8,128)(2,1)S(1)}, bf16[80,512]{1,0:T(8,128)(2,1)S(1)}, u32[]{:S(2)}, u32[]{:S(2)}) collective-permute-start(bf16[80,512]{1,0:T(8,128)(2,1)S(1)} %rotate_out.1.refs_0_), channel_id=1, source_target_pairs={{0,2},{1,3},{2,0},{3,1},{4,6},{5,7},{6,4},{7,5},{8,10},{9,11},{10,... | collective-permute-start | bytes 245768 | tf_op jit(solution)/shard_map/ppermute | solution.py:34
  48.6 14.1 %collective-permute-start.16 = (bf16[3,40,1792]{2,1,0:T(8,128)(2,1)S(1)}, bf16[3,40,1792]{2,1,0:T(8,128)(2,1)S(1)}, u32[]{:S(2)}, u32[]{:S(2)}) collective-permute-start(bf16[3,40,1792]{2,1,0:T(8,128)(2,1)S(1)} %pile.7.z_ref), channel_id=1, source_target_pairs={{0,2},{1,3},{2,0},{3,1},{4,6},{5,7},{6,4},{7,5},{8,10},{9,11},{10,... | collective-permute-start | bytes 1290248 | tf_op jit(solution)/shard_map/ppermute | solution.py:34
  49.2 9.3 %collective-permute-start.18 = (bf16[2,80,512]{2,1,0:T(8,128)(2,1)S(1)}, bf16[2,80,512]{2,1,0:T(8,128)(2,1)S(1)}, u32[]{:S(2)}, u32[]{:S(2)}) collective-permute-start(bf16[2,80,512]{2,1,0:T(8,128)(2,1)S(1)} %pile.6.refs_3_.refs_0_), channel_id=1, source_target_pairs={{0,4},{1,5},{2,6},{3,7},{4,8},{5,9},{6,10},{7,11},{8,12},{9,13},{1... | collective-permute-start | bytes 491528 | tf_op jit(solution)/shard_map/ppermute | solution.py:34
  51.8 11.0 %collective-permute-start.19 = (bf16[2,80,512]{2,1,0:T(8,128)(2,1)S(1)}, bf16[2,80,512]{2,1,0:T(8,128)(2,1)S(1)}, u32[]{:S(2)}, u32[]{:S(2)}) collective-permute-start(bf16[2,80,512]{2,1,0:T(8,128)(2,1)S(1)} %pile.6.refs_3_.refs_0_), channel_id=1, source_target_pairs={{0,8},{1,9},{2,10},{3,11},{4,12},{5,13},{6,14},{7,15},{8,0},{9,1},... | collective-permute-start | bytes 491528 | tf_op jit(solution)/shard_map/ppermute | solution.py:34
  52.0 15.1 %collective-permute-start.20 = (bf16[2,80,512]{2,1,0:T(8,128)(2,1)S(1)}, bf16[2,80,512]{2,1,0:T(8,128)(2,1)S(1)}, u32[]{:S(2)}, u32[]{:S(2)}) collective-permute-start(bf16[2,80,512]{2,1,0:T(8,128)(2,1)S(1)} %pile.6.refs_3_.refs_0_), channel_id=1, source_target_pairs={{0,12},{1,13},{2,14},{3,15},{4,0},{5,1},{6,2},{7,3},{8,4},{9,5},{1... | collective-permute-start | bytes 491528 | tf_op jit(solution)/shard_map/ppermute | solution.py:34
  54.1 13.6 %collective-permute-start.21 = (bf16[2,80,512]{2,1,0:T(8,128)(2,1)S(1)}, bf16[2,80,512]{2,1,0:T(8,128)(2,1)S(1)}, u32[]{:S(2)}, u32[]{:S(2)}) collective-permute-start(bf16[2,80,512]{2,1,0:T(8,128)(2,1)S(1)} %pile.6.refs_3_.refs_0_), channel_id=1, source_target_pairs={{0,1},{1,0},{2,3},{3,2},{4,5},{5,4},{6,7},{7,6},{8,9},{9,8},{10,11... | collective-permute-start | bytes 491528 | tf_op jit(solution)/shard_map/ppermute | solution.py:34
  58.5 9.3 %collective-permute-start.22 = (bf16[2,80,512]{2,1,0:T(8,128)(2,1)S(1)}, bf16[2,80,512]{2,1,0:T(8,128)(2,1)S(1)}, u32[]{:S(2)}, u32[]{:S(2)}) collective-permute-start(bf16[2,80,512]{2,1,0:T(8,128)(2,1)S(1)} %collective-permute-done.18.refs_1_), channel_id=1, source_target_pairs={{0,1},{1,0},{2,3},{3,2},{4,5},{5,4},{6,7},{7,6},{8,9},{9,8},{10,11... | collective-permute-start | bytes 491528 | tf_op jit(solution)/shard_map/ppermute | solution.py:34
  62.7 5.1 %collective-permute-start.23 = (bf16[2,80,512]{2,1,0:T(8,128)(2,1)S(1)}, bf16[2,80,512]{2,1,0:T(8,128)(2,1)S(1)}, u32[]{:S(2)}, u32[]{:S(2)}) collective-permute-start(bf16[2,80,512]{2,1,0:T(8,128)(2,1)S(1)} %collective-permute-done.19.refs_2_), channel_id=1, source_target_pairs={{0,1},{1,0},{2,3},{3,2},{4,5},{5,4},{6,7},{7,6},{8,9},{9,8},{10,11... | collective-permute-start | bytes 491528 | tf_op jit(solution)/shard_map/ppermute | solution.py:34
  67.1 1.8 %collective-permute-start.24 = (bf16[2,80,512]{2,1,0:T(8,128)(2,1)S(1)}, bf16[2,80,512]{2,1,0:T(8,128)(2,1)S(1)}, u32[]{:S(2)}, u32[]{:S(2)}) collective-permute-start(bf16[2,80,512]{2,1,0:T(8,128)(2,1)S(1)} %after.3.refs_3_), channel_id=1, source_target_pairs={{0,1},{1,0},{2,3},{3,2},{4,5},{5,4},{6,7},{7,6},{8,9},{9,8},{10,11... | collective-permute-start | bytes 491528 | tf_op jit(solution)/shard_map/ppermute | solution.py:34
  (4 other events, 33.1 us)

commit v8 on v6

--- a/solution.py
+++ b/solution.py
@@ -109,7 +109,7 @@
             pltpu.VMEM((width // 128, total * SUBLANES, 128), jnp.float32),
             pltpu.VMEM((total, columns), jnp.float32),
         ],
-        compiler_params=pltpu.CompilerParams(vmem_limit_bytes=48 * 2**20),
+        compiler_params=pltpu.CompilerParams(vmem_limit_bytes=24 * 2**20),
         cost_estimate=pl.CostEstimate(
             flops=2 * total * basis.shape[0] * columns, bytes_accessed=2 * basis.size, transcendentals=0
         ),
@@ -157,7 +157,7 @@
         in_specs=[SMEM] + [VMEM] * 4 + [basis] * 2 + [VMEM] * len(before),
         out_specs=VMEM,
         scratch_shapes=[pltpu.VMEM((width // 128, chips * height, 128), jnp.float32)],
-        compiler_params=pltpu.CompilerParams(vmem_limit_bytes=48 * 2**20),
+        compiler_params=pltpu.CompilerParams(vmem_limit_bytes=24 * 2**20),
         cost_estimate=pl.CostEstimate(
             flops=4 * chips * tokens * mine.shape[0] * SUBLANES * width,
             bytes_accessed=4 * mine.shape[0] * SUBLANES * width,
@@ -178,10 +178,43 @@
         out_shape=jax.ShapeDtypeStruct((len(blocks), *blocks[0].shape), blocks[0].dtype),
         in_specs=[VMEM] * len(blocks) + [ANY] * len(waits),
         out_specs=VMEM,
-        compiler_params=pltpu.CompilerParams(vmem_limit_bytes=48 * 2**20),
+        compiler_params=pltpu.CompilerParams(vmem_limit_bytes=24 * 2**20),
         cost_estimate=pl.CostEstimate(flops=0, bytes_accessed=2 * len(blocks) * blocks[0].size, transcendentals=0),
         name="pile",
     )(*blocks, *waits)
+
+
+def fetch_kernel(from_ref, *refs):
+    to_ref, done = refs[-2:]
+    copy = pltpu.make_async_copy(from_ref, to_ref, done)
+    copy.start()
+    copy.wait()
+
+
+def fetch(array, waits):
+    return pl.pallas_call(
+        fetch_kernel,
+        out_shape=jax.ShapeDtypeStruct(array.shape, array.dtype),
+        in_specs=[ANY] * (1 + len(waits)),
+        out_specs=VMEM,
+        scratch_shapes=[pltpu.SemaphoreType.DMA],
+        compiler_params=pltpu.CompilerParams(vmem_limit_bytes=16 * 2**20),
+        cost_estimate=pl.CostEstimate(flops=0, bytes_accessed=2 * array.size, transcendentals=0),
+        name="fetch",
+    )(array, *waits)
+
+
+def after(arrays, waits):
+    return pl.pallas_call(
+        lambda *refs: None,
+        out_shape=[jax.ShapeDtypeStruct(array.shape, array.dtype) for array in arrays],
+        in_specs=[ANY] * (len(arrays) + len(waits)),
+        out_specs=[ANY] * len(arrays),
+        input_output_aliases={i: i for i in range(len(arrays))},
+        compiler_params=pltpu.CompilerParams(vmem_limit_bytes=2**20),
+        cost_estimate=pl.CostEstimate(flops=0, bytes_accessed=0, transcendentals=0),
+        name="after",
+    )(*arrays, *waits)
 
 
 def combine_kernel(me_ref, own_ref, other_ref, z_ref, y_ref, cz_ref, cy_ref, out_ref):
@@ -210,7 +243,7 @@
         out_shape=jax.ShapeDtypeStruct((own.shape[0], features), jnp.bfloat16),
         in_specs=[SMEM] + [VMEM] * 6,
         out_specs=VMEM,
-        compiler_params=pltpu.CompilerParams(vmem_limit_bytes=48 * 2**20),
+        compiler_params=pltpu.CompilerParams(vmem_limit_bytes=24 * 2**20),
         cost_estimate=pl.CostEstimate(
             flops=2 * own.shape[0] * total_tokens * features, bytes_accessed=4 * own.shape[0] * features, transcendentals=0
         ),
@@ -237,7 +270,8 @@
     folded = acts.reshape(tokens, CHUNKS, SUBLANES, width).transpose(1, 0, 2, 3).reshape(CHUNKS, -1, width)
     folded_across = send(folded, across(devices))
     block = grads.reshape(tokens * SUBLANES, -1)
-    grads_z = others(pile([block] + along_all(block), []))
+    basis_out = fetch(basis_out, [block])
+    grads_z = others(pile([block] + along_all(block), [folded_across, basis_out]))
 
     acts_z = [pile(along_all(folded[0]), [])]
     acts_y = [send(acts_z[0], across(devices))]

time: 70.7 us -> 75.8 us (1.072)
  local copies, waits for them, and re-layouts: 2.17 us -> 15.6 us
  waiting for transfers between devices: 25.2 us -> 16.9 us
  Pallas kernels: 16.2 us -> 14.1 us
  starting transfers between devices: 26.8 us -> 28.5 us
    unnamed x0 -> x18, local copies, waits for them, and re-layouts: none -> 13.4 us
    ppermute x23, waiting for transfers between devices: 25.2 us -> 16.9 us  [send(): return lax.ppermute(block, 'wide', pairs)]
    pallas_call x1, Pallas kernels: 5.18 us -> 2.28 us  [rotate_out(): pl.pallas_call(functools.partial(rotate_out_kernel, tokens, len(waits)),...]
    ppermute x23, starting transfers between devices: 26.8 us -> 28.5 us  [send(): return lax.ppermute(block, 'wide', pairs)]
    pallas_call x4, Pallas kernels: 0.1 us -> 1.08 us  [pile(): pl.pallas_call(functools.partial(pile_kernel, len(blocks)), out_shape=jax...]
  transfers between devices with their start and end apart: 23 -> 23, of which waited for: 8 -> 8; matrix products, arithmetic and copies ran while one was open for 3% -> 3% of each run, Pallas kernels for 20% -> 16%
where the time goes in v8:
time: 75.8 us; the launch traced here: 75.3 us
  starting transfers between devices  28.5 us (38%)
  waiting for transfers between devices  16.9 us (22%)
  local copies, waits for them, and re-layouts  15.6 us (21%)
  Pallas kernels  14.1 us (19%)
    ppermute x23, starting transfers between devices, send(): return lax.ppermute(block, 'wide', pairs)  28.5 us
    ppermute x23, waiting for transfers between devices, send(): return lax.ppermute(block, 'wide', pairs)  16.9 us
    unnamed x18, local copies, waits for them, and re-layouts  13.4 us
    pallas_call x2, Pallas kernels, rotate_in(): pl.pallas_call(functools.partial(rotate_in_kernel, tokens, len(before)),...  8.43 us
    pallas_call x1, Pallas kernels, rotate_out(): pl.pallas_call(functools.partial(rotate_out_kernel, tokens, len(waits)),...  2.28 us
    pallas_call x1, Pallas kernels, combine(): pl.pallas_call(combine_kernel, out_shape=jax.ShapeDtypeStruct((own.shape[...  1.76 us
  transfers between devices with their start and end apart: 23, of which 8 were waited for; matrix products, arithmetic and copies ran while one was open for 3% of the time, Pallas kernels for 16%

profile of v8, /device:TPU:0, one launch (start us, length us, event | category | flops | bytes accessed | tf_op | source)
XLA Modules:
  0.0 75.3 jit_solution(7301861974356002981)
XLA Ops:
  0.5 1.1 %copy_bitcast_fusion.1 = (bf16[2,40,1792]{2,1,0:T(8,128)(2,1)S(1)}, bf16[2,5,8,1792]{3,2,1,0:T(8,128)(2,1)S(1)}) fusion(bf16[1,5,16,1792]{3,1,2,0:T(8,128)(2,1)} %bitcast.25), kind=kLoop, calls=%fused_computation.1 | loop fusion | bytes 860160 | tf_op jit(solution)/shard_map/reshape | solution.py:270
  1.5 2.6 %collective-permute-start = (bf16[2,40,1792]{2,1,0:T(8,128)(2,1)S(1)}, bf16[2,40,1792]{2,1,0:T(8,128)(2,1)S(1)}, u32[]{:S(2)}, u32[]{:S(2)}) collective-permute-start(bf16[2,40,1792]{2,1,0:T(8,128)(2,1)S(1)} %get-tuple-element.9), channel_id=1, source_target_pairs={{0,2},{1,3},{2,0},{3,1},{4,6},{5,7},{6,4},{7,5},{8,10},{9,11},{10,... | collective-permute-start | bytes 860168 | tf_op jit(solution)/shard_map/ppermute | solution.py:34
  5.2 1.6 %collective-permute-start.4 = (bf16[40,1024]{1,0:T(8,128)(2,1)S(1)}, bf16[40,1024]{1,0:T(8,128)(2,1)S(1)}, u32[]{:S(2)}, u32[]{:S(2)}) collective-permute-start(bf16[40,1024]{1,0:T(8,128)(2,1)S(1)} %reshape.19.refs_0_), channel_id=1, source_target_pairs={{0,4},{1,5},{2,6},{3,7},{4,8},{5,9},{6,10},{7,11},{8,12},{9,13},{1... | collective-permute-start | bytes 245768 | tf_op jit(solution)/shard_map/ppermute | solution.py:34
  6.8 2.6 %collective-permute-start.5 = (bf16[40,1024]{1,0:T(8,128)(2,1)S(1)}, bf16[40,1024]{1,0:T(8,128)(2,1)S(1)}, u32[]{:S(2)}, u32[]{:S(2)}) collective-permute-start(bf16[40,1024]{1,0:T(8,128)(2,1)S(1)} %reshape.19.refs_0_), channel_id=1, source_target_pairs={{0,8},{1,9},{2,10},{3,11},{4,12},{5,13},{6,14},{7,15},{8,0},{9,1},... | collective-permute-start | bytes 245768 | tf_op jit(solution)/shard_map/ppermute | solution.py:34
  9.4 1.3 %collective-permute-start.6 = (bf16[40,1024]{1,0:T(8,128)(2,1)S(1)}, bf16[40,1024]{1,0:T(8,128)(2,1)S(1)}, u32[]{:S(2)}, u32[]{:S(2)}) collective-permute-start(bf16[40,1024]{1,0:T(8,128)(2,1)S(1)} %reshape.19.refs_0_), channel_id=1, source_target_pairs={{0,12},{1,13},{2,14},{3,15},{4,0},{5,1},{6,2},{7,3},{8,4},{9,5},{1... | collective-permute-start | bytes 245768 | tf_op jit(solution)/shard_map/ppermute | solution.py:34
  10.7 3.4 %copy-done.2 = bf16[8192,512]{1,0:T(8,128)(2,1)S(1)} copy-done((bf16[8192,512]{1,0:T(8,128)(2,1)S(1)}, bf16[8192,512]{1,0:T(8,128)(2,1)}, u32[]{:S(2)}) %copy-start.2) | copy-done | bytes 8388632
  15.5 3.3 %copy-done = bf16[8192,512]{1,0:T(8,128)(2,1)} copy-done((bf16[8192,512]{1,0:T(8,128)(2,1)}, bf16[8192,512]{1,0:T(8,128)(2,1)S(1)}, u32[]{:S(2)}) %copy-start) | copy-done | bytes 8388632
  19.3 2.1 %collective-permute-start.10 = (bf16[40,1792]{1,0:T(8,128)(2,1)S(1)}, bf16[40,1792]{1,0:T(8,128)(2,1)S(1)}, u32[]{:S(2)}, u32[]{:S(2)}) collective-permute-start(bf16[40,1792]{1,0:T(8,128)(2,1)S(1)} %get-tuple-element.7.own_ref), channel_id=1, source_target_pairs={{0,4},{1,5},{2,6},{3,7},{4,8},{5,9},{6,10},{7,11},{8,12},{9,13},{1... | collective-permute-start | bytes 430088 | tf_op jit(solution)/shard_map/ppermute | solution.py:34
  21.4 1.6 %collective-permute-start.11 = (bf16[40,1792]{1,0:T(8,128)(2,1)S(1)}, bf16[40,1792]{1,0:T(8,128)(2,1)S(1)}, u32[]{:S(2)}, u32[]{:S(2)}) collective-permute-start(bf16[40,1792]{1,0:T(8,128)(2,1)S(1)} %get-tuple-element.7.own_ref), channel_id=1, source_target_pairs={{0,8},{1,9},{2,10},{3,11},{4,12},{5,13},{6,14},{7,15},{8,0},{9,1},... | collective-permute-start | bytes 430088 | tf_op jit(solution)/shard_map/ppermute | solution.py:34
  23.9 4.1 %collective-permute-done.10.refs_0_ = bf16[40,1792]{1,0:T(8,128)(2,1)S(1)} collective-permute-done((bf16[40,1792]{1,0:T(8,128)(2,1)S(1)}, bf16[40,1792]{1,0:T(8,128)(2,1)S(1)}, u32[]{:S(2)}, u32[]{:S(2)}) %collective-permute-start.10) | collective-permute-done | bytes 143392 | tf_op jit(solution)/shard_map/ppermute | solution.py:34
  28.5 4.1 %collective-permute-done.11.refs_1_ = bf16[40,1792]{1,0:T(8,128)(2,1)S(1)} collective-permute-done((bf16[40,1792]{1,0:T(8,128)(2,1)S(1)}, bf16[40,1792]{1,0:T(8,128)(2,1)S(1)}, u32[]{:S(2)}, u32[]{:S(2)}) %collective-permute-start.11) | collective-permute-done | bytes 143392 | tf_op jit(solution)/shard_map/ppermute | solution.py:34
  32.6 1.6 %collective-permute-start.15 = (bf16[3,40,1792]{2,1,0:T(8,128)(2,1)S(1)}, bf16[3,40,1792]{2,1,0:T(8,128)(2,1)S(1)}, u32[]{:S(2)}, u32[]{:S(2)}) collective-permute-start(bf16[3,40,1792]{2,1,0:T(8,128)(2,1)S(1)} %pile.5.refs_0_.z_ref), channel_id=1, source_target_pairs={{0,2},{1,3},{2,0},{3,1},{4,6},{5,7},{6,4},{7,5},{8,10},{9,11},{10,... | collective-permute-start | bytes 1290248 | tf_op jit(solution)/shard_map/ppermute | solution.py:34
  34.2 3.5 %collective-permute-start.1 = (bf16[40,1792]{1,0:T(8,128)(2,1)S(1)}, bf16[40,1792]{1,0:T(8,128)(2,1)S(1)}, u32[]{:S(2)}, u32[]{:S(2)}) collective-permute-start(bf16[40,1792]{1,0:T(8,128)(2,1)S(1)} %get-tuple-element.8.own_ref), channel_id=1, source_target_pairs={{0,4},{1,5},{2,6},{3,7},{4,8},{5,9},{6,10},{7,11},{8,12},{9,13},{1... | collective-permute-start | bytes 430088 | tf_op jit(solution)/shard_map/ppermute | solution.py:34
  38.4 1.1 %collective-permute-start.2 = (bf16[40,1792]{1,0:T(8,128)(2,1)S(1)}, bf16[40,1792]{1,0:T(8,128)(2,1)}, u32[]{:S(2)}, u32[]{:S(2)}) collective-permute-start(bf16[40,1792]{1,0:T(8,128)(2,1)S(1)} %get-tuple-element.8.own_ref), channel_id=1, source_target_pairs={{0,8},{1,9},{2,10},{3,11},{4,12},{5,13},{6,14},{7,15},{8,0},{9,1},... | collective-permute-start | bytes 430088 | tf_op jit(solution)/shard_map/ppermute | solution.py:34
  40.3 1.2 %collective-permute-start.3 = (bf16[40,1792]{1,0:T(8,128)(2,1)S(1)}, bf16[40,1792]{1,0:T(8,128)(2,1)}, u32[]{:S(2)}, u32[]{:S(2)}) collective-permute-start(bf16[40,1792]{1,0:T(8,128)(2,1)S(1)} %get-tuple-element.8.own_ref), channel_id=1, source_target_pairs={{0,12},{1,13},{2,14},{3,15},{4,0},{5,1},{6,2},{7,3},{8,4},{9,5},{1... | collective-permute-start | bytes 430088 | tf_op jit(solution)/shard_map/ppermute | solution.py:34
  41.5 3.4 %copy-done.1 = bf16[8192,512]{1,0:T(8,128)(2,1)S(1)} copy-done((bf16[8192,512]{1,0:T(8,128)(2,1)S(1)}, bf16[8192,512]{1,0:T(8,128)(2,1)}, u32[]{:S(2)}) %copy-start.1) | copy-done | bytes 8388632
  46.9 2.3 %rotate_out.1.refs_3_.refs_0_ = bf16[80,512]{1,0:T(8,128)(2,1)S(1)} custom-call(s32[1]{0:T(128)} %bitcast.me_ref, bf16[4,40,1024]{2,1,0:T(8,128)(2,1)S(1)} %pile.4.z_ref, bf16[4,40,1024]{2,1,0:T(8,128)(2,1)S(1)} %collective-permute-done.7.y_ref, bf16[4,40,1024]{2,1,0:T(8,128)(2,1)S(1)} %copy-done.4, bf16[4,40,1024]{2,1,0:T(8,128)(2,1)S(1)} %copy-done.6, ...), custom_call_target="tpu_custom_call" | custom-call | flops 671088640 | bytes 8388608 | tf_op jit(solution)/shard_map/rotate_out/pallas_call | solution.py:102
  50.0 1.8 %collective-permute-start.18 = (bf16[80,512]{1,0:T(8,128)(2,1)S(1)}, bf16[80,512]{1,0:T(8,128)(2,1)S(1)}, u32[]{:S(2)}, u32[]{:S(2)}) collective-permute-start(bf16[80,512]{1,0:T(8,128)(2,1)S(1)} %rotate_out.1.refs_3_.refs_0_), channel_id=1, source_target_pairs={{0,8},{1,9},{2,10},{3,11},{4,12},{5,13},{6,14},{7,15},{8,0},{9,1},... | collective-permute-start | bytes 245768 | tf_op jit(solution)/shard_map/ppermute | solution.py:34
  51.8 1.7 %collective-permute-start.19 = (bf16[80,512]{1,0:T(8,128)(2,1)S(1)}, bf16[80,512]{1,0:T(8,128)(2,1)S(1)}, u32[]{:S(2)}, u32[]{:S(2)}) collective-permute-start(bf16[80,512]{1,0:T(8,128)(2,1)S(1)} %rotate_out.1.refs_3_.refs_0_), channel_id=1, source_target_pairs={{0,12},{1,13},{2,14},{3,15},{4,0},{5,1},{6,2},{7,3},{8,4},{9,5},{1... | collective-permute-start | bytes 245768 | tf_op jit(solution)/shard_map/ppermute | solution.py:34
  55.2 4.2 %rotate_in.2.refs_0_.refs_4_ = f32[192,40]{1,0:T(8,128)S(1)} custom-call(s32[1]{0:T(128)} %bitcast.me_ref, bf16[40,1792]{1,0:T(8,128)(2,1)S(1)} %get-tuple-element.7.own_ref, bf16[40,1792]{1,0:T(8,128)(2,1)S(1)} %get-tuple-element.5.across_ref, bf16[3,40,1792]{2,1,0:T(8,128)(2,1)S(1)} %pile.5.refs_0_.z_ref, ...), custom_call_target="tpu_custom_call" | custom-call | flops 220200960 | bytes 5505024 | tf_op jit(solution)/shard_map/rotate_in/pallas_call | solution.py:153
  59.5 1.6 %collective-permute-start.20 = (bf16[4,80,512]{2,1,0:T(8,128)(2,1)S(1)}, bf16[4,80,512]{2,1,0:T(8,128)(2,1)S(1)}, u32[]{:S(2)}, u32[]{:S(2)}) collective-permute-start(bf16[4,80,512]{2,1,0:T(8,128)(2,1)S(1)} %pile.7.z_ref), channel_id=1, source_target_pairs={{0,2},{1,3},{2,0},{3,1},{4,6},{5,7},{6,4},{7,5},{8,10},{9,11},{10,... | collective-permute-start | bytes 983048 | tf_op jit(solution)/shard_map/ppermute | solution.py:34
  61.1 6.4 %collective-permute-done.13.y_ref = bf16[3,40,1792]{2,1,0:T(8,128)(2,1)S(1)} collective-permute-done((bf16[3,40,1792]{2,1,0:T(8,128)(2,1)S(1)}, bf16[3,40,1792]{2,1,0:T(8,128)(2,1)S(1)}, u32[]{:S(2)}, u32[]{:S(2)}) %collective-permute-start.13) | collective-permute-done | bytes 430112 | tf_op jit(solution)/shard_map/ppermute | solution.py:34
  67.4 4.2 %rotate_in.3 = f32[192,40]{1,0:T(8,128)S(1)} custom-call(s32[1]{0:T(128)} %bitcast.me_ref, bf16[40,1792]{1,0:T(8,128)(2,1)S(1)} %get-tuple-element.8.own_ref, bf16[40,1792]{1,0:T(8,128)(2,1)S(1)} %get-tuple-element.6.across_ref, bf16[3,40,1792]{2,1,0:T(8,128)(2,1)S(1)} %pile.6.z_ref.refs_5_, bf16[3,40,1792]{2,1,0:T(8,128)(2,1)S(1)} %collective-permute-done.13.y_ref, ...), custom_call_target="tpu_custom_call" | custom-call | flops 220200960 | bytes 5505024 | tf_op jit(solution)/shard_map/rotate_in/pallas_call | solution.py:153
  73.5 1.8 %combine.1 = bf16[96,8192]{1,0:T(8,128)(2,1)} custom-call(s32[1]{0:T(128)} %bitcast.me_ref, bf16[96,40]{1,0:T(8,128)(2,1)S(1)} %get-tuple-element.12.own_ref, bf16[96,40]{1,0:T(8,128)(2,1)S(1)} %collective-permute-done.16.other_ref, bf16[4,80,512]{2,1,0:T(8,128)(2,1)S(1)} %pile.7.z_ref, bf16[4,80,512]{2,1,0:T(8,128)(2,1)S(1)} %collective-permute-done.20.y_ref, ...), custom_call_target="tpu_custom_call" | custom-call | flops 125829120 | bytes 3145728 | tf_op jit(solution)/shard_map/combine/pallas_call | solution.py:241
  (56 shorter events, 12.5 us)
Async XLA Ops:
  0.0 55.1 %collective-permute-start.14 = (bf16[96,28672]{1,0:T(8,128)(2,1)}, bf16[96,28672]{1,0:T(8,128)(2,1)}, u32[]{:S(2)}, u32[]{:S(2)}) collective-permute-start(bf16[96,28672]{1,0:T(8,128)(2,1)} %bitcast.20), channel_id=1, source_target_pairs={{0,1},{1,0},{2,3},{3,2},{4,5},{5,4},{6,7},{7,6},{8,9},{9,8},{10,11... | collective-permute-start | bytes 16515080 | tf_op jit(solution)/shard_map/ppermute | solution.py:34
  1.5 13.9 %collective-permute-start = (bf16[2,40,1792]{2,1,0:T(8,128)(2,1)S(1)}, bf16[2,40,1792]{2,1,0:T(8,128)(2,1)S(1)}, u32[]{:S(2)}, u32[]{:S(2)}) collective-permute-start(bf16[2,40,1792]{2,1,0:T(8,128)(2,1)S(1)} %get-tuple-element.9), channel_id=1, source_target_pairs={{0,2},{1,3},{2,0},{3,1},{4,6},{5,7},{6,4},{7,5},{8,10},{9,11},{10,... | collective-permute-start | bytes 860168 | tf_op jit(solution)/shard_map/ppermute | solution.py:34
  5.2 9.5 %collective-permute-start.4 = (bf16[40,1024]{1,0:T(8,128)(2,1)S(1)}, bf16[40,1024]{1,0:T(8,128)(2,1)S(1)}, u32[]{:S(2)}, u32[]{:S(2)}) collective-permute-start(bf16[40,1024]{1,0:T(8,128)(2,1)S(1)} %reshape.19.refs_0_), channel_id=1, source_target_pairs={{0,4},{1,5},{2,6},{3,7},{4,8},{5,9},{6,10},{7,11},{8,12},{9,13},{1... | collective-permute-start | bytes 245768 | tf_op jit(solution)/shard_map/ppermute | solution.py:34
  6.8 8.5 %collective-permute-start.5 = (bf16[40,1024]{1,0:T(8,128)(2,1)S(1)}, bf16[40,1024]{1,0:T(8,128)(2,1)S(1)}, u32[]{:S(2)}, u32[]{:S(2)}) collective-permute-start(bf16[40,1024]{1,0:T(8,128)(2,1)S(1)} %reshape.19.refs_0_), channel_id=1, source_target_pairs={{0,8},{1,9},{2,10},{3,11},{4,12},{5,13},{6,14},{7,15},{8,0},{9,1},... | collective-permute-start | bytes 245768 | tf_op jit(solution)/shard_map/ppermute | solution.py:34
  9.4 6.1 %collective-permute-start.6 = (bf16[40,1024]{1,0:T(8,128)(2,1)S(1)}, bf16[40,1024]{1,0:T(8,128)(2,1)S(1)}, u32[]{:S(2)}, u32[]{:S(2)}) collective-permute-start(bf16[40,1024]{1,0:T(8,128)(2,1)S(1)} %reshape.19.refs_0_), channel_id=1, source_target_pairs={{0,12},{1,13},{2,14},{3,15},{4,0},{5,1},{6,2},{7,3},{8,4},{9,5},{1... | collective-permute-start | bytes 245768 | tf_op jit(solution)/shard_map/ppermute | solution.py:34
  15.5 39.7 %slice-start = ((s8[5505024]{0:T(1024)(128)(4,1)}), s8[1310720]{0:T(1024)(128)(4,1)S(1)}, s32[]{:S(2)}) async-start(s8[5505024]{0:T(1024)(128)(4,1)} %bitcast.21), calls=%async_computation | async-start | bytes 2621440
  18.8 9.4 %collective-permute-start.7 = (bf16[4,40,1024]{2,1,0:T(8,128)(2,1)S(1)}, bf16[4,40,1024]{2,1,0:T(8,128)(2,1)S(1)}, u32[]{:S(2)}, u32[]{:S(2)}) collective-permute-start(bf16[4,40,1024]{2,1,0:T(8,128)(2,1)S(1)} %pile.4.z_ref), channel_id=1, source_target_pairs={{0,2},{1,3},{2,0},{3,1},{4,6},{5,7},{6,4},{7,5},{8,10},{9,11},{10,... | collective-permute-start | bytes 983048 | tf_op jit(solution)/shard_map/ppermute | solution.py:34
  19.3 8.6 %collective-permute-start.10 = (bf16[40,1792]{1,0:T(8,128)(2,1)S(1)}, bf16[40,1792]{1,0:T(8,128)(2,1)S(1)}, u32[]{:S(2)}, u32[]{:S(2)}) collective-permute-start(bf16[40,1792]{1,0:T(8,128)(2,1)S(1)} %get-tuple-element.7.own_ref), channel_id=1, source_target_pairs={{0,4},{1,5},{2,6},{3,7},{4,8},{5,9},{6,10},{7,11},{8,12},{9,13},{1... | collective-permute-start | bytes 430088 | tf_op jit(solution)/shard_map/ppermute | solution.py:34
  21.4 11.1 %collective-permute-start.11 = (bf16[40,1792]{1,0:T(8,128)(2,1)S(1)}, bf16[40,1792]{1,0:T(8,128)(2,1)S(1)}, u32[]{:S(2)}, u32[]{:S(2)}) collective-permute-start(bf16[40,1792]{1,0:T(8,128)(2,1)S(1)} %get-tuple-element.7.own_ref), channel_id=1, source_target_pairs={{0,8},{1,9},{2,10},{3,11},{4,12},{5,13},{6,14},{7,15},{8,0},{9,1},... | collective-permute-start | bytes 430088 | tf_op jit(solution)/shard_map/ppermute | solution.py:34
  23.0 9.5 %collective-permute-start.12 = (bf16[40,1792]{1,0:T(8,128)(2,1)S(1)}, bf16[40,1792]{1,0:T(8,128)(2,1)S(1)}, u32[]{:S(2)}, u32[]{:S(2)}) collective-permute-start(bf16[40,1792]{1,0:T(8,128)(2,1)S(1)} %get-tuple-element.7.own_ref), channel_id=1, source_target_pairs={{0,12},{1,13},{2,14},{3,15},{4,0},{5,1},{6,2},{7,3},{8,4},{9,5},{1... | collective-permute-start | bytes 430088 | tf_op jit(solution)/shard_map/ppermute | solution.py:34
  28.0 9.8 %collective-permute-start.8 = (bf16[4,40,1024]{2,1,0:T(8,128)(2,1)S(1)}, bf16[4,40,1024]{2,1,0:T(8,128)(2,1)S(1)}, u32[]{:S(2)}, u32[]{:S(2)}) collective-permute-start(bf16[4,40,1024]{2,1,0:T(8,128)(2,1)S(1)} %pile.4.z_ref), channel_id=1, source_target_pairs={{0,1},{1,0},{2,3},{3,2},{4,5},{5,4},{6,7},{7,6},{8,9},{9,8},{10,11... | collective-permute-start | bytes 983048 | tf_op jit(solution)/shard_map/ppermute | solution.py:34
  28.2 11.4 %collective-permute-start.9 = (bf16[4,40,1024]{2,1,0:T(8,128)(2,1)S(1)}, bf16[4,40,1024]{2,1,0:T(8,128)(2,1)S(1)}, u32[]{:S(2)}, u32[]{:S(2)}) collective-permute-start(bf16[4,40,1024]{2,1,0:T(8,128)(2,1)S(1)} %collective-permute-done.7.y_ref), channel_id=1, source_target_pairs={{0,1},{1,0},{2,3},{3,2},{4,5},{5,4},{6,7},{7,6},{8,9},{9,8},{10,11... | collective-permute-start | bytes 983048 | tf_op jit(solution)/shard_map/ppermute | solution.py:34
  32.6 21.9 %collective-permute-start.15 = (bf16[3,40,1792]{2,1,0:T(8,128)(2,1)S(1)}, bf16[3,40,1792]{2,1,0:T(8,128)(2,1)S(1)}, u32[]{:S(2)}, u32[]{:S(2)}) collective-permute-start(bf16[3,40,1792]{2,1,0:T(8,128)(2,1)S(1)} %pile.5.refs_0_.z_ref), channel_id=1, source_target_pairs={{0,2},{1,3},{2,0},{3,1},{4,6},{5,7},{6,4},{7,5},{8,10},{9,11},{10,... | collective-permute-start | bytes 1290248 | tf_op jit(solution)/shard_map/ppermute | solution.py:34
  34.2 15.0 %collective-permute-start.1 = (bf16[40,1792]{1,0:T(8,128)(2,1)S(1)}, bf16[40,1792]{1,0:T(8,128)(2,1)S(1)}, u32[]{:S(2)}, u32[]{:S(2)}) collective-permute-start(bf16[40,1792]{1,0:T(8,128)(2,1)S(1)} %get-tuple-element.8.own_ref), channel_id=1, source_target_pairs={{0,4},{1,5},{2,6},{3,7},{4,8},{5,9},{6,10},{7,11},{8,12},{9,13},{1... | collective-permute-start | bytes 430088 | tf_op jit(solution)/shard_map/ppermute | solution.py:34
  38.4 11.6 %collective-permute-start.2 = (bf16[40,1792]{1,0:T(8,128)(2,1)S(1)}, bf16[40,1792]{1,0:T(8,128)(2,1)}, u32[]{:S(2)}, u32[]{:S(2)}) collective-permute-start(bf16[40,1792]{1,0:T(8,128)(2,1)S(1)} %get-tuple-element.8.own_ref), channel_id=1, source_target_pairs={{0,8},{1,9},{2,10},{3,11},{4,12},{5,13},{6,14},{7,15},{8,0},{9,1},... | collective-permute-start | bytes 430088 | tf_op jit(solution)/shard_map/ppermute | solution.py:34
  40.3 11.5 %collective-permute-start.3 = (bf16[40,1792]{1,0:T(8,128)(2,1)S(1)}, bf16[40,1792]{1,0:T(8,128)(2,1)}, u32[]{:S(2)}, u32[]{:S(2)}) collective-permute-start(bf16[40,1792]{1,0:T(8,128)(2,1)S(1)} %get-tuple-element.8.own_ref), channel_id=1, source_target_pairs={{0,12},{1,13},{2,14},{3,15},{4,0},{5,1},{6,2},{7,3},{8,4},{9,5},{1... | collective-permute-start | bytes 430088 | tf_op jit(solution)/shard_map/ppermute | solution.py:34
  49.1 10.3 %collective-permute-start.17 = (bf16[80,512]{1,0:T(8,128)(2,1)S(1)}, bf16[80,512]{1,0:T(8,128)(2,1)S(1)}, u32[]{:S(2)}, u32[]{:S(2)}) collective-permute-start(bf16[80,512]{1,0:T(8,128)(2,1)S(1)} %rotate_out.1.refs_3_.refs_0_), channel_id=1, source_target_pairs={{0,4},{1,5},{2,6},{3,7},{4,8},{5,9},{6,10},{7,11},{8,12},{9,13},{1... | collective-permute-start | bytes 245768 | tf_op jit(solution)/shard_map/ppermute | solution.py:34
  50.0 9.4 %collective-permute-start.18 = (bf16[80,512]{1,0:T(8,128)(2,1)S(1)}, bf16[80,512]{1,0:T(8,128)(2,1)S(1)}, u32[]{:S(2)}, u32[]{:S(2)}) collective-permute-start(bf16[80,512]{1,0:T(8,128)(2,1)S(1)} %rotate_out.1.refs_3_.refs_0_), channel_id=1, source_target_pairs={{0,8},{1,9},{2,10},{3,11},{4,12},{5,13},{6,14},{7,15},{8,0},{9,1},... | collective-permute-start | bytes 245768 | tf_op jit(solution)/shard_map/ppermute | solution.py:34
  51.8 7.6 %collective-permute-start.19 = (bf16[80,512]{1,0:T(8,128)(2,1)S(1)}, bf16[80,512]{1,0:T(8,128)(2,1)S(1)}, u32[]{:S(2)}, u32[]{:S(2)}) collective-permute-start(bf16[80,512]{1,0:T(8,128)(2,1)S(1)} %rotate_out.1.refs_3_.refs_0_), channel_id=1, source_target_pairs={{0,12},{1,13},{2,14},{3,15},{4,0},{5,1},{6,2},{7,3},{8,4},{9,5},{1... | collective-permute-start | bytes 245768 | tf_op jit(solution)/shard_map/ppermute | solution.py:34
  54.5 12.9 %collective-permute-start.13 = (bf16[3,40,1792]{2,1,0:T(8,128)(2,1)S(1)}, bf16[3,40,1792]{2,1,0:T(8,128)(2,1)S(1)}, u32[]{:S(2)}, u32[]{:S(2)}) collective-permute-start(bf16[3,40,1792]{2,1,0:T(8,128)(2,1)S(1)} %pile.6.z_ref.refs_5_), channel_id=1, source_target_pairs={{0,2},{1,3},{2,0},{3,1},{4,6},{5,7},{6,4},{7,5},{8,10},{9,11},{10,... | collective-permute-start | bytes 1290248 | tf_op jit(solution)/shard_map/ppermute | solution.py:34
  59.5 12.4 %collective-permute-start.20 = (bf16[4,80,512]{2,1,0:T(8,128)(2,1)S(1)}, bf16[4,80,512]{2,1,0:T(8,128)(2,1)S(1)}, u32[]{:S(2)}, u32[]{:S(2)}) collective-permute-start(bf16[4,80,512]{2,1,0:T(8,128)(2,1)S(1)} %pile.7.z_ref), channel_id=1, source_target_pairs={{0,2},{1,3},{2,0},{3,1},{4,6},{5,7},{6,4},{7,5},{8,10},{9,11},{10,... | collective-permute-start | bytes 983048 | tf_op jit(solution)/shard_map/ppermute | solution.py:34
  61.1 12.5 %collective-permute-start.21 = (bf16[4,80,512]{2,1,0:T(8,128)(2,1)S(1)}, bf16[4,80,512]{2,1,0:T(8,128)(2,1)S(1)}, u32[]{:S(2)}, u32[]{:S(2)}) collective-permute-start(bf16[4,80,512]{2,1,0:T(8,128)(2,1)S(1)} %pile.7.z_ref), channel_id=1, source_target_pairs={{0,1},{1,0},{2,3},{3,2},{4,5},{5,4},{6,7},{7,6},{8,9},{9,8},{10,11... | collective-permute-start | bytes 983048 | tf_op jit(solution)/shard_map/ppermute | solution.py:34
  71.9 1.7 %collective-permute-start.22 = (bf16[4,80,512]{2,1,0:T(8,128)(2,1)S(1)}, bf16[4,80,512]{2,1,0:T(8,128)(2,1)S(1)}, u32[]{:S(2)}, u32[]{:S(2)}) collective-permute-start(bf16[4,80,512]{2,1,0:T(8,128)(2,1)S(1)} %collective-permute-done.20.y_ref), channel_id=1, source_target_pairs={{0,1},{1,0},{2,3},{3,2},{4,5},{5,4},{6,7},{7,6},{8,9},{9,8},{10,11... | collective-permute-start | bytes 983048 | tf_op jit(solution)/shard_map/ppermute | solution.py:34
  71.9 1.6 %collective-permute-start.16 = (bf16[96,40]{1,0:T(8,128)(2,1)S(1)}, bf16[96,40]{1,0:T(8,128)(2,1)S(1)}, u32[]{:S(2)}, u32[]{:S(2)}) collective-permute-start(bf16[96,40]{1,0:T(8,128)(2,1)S(1)} %get-tuple-element.11), channel_id=1, source_target_pairs={{0,1},{1,0},{2,3},{3,2},{4,5},{5,4},{6,7},{7,6},{8,9},{9,8},{10,11... | collective-permute-start | bytes 23048 | tf_op jit(solution)/shard_map/ppermute | solution.py:34
  (8 other events, 21.7 us)

commit v9 on v8

--- a/solution.py
+++ b/solution.py
@@ -46,6 +46,10 @@
     return pair * PAIR + chip, core
 
 
+def room(mib, blocks):
+    return mib * 2**20 if blocks <= SUBLANES else 24 * 2**20
+
+
 def repeat(times, body, carry=None, loop=False):
     if loop or times > SUBLANES:
         return lax.fori_loop(0, times, body, carry)
@@ -109,7 +113,7 @@
             pltpu.VMEM((width // 128, total * SUBLANES, 128), jnp.float32),
             pltpu.VMEM((total, columns), jnp.float32),
         ],
-        compiler_params=pltpu.CompilerParams(vmem_limit_bytes=24 * 2**20),
+        compiler_params=pltpu.CompilerParams(vmem_limit_bytes=room(10, steps)),
         cost_estimate=pl.CostEstimate(
             flops=2 * total * basis.shape[0] * columns, bytes_accessed=2 * basis.size, transcendentals=0
         ),
@@ -157,7 +161,7 @@
         in_specs=[SMEM] + [VMEM] * 4 + [basis] * 2 + [VMEM] * len(before),
         out_specs=VMEM,
         scratch_shapes=[pltpu.VMEM((width // 128, chips * height, 128), jnp.float32)],
-        compiler_params=pltpu.CompilerParams(vmem_limit_bytes=24 * 2**20),
+        compiler_params=pltpu.CompilerParams(vmem_limit_bytes=room(9, chips)),
         cost_estimate=pl.CostEstimate(
             flops=4 * chips * tokens * mine.shape[0] * SUBLANES * width,
             bytes_accessed=4 * mine.shape[0] * SUBLANES * width,
@@ -178,7 +182,7 @@
         out_shape=jax.ShapeDtypeStruct((len(blocks), *blocks[0].shape), blocks[0].dtype),
         in_specs=[VMEM] * len(blocks) + [ANY] * len(waits),
         out_specs=VMEM,
-        compiler_params=pltpu.CompilerParams(vmem_limit_bytes=24 * 2**20),
+        compiler_params=pltpu.CompilerParams(vmem_limit_bytes=room(3, len(blocks))),
         cost_estimate=pl.CostEstimate(flops=0, bytes_accessed=2 * len(blocks) * blocks[0].size, transcendentals=0),
         name="pile",
     )(*blocks, *waits)
@@ -195,26 +199,13 @@
     return pl.pallas_call(
         fetch_kernel,
         out_shape=jax.ShapeDtypeStruct(array.shape, array.dtype),
-        in_specs=[ANY] * (1 + len(waits)),
+        in_specs=[pl.BlockSpec(memory_space=pltpu.HBM)] + [ANY] * len(waits),
         out_specs=VMEM,
         scratch_shapes=[pltpu.SemaphoreType.DMA],
-        compiler_params=pltpu.CompilerParams(vmem_limit_bytes=16 * 2**20),
+        compiler_params=pltpu.CompilerParams(vmem_limit_bytes=2 * 2**20),
         cost_estimate=pl.CostEstimate(flops=0, bytes_accessed=2 * array.size, transcendentals=0),
         name="fetch",
     )(array, *waits)
-
-
-def after(arrays, waits):
-    return pl.pallas_call(
-        lambda *refs: None,
-        out_shape=[jax.ShapeDtypeStruct(array.shape, array.dtype) for array in arrays],
-        in_specs=[ANY] * (len(arrays) + len(waits)),
-        out_specs=[ANY] * len(arrays),
-        input_output_aliases={i: i for i in range(len(arrays))},
-        compiler_params=pltpu.CompilerParams(vmem_limit_bytes=2**20),
-        cost_estimate=pl.CostEstimate(flops=0, bytes_accessed=0, transcendentals=0),
-        name="after",
-    )(*arrays, *waits)
 
 
 def combine_kernel(me_ref, own_ref, other_ref, z_ref, y_ref, cz_ref, cy_ref, out_ref):
@@ -243,7 +234,7 @@
         out_shape=jax.ShapeDtypeStruct((own.shape[0], features), jnp.bfloat16),
         in_specs=[SMEM] + [VMEM] * 6,
         out_specs=VMEM,
-        compiler_params=pltpu.CompilerParams(vmem_limit_bytes=24 * 2**20),
+        compiler_params=pltpu.CompilerParams(vmem_limit_bytes=room(6, steps)),
         cost_estimate=pl.CostEstimate(
             flops=2 * own.shape[0] * total_tokens * features, bytes_accessed=4 * own.shape[0] * features, transcendentals=0
         ),

time: 75.8 us -> 75.8 us (level)
  no operation moved by 1% of the time
where the time goes in v9:
time: 75.8 us; the launch traced here: 75.3 us
  starting transfers between devices  28.5 us (38%)
  waiting for transfers between devices  16.9 us (22%)
  local copies, waits for them, and re-layouts  15.6 us (21%)
  Pallas kernels  14.1 us (19%)
    ppermute x23, starting transfers between devices, send(): return lax.ppermute(block, 'wide', pairs)  28.5 us
    ppermute x23, waiting for transfers between devices, send(): return lax.ppermute(block, 'wide', pairs)  16.9 us
    unnamed x18, local copies, waits for them, and re-layouts  13.4 us
    pallas_call x2, Pallas kernels, rotate_in(): pl.pallas_call(functools.partial(rotate_in_kernel, tokens, len(before)),...  8.43 us
    pallas_call x1, Pallas kernels, rotate_out(): pl.pallas_call(functools.partial(rotate_out_kernel, tokens, len(waits)),...  2.28 us
    pallas_call x1, Pallas kernels, combine(): pl.pallas_call(combine_kernel, out_shape=jax.ShapeDtypeStruct((own.shape[...  1.76 us
  transfers between devices with their start and end apart: 23, of which 8 were waited for; matrix products, arithmetic and copies ran while one was open for 3% of the time, Pallas kernels for 16%

profile of v9, /device:TPU:0, one launch (start us, length us, event | category | flops | bytes accessed | tf_op | source)
XLA Modules:
  0.0 75.3 jit_solution(10734845050624744516)
XLA Ops:
  0.5 1.1 %copy_bitcast_fusion.1 = (bf16[2,40,1792]{2,1,0:T(8,128)(2,1)S(1)}, bf16[2,5,8,1792]{3,2,1,0:T(8,128)(2,1)S(1)}) fusion(bf16[1,5,16,1792]{3,1,2,0:T(8,128)(2,1)} %bitcast.25), kind=kLoop, calls=%fused_computation.1 | loop fusion | bytes 860160 | tf_op jit(solution)/shard_map/reshape | solution.py:261
  1.5 2.6 %collective-permute-start = (bf16[2,40,1792]{2,1,0:T(8,128)(2,1)S(1)}, bf16[2,40,1792]{2,1,0:T(8,128)(2,1)S(1)}, u32[]{:S(2)}, u32[]{:S(2)}) collective-permute-start(bf16[2,40,1792]{2,1,0:T(8,128)(2,1)S(1)} %get-tuple-element.9), channel_id=1, source_target_pairs={{0,2},{1,3},{2,0},{3,1},{4,6},{5,7},{6,4},{7,5},{8,10},{9,11},{10,... | collective-permute-start | bytes 860168 | tf_op jit(solution)/shard_map/ppermute | solution.py:34
  5.2 1.6 %collective-permute-start.4 = (bf16[40,1024]{1,0:T(8,128)(2,1)S(1)}, bf16[40,1024]{1,0:T(8,128)(2,1)S(1)}, u32[]{:S(2)}, u32[]{:S(2)}) collective-permute-start(bf16[40,1024]{1,0:T(8,128)(2,1)S(1)} %reshape.19.refs_0_), channel_id=1, source_target_pairs={{0,4},{1,5},{2,6},{3,7},{4,8},{5,9},{6,10},{7,11},{8,12},{9,13},{1... | collective-permute-start | bytes 245768 | tf_op jit(solution)/shard_map/ppermute | solution.py:34
  6.8 2.6 %collective-permute-start.5 = (bf16[40,1024]{1,0:T(8,128)(2,1)S(1)}, bf16[40,1024]{1,0:T(8,128)(2,1)S(1)}, u32[]{:S(2)}, u32[]{:S(2)}) collective-permute-start(bf16[40,1024]{1,0:T(8,128)(2,1)S(1)} %reshape.19.refs_0_), channel_id=1, source_target_pairs={{0,8},{1,9},{2,10},{3,11},{4,12},{5,13},{6,14},{7,15},{8,0},{9,1},... | collective-permute-start | bytes 245768 | tf_op jit(solution)/shard_map/ppermute | solution.py:34
  9.4 1.3 %collective-permute-start.6 = (bf16[40,1024]{1,0:T(8,128)(2,1)S(1)}, bf16[40,1024]{1,0:T(8,128)(2,1)S(1)}, u32[]{:S(2)}, u32[]{:S(2)}) collective-permute-start(bf16[40,1024]{1,0:T(8,128)(2,1)S(1)} %reshape.19.refs_0_), channel_id=1, source_target_pairs={{0,12},{1,13},{2,14},{3,15},{4,0},{5,1},{6,2},{7,3},{8,4},{9,5},{1... | collective-permute-start | bytes 245768 | tf_op jit(solution)/shard_map/ppermute | solution.py:34
  10.7 3.4 %copy-done.2 = bf16[8192,512]{1,0:T(8,128)(2,1)S(1)} copy-done((bf16[8192,512]{1,0:T(8,128)(2,1)S(1)}, bf16[8192,512]{1,0:T(8,128)(2,1)}, u32[]{:S(2)}) %copy-start.2) | copy-done | bytes 8388632
  15.5 3.3 %copy-done = bf16[8192,512]{1,0:T(8,128)(2,1)} copy-done((bf16[8192,512]{1,0:T(8,128)(2,1)}, bf16[8192,512]{1,0:T(8,128)(2,1)S(1)}, u32[]{:S(2)}) %copy-start) | copy-done | bytes 8388632
  19.3 2.1 %collective-permute-start.10 = (bf16[40,1792]{1,0:T(8,128)(2,1)S(1)}, bf16[40,1792]{1,0:T(8,128)(2,1)S(1)}, u32[]{:S(2)}, u32[]{:S(2)}) collective-permute-start(bf16[40,1792]{1,0:T(8,128)(2,1)S(1)} %get-tuple-element.7.own_ref), channel_id=1, source_target_pairs={{0,4},{1,5},{2,6},{3,7},{4,8},{5,9},{6,10},{7,11},{8,12},{9,13},{1... | collective-permute-start | bytes 430088 | tf_op jit(solution)/shard_map/ppermute | solution.py:34
  21.4 1.6 %collective-permute-start.11 = (bf16[40,1792]{1,0:T(8,128)(2,1)S(1)}, bf16[40,1792]{1,0:T(8,128)(2,1)S(1)}, u32[]{:S(2)}, u32[]{:S(2)}) collective-permute-start(bf16[40,1792]{1,0:T(8,128)(2,1)S(1)} %get-tuple-element.7.own_ref), channel_id=1, source_target_pairs={{0,8},{1,9},{2,10},{3,11},{4,12},{5,13},{6,14},{7,15},{8,0},{9,1},... | collective-permute-start | bytes 430088 | tf_op jit(solution)/shard_map/ppermute | solution.py:34
  23.9 4.1 %collective-permute-done.10.refs_0_ = bf16[40,1792]{1,0:T(8,128)(2,1)S(1)} collective-permute-done((bf16[40,1792]{1,0:T(8,128)(2,1)S(1)}, bf16[40,1792]{1,0:T(8,128)(2,1)S(1)}, u32[]{:S(2)}, u32[]{:S(2)}) %collective-permute-start.10) | collective-permute-done | bytes 143392 | tf_op jit(solution)/shard_map/ppermute | solution.py:34
  28.5 4.1 %collective-permute-done.11.refs_1_ = bf16[40,1792]{1,0:T(8,128)(2,1)S(1)} collective-permute-done((bf16[40,1792]{1,0:T(8,128)(2,1)S(1)}, bf16[40,1792]{1,0:T(8,128)(2,1)S(1)}, u32[]{:S(2)}, u32[]{:S(2)}) %collective-permute-start.11) | collective-permute-done | bytes 143392 | tf_op jit(solution)/shard_map/ppermute | solution.py:34
  32.6 1.6 %collective-permute-start.15 = (bf16[3,40,1792]{2,1,0:T(8,128)(2,1)S(1)}, bf16[3,40,1792]{2,1,0:T(8,128)(2,1)S(1)}, u32[]{:S(2)}, u32[]{:S(2)}) collective-permute-start(bf16[3,40,1792]{2,1,0:T(8,128)(2,1)S(1)} %pile.5.refs_0_.z_ref), channel_id=1, source_target_pairs={{0,2},{1,3},{2,0},{3,1},{4,6},{5,7},{6,4},{7,5},{8,10},{9,11},{10,... | collective-permute-start | bytes 1290248 | tf_op jit(solution)/shard_map/ppermute | solution.py:34
  34.2 3.5 %collective-permute-start.1 = (bf16[40,1792]{1,0:T(8,128)(2,1)S(1)}, bf16[40,1792]{1,0:T(8,128)(2,1)S(1)}, u32[]{:S(2)}, u32[]{:S(2)}) collective-permute-start(bf16[40,1792]{1,0:T(8,128)(2,1)S(1)} %get-tuple-element.8.own_ref), channel_id=1, source_target_pairs={{0,4},{1,5},{2,6},{3,7},{4,8},{5,9},{6,10},{7,11},{8,12},{9,13},{1... | collective-permute-start | bytes 430088 | tf_op jit(solution)/shard_map/ppermute | solution.py:34
  38.4 1.1 %collective-permute-start.2 = (bf16[40,1792]{1,0:T(8,128)(2,1)S(1)}, bf16[40,1792]{1,0:T(8,128)(2,1)}, u32[]{:S(2)}, u32[]{:S(2)}) collective-permute-start(bf16[40,1792]{1,0:T(8,128)(2,1)S(1)} %get-tuple-element.8.own_ref), channel_id=1, source_target_pairs={{0,8},{1,9},{2,10},{3,11},{4,12},{5,13},{6,14},{7,15},{8,0},{9,1},... | collective-permute-start | bytes 430088 | tf_op jit(solution)/shard_map/ppermute | solution.py:34
  40.3 1.2 %collective-permute-start.3 = (bf16[40,1792]{1,0:T(8,128)(2,1)S(1)}, bf16[40,1792]{1,0:T(8,128)(2,1)}, u32[]{:S(2)}, u32[]{:S(2)}) collective-permute-start(bf16[40,1792]{1,0:T(8,128)(2,1)S(1)} %get-tuple-element.8.own_ref), channel_id=1, source_target_pairs={{0,12},{1,13},{2,14},{3,15},{4,0},{5,1},{6,2},{7,3},{8,4},{9,5},{1... | collective-permute-start | bytes 430088 | tf_op jit(solution)/shard_map/ppermute | solution.py:34
  41.5 3.4 %copy-done.1 = bf16[8192,512]{1,0:T(8,128)(2,1)S(1)} copy-done((bf16[8192,512]{1,0:T(8,128)(2,1)S(1)}, bf16[8192,512]{1,0:T(8,128)(2,1)}, u32[]{:S(2)}) %copy-start.1) | copy-done | bytes 8388632
  46.9 2.3 %rotate_out.1.refs_3_.refs_0_ = bf16[80,512]{1,0:T(8,128)(2,1)S(1)} custom-call(s32[1]{0:T(128)} %bitcast.me_ref, bf16[4,40,1024]{2,1,0:T(8,128)(2,1)S(1)} %pile.4.z_ref, bf16[4,40,1024]{2,1,0:T(8,128)(2,1)S(1)} %collective-permute-done.7.y_ref, bf16[4,40,1024]{2,1,0:T(8,128)(2,1)S(1)} %copy-done.4, bf16[4,40,1024]{2,1,0:T(8,128)(2,1)S(1)} %copy-done.6, ...), custom_call_target="tpu_custom_call" | custom-call | flops 671088640 | bytes 8388608 | tf_op jit(solution)/shard_map/rotate_out/pallas_call | solution.py:106
  50.0 1.8 %collective-permute-start.18 = (bf16[80,512]{1,0:T(8,128)(2,1)S(1)}, bf16[80,512]{1,0:T(8,128)(2,1)S(1)}, u32[]{:S(2)}, u32[]{:S(2)}) collective-permute-start(bf16[80,512]{1,0:T(8,128)(2,1)S(1)} %rotate_out.1.refs_3_.refs_0_), channel_id=1, source_target_pairs={{0,8},{1,9},{2,10},{3,11},{4,12},{5,13},{6,14},{7,15},{8,0},{9,1},... | collective-permute-start | bytes 245768 | tf_op jit(solution)/shard_map/ppermute | solution.py:34
  51.8 1.7 %collective-permute-start.19 = (bf16[80,512]{1,0:T(8,128)(2,1)S(1)}, bf16[80,512]{1,0:T(8,128)(2,1)S(1)}, u32[]{:S(2)}, u32[]{:S(2)}) collective-permute-start(bf16[80,512]{1,0:T(8,128)(2,1)S(1)} %rotate_out.1.refs_3_.refs_0_), channel_id=1, source_target_pairs={{0,12},{1,13},{2,14},{3,15},{4,0},{5,1},{6,2},{7,3},{8,4},{9,5},{1... | collective-permute-start | bytes 245768 | tf_op jit(solution)/shard_map/ppermute | solution.py:34
  55.2 4.2 %rotate_in.2.refs_0_.refs_4_ = f32[192,40]{1,0:T(8,128)S(1)} custom-call(s32[1]{0:T(128)} %bitcast.me_ref, bf16[40,1792]{1,0:T(8,128)(2,1)S(1)} %get-tuple-element.7.own_ref, bf16[40,1792]{1,0:T(8,128)(2,1)S(1)} %get-tuple-element.5.across_ref, bf16[3,40,1792]{2,1,0:T(8,128)(2,1)S(1)} %pile.5.refs_0_.z_ref, ...), custom_call_target="tpu_custom_call" | custom-call | flops 220200960 | bytes 5505024 | tf_op jit(solution)/shard_map/rotate_in/pallas_call | solution.py:157
  59.5 1.6 %collective-permute-start.20 = (bf16[4,80,512]{2,1,0:T(8,128)(2,1)S(1)}, bf16[4,80,512]{2,1,0:T(8,128)(2,1)S(1)}, u32[]{:S(2)}, u32[]{:S(2)}) collective-permute-start(bf16[4,80,512]{2,1,0:T(8,128)(2,1)S(1)} %pile.7.z_ref), channel_id=1, source_target_pairs={{0,2},{1,3},{2,0},{3,1},{4,6},{5,7},{6,4},{7,5},{8,10},{9,11},{10,... | collective-permute-start | bytes 983048 | tf_op jit(solution)/shard_map/ppermute | solution.py:34
  61.1 6.4 %collective-permute-done.13.y_ref = bf16[3,40,1792]{2,1,0:T(8,128)(2,1)S(1)} collective-permute-done((bf16[3,40,1792]{2,1,0:T(8,128)(2,1)S(1)}, bf16[3,40,1792]{2,1,0:T(8,128)(2,1)S(1)}, u32[]{:S(2)}, u32[]{:S(2)}) %collective-permute-start.13) | collective-permute-done | bytes 430112 | tf_op jit(solution)/shard_map/ppermute | solution.py:34
  67.4 4.2 %rotate_in.3 = f32[192,40]{1,0:T(8,128)S(1)} custom-call(s32[1]{0:T(128)} %bitcast.me_ref, bf16[40,1792]{1,0:T(8,128)(2,1)S(1)} %get-tuple-element.8.own_ref, bf16[40,1792]{1,0:T(8,128)(2,1)S(1)} %get-tuple-element.6.across_ref, bf16[3,40,1792]{2,1,0:T(8,128)(2,1)S(1)} %pile.6.z_ref.refs_5_, bf16[3,40,1792]{2,1,0:T(8,128)(2,1)S(1)} %collective-permute-done.13.y_ref, ...), custom_call_target="tpu_custom_call" | custom-call | flops 220200960 | bytes 5505024 | tf_op jit(solution)/shard_map/rotate_in/pallas_call | solution.py:157
  73.5 1.8 %combine.1 = bf16[96,8192]{1,0:T(8,128)(2,1)} custom-call(s32[1]{0:T(128)} %bitcast.me_ref, bf16[96,40]{1,0:T(8,128)(2,1)S(1)} %get-tuple-element.12.own_ref, bf16[96,40]{1,0:T(8,128)(2,1)S(1)} %collective-permute-done.16.other_ref, bf16[4,80,512]{2,1,0:T(8,128)(2,1)S(1)} %pile.7.z_ref, bf16[4,80,512]{2,1,0:T(8,128)(2,1)S(1)} %collective-permute-done.20.y_ref, ...), custom_call_target="tpu_custom_call" | custom-call | flops 125829120 | bytes 3145728 | tf_op jit(solution)/shard_map/combine/pallas_call | solution.py:232
  (56 shorter events, 12.5 us)
Async XLA Ops:
  0.0 55.1 %collective-permute-start.14 = (bf16[96,28672]{1,0:T(8,128)(2,1)}, bf16[96,28672]{1,0:T(8,128)(2,1)}, u32[]{:S(2)}, u32[]{:S(2)}) collective-permute-start(bf16[96,28672]{1,0:T(8,128)(2,1)} %bitcast.20), channel_id=1, source_target_pairs={{0,1},{1,0},{2,3},{3,2},{4,5},{5,4},{6,7},{7,6},{8,9},{9,8},{10,11... | collective-permute-start | bytes 16515080 | tf_op jit(solution)/shard_map/ppermute | solution.py:34
  1.5 13.9 %collective-permute-start = (bf16[2,40,1792]{2,1,0:T(8,128)(2,1)S(1)}, bf16[2,40,1792]{2,1,0:T(8,128)(2,1)S(1)}, u32[]{:S(2)}, u32[]{:S(2)}) collective-permute-start(bf16[2,40,1792]{2,1,0:T(8,128)(2,1)S(1)} %get-tuple-element.9), channel_id=1, source_target_pairs={{0,2},{1,3},{2,0},{3,1},{4,6},{5,7},{6,4},{7,5},{8,10},{9,11},{10,... | collective-permute-start | bytes 860168 | tf_op jit(solution)/shard_map/ppermute | solution.py:34
  5.2 9.5 %collective-permute-start.4 = (bf16[40,1024]{1,0:T(8,128)(2,1)S(1)}, bf16[40,1024]{1,0:T(8,128)(2,1)S(1)}, u32[]{:S(2)}, u32[]{:S(2)}) collective-permute-start(bf16[40,1024]{1,0:T(8,128)(2,1)S(1)} %reshape.19.refs_0_), channel_id=1, source_target_pairs={{0,4},{1,5},{2,6},{3,7},{4,8},{5,9},{6,10},{7,11},{8,12},{9,13},{1... | collective-permute-start | bytes 245768 | tf_op jit(solution)/shard_map/ppermute | solution.py:34
  6.8 8.5 %collective-permute-start.5 = (bf16[40,1024]{1,0:T(8,128)(2,1)S(1)}, bf16[40,1024]{1,0:T(8,128)(2,1)S(1)}, u32[]{:S(2)}, u32[]{:S(2)}) collective-permute-start(bf16[40,1024]{1,0:T(8,128)(2,1)S(1)} %reshape.19.refs_0_), channel_id=1, source_target_pairs={{0,8},{1,9},{2,10},{3,11},{4,12},{5,13},{6,14},{7,15},{8,0},{9,1},... | collective-permute-start | bytes 245768 | tf_op jit(solution)/shard_map/ppermute | solution.py:34
  9.4 6.1 %collective-permute-start.6 = (bf16[40,1024]{1,0:T(8,128)(2,1)S(1)}, bf16[40,1024]{1,0:T(8,128)(2,1)S(1)}, u32[]{:S(2)}, u32[]{:S(2)}) collective-permute-start(bf16[40,1024]{1,0:T(8,128)(2,1)S(1)} %reshape.19.refs_0_), channel_id=1, source_target_pairs={{0,12},{1,13},{2,14},{3,15},{4,0},{5,1},{6,2},{7,3},{8,4},{9,5},{1... | collective-permute-start | bytes 245768 | tf_op jit(solution)/shard_map/ppermute | solution.py:34
  15.5 39.7 %slice-start = ((s8[5505024]{0:T(1024)(128)(4,1)}), s8[1310720]{0:T(1024)(128)(4,1)S(1)}, s32[]{:S(2)}) async-start(s8[5505024]{0:T(1024)(128)(4,1)} %bitcast.21), calls=%async_computation | async-start | bytes 2621440
  18.8 9.4 %collective-permute-start.7 = (bf16[4,40,1024]{2,1,0:T(8,128)(2,1)S(1)}, bf16[4,40,1024]{2,1,0:T(8,128)(2,1)S(1)}, u32[]{:S(2)}, u32[]{:S(2)}) collective-permute-start(bf16[4,40,1024]{2,1,0:T(8,128)(2,1)S(1)} %pile.4.z_ref), channel_id=1, source_target_pairs={{0,2},{1,3},{2,0},{3,1},{4,6},{5,7},{6,4},{7,5},{8,10},{9,11},{10,... | collective-permute-start | bytes 983048 | tf_op jit(solution)/shard_map/ppermute | solution.py:34
  19.3 8.6 %collective-permute-start.10 = (bf16[40,1792]{1,0:T(8,128)(2,1)S(1)}, bf16[40,1792]{1,0:T(8,128)(2,1)S(1)}, u32[]{:S(2)}, u32[]{:S(2)}) collective-permute-start(bf16[40,1792]{1,0:T(8,128)(2,1)S(1)} %get-tuple-element.7.own_ref), channel_id=1, source_target_pairs={{0,4},{1,5},{2,6},{3,7},{4,8},{5,9},{6,10},{7,11},{8,12},{9,13},{1... | collective-permute-start | bytes 430088 | tf_op jit(solution)/shard_map/ppermute | solution.py:34
  21.4 11.1 %collective-permute-start.11 = (bf16[40,1792]{1,0:T(8,128)(2,1)S(1)}, bf16[40,1792]{1,0:T(8,128)(2,1)S(1)}, u32[]{:S(2)}, u32[]{:S(2)}) collective-permute-start(bf16[40,1792]{1,0:T(8,128)(2,1)S(1)} %get-tuple-element.7.own_ref), channel_id=1, source_target_pairs={{0,8},{1,9},{2,10},{3,11},{4,12},{5,13},{6,14},{7,15},{8,0},{9,1},... | collective-permute-start | bytes 430088 | tf_op jit(solution)/shard_map/ppermute | solution.py:34
  23.0 9.5 %collective-permute-start.12 = (bf16[40,1792]{1,0:T(8,128)(2,1)S(1)}, bf16[40,1792]{1,0:T(8,128)(2,1)S(1)}, u32[]{:S(2)}, u32[]{:S(2)}) collective-permute-start(bf16[40,1792]{1,0:T(8,128)(2,1)S(1)} %get-tuple-element.7.own_ref), channel_id=1, source_target_pairs={{0,12},{1,13},{2,14},{3,15},{4,0},{5,1},{6,2},{7,3},{8,4},{9,5},{1... | collective-permute-start | bytes 430088 | tf_op jit(solution)/shard_map/ppermute | solution.py:34
  28.0 9.8 %collective-permute-start.8 = (bf16[4,40,1024]{2,1,0:T(8,128)(2,1)S(1)}, bf16[4,40,1024]{2,1,0:T(8,128)(2,1)S(1)}, u32[]{:S(2)}, u32[]{:S(2)}) collective-permute-start(bf16[4,40,1024]{2,1,0:T(8,128)(2,1)S(1)} %pile.4.z_ref), channel_id=1, source_target_pairs={{0,1},{1,0},{2,3},{3,2},{4,5},{5,4},{6,7},{7,6},{8,9},{9,8},{10,11... | collective-permute-start | bytes 983048 | tf_op jit(solution)/shard_map/ppermute | solution.py:34
  28.2 11.4 %collective-permute-start.9 = (bf16[4,40,1024]{2,1,0:T(8,128)(2,1)S(1)}, bf16[4,40,1024]{2,1,0:T(8,128)(2,1)S(1)}, u32[]{:S(2)}, u32[]{:S(2)}) collective-permute-start(bf16[4,40,1024]{2,1,0:T(8,128)(2,1)S(1)} %collective-permute-done.7.y_ref), channel_id=1, source_target_pairs={{0,1},{1,0},{2,3},{3,2},{4,5},{5,4},{6,7},{7,6},{8,9},{9,8},{10,11... | collective-permute-start | bytes 983048 | tf_op jit(solution)/shard_map/ppermute | solution.py:34
  32.6 21.9 %collective-permute-start.15 = (bf16[3,40,1792]{2,1,0:T(8,128)(2,1)S(1)}, bf16[3,40,1792]{2,1,0:T(8,128)(2,1)S(1)}, u32[]{:S(2)}, u32[]{:S(2)}) collective-permute-start(bf16[3,40,1792]{2,1,0:T(8,128)(2,1)S(1)} %pile.5.refs_0_.z_ref), channel_id=1, source_target_pairs={{0,2},{1,3},{2,0},{3,1},{4,6},{5,7},{6,4},{7,5},{8,10},{9,11},{10,... | collective-permute-start | bytes 1290248 | tf_op jit(solution)/shard_map/ppermute | solution.py:34
  34.2 15.0 %collective-permute-start.1 = (bf16[40,1792]{1,0:T(8,128)(2,1)S(1)}, bf16[40,1792]{1,0:T(8,128)(2,1)S(1)}, u32[]{:S(2)}, u32[]{:S(2)}) collective-permute-start(bf16[40,1792]{1,0:T(8,128)(2,1)S(1)} %get-tuple-element.8.own_ref), channel_id=1, source_target_pairs={{0,4},{1,5},{2,6},{3,7},{4,8},{5,9},{6,10},{7,11},{8,12},{9,13},{1... | collective-permute-start | bytes 430088 | tf_op jit(solution)/shard_map/ppermute | solution.py:34
  38.4 11.6 %collective-permute-start.2 = (bf16[40,1792]{1,0:T(8,128)(2,1)S(1)}, bf16[40,1792]{1,0:T(8,128)(2,1)}, u32[]{:S(2)}, u32[]{:S(2)}) collective-permute-start(bf16[40,1792]{1,0:T(8,128)(2,1)S(1)} %get-tuple-element.8.own_ref), channel_id=1, source_target_pairs={{0,8},{1,9},{2,10},{3,11},{4,12},{5,13},{6,14},{7,15},{8,0},{9,1},... | collective-permute-start | bytes 430088 | tf_op jit(solution)/shard_map/ppermute | solution.py:34
  40.3 11.5 %collective-permute-start.3 = (bf16[40,1792]{1,0:T(8,128)(2,1)S(1)}, bf16[40,1792]{1,0:T(8,128)(2,1)}, u32[]{:S(2)}, u32[]{:S(2)}) collective-permute-start(bf16[40,1792]{1,0:T(8,128)(2,1)S(1)} %get-tuple-element.8.own_ref), channel_id=1, source_target_pairs={{0,12},{1,13},{2,14},{3,15},{4,0},{5,1},{6,2},{7,3},{8,4},{9,5},{1... | collective-permute-start | bytes 430088 | tf_op jit(solution)/shard_map/ppermute | solution.py:34
  49.1 10.3 %collective-permute-start.17 = (bf16[80,512]{1,0:T(8,128)(2,1)S(1)}, bf16[80,512]{1,0:T(8,128)(2,1)S(1)}, u32[]{:S(2)}, u32[]{:S(2)}) collective-permute-start(bf16[80,512]{1,0:T(8,128)(2,1)S(1)} %rotate_out.1.refs_3_.refs_0_), channel_id=1, source_target_pairs={{0,4},{1,5},{2,6},{3,7},{4,8},{5,9},{6,10},{7,11},{8,12},{9,13},{1... | collective-permute-start | bytes 245768 | tf_op jit(solution)/shard_map/ppermute | solution.py:34
  50.0 9.4 %collective-permute-start.18 = (bf16[80,512]{1,0:T(8,128)(2,1)S(1)}, bf16[80,512]{1,0:T(8,128)(2,1)S(1)}, u32[]{:S(2)}, u32[]{:S(2)}) collective-permute-start(bf16[80,512]{1,0:T(8,128)(2,1)S(1)} %rotate_out.1.refs_3_.refs_0_), channel_id=1, source_target_pairs={{0,8},{1,9},{2,10},{3,11},{4,12},{5,13},{6,14},{7,15},{8,0},{9,1},... | collective-permute-start | bytes 245768 | tf_op jit(solution)/shard_map/ppermute | solution.py:34
  51.8 7.6 %collective-permute-start.19 = (bf16[80,512]{1,0:T(8,128)(2,1)S(1)}, bf16[80,512]{1,0:T(8,128)(2,1)S(1)}, u32[]{:S(2)}, u32[]{:S(2)}) collective-permute-start(bf16[80,512]{1,0:T(8,128)(2,1)S(1)} %rotate_out.1.refs_3_.refs_0_), channel_id=1, source_target_pairs={{0,12},{1,13},{2,14},{3,15},{4,0},{5,1},{6,2},{7,3},{8,4},{9,5},{1... | collective-permute-start | bytes 245768 | tf_op jit(solution)/shard_map/ppermute | solution.py:34
  54.5 12.9 %collective-permute-start.13 = (bf16[3,40,1792]{2,1,0:T(8,128)(2,1)S(1)}, bf16[3,40,1792]{2,1,0:T(8,128)(2,1)S(1)}, u32[]{:S(2)}, u32[]{:S(2)}) collective-permute-start(bf16[3,40,1792]{2,1,0:T(8,128)(2,1)S(1)} %pile.6.z_ref.refs_5_), channel_id=1, source_target_pairs={{0,2},{1,3},{2,0},{3,1},{4,6},{5,7},{6,4},{7,5},{8,10},{9,11},{10,... | collective-permute-start | bytes 1290248 | tf_op jit(solution)/shard_map/ppermute | solution.py:34
  59.5 12.4 %collective-permute-start.20 = (bf16[4,80,512]{2,1,0:T(8,128)(2,1)S(1)}, bf16[4,80,512]{2,1,0:T(8,128)(2,1)S(1)}, u32[]{:S(2)}, u32[]{:S(2)}) collective-permute-start(bf16[4,80,512]{2,1,0:T(8,128)(2,1)S(1)} %pile.7.z_ref), channel_id=1, source_target_pairs={{0,2},{1,3},{2,0},{3,1},{4,6},{5,7},{6,4},{7,5},{8,10},{9,11},{10,... | collective-permute-start | bytes 983048 | tf_op jit(solution)/shard_map/ppermute | solution.py:34
  61.1 12.5 %collective-permute-start.21 = (bf16[4,80,512]{2,1,0:T(8,128)(2,1)S(1)}, bf16[4,80,512]{2,1,0:T(8,128)(2,1)S(1)}, u32[]{:S(2)}, u32[]{:S(2)}) collective-permute-start(bf16[4,80,512]{2,1,0:T(8,128)(2,1)S(1)} %pile.7.z_ref), channel_id=1, source_target_pairs={{0,1},{1,0},{2,3},{3,2},{4,5},{5,4},{6,7},{7,6},{8,9},{9,8},{10,11... | collective-permute-start | bytes 983048 | tf_op jit(solution)/shard_map/ppermute | solution.py:34
  71.9 1.7 %collective-permute-start.22 = (bf16[4,80,512]{2,1,0:T(8,128)(2,1)S(1)}, bf16[4,80,512]{2,1,0:T(8,128)(2,1)S(1)}, u32[]{:S(2)}, u32[]{:S(2)}) collective-permute-start(bf16[4,80,512]{2,1,0:T(8,128)(2,1)S(1)} %collective-permute-done.20.y_ref), channel_id=1, source_target_pairs={{0,1},{1,0},{2,3},{3,2},{4,5},{5,4},{6,7},{7,6},{8,9},{9,8},{10,11... | collective-permute-start | bytes 983048 | tf_op jit(solution)/shard_map/ppermute | solution.py:34
  71.9 1.6 %collective-permute-start.16 = (bf16[96,40]{1,0:T(8,128)(2,1)S(1)}, bf16[96,40]{1,0:T(8,128)(2,1)S(1)}, u32[]{:S(2)}, u32[]{:S(2)}) collective-permute-start(bf16[96,40]{1,0:T(8,128)(2,1)S(1)} %get-tuple-element.11), channel_id=1, source_target_pairs={{0,1},{1,0},{2,3},{3,2},{4,5},{5,4},{6,7},{7,6},{8,9},{9,8},{10,11... | collective-permute-start | bytes 23048 | tf_op jit(solution)/shard_map/ppermute | solution.py:34
  (8 other events, 21.7 us)

commit v10 on v6

v10 whole, which is shorter than its diff:
```python
import functools

import jax
import jax.numpy as jnp
from jax import lax
from jax.experimental import pallas as pl
from jax.experimental.pallas import tpu as pltpu
from jax.sharding import PartitionSpec as P

CORES = 2
PAIR = 2
SUBLANES = 8
FOLDS = 2
CHUNKS = 2
VMEM = pl.BlockSpec(memory_space=pltpu.VMEM)
ANY = pl.BlockSpec(memory_space=pl.ANY)


def along(devices, by):
    each = CORES * PAIR
    return [(d, (d + by * each) % devices) for d in range(devices)]


def across(devices):
    return [(d, d ^ CORES) for d in range(devices)]


def swap(devices):
    return [(d, d ^ 1) for d in range(devices)]


def send(block, pairs):
    return lax.ppermute(block, "wide", pairs)


def origin(me, devices, step, other_chip, other_core):
    each = CORES * PAIR
    pair = lax.rem(me // each + devices // each - step, devices // each)
    chip = lax.rem(me // CORES, PAIR)
    core = lax.rem(me, CORES)
    if other_chip:
        chip = 1 - chip
    if other_core:
        core = 1 - core
    return pair * PAIR + chip, core


def room(mib, blocks):
    return mib * 2**20 if blocks <= SUBLANES else 24 * 2**20


def repeat(times, body, carry=None, loop=False):
    if loop or times > SUBLANES:
        return lax.fori_loop(0, times, body, carry)
    for step in range(times):
        carry = body(step, carry)
    return carry


def unfold_store(rows, slot, block):
    height = block.shape[0]
    at = pl.ds(pl.multiple_of(slot * height, SUBLANES), height)
    for tile in range(rows.shape[0]):
        rows[tile, at, :] = block[:, tile * 128 : (tile + 1) * 128].astype(jnp.float32)


def unfold_load(rows, fold, tokens):
    tiles = [rows[tile, pl.ds(fold, tokens, stride=SUBLANES), :] for tile in range(rows.shape[0])]
    return jnp.concatenate([tile.astype(jnp.bfloat16) for tile in tiles], 1)


def rotate_out_kernel(tokens, waits, z_ref, y_ref, cz_ref, cy_ref, basis_ref, *refs):
    sq_ref, rows, total = refs[waits:]
    steps, height, width = z_ref.shape
    devices = steps * CORES * PAIR
    me = lax.axis_index("wide")

    @pl.when(pl.program_id(0) == 0)
    def _():
        for ref, chip_bit, core_bit in ((z_ref, 0, 0), (y_ref, 1, 0), (cz_ref, 0, 1), (cy_ref, 1, 1)):

            def put(step, _, ref=ref, chip_bit=chip_bit, core_bit=core_bit):
                chip, core = origin(me, devices, step, chip_bit, core_bit)
                unfold_store(rows, core * (devices // CORES) + chip, ref[step])

            repeat(steps, put)
        total[...] = jnp.zeros_like(total)

    def add(fold, _):
        left = unfold_load(rows, pl.program_id(0) * FOLDS + fold, devices * tokens)
        right = basis_ref[pl.ds(pl.multiple_of(fold * width, 128), width), :]
        total[...] += jnp.dot(left, right, preferred_element_type=jnp.float32)

    repeat(FOLDS, add, None, steps > SUBLANES)

    @pl.when(pl.program_id(0) == pl.num_programs(0) - 1)
    def _():
        sq_ref[...] = (total[...] * total[...]).astype(sq_ref.dtype)


def rotate_out(tokens, z, y, cz, cy, basis, waits):
    steps, height, width = z.shape
    total = steps * CORES * PAIR * tokens
    columns = basis.shape[1]
    return pl.pallas_call(
        functools.partial(rotate_out_kernel, tokens, len(waits)),
        grid=(SUBLANES // FOLDS,),
        out_shape=jax.ShapeDtypeStruct((total, columns), jnp.bfloat16),
        in_specs=[VMEM] * 4 + [pl.BlockSpec((FOLDS * width, columns), lambda i: (i, 0))] + [ANY] * len(waits),
        out_specs=VMEM,
        scratch_shapes=[
            pltpu.VMEM((width // 128, total * SUBLANES, 128), jnp.float32),
            pltpu.VMEM((total, columns), jnp.float32),
        ],
        compiler_params=pltpu.CompilerParams(vmem_limit_bytes=room(10, steps)),
        cost_estimate=pl.CostEstimate(
            flops=2 * total * basis.shape[0] * columns, bytes_accessed=2 * basis.size, transcendentals=0
        ),
        name="rotate_out",
    )(z, y, cz, cy, basis, *waits)


def rotate_in_kernel(tokens, chunk, before, last, own_ref, across_ref, z_ref, y_ref, mine_ref, theirs_ref, *refs):
    outs, (total, rows) = refs[before:-2], refs[-2:]
    height, width = own_ref.shape
    steps = z_ref.shape[0] + 1
    devices = steps * CORES * PAIR
    chips = devices // CORES
    me = lax.axis_index("wide")

    def put(chip, block):
        unfold_store(rows, chip, block)

    @pl.when(pl.program_id(0) == 0)
    def _():
        put(origin(me, devices, 0, 0, 0)[0], own_ref[...])
        put(origin(me, devices, 0, 1, 0)[0], across_ref[chunk])
        for ref, chip_bit in ((z_ref, 0), (y_ref, 1)):

            def put_far(step, _, ref=ref, chip_bit=chip_bit):
                put(origin(me, devices, step + 1, chip_bit, 0)[0], ref[step])

            repeat(steps - 1, put_far)
        total[...] = refs[0][...] if before else jnp.zeros_like(total)

    def add(fold, _):
        at = pl.ds(pl.multiple_of(fold * width, 128), width)
        right = unfold_load(rows, pl.program_id(0) * FOLDS + fold, chips * tokens)
        left = jnp.concatenate([mine_ref[:, at], theirs_ref[:, at]])
        total[...] += lax.dot_general(left, right, (((1,), (1,)), ((), ())), preferred_element_type=jnp.float32)

    repeat(FOLDS, add, None, steps > SUBLANES)

    @pl.when(pl.program_id(0) == pl.num_programs(0) - 1)
    def _():
        if last:
            squares = (total[...] * total[...]).astype(jnp.bfloat16)
            outs[0][...] = squares[: outs[0].shape[0]]
            outs[1][...] = squares[outs[0].shape[0] :]
        else:
            outs[0][...] = total[...]


def rotate_in(tokens, chunk, own, across, z, y, mine, theirs, before):
    height, width = own.shape
    chips = (z.shape[0] + 1) * PAIR
    last = chunk == CHUNKS - 1
    basis = pl.BlockSpec((mine.shape[0], FOLDS * width), lambda i: (0, chunk * (SUBLANES // FOLDS) + i))
    whole = jax.ShapeDtypeStruct((2 * mine.shape[0], chips * tokens), jnp.float32)
    half = jax.ShapeDtypeStruct((mine.shape[0], chips * tokens), jnp.bfloat16)
    return pl.pallas_call(
        functools.partial(rotate_in_kernel, tokens, chunk, len(before), last),
        grid=(SUBLANES // FOLDS,),
        out_shape=(half, half) if last else (whole,),
        in_specs=[VMEM] * 4 + [basis] * 2 + [VMEM] * len(before),
        out_specs=(VMEM, VMEM) if last else (VMEM,),
        scratch_shapes=[
            pltpu.VMEM(whole.shape, jnp.float32),
            pltpu.VMEM((width // 128, chips * height, 128), jnp.float32),
        ],
        compiler_params=pltpu.CompilerParams(vmem_limit_bytes=room(9, chips)),
        cost_estimate=pl.CostEstimate(
            flops=4 * chips * tokens * mine.shape[0] * SUBLANES * width,
            bytes_accessed=4 * mine.shape[0] * SUBLANES * width,
            transcendentals=0,
        ),
        name="rotate_in",
    )(own, across, z, y, mine, theirs, *before)


def fold_kernel(waits, from_ref, *refs):
    outs, rows = refs[waits:-1], refs[-1]
    tokens = from_ref.shape[0]
    chunks = max(1, len(outs) - 1)
    tiles = from_ref.shape[1] // (chunks * SUBLANES * 128)
    for chunk in range(chunks):
        for tile in range(tiles):
            for fold in range(SUBLANES):
                at = ((chunk * SUBLANES + fold) * tiles + tile) * 128
                rows[tile, pl.ds(fold, tokens, stride=SUBLANES), :] = from_ref[:, at : at + 128].astype(jnp.float32)
        for tile in range(tiles):
            block = rows[tile].astype(jnp.bfloat16)
            outs[chunk][:, tile * 128 : (tile + 1) * 128] = block
            if chunks > 1:
                outs[-1][chunk, :, tile * 128 : (tile + 1) * 128] = block


def folded(array, chunks, waits):
    shape = (array.shape[0] * SUBLANES, array.shape[1] // (chunks * SUBLANES))
    outs = [jax.ShapeDtypeStruct(shape, array.dtype)] * chunks
    if chunks > 1:
        outs.append(jax.ShapeDtypeStruct((chunks, *shape), array.dtype))
    return pl.pallas_call(
        functools.partial(fold_kernel, len(waits)),
        out_shape=outs,
        in_specs=[VMEM] + [ANY] * len(waits),
        out_specs=[VMEM] * len(outs),
        scratch_shapes=[pltpu.VMEM((shape[1] // 128, shape[0], 128), jnp.float32)],
        compiler_params=pltpu.CompilerParams(vmem_limit_bytes=4 * 2**20),
        cost_estimate=pl.CostEstimate(flops=0, bytes_accessed=4 * array.size, transcendentals=0),
        name="fold",
    )(array, *waits)


def pile_kernel(blocks, *refs):
    for step in range(blocks):
        refs[-1][step] = refs[step][...]


def pile(blocks, waits):
    return pl.pallas_call(
        functools.partial(pile_kernel, len(blocks)),
        out_shape=jax.ShapeDtypeStruct((len(blocks), *blocks[0].shape), blocks[0].dtype),
        in_specs=[VMEM] * len(blocks) + [ANY] * len(waits),
        out_specs=VMEM,
        compiler_params=pltpu.CompilerParams(vmem_limit_bytes=room(3, len(blocks))),
        cost_estimate=pl.CostEstimate(flops=0, bytes_accessed=2 * len(blocks) * blocks[0].size, transcendentals=0),
        name="pile",
    )(*blocks, *waits)


def after(arrays, waits):
    return pl.pallas_call(
        lambda *refs: None,
        out_shape=[jax.ShapeDtypeStruct(array.shape, array.dtype) for array in arrays],
        in_specs=[ANY] * (len(arrays) + len(waits)),
        out_specs=[ANY] * len(arrays),
        input_output_aliases={i: i for i in range(len(arrays))},
        compiler_params=pltpu.CompilerParams(vmem_limit_bytes=2**20),
        cost_estimate=pl.CostEstimate(flops=0, bytes_accessed=0, transcendentals=0),
        name="after",
    )(*arrays, *waits)


def combine_kernel(own_ref, other_ref, z_ref, y_ref, cz_ref, cy_ref, out_ref):
    steps, total_tokens, width = z_ref.shape
    devices = steps * CORES * PAIR
    me = lax.axis_index("wide")
    own, other = own_ref[...].astype(jnp.float32), other_ref[...].astype(jnp.float32)
    first = lax.rem(me, CORES) == 0
    left = jnp.concatenate([jnp.where(first, own, other), jnp.where(first, other, own)], 1).astype(jnp.bfloat16)
    for ref, chip_bit, core_bit in ((z_ref, 0, 0), (y_ref, 1, 0), (cz_ref, 0, 1), (cy_ref, 1, 1)):

        def put(step, _, ref=ref, chip_bit=chip_bit, core_bit=core_bit):
            chip, core = origin(me, devices, step, chip_bit, core_bit)
            at = pl.multiple_of((chip * CORES + core) * width, 128)
            total = jnp.dot(left, ref[step], preferred_element_type=jnp.float32)
            out_ref[:, pl.ds(at, width)] = (total / total_tokens).astype(out_ref.dtype)

        repeat(steps, put)


def combine(own, other, z, y, cz, cy):
    steps, total_tokens, width = z.shape
    features = steps * CORES * PAIR * width
    return pl.pallas_call(
        combine_kernel,
        out_shape=jax.ShapeDtypeStruct((own.shape[0], features), jnp.bfloat16),
        in_specs=[VMEM] * 6,
        out_specs=VMEM,
        compiler_params=pltpu.CompilerParams(vmem_limit_bytes=room(6, steps)),
        cost_estimate=pl.CostEstimate(
            flops=2 * own.shape[0] * total_tokens * features, bytes_accessed=4 * own.shape[0] * features, transcendentals=0
        ),
        name="combine",
    )(own, other, z, y, cz, cy)


def local(acts, grads, basis_in, basis_out):
    devices = lax.axis_size("wide")
    steps = devices // (CORES * PAIR)
    tokens = acts.shape[0]

    def along_all(block):
        return [send(block, along(devices, step)) for step in range(1, steps)]

    def others(z):
        y = send(z, across(devices))
        return z, y, send(z, swap(devices)), send(y, swap(devices))

    [block] = folded(grads, 1, [])
    mine = basis_in.T
    theirs = send(mine, swap(devices))
    *own, every = folded(acts, CHUNKS, [block])
    own_across = send(every, across(devices))
    grads_all = others(pile([block] + along_all(block), [own_across]))

    acts_z, acts_y = [], []

    def chunk_along(chunk, waits):
        acts_z.append(pile(along_all(own[chunk]), waits))
        acts_y.append(send(acts_z[-1], across(devices)))

    def part(chunk, before):
        return rotate_in(tokens, chunk, own[chunk], own_across, acts_z[chunk], acts_y[chunk], mine, theirs, before)

    chunk_along(0, [])
    sq_out = rotate_out(tokens, *grads_all, basis_out, [acts_z[0]])
    came = along_all(sq_out)
    for chunk in range(1, CHUNKS):
        chunk_along(chunk, [sq_out])
    total = part(0, [])
    z = pile([sq_out] + came, [*total, acts_z[-1]])
    y = send(z, across(devices))
    for chunk in range(1, CHUNKS):
        total = part(chunk, total)
    sq_in, given = total
    [y] = after([y], [sq_in])
    return combine(sq_in, send(given, swap(devices)), z, y, send(z, swap(devices)), send(y, swap(devices)))


def solution(mesh):
    return jax.shard_map(
        local,
        mesh=mesh,
        in_specs=(
            P(("groups", "wide"), None),
            P(("groups", "wide"), None),
            P("groups", "wide"),
            P("groups", "wide"),
        ),
        out_specs=P(("groups", "wide"), None),
        check_vma=False,
    )
```

time: 70.7 us -> 68.8 us (0.973)
  Pallas kernels: 16.2 us -> 10.1 us
  local copies, waits for them, and re-layouts: 2.17 us -> 5.31 us
  starting transfers between devices: 26.8 us -> 29.9 us
  waiting for transfers between devices: 25.2 us -> 23.3 us
    unnamed x0 -> x10, local copies, waits for them, and re-layouts: none -> 5.31 us
    pallas_call x2 -> x5, Pallas kernels: 9.11 us -> 5.9 us  [the longest x2 5.62 us: rotate_in(): pl.pallas_call(functools.partial(rotate_in_kernel, tokens, chunk, len(bef...]
    ppermute x23, starting transfers between devices: 26.8 us -> 29.9 us  [send(): return lax.ppermute(block, 'wide', pairs)]
    pallas_call x1, Pallas kernels: 5.18 us -> 2.29 us  [rotate_out(): pl.pallas_call(functools.partial(rotate_out_kernel, tokens, len(waits)),...]
    reshape x2 -> x0, local copies, waits for them, and re-layouts: 2.12 us -> none  [the longest x1 1.08 us: local(): acts.reshape(tokens, CHUNKS, SUBLANES, width).transpose(1, 0, 2, 3)]
    ppermute x23, waiting for transfers between devices: 25.2 us -> 23.3 us  [send(): return lax.ppermute(block, 'wide', pairs)]
  transfers between devices with their start and end apart: 23 -> 23, of which waited for: 8 -> 11; matrix products, arithmetic and copies ran while one was open for 3% -> 0% of each run, Pallas kernels for 20% -> 12%
where the time goes in v10:
time: 68.8 us; the launch traced here: 68.6 us
  starting transfers between devices  29.9 us (43%)
  waiting for transfers between devices  23.3 us (34%)
  Pallas kernels  10.1 us (15%)
  local copies, waits for them, and re-layouts  5.31 us (8%)
    ppermute x23, starting transfers between devices, send(): return lax.ppermute(block, 'wide', pairs)  29.9 us
    ppermute x23, waiting for transfers between devices, send(): return lax.ppermute(block, 'wide', pairs)  23.3 us
    pallas_call x2, Pallas kernels, rotate_in(): pl.pallas_call(functools.partial(rotate_in_kernel, tokens, chunk, len(bef...  5.62 us
    unnamed x10, local copies, waits for them, and re-layouts  5.31 us
    pallas_call x1, Pallas kernels, rotate_out(): pl.pallas_call(functools.partial(rotate_out_kernel, tokens, len(waits)),...  2.29 us
    pallas_call x1, Pallas kernels, combine(): pl.pallas_call(combine_kernel, out_shape=jax.ShapeDtypeStruct((own.shape[...  1.76 us
  transfers between devices with their start and end apart: 23, of which 11 were waited for; matrix products, arithmetic and copies ran while one was open for 0% of the time, Pallas kernels for 12%

profile of v10, /device:TPU:0, one launch (start us, length us, event | category | flops | bytes accessed | tf_op | source)
XLA Modules:
  0.0 68.6 jit_solution(12019512617046728397)
XLA Ops:
  2.7 2.6 %collective-permute-start = (bf16[2,40,1792]{2,1,0:T(8,128)(2,1)S(1)}, bf16[2,40,1792]{2,1,0:T(8,128)(2,1)S(1)}, u32[]{:S(2)}, u32[]{:S(2)}) collective-permute-start(bf16[2,40,1792]{2,1,0:T(8,128)(2,1)S(1)} %get-tuple-element.11), channel_id=1, source_target_pairs={{0,2},{1,3},{2,0},{3,1},{4,6},{5,7},{6,4},{7,5},{8,10},{9,11},{10,... | collective-permute-start | bytes 860168 | tf_op jit(solution)/shard_map/ppermute | solution.py:33
  5.3 1.6 %collective-permute-start.4 = (bf16[40,1024]{1,0:T(8,128)(2,1)S(1)}, bf16[40,1024]{1,0:T(8,128)(2,1)S(1)}, u32[]{:S(2)}, u32[]{:S(2)}) collective-permute-start(bf16[40,1024]{1,0:T(8,128)(2,1)S(1)} %fold.2.refs_0_), channel_id=1, source_target_pairs={{0,4},{1,5},{2,6},{3,7},{4,8},{5,9},{6,10},{7,11},{8,12},{9,13},{1... | collective-permute-start | bytes 245768 | tf_op jit(solution)/shard_map/ppermute | solution.py:33
  6.8 2.6 %collective-permute-start.5 = (bf16[40,1024]{1,0:T(8,128)(2,1)S(1)}, bf16[40,1024]{1,0:T(8,128)(2,1)S(1)}, u32[]{:S(2)}, u32[]{:S(2)}) collective-permute-start(bf16[40,1024]{1,0:T(8,128)(2,1)S(1)} %fold.2.refs_0_), channel_id=1, source_target_pairs={{0,8},{1,9},{2,10},{3,11},{4,12},{5,13},{6,14},{7,15},{8,0},{9,1},... | collective-permute-start | bytes 245768 | tf_op jit(solution)/shard_map/ppermute | solution.py:33
  9.4 1.3 %collective-permute-start.6 = (bf16[40,1024]{1,0:T(8,128)(2,1)S(1)}, bf16[40,1024]{1,0:T(8,128)(2,1)S(1)}, u32[]{:S(2)}, u32[]{:S(2)}) collective-permute-start(bf16[40,1024]{1,0:T(8,128)(2,1)S(1)} %fold.2.refs_0_), channel_id=1, source_target_pairs={{0,12},{1,13},{2,14},{3,15},{4,0},{5,1},{6,2},{7,3},{8,4},{9,5},{1... | collective-permute-start | bytes 245768 | tf_op jit(solution)/shard_map/ppermute | solution.py:33
  10.8 1.5 %collective-permute-done.4.refs_1_ = bf16[40,1024]{1,0:T(8,128)(2,1)S(1)} collective-permute-done((bf16[40,1024]{1,0:T(8,128)(2,1)S(1)}, bf16[40,1024]{1,0:T(8,128)(2,1)S(1)}, u32[]{:S(2)}, u32[]{:S(2)}) %collective-permute-start.4) | collective-permute-done | bytes 81952 | tf_op jit(solution)/shard_map/ppermute | solution.py:33
  12.2 3.1 %collective-permute-done.5.refs_2_ = bf16[40,1024]{1,0:T(8,128)(2,1)S(1)} collective-permute-done((bf16[40,1024]{1,0:T(8,128)(2,1)S(1)}, bf16[40,1024]{1,0:T(8,128)(2,1)S(1)}, u32[]{:S(2)}, u32[]{:S(2)}) %collective-permute-start.5) | collective-permute-done | bytes 81952 | tf_op jit(solution)/shard_map/ppermute | solution.py:33
  16.1 2.1 %collective-permute-start.10 = (bf16[40,1792]{1,0:T(8,128)(2,1)S(1)}, bf16[40,1792]{1,0:T(8,128)(2,1)S(1)}, u32[]{:S(2)}, u32[]{:S(2)}) collective-permute-start(bf16[40,1792]{1,0:T(8,128)(2,1)S(1)} %get-tuple-element.12.own_ref), channel_id=1, source_target_pairs={{0,4},{1,5},{2,6},{3,7},{4,8},{5,9},{6,10},{7,11},{8,12},{9,13},{1... | collective-permute-start | bytes 430088 | tf_op jit(solution)/shard_map/ppermute | solution.py:33
  18.2 1.6 %collective-permute-start.11 = (bf16[40,1792]{1,0:T(8,128)(2,1)S(1)}, bf16[40,1792]{1,0:T(8,128)(2,1)S(1)}, u32[]{:S(2)}, u32[]{:S(2)}) collective-permute-start(bf16[40,1792]{1,0:T(8,128)(2,1)S(1)} %get-tuple-element.12.own_ref), channel_id=1, source_target_pairs={{0,8},{1,9},{2,10},{3,11},{4,12},{5,13},{6,14},{7,15},{8,0},{9,1},... | collective-permute-start | bytes 430088 | tf_op jit(solution)/shard_map/ppermute | solution.py:33
  20.5 4.2 %collective-permute-done.10.refs_0_ = bf16[40,1792]{1,0:T(8,128)(2,1)S(1)} collective-permute-done((bf16[40,1792]{1,0:T(8,128)(2,1)S(1)}, bf16[40,1792]{1,0:T(8,128)(2,1)S(1)}, u32[]{:S(2)}, u32[]{:S(2)}) %collective-permute-start.10) | collective-permute-done | bytes 143392 | tf_op jit(solution)/shard_map/ppermute | solution.py:33
  25.2 4.1 %collective-permute-done.11.refs_1_ = bf16[40,1792]{1,0:T(8,128)(2,1)S(1)} collective-permute-done((bf16[40,1792]{1,0:T(8,128)(2,1)S(1)}, bf16[40,1792]{1,0:T(8,128)(2,1)S(1)}, u32[]{:S(2)}, u32[]{:S(2)}) %collective-permute-start.11) | collective-permute-done | bytes 143392 | tf_op jit(solution)/shard_map/ppermute | solution.py:33
  29.3 1.6 %collective-permute-start.15 = (bf16[3,40,1792]{2,1,0:T(8,128)(2,1)S(1)}, bf16[3,40,1792]{2,1,0:T(8,128)(2,1)S(1)}, u32[]{:S(2)}, u32[]{:S(2)}) collective-permute-start(bf16[3,40,1792]{2,1,0:T(8,128)(2,1)S(1)} %pile.5.refs_0_.z_ref), channel_id=1, source_target_pairs={{0,2},{1,3},{2,0},{3,1},{4,6},{5,7},{6,4},{7,5},{8,10},{9,11},{10,... | collective-permute-start | bytes 1290248 | tf_op jit(solution)/shard_map/ppermute | solution.py:33
  30.9 3.5 %collective-permute-start.1 = (bf16[40,1792]{1,0:T(8,128)(2,1)S(1)}, bf16[40,1792]{1,0:T(8,128)(2,1)S(1)}, u32[]{:S(2)}, u32[]{:S(2)}) collective-permute-start(bf16[40,1792]{1,0:T(8,128)(2,1)S(1)} %get-tuple-element.10.own_ref), channel_id=1, source_target_pairs={{0,4},{1,5},{2,6},{3,7},{4,8},{5,9},{6,10},{7,11},{8,12},{9,13},{1... | collective-permute-start | bytes 430088 | tf_op jit(solution)/shard_map/ppermute | solution.py:33
  35.6 1.3 %collective-permute-start.3 = (bf16[40,1792]{1,0:T(8,128)(2,1)S(1)}, bf16[40,1792]{1,0:T(8,128)(2,1)S(1)}, u32[]{:S(2)}, u32[]{:S(2)}) collective-permute-start(bf16[40,1792]{1,0:T(8,128)(2,1)S(1)} %get-tuple-element.10.own_ref), channel_id=1, source_target_pairs={{0,12},{1,13},{2,14},{3,15},{4,0},{5,1},{6,2},{7,3},{8,4},{9,5},{1... | collective-permute-start | bytes 430088 | tf_op jit(solution)/shard_map/ppermute | solution.py:33
  36.9 3.4 %copy-done = bf16[8192,512]{1,0:T(8,128)(2,1)S(1)} copy-done((bf16[8192,512]{1,0:T(8,128)(2,1)S(1)}, bf16[8192,512]{1,0:T(8,128)(2,1)}, u32[]{:S(2)}) %copy-start) | copy-done | bytes 8388632
  40.3 2.3 %rotate_out.1.refs_3_.refs_0_ = bf16[80,512]{1,0:T(8,128)(2,1)S(1)} custom-call(bf16[4,40,1024]{2,1,0:T(8,128)(2,1)S(1)} %pile.4.z_ref, bf16[4,40,1024]{2,1,0:T(8,128)(2,1)S(1)} %collective-permute-done.7.y_ref, bf16[4,40,1024]{2,1,0:T(8,128)(2,1)S(1)} %collective-permute-done.8.cz_ref, bf16[4,40,1024]{2,1,0:T(8,128)(2,1)S(1)} %collective-permute-done.9.cy_ref, ...), custom_call_target="tpu_custom_call" | custom-call | flops 671088640 | bytes 8388608 | tf_op jit(solution)/shard_map/rotate_out/pallas_call | solution.py:105
  42.6 1.8 %collective-permute-done.2.refs_1_ = bf16[40,1792]{1,0:T(8,128)(2,1)S(1)} collective-permute-done((bf16[40,1792]{1,0:T(8,128)(2,1)S(1)}, bf16[40,1792]{1,0:T(8,128)(2,1)S(1)}, u32[]{:S(2)}, u32[]{:S(2)}) %collective-permute-start.2) | collective-permute-done | bytes 143392 | tf_op jit(solution)/shard_map/ppermute | solution.py:33
  45.0 3.5 %collective-permute-start.17 = (bf16[80,512]{1,0:T(8,128)(2,1)S(1)}, bf16[80,512]{1,0:T(8,128)(2,1)S(1)}, u32[]{:S(2)}, u32[]{:S(2)}) collective-permute-start(bf16[80,512]{1,0:T(8,128)(2,1)S(1)} %rotate_out.1.refs_3_.refs_0_), channel_id=1, source_target_pairs={{0,4},{1,5},{2,6},{3,7},{4,8},{5,9},{6,10},{7,11},{8,12},{9,13},{1... | collective-permute-start | bytes 245768 | tf_op jit(solution)/shard_map/ppermute | solution.py:33
  48.5 2.4 %collective-permute-start.18 = (bf16[80,512]{1,0:T(8,128)(2,1)S(1)}, bf16[80,512]{1,0:T(8,128)(2,1)S(1)}, u32[]{:S(2)}, u32[]{:S(2)}) collective-permute-start(bf16[80,512]{1,0:T(8,128)(2,1)S(1)} %rotate_out.1.refs_3_.refs_0_), channel_id=1, source_target_pairs={{0,8},{1,9},{2,10},{3,11},{4,12},{5,13},{6,14},{7,15},{8,0},{9,1},... | collective-permute-start | bytes 245768 | tf_op jit(solution)/shard_map/ppermute | solution.py:33
  50.9 2.8 %rotate_in.2.refs_0_.refs_4_ = f32[192,40]{1,0:T(8,128)S(1)} custom-call(bf16[40,1792]{1,0:T(8,128)(2,1)S(1)} %get-tuple-element.12.own_ref, bf16[2,40,1792]{2,1,0:T(8,128)(2,1)S(1)} %collective-permute-done.refs_4_.across_ref, bf16[3,40,1792]{2,1,0:T(8,128)(2,1)S(1)} %pile.5.refs_0_.z_ref, bf16[3,40,1792]{2,1,0:T(8,128)(2,1)S(1)} %collective-permute-done.15.y_ref, ...), custom_call_target="tpu_custom_call" | custom-call | flops 220200960 | bytes 5505024 | tf_op jit(solution)/shard_map/rotate_in/pallas_call | solution.py:171
  53.7 2.0 %collective-permute-done.18.refs_2_ = bf16[80,512]{1,0:T(8,128)(2,1)S(1)} collective-permute-done((bf16[80,512]{1,0:T(8,128)(2,1)S(1)}, bf16[80,512]{1,0:T(8,128)(2,1)S(1)}, u32[]{:S(2)}, u32[]{:S(2)}) %collective-permute-start.18) | collective-permute-done | bytes 81952 | tf_op jit(solution)/shard_map/ppermute | solution.py:33
  56.2 1.6 %collective-permute-start.20 = (bf16[4,80,512]{2,1,0:T(8,128)(2,1)S(1)}, bf16[4,80,512]{2,1,0:T(8,128)(2,1)S(1)}, u32[]{:S(2)}, u32[]{:S(2)}) collective-permute-start(bf16[4,80,512]{2,1,0:T(8,128)(2,1)S(1)} %pile.7.z_ref), channel_id=1, source_target_pairs={{0,2},{1,3},{2,0},{3,1},{4,6},{5,7},{6,4},{7,5},{8,10},{9,11},{10,... | collective-permute-start | bytes 983048 | tf_op jit(solution)/shard_map/ppermute | solution.py:33
  57.8 2.8 %rotate_in.3 = (bf16[96,40]{1,0:T(8,128)(2,1)S(1)}, bf16[96,40]{1,0:T(8,128)(2,1)S(1)}) custom-call(bf16[40,1792]{1,0:T(8,128)(2,1)S(1)} %get-tuple-element.10.own_ref, bf16[2,40,1792]{2,1,0:T(8,128)(2,1)S(1)} %collective-permute-done.refs_4_.across_ref, bf16[3,40,1792]{2,1,0:T(8,128)(2,1)S(1)} %pile.6.z_ref.refs_5_, ...), custom_call_target="tpu_custom_call" | custom-call | flops 220200960 | bytes 5505024 | tf_op jit(solution)/shard_map/rotate_in/pallas_call | solution.py:171
  60.6 4.6 %collective-permute-done.20.refs_0_ = bf16[4,80,512]{2,1,0:T(8,128)(2,1)S(1)} collective-permute-done((bf16[4,80,512]{2,1,0:T(8,128)(2,1)S(1)}, bf16[4,80,512]{2,1,0:T(8,128)(2,1)S(1)}, u32[]{:S(2)}, u32[]{:S(2)}) %collective-permute-start.20) | collective-permute-done | bytes 327712 | tf_op jit(solution)/shard_map/ppermute | solution.py:33
  66.9 1.8 %combine.1 = bf16[96,8192]{1,0:T(8,128)(2,1)} custom-call(bf16[96,40]{1,0:T(8,128)(2,1)S(1)} %get-tuple-element.13.refs_1_.own_ref, bf16[96,40]{1,0:T(8,128)(2,1)S(1)} %collective-permute-done.16.other_ref, bf16[4,80,512]{2,1,0:T(8,128)(2,1)S(1)} %pile.7.z_ref, bf16[4,80,512]{2,1,0:T(8,128)(2,1)S(1)} %after.1.y_ref, ...), custom_call_target="tpu_custom_call" | custom-call | flops 125829120 | bytes 3145728 | tf_op jit(solution)/shard_map/combine/pallas_call | solution.py:276
  (44 shorter events, 8.7 us)
Async XLA Ops:
  0.0 50.9 %collective-permute-start.14 = (bf16[96,28672]{1,0:T(8,128)(2,1)}, bf16[96,28672]{1,0:T(8,128)(2,1)S(1)}, u32[]{:S(2)}, u32[]{:S(2)}) collective-permute-start(bf16[96,28672]{1,0:T(8,128)(2,1)} %bitcast.1), channel_id=1, source_target_pairs={{0,1},{1,0},{2,3},{3,2},{4,5},{5,4},{6,7},{7,6},{8,9},{9,8},{10,11... | collective-permute-start | bytes 16515080 | tf_op jit(solution)/shard_map/ppermute | solution.py:33
  2.7 12.9 %collective-permute-start = (bf16[2,40,1792]{2,1,0:T(8,128)(2,1)S(1)}, bf16[2,40,1792]{2,1,0:T(8,128)(2,1)S(1)}, u32[]{:S(2)}, u32[]{:S(2)}) collective-permute-start(bf16[2,40,1792]{2,1,0:T(8,128)(2,1)S(1)} %get-tuple-element.11), channel_id=1, source_target_pairs={{0,2},{1,3},{2,0},{3,1},{4,6},{5,7},{6,4},{7,5},{8,10},{9,11},{10,... | collective-permute-start | bytes 860168 | tf_op jit(solution)/shard_map/ppermute | solution.py:33
  5.3 7.0 %collective-permute-start.4 = (bf16[40,1024]{1,0:T(8,128)(2,1)S(1)}, bf16[40,1024]{1,0:T(8,128)(2,1)S(1)}, u32[]{:S(2)}, u32[]{:S(2)}) collective-permute-start(bf16[40,1024]{1,0:T(8,128)(2,1)S(1)} %fold.2.refs_0_), channel_id=1, source_target_pairs={{0,4},{1,5},{2,6},{3,7},{4,8},{5,9},{6,10},{7,11},{8,12},{9,13},{1... | collective-permute-start | bytes 245768 | tf_op jit(solution)/shard_map/ppermute | solution.py:33
  6.8 8.5 %collective-permute-start.5 = (bf16[40,1024]{1,0:T(8,128)(2,1)S(1)}, bf16[40,1024]{1,0:T(8,128)(2,1)S(1)}, u32[]{:S(2)}, u32[]{:S(2)}) collective-permute-start(bf16[40,1024]{1,0:T(8,128)(2,1)S(1)} %fold.2.refs_0_), channel_id=1, source_target_pairs={{0,8},{1,9},{2,10},{3,11},{4,12},{5,13},{6,14},{7,15},{8,0},{9,1},... | collective-permute-start | bytes 245768 | tf_op jit(solution)/shard_map/ppermute | solution.py:33
  9.4 6.1 %collective-permute-start.6 = (bf16[40,1024]{1,0:T(8,128)(2,1)S(1)}, bf16[40,1024]{1,0:T(8,128)(2,1)S(1)}, u32[]{:S(2)}, u32[]{:S(2)}) collective-permute-start(bf16[40,1024]{1,0:T(8,128)(2,1)S(1)} %fold.2.refs_0_), channel_id=1, source_target_pairs={{0,12},{1,13},{2,14},{3,15},{4,0},{5,1},{6,2},{7,3},{8,4},{9,5},{1... | collective-permute-start | bytes 245768 | tf_op jit(solution)/shard_map/ppermute | solution.py:33
  15.6 9.4 %collective-permute-start.7 = (bf16[4,40,1024]{2,1,0:T(8,128)(2,1)S(1)}, bf16[4,40,1024]{2,1,0:T(8,128)(2,1)S(1)}, u32[]{:S(2)}, u32[]{:S(2)}) collective-permute-start(bf16[4,40,1024]{2,1,0:T(8,128)(2,1)S(1)} %pile.4.z_ref), channel_id=1, source_target_pairs={{0,2},{1,3},{2,0},{3,1},{4,6},{5,7},{6,4},{7,5},{8,10},{9,11},{10,... | collective-permute-start | bytes 983048 | tf_op jit(solution)/shard_map/ppermute | solution.py:33
  16.1 8.6 %collective-permute-start.10 = (bf16[40,1792]{1,0:T(8,128)(2,1)S(1)}, bf16[40,1792]{1,0:T(8,128)(2,1)S(1)}, u32[]{:S(2)}, u32[]{:S(2)}) collective-permute-start(bf16[40,1792]{1,0:T(8,128)(2,1)S(1)} %get-tuple-element.12.own_ref), channel_id=1, source_target_pairs={{0,4},{1,5},{2,6},{3,7},{4,8},{5,9},{6,10},{7,11},{8,12},{9,13},{1... | collective-permute-start | bytes 430088 | tf_op jit(solution)/shard_map/ppermute | solution.py:33
  18.2 11.1 %collective-permute-start.11 = (bf16[40,1792]{1,0:T(8,128)(2,1)S(1)}, bf16[40,1792]{1,0:T(8,128)(2,1)S(1)}, u32[]{:S(2)}, u32[]{:S(2)}) collective-permute-start(bf16[40,1792]{1,0:T(8,128)(2,1)S(1)} %get-tuple-element.12.own_ref), channel_id=1, source_target_pairs={{0,8},{1,9},{2,10},{3,11},{4,12},{5,13},{6,14},{7,15},{8,0},{9,1},... | collective-permute-start | bytes 430088 | tf_op jit(solution)/shard_map/ppermute | solution.py:33
  19.8 9.5 %collective-permute-start.12 = (bf16[40,1792]{1,0:T(8,128)(2,1)S(1)}, bf16[40,1792]{1,0:T(8,128)(2,1)S(1)}, u32[]{:S(2)}, u32[]{:S(2)}) collective-permute-start(bf16[40,1792]{1,0:T(8,128)(2,1)S(1)} %get-tuple-element.12.own_ref), channel_id=1, source_target_pairs={{0,12},{1,13},{2,14},{3,15},{4,0},{5,1},{6,2},{7,3},{8,4},{9,5},{1... | collective-permute-start | bytes 430088 | tf_op jit(solution)/shard_map/ppermute | solution.py:33
  24.7 9.8 %collective-permute-start.8 = (bf16[4,40,1024]{2,1,0:T(8,128)(2,1)S(1)}, bf16[4,40,1024]{2,1,0:T(8,128)(2,1)S(1)}, u32[]{:S(2)}, u32[]{:S(2)}) collective-permute-start(bf16[4,40,1024]{2,1,0:T(8,128)(2,1)S(1)} %pile.4.z_ref), channel_id=1, source_target_pairs={{0,1},{1,0},{2,3},{3,2},{4,5},{5,4},{6,7},{7,6},{8,9},{9,8},{10,11... | collective-permute-start | bytes 983048 | tf_op jit(solution)/shard_map/ppermute | solution.py:33
  25.0 10.6 %collective-permute-start.9 = (bf16[4,40,1024]{2,1,0:T(8,128)(2,1)S(1)}, bf16[4,40,1024]{2,1,0:T(8,128)(2,1)S(1)}, u32[]{:S(2)}, u32[]{:S(2)}) collective-permute-start(bf16[4,40,1024]{2,1,0:T(8,128)(2,1)S(1)} %collective-permute-done.7.y_ref), channel_id=1, source_target_pairs={{0,1},{1,0},{2,3},{3,2},{4,5},{5,4},{6,7},{7,6},{8,9},{9,8},{10,11... | collective-permute-start | bytes 983048 | tf_op jit(solution)/shard_map/ppermute | solution.py:33
  29.3 21.5 %collective-permute-start.15 = (bf16[3,40,1792]{2,1,0:T(8,128)(2,1)S(1)}, bf16[3,40,1792]{2,1,0:T(8,128)(2,1)S(1)}, u32[]{:S(2)}, u32[]{:S(2)}) collective-permute-start(bf16[3,40,1792]{2,1,0:T(8,128)(2,1)S(1)} %pile.5.refs_0_.z_ref), channel_id=1, source_target_pairs={{0,2},{1,3},{2,0},{3,1},{4,6},{5,7},{6,4},{7,5},{8,10},{9,11},{10,... | collective-permute-start | bytes 1290248 | tf_op jit(solution)/shard_map/ppermute | solution.py:33
  30.9 20.0 %slice-start.1 = ((s8[5505024]{0:T(1024)(128)(4,1)}), s8[1310720]{0:T(1024)(128)(4,1)S(1)}, s32[]{:S(2)}) async-start(s8[5505024]{0:T(1024)(128)(4,1)} %bitcast.2), calls=%async_computation.1 | async-start | bytes 2621440
  30.9 11.7 %collective-permute-start.1 = (bf16[40,1792]{1,0:T(8,128)(2,1)S(1)}, bf16[40,1792]{1,0:T(8,128)(2,1)S(1)}, u32[]{:S(2)}, u32[]{:S(2)}) collective-permute-start(bf16[40,1792]{1,0:T(8,128)(2,1)S(1)} %get-tuple-element.10.own_ref), channel_id=1, source_target_pairs={{0,4},{1,5},{2,6},{3,7},{4,8},{5,9},{6,10},{7,11},{8,12},{9,13},{1... | collective-permute-start | bytes 430088 | tf_op jit(solution)/shard_map/ppermute | solution.py:33
  34.5 9.9 %collective-permute-start.2 = (bf16[40,1792]{1,0:T(8,128)(2,1)S(1)}, bf16[40,1792]{1,0:T(8,128)(2,1)S(1)}, u32[]{:S(2)}, u32[]{:S(2)}) collective-permute-start(bf16[40,1792]{1,0:T(8,128)(2,1)S(1)} %get-tuple-element.10.own_ref), channel_id=1, source_target_pairs={{0,8},{1,9},{2,10},{3,11},{4,12},{5,13},{6,14},{7,15},{8,0},{9,1},... | collective-permute-start | bytes 430088 | tf_op jit(solution)/shard_map/ppermute | solution.py:33
  35.6 8.7 %collective-permute-start.3 = (bf16[40,1792]{1,0:T(8,128)(2,1)S(1)}, bf16[40,1792]{1,0:T(8,128)(2,1)S(1)}, u32[]{:S(2)}, u32[]{:S(2)}) collective-permute-start(bf16[40,1792]{1,0:T(8,128)(2,1)S(1)} %get-tuple-element.10.own_ref), channel_id=1, source_target_pairs={{0,12},{1,13},{2,14},{3,15},{4,0},{5,1},{6,2},{7,3},{8,4},{9,5},{1... | collective-permute-start | bytes 430088 | tf_op jit(solution)/shard_map/ppermute | solution.py:33
  44.4 13.4 %collective-permute-start.13 = (bf16[3,40,1792]{2,1,0:T(8,128)(2,1)S(1)}, bf16[3,40,1792]{2,1,0:T(8,128)(2,1)S(1)}, u32[]{:S(2)}, u32[]{:S(2)}) collective-permute-start(bf16[3,40,1792]{2,1,0:T(8,128)(2,1)S(1)} %pile.6.z_ref.refs_5_), channel_id=1, source_target_pairs={{0,2},{1,3},{2,0},{3,1},{4,6},{5,7},{6,4},{7,5},{8,10},{9,11},{10,... | collective-permute-start | bytes 1290248 | tf_op jit(solution)/shard_map/ppermute | solution.py:33
  45.0 8.8 %collective-permute-start.17 = (bf16[80,512]{1,0:T(8,128)(2,1)S(1)}, bf16[80,512]{1,0:T(8,128)(2,1)S(1)}, u32[]{:S(2)}, u32[]{:S(2)}) collective-permute-start(bf16[80,512]{1,0:T(8,128)(2,1)S(1)} %rotate_out.1.refs_3_.refs_0_), channel_id=1, source_target_pairs={{0,4},{1,5},{2,6},{3,7},{4,8},{5,9},{6,10},{7,11},{8,12},{9,13},{1... | collective-permute-start | bytes 245768 | tf_op jit(solution)/shard_map/ppermute | solution.py:33
  48.5 7.2 %collective-permute-start.18 = (bf16[80,512]{1,0:T(8,128)(2,1)S(1)}, bf16[80,512]{1,0:T(8,128)(2,1)S(1)}, u32[]{:S(2)}, u32[]{:S(2)}) collective-permute-start(bf16[80,512]{1,0:T(8,128)(2,1)S(1)} %rotate_out.1.refs_3_.refs_0_), channel_id=1, source_target_pairs={{0,8},{1,9},{2,10},{3,11},{4,12},{5,13},{6,14},{7,15},{8,0},{9,1},... | collective-permute-start | bytes 245768 | tf_op jit(solution)/shard_map/ppermute | solution.py:33
  50.9 5.3 %collective-permute-start.19 = (bf16[80,512]{1,0:T(8,128)(2,1)S(1)}, bf16[80,512]{1,0:T(8,128)(2,1)S(1)}, u32[]{:S(2)}, u32[]{:S(2)}) collective-permute-start(bf16[80,512]{1,0:T(8,128)(2,1)S(1)} %rotate_out.1.refs_3_.refs_0_), channel_id=1, source_target_pairs={{0,12},{1,13},{2,14},{3,15},{4,0},{5,1},{6,2},{7,3},{8,4},{9,5},{1... | collective-permute-start | bytes 245768 | tf_op jit(solution)/shard_map/ppermute | solution.py:33
  56.2 9.0 %collective-permute-start.20 = (bf16[4,80,512]{2,1,0:T(8,128)(2,1)S(1)}, bf16[4,80,512]{2,1,0:T(8,128)(2,1)S(1)}, u32[]{:S(2)}, u32[]{:S(2)}) collective-permute-start(bf16[4,80,512]{2,1,0:T(8,128)(2,1)S(1)} %pile.7.z_ref), channel_id=1, source_target_pairs={{0,2},{1,3},{2,0},{3,1},{4,6},{5,7},{6,4},{7,5},{8,10},{9,11},{10,... | collective-permute-start | bytes 983048 | tf_op jit(solution)/shard_map/ppermute | solution.py:33
  57.8 9.1 %collective-permute-start.21 = (bf16[4,80,512]{2,1,0:T(8,128)(2,1)S(1)}, bf16[4,80,512]{2,1,0:T(8,128)(2,1)S(1)}, u32[]{:S(2)}, u32[]{:S(2)}) collective-permute-start(bf16[4,80,512]{2,1,0:T(8,128)(2,1)S(1)} %pile.7.z_ref), channel_id=1, source_target_pairs={{0,1},{1,0},{2,3},{3,2},{4,5},{5,4},{6,7},{7,6},{8,9},{9,8},{10,11... | collective-permute-start | bytes 983048 | tf_op jit(solution)/shard_map/ppermute | solution.py:33
  65.2 1.7 %collective-permute-start.22 = (bf16[4,80,512]{2,1,0:T(8,128)(2,1)S(1)}, bf16[4,80,512]{2,1,0:T(8,128)(2,1)S(1)}, u32[]{:S(2)}, u32[]{:S(2)}) collective-permute-start(bf16[4,80,512]{2,1,0:T(8,128)(2,1)S(1)} %after.1.y_ref), channel_id=1, source_target_pairs={{0,1},{1,0},{2,3},{3,2},{4,5},{5,4},{6,7},{7,6},{8,9},{9,8},{10,11... | collective-permute-start | bytes 983048 | tf_op jit(solution)/shard_map/ppermute | solution.py:33
  65.2 1.7 %collective-permute-start.16 = (bf16[96,40]{1,0:T(8,128)(2,1)S(1)}, bf16[96,40]{1,0:T(8,128)(2,1)S(1)}, u32[]{:S(2)}, u32[]{:S(2)}) collective-permute-start(bf16[96,40]{1,0:T(8,128)(2,1)S(1)} %get-tuple-element.14), channel_id=1, source_target_pairs={{0,1},{1,0},{2,3},{3,2},{4,5},{5,4},{6,7},{7,6},{8,9},{9,8},{10,11... | collective-permute-start | bytes 23048 | tf_op jit(solution)/shard_map/ppermute | solution.py:33
  (4 other events, 25.3 us)

commit v11 on v10

--- a/solution.py
+++ b/solution.py
@@ -120,27 +120,21 @@
     )(z, y, cz, cy, basis, *waits)
 
 
-def rotate_in_kernel(tokens, chunk, before, last, own_ref, across_ref, z_ref, y_ref, mine_ref, theirs_ref, *refs):
+def rotate_in_kernel(tokens, before, last, z_ref, y_ref, mine_ref, theirs_ref, *refs):
     outs, (total, rows) = refs[before:-2], refs[-2:]
-    height, width = own_ref.shape
-    steps = z_ref.shape[0] + 1
+    steps, height, width = z_ref.shape
     devices = steps * CORES * PAIR
     chips = devices // CORES
     me = lax.axis_index("wide")
 
-    def put(chip, block):
-        unfold_store(rows, chip, block)
-
     @pl.when(pl.program_id(0) == 0)
     def _():
-        put(origin(me, devices, 0, 0, 0)[0], own_ref[...])
-        put(origin(me, devices, 0, 1, 0)[0], across_ref[chunk])
         for ref, chip_bit in ((z_ref, 0), (y_ref, 1)):
 
-            def put_far(step, _, ref=ref, chip_bit=chip_bit):
-                put(origin(me, devices, step + 1, chip_bit, 0)[0], ref[step])
-
-            repeat(steps - 1, put_far)
+            def put(step, _, ref=ref, chip_bit=chip_bit):
+                unfold_store(rows, origin(me, devices, step, chip_bit, 0)[0], ref[step])
+
+            repeat(steps, put)
         total[...] = refs[0][...] if before else jnp.zeros_like(total)
 
     def add(fold, _):
@@ -161,18 +155,18 @@
             outs[0][...] = total[...]
 
 
-def rotate_in(tokens, chunk, own, across, z, y, mine, theirs, before):
-    height, width = own.shape
-    chips = (z.shape[0] + 1) * PAIR
+def rotate_in(tokens, chunk, z, y, mine, theirs, before):
+    steps, height, width = z.shape
+    chips = steps * PAIR
     last = chunk == CHUNKS - 1
     basis = pl.BlockSpec((mine.shape[0], FOLDS * width), lambda i: (0, chunk * (SUBLANES // FOLDS) + i))
     whole = jax.ShapeDtypeStruct((2 * mine.shape[0], chips * tokens), jnp.float32)
     half = jax.ShapeDtypeStruct((mine.shape[0], chips * tokens), jnp.bfloat16)
     return pl.pallas_call(
-        functools.partial(rotate_in_kernel, tokens, chunk, len(before), last),
+        functools.partial(rotate_in_kernel, tokens, len(before), last),
         grid=(SUBLANES // FOLDS,),
         out_shape=(half, half) if last else (whole,),
-        in_specs=[VMEM] * 4 + [basis] * 2 + [VMEM] * len(before),
+        in_specs=[VMEM] * 2 + [basis] * 2 + [VMEM] * len(before),
         out_specs=(VMEM, VMEM) if last else (VMEM,),
         scratch_shapes=[
             pltpu.VMEM(whole.shape, jnp.float32),
@@ -185,36 +179,29 @@
             transcendentals=0,
         ),
         name="rotate_in",
-    )(own, across, z, y, mine, theirs, *before)
+    )(z, y, mine, theirs, *before)
 
 
 def fold_kernel(waits, from_ref, *refs):
     outs, rows = refs[waits:-1], refs[-1]
     tokens = from_ref.shape[0]
-    chunks = max(1, len(outs) - 1)
-    tiles = from_ref.shape[1] // (chunks * SUBLANES * 128)
-    for chunk in range(chunks):
+    tiles = rows.shape[0]
+    for chunk, out_ref in enumerate(outs):
         for tile in range(tiles):
             for fold in range(SUBLANES):
                 at = ((chunk * SUBLANES + fold) * tiles + tile) * 128
                 rows[tile, pl.ds(fold, tokens, stride=SUBLANES), :] = from_ref[:, at : at + 128].astype(jnp.float32)
         for tile in range(tiles):
-            block = rows[tile].astype(jnp.bfloat16)
-            outs[chunk][:, tile * 128 : (tile + 1) * 128] = block
-            if chunks > 1:
-                outs[-1][chunk, :, tile * 128 : (tile + 1) * 128] = block
+            out_ref[:, tile * 128 : (tile + 1) * 128] = rows[tile].astype(jnp.bfloat16)
 
 
 def folded(array, chunks, waits):
     shape = (array.shape[0] * SUBLANES, array.shape[1] // (chunks * SUBLANES))
-    outs = [jax.ShapeDtypeStruct(shape, array.dtype)] * chunks
-    if chunks > 1:
-        outs.append(jax.ShapeDtypeStruct((chunks, *shape), array.dtype))
     return pl.pallas_call(
         functools.partial(fold_kernel, len(waits)),
-        out_shape=outs,
+        out_shape=[jax.ShapeDtypeStruct(shape, array.dtype)] * chunks,
         in_specs=[VMEM] + [ANY] * len(waits),
-        out_specs=[VMEM] * len(outs),
+        out_specs=[VMEM] * chunks,
         scratch_shapes=[pltpu.VMEM((shape[1] // 128, shape[0], 128), jnp.float32)],
         compiler_params=pltpu.CompilerParams(vmem_limit_bytes=4 * 2**20),
         cost_estimate=pl.CostEstimate(flops=0, bytes_accessed=4 * array.size, transcendentals=0),
@@ -237,6 +224,26 @@
         cost_estimate=pl.CostEstimate(flops=0, bytes_accessed=2 * len(blocks) * blocks[0].size, transcendentals=0),
         name="pile",
     )(*blocks, *waits)
+
+
+def fetch_kernel(from_ref, *refs):
+    to_ref, done = refs[-2:]
+    copy = pltpu.make_async_copy(from_ref, to_ref, done)
+    copy.start()
+    copy.wait()
+
+
+def fetch(array, waits):
+    return pl.pallas_call(
+        fetch_kernel,
+        out_shape=jax.ShapeDtypeStruct(array.shape, array.dtype),
+        in_specs=[ANY] * (1 + len(waits)),
+        out_specs=VMEM,
+        scratch_shapes=[pltpu.SemaphoreType.DMA],
+        compiler_params=pltpu.CompilerParams(vmem_limit_bytes=2**20),
+        cost_estimate=pl.CostEstimate(flops=0, bytes_accessed=2 * array.size, transcendentals=0),
+        name="fetch",
+    )(array, *waits)
 
 
 def after(arrays, waits):
@@ -299,23 +306,24 @@
         return z, y, send(z, swap(devices)), send(y, swap(devices))
 
     [block] = folded(grads, 1, [])
+    fetched = fetch(basis_out, [block])
     mine = basis_in.T
     theirs = send(mine, swap(devices))
-    *own, every = folded(acts, CHUNKS, [block])
-    own_across = send(every, across(devices))
-    grads_all = others(pile([block] + along_all(block), [own_across]))
+    own = folded(acts, CHUNKS, [block])
+    first = along_all(own[0])
+    grads_all = others(pile([block] + along_all(block), [fetched, first[0]]))
 
     acts_z, acts_y = [], []
 
     def chunk_along(chunk, waits):
-        acts_z.append(pile(along_all(own[chunk]), waits))
+        acts_z.append(pile([own[chunk]] + (along_all(own[chunk]) if chunk else first), waits))
         acts_y.append(send(acts_z[-1], across(devices)))
 
     def part(chunk, before):
-        return rotate_in(tokens, chunk, own[chunk], own_across, acts_z[chunk], acts_y[chunk], mine, theirs, before)
+        return rotate_in(tokens, chunk, acts_z[chunk], acts_y[chunk], mine, theirs, before)
 
     chunk_along(0, [])
-    sq_out = rotate_out(tokens, *grads_all, basis_out, [acts_z[0]])
+    sq_out = rotate_out(tokens, *grads_all, fetched, [acts_z[0]])
     came = along_all(sq_out)
     for chunk in range(1, CHUNKS):
         chunk_along(chunk, [sq_out])

time: 68.8 us -> 70.3 us (1.022); the launches traced: 68.6 us -> 69.2 us
  starting transfers between devices: 29.9 us -> 28.8 us
  waiting for transfers between devices: 23.3 us -> 24.4 us
    ppermute x23 -> x22, waiting for transfers between devices: 23.3 us -> 24.4 us  [send(): return lax.ppermute(block, 'wide', pairs)]
    ppermute x23 -> x22, starting transfers between devices: 29.9 us -> 28.8 us  [send(): return lax.ppermute(block, 'wide', pairs)]
    pallas_call x4 -> x5, Pallas kernels: 5.9 us -> 6.44 us  [the longest x2 5.61 us: rotate_in(): pl.pallas_call(functools.partial(rotate_in_kernel, tokens, len(before), l...]
  transfers between devices with their start and end apart: 23 -> 22, of which waited for: 11 -> 9; matrix products, arithmetic and copies ran while one was open for 0% -> 0% of each run, Pallas kernels for 12% -> 13%
where the time goes in v11:
time: 70.3 us; the launch traced here: 69.2 us
  starting transfers between devices  28.8 us (41%)
  waiting for transfers between devices  24.4 us (35%)
  Pallas kernels  10.6 us (15%)
  local copies, waits for them, and re-layouts  5.31 us (8%)
    ppermute x22, starting transfers between devices, send(): return lax.ppermute(block, 'wide', pairs)  28.8 us
    ppermute x22, waiting for transfers between devices, send(): return lax.ppermute(block, 'wide', pairs)  24.4 us
    pallas_call x2, Pallas kernels, rotate_in(): pl.pallas_call(functools.partial(rotate_in_kernel, tokens, len(before), l...  5.61 us
    unnamed x10, local copies, waits for them, and re-layouts  5.31 us
    pallas_call x1, Pallas kernels, rotate_out(): pl.pallas_call(functools.partial(rotate_out_kernel, tokens, len(waits)),...  2.29 us
    pallas_call x1, Pallas kernels, combine(): pl.pallas_call(combine_kernel, out_shape=jax.ShapeDtypeStruct((own.shape[...  1.77 us
  transfers between devices with their start and end apart: 22, of which 9 were waited for; matrix products, arithmetic and copies ran while one was open for 0% of the time, Pallas kernels for 13%

profile of v11, /device:TPU:0, one launch (start us, length us, event | category | flops | bytes accessed | tf_op | source)
XLA Modules:
  0.0 69.2 jit_solution(3965399281087612476)
XLA Ops:
  2.6 2.6 %collective-permute-start.6 = (bf16[40,1792]{1,0:T(8,128)(2,1)S(1)}, bf16[40,1792]{1,0:T(8,128)(2,1)S(1)}, u32[]{:S(2)}, u32[]{:S(2)}) collective-permute-start(bf16[40,1792]{1,0:T(8,128)(2,1)S(1)} %get-tuple-element.10.refs_0_), channel_id=1, source_target_pairs={{0,4},{1,5},{2,6},{3,7},{4,8},{5,9},{6,10},{7,11},{8,12},{9,13},{1... | collective-permute-start | bytes 430088 | tf_op jit(solution)/shard_map/ppermute | solution.py:33
  5.3 1.6 %collective-permute-start.3 = (bf16[40,1024]{1,0:T(8,128)(2,1)S(1)}, bf16[40,1024]{1,0:T(8,128)(2,1)S(1)}, u32[]{:S(2)}, u32[]{:S(2)}) collective-permute-start(bf16[40,1024]{1,0:T(8,128)(2,1)S(1)} %fold.2.refs_0_), channel_id=1, source_target_pairs={{0,4},{1,5},{2,6},{3,7},{4,8},{5,9},{6,10},{7,11},{8,12},{9,13},{1... | collective-permute-start | bytes 245768 | tf_op jit(solution)/shard_map/ppermute | solution.py:33
  7.9 2.9 %collective-permute-start.5 = (bf16[40,1024]{1,0:T(8,128)(2,1)S(1)}, bf16[40,1024]{1,0:T(8,128)(2,1)S(1)}, u32[]{:S(2)}, u32[]{:S(2)}) collective-permute-start(bf16[40,1024]{1,0:T(8,128)(2,1)S(1)} %fold.2.refs_0_), channel_id=1, source_target_pairs={{0,12},{1,13},{2,14},{3,15},{4,0},{5,1},{6,2},{7,3},{8,4},{9,5},{1... | collective-permute-start | bytes 245768 | tf_op jit(solution)/shard_map/ppermute | solution.py:33
  10.8 3.4 %copy-done = bf16[8192,512]{1,0:T(8,128)(2,1)S(1)} copy-done((bf16[8192,512]{1,0:T(8,128)(2,1)S(1)}, bf16[8192,512]{1,0:T(8,128)(2,1)}, u32[]{:S(2)}) %copy-start) | copy-done | bytes 8388632
  14.8 2.4 %collective-permute-done.4.refs_2_ = bf16[40,1024]{1,0:T(8,128)(2,1)S(1)} collective-permute-done((bf16[40,1024]{1,0:T(8,128)(2,1)S(1)}, bf16[40,1024]{1,0:T(8,128)(2,1)S(1)}, u32[]{:S(2)}, u32[]{:S(2)}) %collective-permute-start.4) | collective-permute-done | bytes 81952 | tf_op jit(solution)/shard_map/ppermute | solution.py:33
  17.2 1.6 %collective-permute-start.7 = (bf16[4,40,1024]{2,1,0:T(8,128)(2,1)S(1)}, bf16[4,40,1024]{2,1,0:T(8,128)(2,1)S(1)}, u32[]{:S(2)}, u32[]{:S(2)}) collective-permute-start(bf16[4,40,1024]{2,1,0:T(8,128)(2,1)S(1)} %pile.4.z_ref), channel_id=1, source_target_pairs={{0,2},{1,3},{2,0},{3,1},{4,6},{5,7},{6,4},{7,5},{8,10},{9,11},{10,... | collective-permute-start | bytes 983048 | tf_op jit(solution)/shard_map/ppermute | solution.py:33
  18.8 1.2 %collective-permute-start.10 = (bf16[40,1792]{1,0:T(8,128)(2,1)S(1)}, bf16[40,1792]{1,0:T(8,128)(2,1)S(1)}, u32[]{:S(2)}, u32[]{:S(2)}) collective-permute-start(bf16[40,1792]{1,0:T(8,128)(2,1)S(1)} %get-tuple-element.10.refs_0_), channel_id=1, source_target_pairs={{0,8},{1,9},{2,10},{3,11},{4,12},{5,13},{6,14},{7,15},{8,0},{9,1},... | collective-permute-start | bytes 430088 | tf_op jit(solution)/shard_map/ppermute | solution.py:33
  20.0 3.4 %collective-permute-start.11 = (bf16[40,1792]{1,0:T(8,128)(2,1)S(1)}, bf16[40,1792]{1,0:T(8,128)(2,1)S(1)}, u32[]{:S(2)}, u32[]{:S(2)}) collective-permute-start(bf16[40,1792]{1,0:T(8,128)(2,1)S(1)} %get-tuple-element.10.refs_0_), channel_id=1, source_target_pairs={{0,12},{1,13},{2,14},{3,15},{4,0},{5,1},{6,2},{7,3},{8,4},{9,5},{1... | collective-permute-start | bytes 430088 | tf_op jit(solution)/shard_map/ppermute | solution.py:33
  23.3 3.4 %collective-permute-done.7.y_ref = bf16[4,40,1024]{2,1,0:T(8,128)(2,1)S(1)} collective-permute-done((bf16[4,40,1024]{2,1,0:T(8,128)(2,1)S(1)}, bf16[4,40,1024]{2,1,0:T(8,128)(2,1)S(1)}, u32[]{:S(2)}, u32[]{:S(2)}) %collective-permute-start.7) | collective-permute-done | bytes 327712 | tf_op jit(solution)/shard_map/ppermute | solution.py:33
  26.8 2.5 %collective-permute-done.10.refs_2_ = bf16[40,1792]{1,0:T(8,128)(2,1)S(1)} collective-permute-done((bf16[40,1792]{1,0:T(8,128)(2,1)S(1)}, bf16[40,1792]{1,0:T(8,128)(2,1)S(1)}, u32[]{:S(2)}, u32[]{:S(2)}) %collective-permute-start.10) | collective-permute-done | bytes 143392 | tf_op jit(solution)/shard_map/ppermute | solution.py:33
  29.9 2.4 %collective-permute-start = (bf16[40,1792]{1,0:T(8,128)(2,1)S(1)}, bf16[40,1792]{1,0:T(8,128)(2,1)S(1)}, u32[]{:S(2)}, u32[]{:S(2)}) collective-permute-start(bf16[40,1792]{1,0:T(8,128)(2,1)S(1)} %get-tuple-element.9.refs_0_), channel_id=1, source_target_pairs={{0,4},{1,5},{2,6},{3,7},{4,8},{5,9},{6,10},{7,11},{8,12},{9,13},{1... | collective-permute-start | bytes 430088 | tf_op jit(solution)/shard_map/ppermute | solution.py:33
  32.3 2.2 %collective-permute-start.1 = (bf16[40,1792]{1,0:T(8,128)(2,1)S(1)}, bf16[40,1792]{1,0:T(8,128)(2,1)S(1)}, u32[]{:S(2)}, u32[]{:S(2)}) collective-permute-start(bf16[40,1792]{1,0:T(8,128)(2,1)S(1)} %get-tuple-element.9.refs_0_), channel_id=1, source_target_pairs={{0,8},{1,9},{2,10},{3,11},{4,12},{5,13},{6,14},{7,15},{8,0},{9,1},... | collective-permute-start | bytes 430088 | tf_op jit(solution)/shard_map/ppermute | solution.py:33
  34.7 2.3 %rotate_out.1.refs_4_.refs_0_ = bf16[80,512]{1,0:T(8,128)(2,1)S(1)} custom-call(bf16[4,40,1024]{2,1,0:T(8,128)(2,1)S(1)} %pile.4.z_ref, bf16[4,40,1024]{2,1,0:T(8,128)(2,1)S(1)} %collective-permute-done.7.y_ref, bf16[4,40,1024]{2,1,0:T(8,128)(2,1)S(1)} %collective-permute-done.8.cz_ref, bf16[4,40,1024]{2,1,0:T(8,128)(2,1)S(1)} %collective-permute-done.9.cy_ref, ...), custom_call_target="tpu_custom_call" | custom-call | flops 671088640 | bytes 8388608 | tf_op jit(solution)/shard_map/rotate_out/pallas_call | solution.py:105
  37.0 1.6 %collective-permute-done.refs_1_ = bf16[40,1792]{1,0:T(8,128)(2,1)S(1)} collective-permute-done((bf16[40,1792]{1,0:T(8,128)(2,1)S(1)}, bf16[40,1792]{1,0:T(8,128)(2,1)S(1)}, u32[]{:S(2)}, u32[]{:S(2)}) %collective-permute-start) | collective-permute-done | bytes 143392 | tf_op jit(solution)/shard_map/ppermute | solution.py:33
  38.6 5.2 %collective-permute-done.1.refs_2_ = bf16[40,1792]{1,0:T(8,128)(2,1)S(1)} collective-permute-done((bf16[40,1792]{1,0:T(8,128)(2,1)S(1)}, bf16[40,1792]{1,0:T(8,128)(2,1)S(1)}, u32[]{:S(2)}, u32[]{:S(2)}) %collective-permute-start.1) | collective-permute-done | bytes 143392 | tf_op jit(solution)/shard_map/ppermute | solution.py:33
  43.9 1.6 %collective-permute-start.12 = (bf16[4,40,1792]{2,1,0:T(8,128)(2,1)S(1)}, bf16[4,40,1792]{2,1,0:T(8,128)(2,1)S(1)}, u32[]{:S(2)}, u32[]{:S(2)}) collective-permute-start(bf16[4,40,1792]{2,1,0:T(8,128)(2,1)S(1)} %pile.6.z_ref.refs_5_), channel_id=1, source_target_pairs={{0,2},{1,3},{2,0},{3,1},{4,6},{5,7},{6,4},{7,5},{8,10},{9,11},{10,... | collective-permute-start | bytes 1720328 | tf_op jit(solution)/shard_map/ppermute | solution.py:33
  45.4 3.5 %collective-permute-start.16 = (bf16[80,512]{1,0:T(8,128)(2,1)S(1)}, bf16[80,512]{1,0:T(8,128)(2,1)S(1)}, u32[]{:S(2)}, u32[]{:S(2)}) collective-permute-start(bf16[80,512]{1,0:T(8,128)(2,1)S(1)} %rotate_out.1.refs_4_.refs_0_), channel_id=1, source_target_pairs={{0,4},{1,5},{2,6},{3,7},{4,8},{5,9},{6,10},{7,11},{8,12},{9,13},{1... | collective-permute-start | bytes 245768 | tf_op jit(solution)/shard_map/ppermute | solution.py:33
  49.1 2.2 %collective-permute-start.18 = (bf16[80,512]{1,0:T(8,128)(2,1)S(1)}, bf16[80,512]{1,0:T(8,128)(2,1)S(1)}, u32[]{:S(2)}, u32[]{:S(2)}) collective-permute-start(bf16[80,512]{1,0:T(8,128)(2,1)S(1)} %rotate_out.1.refs_4_.refs_0_), channel_id=1, source_target_pairs={{0,12},{1,13},{2,14},{3,15},{4,0},{5,1},{6,2},{7,3},{8,4},{9,5},{1... | collective-permute-start | bytes 245768 | tf_op jit(solution)/shard_map/ppermute | solution.py:33
  51.4 2.8 %rotate_in.2.refs_0_.refs_4_ = f32[192,40]{1,0:T(8,128)S(1)} custom-call(bf16[4,40,1792]{2,1,0:T(8,128)(2,1)S(1)} %pile.5.refs_0_.z_ref, bf16[4,40,1792]{2,1,0:T(8,128)(2,1)S(1)} %collective-permute-done.14.y_ref, bf16[96,28672]{1,0:T(8,128)(2,1)S(1)} %bitcast.4, bf16[96,28672]{1,0:T(8,128)(2,1)S(1)} %collective-permute-done.13.theirs_ref), custom_call_target="tpu_custom_call" | custom-call | flops 220200960 | bytes 5505024 | tf_op jit(solution)/shard_map/rotate_in/pallas_call | solution.py:165
  54.2 1.5 %collective-permute-done.17.refs_2_ = bf16[80,512]{1,0:T(8,128)(2,1)S(1)} collective-permute-done((bf16[80,512]{1,0:T(8,128)(2,1)S(1)}, bf16[80,512]{1,0:T(8,128)(2,1)S(1)}, u32[]{:S(2)}, u32[]{:S(2)}) %collective-permute-start.17) | collective-permute-done | bytes 81952 | tf_op jit(solution)/shard_map/ppermute | solution.py:33
  56.4 3.4 %collective-permute-done.12.y_ref = bf16[4,40,1792]{2,1,0:T(8,128)(2,1)S(1)} collective-permute-done((bf16[4,40,1792]{2,1,0:T(8,128)(2,1)S(1)}, bf16[4,40,1792]{2,1,0:T(8,128)(2,1)S(1)}, u32[]{:S(2)}, u32[]{:S(2)}) %collective-permute-start.12) | collective-permute-done | bytes 573472 | tf_op jit(solution)/shard_map/ppermute | solution.py:33
  59.8 2.8 %rotate_in.3 = (bf16[96,40]{1,0:T(8,128)(2,1)S(1)}, bf16[96,40]{1,0:T(8,128)(2,1)S(1)}) custom-call(bf16[4,40,1792]{2,1,0:T(8,128)(2,1)S(1)} %pile.6.z_ref.refs_5_, bf16[4,40,1792]{2,1,0:T(8,128)(2,1)S(1)} %collective-permute-done.12.y_ref, bf16[96,28672]{1,0:T(8,128)(2,1)S(1)} %bitcast.5, bf16[96,28672]{1,0:T(8,128)(2,1)S(1)} %collective-permute-done.13.theirs_ref, ...), custom_call_target="tpu_custom_call" | custom-call | flops 220200960 | bytes 5505024 | tf_op jit(solution)/shard_map/rotate_in/pallas_call | solution.py:165
  62.6 3.2 %collective-permute-done.19.refs_0_ = bf16[4,80,512]{2,1,0:T(8,128)(2,1)S(1)} collective-permute-done((bf16[4,80,512]{2,1,0:T(8,128)(2,1)S(1)}, bf16[4,80,512]{2,1,0:T(8,128)(2,1)S(1)}, u32[]{:S(2)}, u32[]{:S(2)}) %collective-permute-start.19) | collective-permute-done | bytes 327712 | tf_op jit(solution)/shard_map/ppermute | solution.py:33
  67.4 1.8 %combine.1 = bf16[96,8192]{1,0:T(8,128)(2,1)} custom-call(bf16[96,40]{1,0:T(8,128)(2,1)S(1)} %get-tuple-element.11.refs_1_.own_ref, bf16[96,40]{1,0:T(8,128)(2,1)S(1)} %collective-permute-done.15.other_ref, bf16[4,80,512]{2,1,0:T(8,128)(2,1)S(1)} %pile.7.z_ref, bf16[4,80,512]{2,1,0:T(8,128)(2,1)S(1)} %after.1.y_ref, ...), custom_call_target="tpu_custom_call" | custom-call | flops 125829120 | bytes 3145728 | tf_op jit(solution)/shard_map/combine/pallas_call | solution.py:283
  (43 shorter events, 7.6 us)
Async XLA Ops:
  0.0 51.4 %collective-permute-start.13 = (bf16[96,28672]{1,0:T(8,128)(2,1)}, bf16[96,28672]{1,0:T(8,128)(2,1)S(1)}, u32[]{:S(2)}, u32[]{:S(2)}) collective-permute-start(bf16[96,28672]{1,0:T(8,128)(2,1)} %bitcast.1), channel_id=1, source_target_pairs={{0,1},{1,0},{2,3},{3,2},{4,5},{5,4},{6,7},{7,6},{8,9},{9,8},{10,11... | collective-permute-start | bytes 16515080 | tf_op jit(solution)/shard_map/ppermute | solution.py:33
  2.6 14.5 %collective-permute-start.6 = (bf16[40,1792]{1,0:T(8,128)(2,1)S(1)}, bf16[40,1792]{1,0:T(8,128)(2,1)S(1)}, u32[]{:S(2)}, u32[]{:S(2)}) collective-permute-start(bf16[40,1792]{1,0:T(8,128)(2,1)S(1)} %get-tuple-element.10.refs_0_), channel_id=1, source_target_pairs={{0,4},{1,5},{2,6},{3,7},{4,8},{5,9},{6,10},{7,11},{8,12},{9,13},{1... | collective-permute-start | bytes 430088 | tf_op jit(solution)/shard_map/ppermute | solution.py:33
  5.3 9.5 %collective-permute-start.3 = (bf16[40,1024]{1,0:T(8,128)(2,1)S(1)}, bf16[40,1024]{1,0:T(8,128)(2,1)S(1)}, u32[]{:S(2)}, u32[]{:S(2)}) collective-permute-start(bf16[40,1024]{1,0:T(8,128)(2,1)S(1)} %fold.2.refs_0_), channel_id=1, source_target_pairs={{0,4},{1,5},{2,6},{3,7},{4,8},{5,9},{6,10},{7,11},{8,12},{9,13},{1... | collective-permute-start | bytes 245768 | tf_op jit(solution)/shard_map/ppermute | solution.py:33
  6.8 10.3 %collective-permute-start.4 = (bf16[40,1024]{1,0:T(8,128)(2,1)S(1)}, bf16[40,1024]{1,0:T(8,128)(2,1)S(1)}, u32[]{:S(2)}, u32[]{:S(2)}) collective-permute-start(bf16[40,1024]{1,0:T(8,128)(2,1)S(1)} %fold.2.refs_0_), channel_id=1, source_target_pairs={{0,8},{1,9},{2,10},{3,11},{4,12},{5,13},{6,14},{7,15},{8,0},{9,1},... | collective-permute-start | bytes 245768 | tf_op jit(solution)/shard_map/ppermute | solution.py:33
  7.9 9.2 %collective-permute-start.5 = (bf16[40,1024]{1,0:T(8,128)(2,1)S(1)}, bf16[40,1024]{1,0:T(8,128)(2,1)S(1)}, u32[]{:S(2)}, u32[]{:S(2)}) collective-permute-start(bf16[40,1024]{1,0:T(8,128)(2,1)S(1)} %fold.2.refs_0_), channel_id=1, source_target_pairs={{0,12},{1,13},{2,14},{3,15},{4,0},{5,1},{6,2},{7,3},{8,4},{9,5},{1... | collective-permute-start | bytes 245768 | tf_op jit(solution)/shard_map/ppermute | solution.py:33
  17.2 9.6 %collective-permute-start.7 = (bf16[4,40,1024]{2,1,0:T(8,128)(2,1)S(1)}, bf16[4,40,1024]{2,1,0:T(8,128)(2,1)S(1)}, u32[]{:S(2)}, u32[]{:S(2)}) collective-permute-start(bf16[4,40,1024]{2,1,0:T(8,128)(2,1)S(1)} %pile.4.z_ref), channel_id=1, source_target_pairs={{0,2},{1,3},{2,0},{3,1},{4,6},{5,7},{6,4},{7,5},{8,10},{9,11},{10,... | collective-permute-start | bytes 983048 | tf_op jit(solution)/shard_map/ppermute | solution.py:33
  18.8 10.5 %collective-permute-start.10 = (bf16[40,1792]{1,0:T(8,128)(2,1)S(1)}, bf16[40,1792]{1,0:T(8,128)(2,1)S(1)}, u32[]{:S(2)}, u32[]{:S(2)}) collective-permute-start(bf16[40,1792]{1,0:T(8,128)(2,1)S(1)} %get-tuple-element.10.refs_0_), channel_id=1, source_target_pairs={{0,8},{1,9},{2,10},{3,11},{4,12},{5,13},{6,14},{7,15},{8,0},{9,1},... | collective-permute-start | bytes 430088 | tf_op jit(solution)/shard_map/ppermute | solution.py:33
  20.0 9.3 %collective-permute-start.11 = (bf16[40,1792]{1,0:T(8,128)(2,1)S(1)}, bf16[40,1792]{1,0:T(8,128)(2,1)S(1)}, u32[]{:S(2)}, u32[]{:S(2)}) collective-permute-start(bf16[40,1792]{1,0:T(8,128)(2,1)S(1)} %get-tuple-element.10.refs_0_), channel_id=1, source_target_pairs={{0,12},{1,13},{2,14},{3,15},{4,0},{5,1},{6,2},{7,3},{8,4},{9,5},{1... | collective-permute-start | bytes 430088 | tf_op jit(solution)/shard_map/ppermute | solution.py:33
  23.3 9.0 %collective-permute-start.8 = (bf16[4,40,1024]{2,1,0:T(8,128)(2,1)S(1)}, bf16[4,40,1024]{2,1,0:T(8,128)(2,1)S(1)}, u32[]{:S(2)}, u32[]{:S(2)}) collective-permute-start(bf16[4,40,1024]{2,1,0:T(8,128)(2,1)S(1)} %pile.4.z_ref), channel_id=1, source_target_pairs={{0,1},{1,0},{2,3},{3,2},{4,5},{5,4},{6,7},{7,6},{8,9},{9,8},{10,11... | collective-permute-start | bytes 983048 | tf_op jit(solution)/shard_map/ppermute | solution.py:33
  26.8 7.7 %collective-permute-start.9 = (bf16[4,40,1024]{2,1,0:T(8,128)(2,1)S(1)}, bf16[4,40,1024]{2,1,0:T(8,128)(2,1)S(1)}, u32[]{:S(2)}, u32[]{:S(2)}) collective-permute-start(bf16[4,40,1024]{2,1,0:T(8,128)(2,1)S(1)} %collective-permute-done.7.y_ref), channel_id=1, source_target_pairs={{0,1},{1,0},{2,3},{3,2},{4,5},{5,4},{6,7},{7,6},{8,9},{9,8},{10,11... | collective-permute-start | bytes 983048 | tf_op jit(solution)/shard_map/ppermute | solution.py:33
  29.3 19.8 %collective-permute-start.14 = (bf16[4,40,1792]{2,1,0:T(8,128)(2,1)S(1)}, bf16[4,40,1792]{2,1,0:T(8,128)(2,1)S(1)}, u32[]{:S(2)}, u32[]{:S(2)}) collective-permute-start(bf16[4,40,1792]{2,1,0:T(8,128)(2,1)S(1)} %pile.5.refs_0_.z_ref), channel_id=1, source_target_pairs={{0,2},{1,3},{2,0},{3,1},{4,6},{5,7},{6,4},{7,5},{8,10},{9,11},{10,... | collective-permute-start | bytes 1720328 | tf_op jit(solution)/shard_map/ppermute | solution.py:33
  29.9 21.5 %slice-start = ((s8[5505024]{0:T(1024)(128)(4,1)}), s8[4194304]{0:T(1024)(128)(4,1)S(1)}, s32[]{:S(2)}) async-start(s8[5505024]{0:T(1024)(128)(4,1)} %bitcast.2), calls=%async_computation | async-start | bytes 8388608
  29.9 21.5 %slice-start.1 = ((s8[5505024]{0:T(1024)(128)(4,1)}), s8[1310720]{0:T(1024)(128)(4,1)S(1)}, s32[]{:S(2)}) async-start(s8[5505024]{0:T(1024)(128)(4,1)} %bitcast.2), calls=%async_computation.1 | async-start | bytes 2621440
  29.9 8.7 %collective-permute-start = (bf16[40,1792]{1,0:T(8,128)(2,1)S(1)}, bf16[40,1792]{1,0:T(8,128)(2,1)S(1)}, u32[]{:S(2)}, u32[]{:S(2)}) collective-permute-start(bf16[40,1792]{1,0:T(8,128)(2,1)S(1)} %get-tuple-element.9.refs_0_), channel_id=1, source_target_pairs={{0,4},{1,5},{2,6},{3,7},{4,8},{5,9},{6,10},{7,11},{8,12},{9,13},{1... | collective-permute-start | bytes 430088 | tf_op jit(solution)/shard_map/ppermute | solution.py:33
  32.3 11.5 %collective-permute-start.1 = (bf16[40,1792]{1,0:T(8,128)(2,1)S(1)}, bf16[40,1792]{1,0:T(8,128)(2,1)S(1)}, u32[]{:S(2)}, u32[]{:S(2)}) collective-permute-start(bf16[40,1792]{1,0:T(8,128)(2,1)S(1)} %get-tuple-element.9.refs_0_), channel_id=1, source_target_pairs={{0,8},{1,9},{2,10},{3,11},{4,12},{5,13},{6,14},{7,15},{8,0},{9,1},... | collective-permute-start | bytes 430088 | tf_op jit(solution)/shard_map/ppermute | solution.py:33
  34.5 9.3 %collective-permute-start.2 = (bf16[40,1792]{1,0:T(8,128)(2,1)S(1)}, bf16[40,1792]{1,0:T(8,128)(2,1)S(1)}, u32[]{:S(2)}, u32[]{:S(2)}) collective-permute-start(bf16[40,1792]{1,0:T(8,128)(2,1)S(1)} %get-tuple-element.9.refs_0_), channel_id=1, source_target_pairs={{0,12},{1,13},{2,14},{3,15},{4,0},{5,1},{6,2},{7,3},{8,4},{9,5},{1... | collective-permute-start | bytes 430088 | tf_op jit(solution)/shard_map/ppermute | solution.py:33
  43.9 15.9 %collective-permute-start.12 = (bf16[4,40,1792]{2,1,0:T(8,128)(2,1)S(1)}, bf16[4,40,1792]{2,1,0:T(8,128)(2,1)S(1)}, u32[]{:S(2)}, u32[]{:S(2)}) collective-permute-start(bf16[4,40,1792]{2,1,0:T(8,128)(2,1)S(1)} %pile.6.z_ref.refs_5_), channel_id=1, source_target_pairs={{0,2},{1,3},{2,0},{3,1},{4,6},{5,7},{6,4},{7,5},{8,10},{9,11},{10,... | collective-permute-start | bytes 1720328 | tf_op jit(solution)/shard_map/ppermute | solution.py:33
  45.4 8.7 %collective-permute-start.16 = (bf16[80,512]{1,0:T(8,128)(2,1)S(1)}, bf16[80,512]{1,0:T(8,128)(2,1)S(1)}, u32[]{:S(2)}, u32[]{:S(2)}) collective-permute-start(bf16[80,512]{1,0:T(8,128)(2,1)S(1)} %rotate_out.1.refs_4_.refs_0_), channel_id=1, source_target_pairs={{0,4},{1,5},{2,6},{3,7},{4,8},{5,9},{6,10},{7,11},{8,12},{9,13},{1... | collective-permute-start | bytes 245768 | tf_op jit(solution)/shard_map/ppermute | solution.py:33
  49.0 6.8 %collective-permute-start.17 = (bf16[80,512]{1,0:T(8,128)(2,1)S(1)}, bf16[80,512]{1,0:T(8,128)(2,1)S(1)}, u32[]{:S(2)}, u32[]{:S(2)}) collective-permute-start(bf16[80,512]{1,0:T(8,128)(2,1)S(1)} %rotate_out.1.refs_4_.refs_0_), channel_id=1, source_target_pairs={{0,8},{1,9},{2,10},{3,11},{4,12},{5,13},{6,14},{7,15},{8,0},{9,1},... | collective-permute-start | bytes 245768 | tf_op jit(solution)/shard_map/ppermute | solution.py:33
  49.1 6.6 %collective-permute-start.18 = (bf16[80,512]{1,0:T(8,128)(2,1)S(1)}, bf16[80,512]{1,0:T(8,128)(2,1)S(1)}, u32[]{:S(2)}, u32[]{:S(2)}) collective-permute-start(bf16[80,512]{1,0:T(8,128)(2,1)S(1)} %rotate_out.1.refs_4_.refs_0_), channel_id=1, source_target_pairs={{0,12},{1,13},{2,14},{3,15},{4,0},{5,1},{6,2},{7,3},{8,4},{9,5},{1... | collective-permute-start | bytes 245768 | tf_op jit(solution)/shard_map/ppermute | solution.py:33
  55.8 10.0 %collective-permute-start.19 = (bf16[4,80,512]{2,1,0:T(8,128)(2,1)S(1)}, bf16[4,80,512]{2,1,0:T(8,128)(2,1)S(1)}, u32[]{:S(2)}, u32[]{:S(2)}) collective-permute-start(bf16[4,80,512]{2,1,0:T(8,128)(2,1)S(1)} %pile.7.z_ref), channel_id=1, source_target_pairs={{0,2},{1,3},{2,0},{3,1},{4,6},{5,7},{6,4},{7,5},{8,10},{9,11},{10,... | collective-permute-start | bytes 983048 | tf_op jit(solution)/shard_map/ppermute | solution.py:33
  56.4 11.1 %collective-permute-start.20 = (bf16[4,80,512]{2,1,0:T(8,128)(2,1)S(1)}, bf16[4,80,512]{2,1,0:T(8,128)(2,1)S(1)}, u32[]{:S(2)}, u32[]{:S(2)}) collective-permute-start(bf16[4,80,512]{2,1,0:T(8,128)(2,1)S(1)} %pile.7.z_ref), channel_id=1, source_target_pairs={{0,1},{1,0},{2,3},{3,2},{4,5},{5,4},{6,7},{7,6},{8,9},{9,8},{10,11... | collective-permute-start | bytes 983048 | tf_op jit(solution)/shard_map/ppermute | solution.py:33
  65.8 1.7 %collective-permute-start.21 = (bf16[4,80,512]{2,1,0:T(8,128)(2,1)S(1)}, bf16[4,80,512]{2,1,0:T(8,128)(2,1)S(1)}, u32[]{:S(2)}, u32[]{:S(2)}) collective-permute-start(bf16[4,80,512]{2,1,0:T(8,128)(2,1)S(1)} %after.1.y_ref), channel_id=1, source_target_pairs={{0,1},{1,0},{2,3},{3,2},{4,5},{5,4},{6,7},{7,6},{8,9},{9,8},{10,11... | collective-permute-start | bytes 983048 | tf_op jit(solution)/shard_map/ppermute | solution.py:33
  65.8 1.7 %collective-permute-start.15 = (bf16[96,40]{1,0:T(8,128)(2,1)S(1)}, bf16[96,40]{1,0:T(8,128)(2,1)S(1)}, u32[]{:S(2)}, u32[]{:S(2)}) collective-permute-start(bf16[96,40]{1,0:T(8,128)(2,1)S(1)} %get-tuple-element.12), channel_id=1, source_target_pairs={{0,1},{1,0},{2,3},{3,2},{4,5},{5,4},{6,7},{7,6},{8,9},{9,8},{10,11... | collective-permute-start | bytes 23048 | tf_op jit(solution)/shard_map/ppermute | solution.py:33
  (3 other events, 5.3 us)

commit v12 on v10

--- a/solution.py
+++ b/solution.py
@@ -188,38 +188,41 @@
     )(own, across, z, y, mine, theirs, *before)
 
 
-def fold_kernel(waits, from_ref, *refs):
-    outs, rows = refs[waits:-1], refs[-1]
+def fold_one(from_ref, start, out_refs, rows):
     tokens = from_ref.shape[0]
-    chunks = max(1, len(outs) - 1)
-    tiles = from_ref.shape[1] // (chunks * SUBLANES * 128)
-    for chunk in range(chunks):
-        for tile in range(tiles):
-            for fold in range(SUBLANES):
-                at = ((chunk * SUBLANES + fold) * tiles + tile) * 128
-                rows[tile, pl.ds(fold, tokens, stride=SUBLANES), :] = from_ref[:, at : at + 128].astype(jnp.float32)
-        for tile in range(tiles):
-            block = rows[tile].astype(jnp.bfloat16)
-            outs[chunk][:, tile * 128 : (tile + 1) * 128] = block
-            if chunks > 1:
-                outs[-1][chunk, :, tile * 128 : (tile + 1) * 128] = block
-
-
-def folded(array, chunks, waits):
-    shape = (array.shape[0] * SUBLANES, array.shape[1] // (chunks * SUBLANES))
-    outs = [jax.ShapeDtypeStruct(shape, array.dtype)] * chunks
-    if chunks > 1:
-        outs.append(jax.ShapeDtypeStruct((chunks, *shape), array.dtype))
-    return pl.pallas_call(
-        functools.partial(fold_kernel, len(waits)),
-        out_shape=outs,
-        in_specs=[VMEM] + [ANY] * len(waits),
-        out_specs=[VMEM] * len(outs),
-        scratch_shapes=[pltpu.VMEM((shape[1] // 128, shape[0], 128), jnp.float32)],
+    tiles = out_refs[0].shape[1] // 128
+    for tile in range(tiles):
+        for fold in range(SUBLANES):
+            at = start + (fold * tiles + tile) * 128
+            rows[tile, pl.ds(fold, tokens, stride=SUBLANES), :] = from_ref[:, at : at + 128].astype(jnp.float32)
+    for tile in range(tiles):
+        block = rows[tile].astype(jnp.bfloat16)
+        for out_ref in out_refs:
+            out_ref[:, tile * 128 : (tile + 1) * 128] = block
+
+
+def fold_kernel(grads_ref, acts_ref, block_ref, *refs):
+    own, every_ref, rows = refs[:-2], refs[-2], refs[-1]
+    fold_one(grads_ref, 0, [block_ref], rows)
+    for chunk, out_ref in enumerate(own):
+        fold_one(acts_ref, chunk * SUBLANES * out_ref.shape[1], [out_ref, every_ref.at[chunk]], rows)
+
+
+def folded(grads, acts):
+    height = grads.shape[0] * SUBLANES
+    width = acts.shape[1] // (CHUNKS * SUBLANES)
+    shapes = [(height, grads.shape[1] // SUBLANES)] + [(height, width)] * CHUNKS + [(CHUNKS, height, width)]
+    tiles = max(shape[-1] for shape in shapes) // 128
+    return pl.pallas_call(
+        fold_kernel,
+        out_shape=[jax.ShapeDtypeStruct(shape, acts.dtype) for shape in shapes],
+        in_specs=[VMEM] * 2,
+        out_specs=[VMEM] * len(shapes),
+        scratch_shapes=[pltpu.VMEM((tiles, height, 128), jnp.float32)],
         compiler_params=pltpu.CompilerParams(vmem_limit_bytes=4 * 2**20),
-        cost_estimate=pl.CostEstimate(flops=0, bytes_accessed=4 * array.size, transcendentals=0),
+        cost_estimate=pl.CostEstimate(flops=0, bytes_accessed=4 * acts.size, transcendentals=0),
         name="fold",
-    )(array, *waits)
+    )(grads, acts)
 
 
 def pile_kernel(blocks, *refs):
@@ -237,6 +240,26 @@
         cost_estimate=pl.CostEstimate(flops=0, bytes_accessed=2 * len(blocks) * blocks[0].size, transcendentals=0),
         name="pile",
     )(*blocks, *waits)
+
+
+def fetch_kernel(from_ref, *refs):
+    to_ref, done = refs[-2:]
+    copy = pltpu.make_async_copy(from_ref, to_ref, done)
+    copy.start()
+    copy.wait()
+
+
+def fetch(array, waits):
+    return pl.pallas_call(
+        fetch_kernel,
+        out_shape=jax.ShapeDtypeStruct(array.shape, array.dtype),
+        in_specs=[ANY] * (1 + len(waits)),
+        out_specs=VMEM,
+        scratch_shapes=[pltpu.SemaphoreType.DMA],
+        compiler_params=pltpu.CompilerParams(vmem_limit_bytes=16 * 2**20),
+        cost_estimate=pl.CostEstimate(flops=0, bytes_accessed=2 * array.size, transcendentals=0),
+        name="fetch",
+    )(array, *waits)
 
 
 def after(arrays, waits):
@@ -252,38 +275,83 @@
     )(*arrays, *waits)
 
 
-def combine_kernel(own_ref, other_ref, z_ref, y_ref, cz_ref, cy_ref, out_ref):
-    steps, total_tokens, width = z_ref.shape
+def both_classes(own_ref, other_ref):
+    own, other = own_ref[...].astype(jnp.float32), other_ref[...].astype(jnp.float32)
+    first = lax.rem(lax.axis_index("wide"), CORES) == 0
+    left = jnp.concatenate([jnp.where(first, own, other), jnp.where(first, other, own)], 1)
+    return left.astype(jnp.bfloat16)
+
+
+def eigenvalues(left, block):
+    total = jnp.dot(left, block, preferred_element_type=jnp.float32)
+    return (total / block.shape[0]).astype(jnp.bfloat16)
+
+
+def combine_kernel(own_ref, other_ref, z_ref, y_ref, cz_ref, out_ref):
+    steps, _, width = z_ref.shape
     devices = steps * CORES * PAIR
     me = lax.axis_index("wide")
-    own, other = own_ref[...].astype(jnp.float32), other_ref[...].astype(jnp.float32)
-    first = lax.rem(me, CORES) == 0
-    left = jnp.concatenate([jnp.where(first, own, other), jnp.where(first, other, own)], 1).astype(jnp.bfloat16)
-    for ref, chip_bit, core_bit in ((z_ref, 0, 0), (y_ref, 1, 0), (cz_ref, 0, 1), (cy_ref, 1, 1)):
+    left = both_classes(own_ref, other_ref)
+    for ref, chip_bit, core_bit in ((z_ref, 0, 0), (y_ref, 1, 0), (cz_ref, 0, 1)):
 
         def put(step, _, ref=ref, chip_bit=chip_bit, core_bit=core_bit):
             chip, core = origin(me, devices, step, chip_bit, core_bit)
             at = pl.multiple_of((chip * CORES + core) * width, 128)
-            total = jnp.dot(left, ref[step], preferred_element_type=jnp.float32)
-            out_ref[:, pl.ds(at, width)] = (total / total_tokens).astype(out_ref.dtype)
+            out_ref[:, pl.ds(at, width)] = eigenvalues(left, ref[step])
 
         repeat(steps, put)
 
 
-def combine(own, other, z, y, cz, cy):
+def combine(own, other, z, y, cz):
     steps, total_tokens, width = z.shape
     features = steps * CORES * PAIR * width
     return pl.pallas_call(
         combine_kernel,
         out_shape=jax.ShapeDtypeStruct((own.shape[0], features), jnp.bfloat16),
-        in_specs=[VMEM] * 6,
+        in_specs=[VMEM] * 5,
         out_specs=VMEM,
         compiler_params=pltpu.CompilerParams(vmem_limit_bytes=room(6, steps)),
         cost_estimate=pl.CostEstimate(
             flops=2 * own.shape[0] * total_tokens * features, bytes_accessed=4 * own.shape[0] * features, transcendentals=0
         ),
         name="combine",
-    )(own, other, z, y, cz, cy)
+    )(own, other, z, y, cz)
+
+
+def finish_kernel(own_ref, other_ref, cy_ref, _, out_ref, blocks, done):
+    steps, _, width = cy_ref.shape
+    devices = steps * CORES * PAIR
+    me = lax.axis_index("wide")
+    left = both_classes(own_ref, other_ref)
+    copies = []
+    for step in range(steps):
+        chip, core = origin(me, devices, step, 1, 1)
+        at = pl.multiple_of((chip * CORES + core) * width, 128)
+        blocks[step] = eigenvalues(left, cy_ref[step])
+        copies.append(pltpu.make_async_copy(blocks.at[step], out_ref.at[:, pl.ds(at, width)], done.at[step]))
+        copies[-1].start()
+    for copy in copies:
+        copy.wait()
+
+
+def finish(own, other, cy, result):
+    steps, total_tokens, width = cy.shape
+    return pl.pallas_call(
+        finish_kernel,
+        out_shape=jax.ShapeDtypeStruct(result.shape, result.dtype),
+        in_specs=[VMEM] * 3 + [ANY],
+        out_specs=ANY,
+        scratch_shapes=[
+            pltpu.VMEM((steps, own.shape[0], width), result.dtype),
+            pltpu.SemaphoreType.DMA((steps,)),
+        ],
+        input_output_aliases={3: 0},
+        compiler_params=pltpu.CompilerParams(vmem_limit_bytes=room(4, steps)),
+        cost_estimate=pl.CostEstimate(
+            flops=2 * own.shape[0] * total_tokens * steps * width, bytes_accessed=4 * cy.size, transcendentals=0
+        ),
+        name="finish",
+    )(own, other, cy, result)
 
 
 def local(acts, grads, basis_in, basis_out):
@@ -298,12 +366,12 @@
         y = send(z, across(devices))
         return z, y, send(z, swap(devices)), send(y, swap(devices))
 
-    [block] = folded(grads, 1, [])
+    block, *own, every = folded(grads, acts)
+    fetched = fetch(basis_out, [block])
     mine = basis_in.T
     theirs = send(mine, swap(devices))
-    *own, every = folded(acts, CHUNKS, [block])
     own_across = send(every, across(devices))
-    grads_all = others(pile([block] + along_all(block), [own_across]))
+    grads_all = others(pile([block] + along_all(block), [own_across, fetched]))
 
     acts_z, acts_y = [], []
 
@@ -315,7 +383,7 @@
         return rotate_in(tokens, chunk, own[chunk], own_across, acts_z[chunk], acts_y[chunk], mine, theirs, before)
 
     chunk_along(0, [])
-    sq_out = rotate_out(tokens, *grads_all, basis_out, [acts_z[0]])
+    sq_out = rotate_out(tokens, *grads_all, fetched, [acts_z[0]])
     came = along_all(sq_out)
     for chunk in range(1, CHUNKS):
         chunk_along(chunk, [sq_out])
@@ -325,8 +393,10 @@
     for chunk in range(1, CHUNKS):
         total = part(chunk, total)
     sq_in, given = total
-    [y] = after([y], [sq_in])
-    return combine(sq_in, send(given, swap(devices)), z, y, send(z, swap(devices)), send(y, swap(devices)))
+    other = send(given, swap(devices))
+    [y] = after([y], [other])
+    cz, cy = send(z, swap(devices)), send(y, swap(devices))
+    return finish(sq_in, other, cy, combine(sq_in, other, z, y, cz))
 
 
 def solution(mesh):

time: 68.8 us -> 68.1 us (0.990)
  waiting for transfers between devices: 23.3 us -> 20.9 us
  Pallas kernels: 10.1 us -> 11.5 us
    ppermute x23, waiting for transfers between devices: 23.3 us -> 20.9 us  [send(): return lax.ppermute(block, 'wide', pairs)]
    pallas_call x2 -> x3, Pallas kernels: 0.29 us -> 1.86 us  [the longest x1 1 us: finish(): pl.pallas_call(finish_kernel, out_shape=jax.ShapeDtypeStruct(result.shape...]
  transfers between devices with their start and end apart: 23 -> 23, of which waited for: 11 -> 10; matrix products, arithmetic and copies ran while one was open for 0% -> 0% of each run, Pallas kernels for 12% -> 16%
where the time goes in v12:
time: 68.1 us; the launch traced here: 67.9 us
  starting transfers between devices  29.9 us (44%)
  waiting for transfers between devices  20.9 us (31%)
  Pallas kernels  11.5 us (17%)
  local copies, waits for them, and re-layouts  5.31 us (8%)
    ppermute x23, starting transfers between devices, send(): return lax.ppermute(block, 'wide', pairs)  29.9 us
    ppermute x23, waiting for transfers between devices, send(): return lax.ppermute(block, 'wide', pairs)  20.9 us
    pallas_call x2, Pallas kernels, rotate_in(): pl.pallas_call(functools.partial(rotate_in_kernel, tokens, chunk, len(bef...  5.61 us
    unnamed x10, local copies, waits for them, and re-layouts  5.31 us
    pallas_call x1, Pallas kernels, rotate_out(): pl.pallas_call(functools.partial(rotate_out_kernel, tokens, len(waits)),...  2.3 us
    pallas_call x1, Pallas kernels, combine(): pl.pallas_call(combine_kernel, out_shape=jax.ShapeDtypeStruct((own.shape[...  1.66 us
  transfers between devices with their start and end apart: 23, of which 10 were waited for; matrix products, arithmetic and copies ran while one was open for 0% of the time, Pallas kernels for 16%

profile of v12, /device:TPU:0, one launch (start us, length us, event | category | flops | bytes accessed | tf_op | source)
XLA Modules:
  0.0 67.9 jit_solution(5513863101357009476)
XLA Ops:
  0.5 1.0 %copy-done.1 = bf16[5,28672]{1,0:T(8,128)(2,1)S(1)} copy-done((bf16[5,28672]{1,0:T(8,128)(2,1)S(1)}, bf16[5,28672]{1,0:T(8,128)(2,1)}, u32[]{:S(2)}) %copy-start.1) | copy-done | bytes 286744
  2.7 2.6 %collective-permute-start = (bf16[2,40,1792]{2,1,0:T(8,128)(2,1)S(1)}, bf16[2,40,1792]{2,1,0:T(8,128)(2,1)S(1)}, u32[]{:S(2)}, u32[]{:S(2)}) collective-permute-start(bf16[2,40,1792]{2,1,0:T(8,128)(2,1)S(1)} %get-tuple-element.12), channel_id=1, source_target_pairs={{0,2},{1,3},{2,0},{3,1},{4,6},{5,7},{6,4},{7,5},{8,10},{9,11},{10,... | collective-permute-start | bytes 860168 | tf_op jit(solution)/shard_map/ppermute | solution.py:33
  5.2 1.6 %collective-permute-start.4 = (bf16[40,1024]{1,0:T(8,128)(2,1)S(1)}, bf16[40,1024]{1,0:T(8,128)(2,1)S(1)}, u32[]{:S(2)}, u32[]{:S(2)}) collective-permute-start(bf16[40,1024]{1,0:T(8,128)(2,1)S(1)} %get-tuple-element.13.refs_0_), channel_id=1, source_target_pairs={{0,4},{1,5},{2,6},{3,7},{4,8},{5,9},{6,10},{7,11},{8,12},{9,13},{1... | collective-permute-start | bytes 245768 | tf_op jit(solution)/shard_map/ppermute | solution.py:33
  6.8 2.6 %collective-permute-start.5 = (bf16[40,1024]{1,0:T(8,128)(2,1)S(1)}, bf16[40,1024]{1,0:T(8,128)(2,1)S(1)}, u32[]{:S(2)}, u32[]{:S(2)}) collective-permute-start(bf16[40,1024]{1,0:T(8,128)(2,1)S(1)} %get-tuple-element.13.refs_0_), channel_id=1, source_target_pairs={{0,8},{1,9},{2,10},{3,11},{4,12},{5,13},{6,14},{7,15},{8,0},{9,1},... | collective-permute-start | bytes 245768 | tf_op jit(solution)/shard_map/ppermute | solution.py:33
  9.4 1.3 %collective-permute-start.6 = (bf16[40,1024]{1,0:T(8,128)(2,1)S(1)}, bf16[40,1024]{1,0:T(8,128)(2,1)S(1)}, u32[]{:S(2)}, u32[]{:S(2)}) collective-permute-start(bf16[40,1024]{1,0:T(8,128)(2,1)S(1)} %get-tuple-element.13.refs_0_), channel_id=1, source_target_pairs={{0,12},{1,13},{2,14},{3,15},{4,0},{5,1},{6,2},{7,3},{8,4},{9,5},{1... | collective-permute-start | bytes 245768 | tf_op jit(solution)/shard_map/ppermute | solution.py:33
  10.8 3.4 %copy-done = bf16[8192,512]{1,0:T(8,128)(2,1)S(1)} copy-done((bf16[8192,512]{1,0:T(8,128)(2,1)S(1)}, bf16[8192,512]{1,0:T(8,128)(2,1)}, u32[]{:S(2)}) %copy-start) | copy-done | bytes 8388632
  16.1 2.1 %collective-permute-start.10 = (bf16[40,1792]{1,0:T(8,128)(2,1)S(1)}, bf16[40,1792]{1,0:T(8,128)(2,1)S(1)}, u32[]{:S(2)}, u32[]{:S(2)}) collective-permute-start(bf16[40,1792]{1,0:T(8,128)(2,1)S(1)} %get-tuple-element.14.own_ref), channel_id=1, source_target_pairs={{0,4},{1,5},{2,6},{3,7},{4,8},{5,9},{6,10},{7,11},{8,12},{9,13},{1... | collective-permute-start | bytes 430088 | tf_op jit(solution)/shard_map/ppermute | solution.py:33
  18.2 1.6 %collective-permute-start.11 = (bf16[40,1792]{1,0:T(8,128)(2,1)S(1)}, bf16[40,1792]{1,0:T(8,128)(2,1)S(1)}, u32[]{:S(2)}, u32[]{:S(2)}) collective-permute-start(bf16[40,1792]{1,0:T(8,128)(2,1)S(1)} %get-tuple-element.14.own_ref), channel_id=1, source_target_pairs={{0,8},{1,9},{2,10},{3,11},{4,12},{5,13},{6,14},{7,15},{8,0},{9,1},... | collective-permute-start | bytes 430088 | tf_op jit(solution)/shard_map/ppermute | solution.py:33
  20.5 4.2 %collective-permute-done.10.refs_0_ = bf16[40,1792]{1,0:T(8,128)(2,1)S(1)} collective-permute-done((bf16[40,1792]{1,0:T(8,128)(2,1)S(1)}, bf16[40,1792]{1,0:T(8,128)(2,1)S(1)}, u32[]{:S(2)}, u32[]{:S(2)}) %collective-permute-start.10) | collective-permute-done | bytes 143392 | tf_op jit(solution)/shard_map/ppermute | solution.py:33
  25.2 4.1 %collective-permute-done.11.refs_1_ = bf16[40,1792]{1,0:T(8,128)(2,1)S(1)} collective-permute-done((bf16[40,1792]{1,0:T(8,128)(2,1)S(1)}, bf16[40,1792]{1,0:T(8,128)(2,1)S(1)}, u32[]{:S(2)}, u32[]{:S(2)}) %collective-permute-start.11) | collective-permute-done | bytes 143392 | tf_op jit(solution)/shard_map/ppermute | solution.py:33
  29.3 1.6 %collective-permute-start.15 = (bf16[3,40,1792]{2,1,0:T(8,128)(2,1)S(1)}, bf16[3,40,1792]{2,1,0:T(8,128)(2,1)S(1)}, u32[]{:S(2)}, u32[]{:S(2)}) collective-permute-start(bf16[3,40,1792]{2,1,0:T(8,128)(2,1)S(1)} %pile.5.refs_0_.z_ref), channel_id=1, source_target_pairs={{0,2},{1,3},{2,0},{3,1},{4,6},{5,7},{6,4},{7,5},{8,10},{9,11},{10,... | collective-permute-start | bytes 1290248 | tf_op jit(solution)/shard_map/ppermute | solution.py:33
  30.9 3.5 %collective-permute-start.1 = (bf16[40,1792]{1,0:T(8,128)(2,1)S(1)}, bf16[40,1792]{1,0:T(8,128)(2,1)S(1)}, u32[]{:S(2)}, u32[]{:S(2)}) collective-permute-start(bf16[40,1792]{1,0:T(8,128)(2,1)S(1)} %get-tuple-element.11.own_ref), channel_id=1, source_target_pairs={{0,4},{1,5},{2,6},{3,7},{4,8},{5,9},{6,10},{7,11},{8,12},{9,13},{1... | collective-permute-start | bytes 430088 | tf_op jit(solution)/shard_map/ppermute | solution.py:33
  34.5 1.1 %collective-permute-start.2 = (bf16[40,1792]{1,0:T(8,128)(2,1)S(1)}, bf16[40,1792]{1,0:T(8,128)(2,1)S(1)}, u32[]{:S(2)}, u32[]{:S(2)}) collective-permute-start(bf16[40,1792]{1,0:T(8,128)(2,1)S(1)} %get-tuple-element.11.own_ref), channel_id=1, source_target_pairs={{0,8},{1,9},{2,10},{3,11},{4,12},{5,13},{6,14},{7,15},{8,0},{9,1},... | collective-permute-start | bytes 430088 | tf_op jit(solution)/shard_map/ppermute | solution.py:33
  35.6 1.3 %collective-permute-start.3 = (bf16[40,1792]{1,0:T(8,128)(2,1)S(1)}, bf16[40,1792]{1,0:T(8,128)(2,1)S(1)}, u32[]{:S(2)}, u32[]{:S(2)}) collective-permute-start(bf16[40,1792]{1,0:T(8,128)(2,1)S(1)} %get-tuple-element.11.own_ref), channel_id=1, source_target_pairs={{0,12},{1,13},{2,14},{3,15},{4,0},{5,1},{6,2},{7,3},{8,4},{9,5},{1... | collective-permute-start | bytes 430088 | tf_op jit(solution)/shard_map/ppermute | solution.py:33
  36.9 2.3 %rotate_out.1.refs_3_.refs_0_ = bf16[80,512]{1,0:T(8,128)(2,1)S(1)} custom-call(bf16[4,40,1024]{2,1,0:T(8,128)(2,1)S(1)} %pile.4.z_ref, bf16[4,40,1024]{2,1,0:T(8,128)(2,1)S(1)} %collective-permute-done.7.y_ref, bf16[4,40,1024]{2,1,0:T(8,128)(2,1)S(1)} %collective-permute-done.8.cz_ref, bf16[4,40,1024]{2,1,0:T(8,128)(2,1)S(1)} %collective-permute-done.9.cy_ref, ...), custom_call_target="tpu_custom_call" | custom-call | flops 671088640 | bytes 8388608 | tf_op jit(solution)/shard_map/rotate_out/pallas_call | solution.py:105
  39.2 5.1 %collective-permute-done.2.refs_1_ = bf16[40,1792]{1,0:T(8,128)(2,1)S(1)} collective-permute-done((bf16[40,1792]{1,0:T(8,128)(2,1)S(1)}, bf16[40,1792]{1,0:T(8,128)(2,1)S(1)}, u32[]{:S(2)}, u32[]{:S(2)}) %collective-permute-start.2) | collective-permute-done | bytes 143392 | tf_op jit(solution)/shard_map/ppermute | solution.py:33
  44.9 3.5 %collective-permute-start.17 = (bf16[80,512]{1,0:T(8,128)(2,1)S(1)}, bf16[80,512]{1,0:T(8,128)(2,1)S(1)}, u32[]{:S(2)}, u32[]{:S(2)}) collective-permute-start(bf16[80,512]{1,0:T(8,128)(2,1)S(1)} %rotate_out.1.refs_3_.refs_0_), channel_id=1, source_target_pairs={{0,4},{1,5},{2,6},{3,7},{4,8},{5,9},{6,10},{7,11},{8,12},{9,13},{1... | collective-permute-start | bytes 245768 | tf_op jit(solution)/shard_map/ppermute | solution.py:33
  48.5 2.4 %collective-permute-start.18 = (bf16[80,512]{1,0:T(8,128)(2,1)S(1)}, bf16[80,512]{1,0:T(8,128)(2,1)S(1)}, u32[]{:S(2)}, u32[]{:S(2)}) collective-permute-start(bf16[80,512]{1,0:T(8,128)(2,1)S(1)} %rotate_out.1.refs_3_.refs_0_), channel_id=1, source_target_pairs={{0,8},{1,9},{2,10},{3,11},{4,12},{5,13},{6,14},{7,15},{8,0},{9,1},... | collective-permute-start | bytes 245768 | tf_op jit(solution)/shard_map/ppermute | solution.py:33
  50.9 2.8 %rotate_in.2.refs_0_.refs_4_ = f32[192,40]{1,0:T(8,128)S(1)} custom-call(bf16[40,1792]{1,0:T(8,128)(2,1)S(1)} %get-tuple-element.14.own_ref, bf16[2,40,1792]{2,1,0:T(8,128)(2,1)S(1)} %collective-permute-done.refs_4_.across_ref, bf16[3,40,1792]{2,1,0:T(8,128)(2,1)S(1)} %pile.5.refs_0_.z_ref, bf16[3,40,1792]{2,1,0:T(8,128)(2,1)S(1)} %collective-permute-done.15.y_ref, ...), custom_call_target="tpu_custom_call" | custom-call | flops 220200960 | bytes 5505024 | tf_op jit(solution)/shard_map/rotate_in/pallas_call | solution.py:171
  53.7 2.0 %collective-permute-done.18.refs_2_ = bf16[80,512]{1,0:T(8,128)(2,1)S(1)} collective-permute-done((bf16[80,512]{1,0:T(8,128)(2,1)S(1)}, bf16[80,512]{1,0:T(8,128)(2,1)S(1)}, u32[]{:S(2)}, u32[]{:S(2)}) %collective-permute-start.18) | collective-permute-done | bytes 81952 | tf_op jit(solution)/shard_map/ppermute | solution.py:33
  56.2 1.6 %collective-permute-start.20 = (bf16[4,80,512]{2,1,0:T(8,128)(2,1)S(1)}, bf16[4,80,512]{2,1,0:T(8,128)(2,1)S(1)}, u32[]{:S(2)}, u32[]{:S(2)}) collective-permute-start(bf16[4,80,512]{2,1,0:T(8,128)(2,1)S(1)} %pile.7.z_ref), channel_id=1, source_target_pairs={{0,2},{1,3},{2,0},{3,1},{4,6},{5,7},{6,4},{7,5},{8,10},{9,11},{10,... | collective-permute-start | bytes 983048 | tf_op jit(solution)/shard_map/ppermute | solution.py:33
  57.8 2.8 %rotate_in.3 = (bf16[96,40]{1,0:T(8,128)(2,1)S(1)}, bf16[96,40]{1,0:T(8,128)(2,1)S(1)}) custom-call(bf16[40,1792]{1,0:T(8,128)(2,1)S(1)} %get-tuple-element.11.own_ref, bf16[2,40,1792]{2,1,0:T(8,128)(2,1)S(1)} %collective-permute-done.refs_4_.across_ref, bf16[3,40,1792]{2,1,0:T(8,128)(2,1)S(1)} %pile.6.z_ref.refs_5_, ...), custom_call_target="tpu_custom_call" | custom-call | flops 220200960 | bytes 5505024 | tf_op jit(solution)/shard_map/rotate_in/pallas_call | solution.py:171
  62.0 3.2 %collective-permute-done.20.refs_0_ = bf16[4,80,512]{2,1,0:T(8,128)(2,1)S(1)} collective-permute-done((bf16[4,80,512]{2,1,0:T(8,128)(2,1)S(1)}, bf16[4,80,512]{2,1,0:T(8,128)(2,1)S(1)}, u32[]{:S(2)}, u32[]{:S(2)}) %collective-permute-start.20) | collective-permute-done | bytes 327712 | tf_op jit(solution)/shard_map/ppermute | solution.py:33
  65.2 1.7 %combine.1._ = bf16[96,8192]{1,0:T(8,128)(2,1)} custom-call(bf16[96,40]{1,0:T(8,128)(2,1)S(1)} %get-tuple-element.15.own_ref, bf16[96,40]{1,0:T(8,128)(2,1)S(1)} %collective-permute-done.16.refs_1_.other_ref, bf16[4,80,512]{2,1,0:T(8,128)(2,1)S(1)} %pile.7.z_ref, bf16[4,80,512]{2,1,0:T(8,128)(2,1)S(1)} %after.1.y_ref, ...), custom_call_target="tpu_custom_call" | custom-call | flops 125829120 | bytes 3145728 | tf_op jit(solution)/shard_map/combine/pallas_call | solution.py:308
  (45 shorter events, 8.4 us)
Async XLA Ops:
  0.0 50.9 %collective-permute-start.14 = (bf16[96,28672]{1,0:T(8,128)(2,1)}, bf16[96,28672]{1,0:T(8,128)(2,1)S(1)}, u32[]{:S(2)}, u32[]{:S(2)}) collective-permute-start(bf16[96,28672]{1,0:T(8,128)(2,1)} %bitcast.1), channel_id=1, source_target_pairs={{0,1},{1,0},{2,3},{3,2},{4,5},{5,4},{6,7},{7,6},{8,9},{9,8},{10,11... | collective-permute-start | bytes 16515080 | tf_op jit(solution)/shard_map/ppermute | solution.py:33
  2.7 12.9 %collective-permute-start = (bf16[2,40,1792]{2,1,0:T(8,128)(2,1)S(1)}, bf16[2,40,1792]{2,1,0:T(8,128)(2,1)S(1)}, u32[]{:S(2)}, u32[]{:S(2)}) collective-permute-start(bf16[2,40,1792]{2,1,0:T(8,128)(2,1)S(1)} %get-tuple-element.12), channel_id=1, source_target_pairs={{0,2},{1,3},{2,0},{3,1},{4,6},{5,7},{6,4},{7,5},{8,10},{9,11},{10,... | collective-permute-start | bytes 860168 | tf_op jit(solution)/shard_map/ppermute | solution.py:33
  5.2 9.5 %collective-permute-start.4 = (bf16[40,1024]{1,0:T(8,128)(2,1)S(1)}, bf16[40,1024]{1,0:T(8,128)(2,1)S(1)}, u32[]{:S(2)}, u32[]{:S(2)}) collective-permute-start(bf16[40,1024]{1,0:T(8,128)(2,1)S(1)} %get-tuple-element.13.refs_0_), channel_id=1, source_target_pairs={{0,4},{1,5},{2,6},{3,7},{4,8},{5,9},{6,10},{7,11},{8,12},{9,13},{1... | collective-permute-start | bytes 245768 | tf_op jit(solution)/shard_map/ppermute | solution.py:33
  6.8 8.5 %collective-permute-start.5 = (bf16[40,1024]{1,0:T(8,128)(2,1)S(1)}, bf16[40,1024]{1,0:T(8,128)(2,1)S(1)}, u32[]{:S(2)}, u32[]{:S(2)}) collective-permute-start(bf16[40,1024]{1,0:T(8,128)(2,1)S(1)} %get-tuple-element.13.refs_0_), channel_id=1, source_target_pairs={{0,8},{1,9},{2,10},{3,11},{4,12},{5,13},{6,14},{7,15},{8,0},{9,1},... | collective-permute-start | bytes 245768 | tf_op jit(solution)/shard_map/ppermute | solution.py:33
  9.4 6.1 %collective-permute-start.6 = (bf16[40,1024]{1,0:T(8,128)(2,1)S(1)}, bf16[40,1024]{1,0:T(8,128)(2,1)S(1)}, u32[]{:S(2)}, u32[]{:S(2)}) collective-permute-start(bf16[40,1024]{1,0:T(8,128)(2,1)S(1)} %get-tuple-element.13.refs_0_), channel_id=1, source_target_pairs={{0,12},{1,13},{2,14},{3,15},{4,0},{5,1},{6,2},{7,3},{8,4},{9,5},{1... | collective-permute-start | bytes 245768 | tf_op jit(solution)/shard_map/ppermute | solution.py:33
  15.5 9.4 %collective-permute-start.7 = (bf16[4,40,1024]{2,1,0:T(8,128)(2,1)S(1)}, bf16[4,40,1024]{2,1,0:T(8,128)(2,1)S(1)}, u32[]{:S(2)}, u32[]{:S(2)}) collective-permute-start(bf16[4,40,1024]{2,1,0:T(8,128)(2,1)S(1)} %pile.4.z_ref), channel_id=1, source_target_pairs={{0,2},{1,3},{2,0},{3,1},{4,6},{5,7},{6,4},{7,5},{8,10},{9,11},{10,... | collective-permute-start | bytes 983048 | tf_op jit(solution)/shard_map/ppermute | solution.py:33
  16.1 8.6 %collective-permute-start.10 = (bf16[40,1792]{1,0:T(8,128)(2,1)S(1)}, bf16[40,1792]{1,0:T(8,128)(2,1)S(1)}, u32[]{:S(2)}, u32[]{:S(2)}) collective-permute-start(bf16[40,1792]{1,0:T(8,128)(2,1)S(1)} %get-tuple-element.14.own_ref), channel_id=1, source_target_pairs={{0,4},{1,5},{2,6},{3,7},{4,8},{5,9},{6,10},{7,11},{8,12},{9,13},{1... | collective-permute-start | bytes 430088 | tf_op jit(solution)/shard_map/ppermute | solution.py:33
  18.2 11.1 %collective-permute-start.11 = (bf16[40,1792]{1,0:T(8,128)(2,1)S(1)}, bf16[40,1792]{1,0:T(8,128)(2,1)S(1)}, u32[]{:S(2)}, u32[]{:S(2)}) collective-permute-start(bf16[40,1792]{1,0:T(8,128)(2,1)S(1)} %get-tuple-element.14.own_ref), channel_id=1, source_target_pairs={{0,8},{1,9},{2,10},{3,11},{4,12},{5,13},{6,14},{7,15},{8,0},{9,1},... | collective-permute-start | bytes 430088 | tf_op jit(solution)/shard_map/ppermute | solution.py:33
  19.8 9.5 %collective-permute-start.12 = (bf16[40,1792]{1,0:T(8,128)(2,1)S(1)}, bf16[40,1792]{1,0:T(8,128)(2,1)S(1)}, u32[]{:S(2)}, u32[]{:S(2)}) collective-permute-start(bf16[40,1792]{1,0:T(8,128)(2,1)S(1)} %get-tuple-element.14.own_ref), channel_id=1, source_target_pairs={{0,12},{1,13},{2,14},{3,15},{4,0},{5,1},{6,2},{7,3},{8,4},{9,5},{1... | collective-permute-start | bytes 430088 | tf_op jit(solution)/shard_map/ppermute | solution.py:33
  24.7 9.8 %collective-permute-start.8 = (bf16[4,40,1024]{2,1,0:T(8,128)(2,1)S(1)}, bf16[4,40,1024]{2,1,0:T(8,128)(2,1)S(1)}, u32[]{:S(2)}, u32[]{:S(2)}) collective-permute-start(bf16[4,40,1024]{2,1,0:T(8,128)(2,1)S(1)} %pile.4.z_ref), channel_id=1, source_target_pairs={{0,1},{1,0},{2,3},{3,2},{4,5},{5,4},{6,7},{7,6},{8,9},{9,8},{10,11... | collective-permute-start | bytes 983048 | tf_op jit(solution)/shard_map/ppermute | solution.py:33
  25.0 10.6 %collective-permute-start.9 = (bf16[4,40,1024]{2,1,0:T(8,128)(2,1)S(1)}, bf16[4,40,1024]{2,1,0:T(8,128)(2,1)S(1)}, u32[]{:S(2)}, u32[]{:S(2)}) collective-permute-start(bf16[4,40,1024]{2,1,0:T(8,128)(2,1)S(1)} %collective-permute-done.7.y_ref), channel_id=1, source_target_pairs={{0,1},{1,0},{2,3},{3,2},{4,5},{5,4},{6,7},{7,6},{8,9},{9,8},{10,11... | collective-permute-start | bytes 983048 | tf_op jit(solution)/shard_map/ppermute | solution.py:33
  29.3 21.5 %collective-permute-start.15 = (bf16[3,40,1792]{2,1,0:T(8,128)(2,1)S(1)}, bf16[3,40,1792]{2,1,0:T(8,128)(2,1)S(1)}, u32[]{:S(2)}, u32[]{:S(2)}) collective-permute-start(bf16[3,40,1792]{2,1,0:T(8,128)(2,1)S(1)} %pile.5.refs_0_.z_ref), channel_id=1, source_target_pairs={{0,2},{1,3},{2,0},{3,1},{4,6},{5,7},{6,4},{7,5},{8,10},{9,11},{10,... | collective-permute-start | bytes 1290248 | tf_op jit(solution)/shard_map/ppermute | solution.py:33
  30.9 20.0 %slice-start.1 = ((s8[5505024]{0:T(1024)(128)(4,1)}), s8[1310720]{0:T(1024)(128)(4,1)S(1)}, s32[]{:S(2)}) async-start(s8[5505024]{0:T(1024)(128)(4,1)} %bitcast.2), calls=%async_computation.1 | async-start | bytes 2621440
  30.9 8.3 %collective-permute-start.1 = (bf16[40,1792]{1,0:T(8,128)(2,1)S(1)}, bf16[40,1792]{1,0:T(8,128)(2,1)S(1)}, u32[]{:S(2)}, u32[]{:S(2)}) collective-permute-start(bf16[40,1792]{1,0:T(8,128)(2,1)S(1)} %get-tuple-element.11.own_ref), channel_id=1, source_target_pairs={{0,4},{1,5},{2,6},{3,7},{4,8},{5,9},{6,10},{7,11},{8,12},{9,13},{1... | collective-permute-start | bytes 430088 | tf_op jit(solution)/shard_map/ppermute | solution.py:33
  34.5 9.9 %collective-permute-start.2 = (bf16[40,1792]{1,0:T(8,128)(2,1)S(1)}, bf16[40,1792]{1,0:T(8,128)(2,1)S(1)}, u32[]{:S(2)}, u32[]{:S(2)}) collective-permute-start(bf16[40,1792]{1,0:T(8,128)(2,1)S(1)} %get-tuple-element.11.own_ref), channel_id=1, source_target_pairs={{0,8},{1,9},{2,10},{3,11},{4,12},{5,13},{6,14},{7,15},{8,0},{9,1},... | collective-permute-start | bytes 430088 | tf_op jit(solution)/shard_map/ppermute | solution.py:33
  35.6 8.7 %collective-permute-start.3 = (bf16[40,1792]{1,0:T(8,128)(2,1)S(1)}, bf16[40,1792]{1,0:T(8,128)(2,1)S(1)}, u32[]{:S(2)}, u32[]{:S(2)}) collective-permute-start(bf16[40,1792]{1,0:T(8,128)(2,1)S(1)} %get-tuple-element.11.own_ref), channel_id=1, source_target_pairs={{0,12},{1,13},{2,14},{3,15},{4,0},{5,1},{6,2},{7,3},{8,4},{9,5},{1... | collective-permute-start | bytes 430088 | tf_op jit(solution)/shard_map/ppermute | solution.py:33
  44.4 13.4 %collective-permute-start.13 = (bf16[3,40,1792]{2,1,0:T(8,128)(2,1)S(1)}, bf16[3,40,1792]{2,1,0:T(8,128)(2,1)S(1)}, u32[]{:S(2)}, u32[]{:S(2)}) collective-permute-start(bf16[3,40,1792]{2,1,0:T(8,128)(2,1)S(1)} %pile.6.z_ref.refs_5_), channel_id=1, source_target_pairs={{0,2},{1,3},{2,0},{3,1},{4,6},{5,7},{6,4},{7,5},{8,10},{9,11},{10,... | collective-permute-start | bytes 1290248 | tf_op jit(solution)/shard_map/ppermute | solution.py:33
  44.9 8.8 %collective-permute-start.17 = (bf16[80,512]{1,0:T(8,128)(2,1)S(1)}, bf16[80,512]{1,0:T(8,128)(2,1)S(1)}, u32[]{:S(2)}, u32[]{:S(2)}) collective-permute-start(bf16[80,512]{1,0:T(8,128)(2,1)S(1)} %rotate_out.1.refs_3_.refs_0_), channel_id=1, source_target_pairs={{0,4},{1,5},{2,6},{3,7},{4,8},{5,9},{6,10},{7,11},{8,12},{9,13},{1... | collective-permute-start | bytes 245768 | tf_op jit(solution)/shard_map/ppermute | solution.py:33
  48.5 7.2 %collective-permute-start.18 = (bf16[80,512]{1,0:T(8,128)(2,1)S(1)}, bf16[80,512]{1,0:T(8,128)(2,1)S(1)}, u32[]{:S(2)}, u32[]{:S(2)}) collective-permute-start(bf16[80,512]{1,0:T(8,128)(2,1)S(1)} %rotate_out.1.refs_3_.refs_0_), channel_id=1, source_target_pairs={{0,8},{1,9},{2,10},{3,11},{4,12},{5,13},{6,14},{7,15},{8,0},{9,1},... | collective-permute-start | bytes 245768 | tf_op jit(solution)/shard_map/ppermute | solution.py:33
  50.9 5.3 %collective-permute-start.19 = (bf16[80,512]{1,0:T(8,128)(2,1)S(1)}, bf16[80,512]{1,0:T(8,128)(2,1)S(1)}, u32[]{:S(2)}, u32[]{:S(2)}) collective-permute-start(bf16[80,512]{1,0:T(8,128)(2,1)S(1)} %rotate_out.1.refs_3_.refs_0_), channel_id=1, source_target_pairs={{0,12},{1,13},{2,14},{3,15},{4,0},{5,1},{6,2},{7,3},{8,4},{9,5},{1... | collective-permute-start | bytes 245768 | tf_op jit(solution)/shard_map/ppermute | solution.py:33
  56.2 9.0 %collective-permute-start.20 = (bf16[4,80,512]{2,1,0:T(8,128)(2,1)S(1)}, bf16[4,80,512]{2,1,0:T(8,128)(2,1)S(1)}, u32[]{:S(2)}, u32[]{:S(2)}) collective-permute-start(bf16[4,80,512]{2,1,0:T(8,128)(2,1)S(1)} %pile.7.z_ref), channel_id=1, source_target_pairs={{0,2},{1,3},{2,0},{3,1},{4,6},{5,7},{6,4},{7,5},{8,10},{9,11},{10,... | collective-permute-start | bytes 983048 | tf_op jit(solution)/shard_map/ppermute | solution.py:33
  57.8 7.4 %collective-permute-start.22 = (bf16[4,80,512]{2,1,0:T(8,128)(2,1)S(1)}, bf16[4,80,512]{2,1,0:T(8,128)(2,1)S(1)}, u32[]{:S(2)}, u32[]{:S(2)}) collective-permute-start(bf16[4,80,512]{2,1,0:T(8,128)(2,1)S(1)} %pile.7.z_ref), channel_id=1, source_target_pairs={{0,1},{1,0},{2,3},{3,2},{4,5},{5,4},{6,7},{7,6},{8,9},{9,8},{10,11... | collective-permute-start | bytes 983048 | tf_op jit(solution)/shard_map/ppermute | solution.py:33
  60.6 1.4 %collective-permute-start.16 = (bf16[96,40]{1,0:T(8,128)(2,1)S(1)}, bf16[96,40]{1,0:T(8,128)(2,1)S(1)}, u32[]{:S(2)}, u32[]{:S(2)}) collective-permute-start(bf16[96,40]{1,0:T(8,128)(2,1)S(1)} %get-tuple-element.16), channel_id=1, source_target_pairs={{0,1},{1,0},{2,3},{3,2},{4,5},{5,4},{6,7},{7,6},{8,9},{9,8},{10,11... | collective-permute-start | bytes 23048 | tf_op jit(solution)/shard_map/ppermute | solution.py:33
  65.2 1.7 %collective-permute-start.21 = (bf16[4,80,512]{2,1,0:T(8,128)(2,1)S(1)}, bf16[4,80,512]{2,1,0:T(8,128)(2,1)S(1)}, u32[]{:S(2)}, u32[]{:S(2)}) collective-permute-start(bf16[4,80,512]{2,1,0:T(8,128)(2,1)S(1)} %after.1.y_ref), channel_id=1, source_target_pairs={{0,1},{1,0},{2,3},{3,2},{4,5},{5,4},{6,7},{7,6},{8,9},{9,8},{10,11... | collective-permute-start | bytes 983048 | tf_op jit(solution)/shard_map/ppermute | solution.py:33
  (4 other events, 25.3 us)

commit v13 on v12

--- a/solution.py
+++ b/solution.py
@@ -371,19 +371,23 @@
     mine = basis_in.T
     theirs = send(mine, swap(devices))
     own_across = send(every, across(devices))
-    grads_all = others(pile([block] + along_all(block), [own_across, fetched]))
+    grads_z = pile([block] + along_all(block), [own_across, fetched, theirs])
+    grads_y = send(grads_z, across(devices))
 
     acts_z, acts_y = [], []
 
+    sent = [along_all(block) for block in own]
+
     def chunk_along(chunk, waits):
-        acts_z.append(pile(along_all(own[chunk]), waits))
+        acts_z.append(pile(sent[chunk], waits))
         acts_y.append(send(acts_z[-1], across(devices)))
 
     def part(chunk, before):
         return rotate_in(tokens, chunk, own[chunk], own_across, acts_z[chunk], acts_y[chunk], mine, theirs, before)
 
-    chunk_along(0, [])
-    sq_out = rotate_out(tokens, *grads_all, fetched, [acts_z[0]])
+    chunk_along(0, [sent[1][0]])
+    grads_cz, grads_cy = send(grads_z, swap(devices)), send(grads_y, swap(devices))
+    sq_out = rotate_out(tokens, grads_z, grads_y, grads_cz, grads_cy, fetched, [acts_z[0]])
     came = along_all(sq_out)
     for chunk in range(1, CHUNKS):
         chunk_along(chunk, [sq_out])

time: 68.1 us -> 71.1 us (1.044)
  waiting for transfers between devices: 20.9 us -> 32.8 us
  starting transfers between devices: 29.9 us -> 21.1 us
    ppermute x23, waiting for transfers between devices: 20.9 us -> 32.8 us  [send(): return lax.ppermute(block, 'wide', pairs)]
    ppermute x23, starting transfers between devices: 29.9 us -> 21.1 us  [send(): return lax.ppermute(block, 'wide', pairs)]
  transfers between devices with their start and end apart: 23 -> 23, of which waited for: 10 -> 8; matrix products, arithmetic and copies ran while one was open for 0% -> 0% of each run, Pallas kernels for 16% -> 15%
where the time goes in v13:
time: 71.1 us; the launch traced here: 70.8 us
  waiting for transfers between devices  32.8 us (46%)
  starting transfers between devices  21.1 us (30%)
  Pallas kernels  11.5 us (16%)
  local copies, waits for them, and re-layouts  5.31 us (7%)
    ppermute x23, waiting for transfers between devices, send(): return lax.ppermute(block, 'wide', pairs)  32.8 us
    ppermute x23, starting transfers between devices, send(): return lax.ppermute(block, 'wide', pairs)  21.1 us
    pallas_call x2, Pallas kernels, rotate_in(): pl.pallas_call(functools.partial(rotate_in_kernel, tokens, chunk, len(bef...  5.62 us
    unnamed x10, local copies, waits for them, and re-layouts  5.31 us
    pallas_call x1, Pallas kernels, rotate_out(): pl.pallas_call(functools.partial(rotate_out_kernel, tokens, len(waits)),...  2.29 us
    pallas_call x1, Pallas kernels, combine(): pl.pallas_call(combine_kernel, out_shape=jax.ShapeDtypeStruct((own.shape[...  1.67 us
  transfers between devices with their start and end apart: 23, of which 8 were waited for; matrix products, arithmetic and copies ran while one was open for 0% of the time, Pallas kernels for 15%

profile of v13, /device:TPU:0, one launch (start us, length us, event | category | flops | bytes accessed | tf_op | source)
XLA Modules:
  0.0 70.8 jit_solution(3159121189579333911)
XLA Ops:
  0.5 1.0 %copy-done.1 = bf16[5,28672]{1,0:T(8,128)(2,1)S(1)} copy-done((bf16[5,28672]{1,0:T(8,128)(2,1)S(1)}, bf16[5,28672]{1,0:T(8,128)(2,1)}, u32[]{:S(2)}) %copy-start.1) | copy-done | bytes 286744
  1.5 0.9 %copy-done.2 = bf16[5,8192]{1,0:T(8,128)(2,1)S(1)} copy-done((bf16[5,8192]{1,0:T(8,128)(2,1)S(1)}, bf16[5,8192]{1,0:T(8,128)(2,1)}, u32[]{:S(2)}) %copy-start.2) | copy-done | bytes 81944
  2.7 2.6 %collective-permute-start = (bf16[2,40,1792]{2,1,0:T(8,128)(2,1)S(1)}, bf16[2,40,1792]{2,1,0:T(8,128)(2,1)S(1)}, u32[]{:S(2)}, u32[]{:S(2)}) collective-permute-start(bf16[2,40,1792]{2,1,0:T(8,128)(2,1)S(1)} %get-tuple-element.12), channel_id=1, source_target_pairs={{0,2},{1,3},{2,0},{3,1},{4,6},{5,7},{6,4},{7,5},{8,10},{9,11},{10,... | collective-permute-start | bytes 860168 | tf_op jit(solution)/shard_map/ppermute | solution.py:33
  5.2 3.6 %collective-permute-start.6 = (bf16[40,1024]{1,0:T(8,128)(2,1)S(1)}, bf16[40,1024]{1,0:T(8,128)(2,1)S(1)}, u32[]{:S(2)}, u32[]{:S(2)}) collective-permute-start(bf16[40,1024]{1,0:T(8,128)(2,1)S(1)} %get-tuple-element.13.refs_0_), channel_id=1, source_target_pairs={{0,12},{1,13},{2,14},{3,15},{4,0},{5,1},{6,2},{7,3},{8,4},{9,5},{1... | collective-permute-start | bytes 245768 | tf_op jit(solution)/shard_map/ppermute | solution.py:33
  8.9 1.0 %collective-permute-start.4 = (bf16[40,1024]{1,0:T(8,128)(2,1)S(1)}, bf16[40,1024]{1,0:T(8,128)(2,1)S(1)}, u32[]{:S(2)}, u32[]{:S(2)}) collective-permute-start(bf16[40,1024]{1,0:T(8,128)(2,1)S(1)} %get-tuple-element.13.refs_0_), channel_id=1, source_target_pairs={{0,4},{1,5},{2,6},{3,7},{4,8},{5,9},{6,10},{7,11},{8,12},{9,13},{1... | collective-permute-start | bytes 245768 | tf_op jit(solution)/shard_map/ppermute | solution.py:33
  9.9 3.4 %copy-done = bf16[8192,512]{1,0:T(8,128)(2,1)S(1)} copy-done((bf16[8192,512]{1,0:T(8,128)(2,1)S(1)}, bf16[8192,512]{1,0:T(8,128)(2,1)}, u32[]{:S(2)}) %copy-start) | copy-done | bytes 8388632
  13.8 3.2 %collective-permute-done.5.refs_2_ = bf16[40,1024]{1,0:T(8,128)(2,1)S(1)} collective-permute-done((bf16[40,1024]{1,0:T(8,128)(2,1)S(1)}, bf16[40,1024]{1,0:T(8,128)(2,1)S(1)}, u32[]{:S(2)}, u32[]{:S(2)}) %collective-permute-start.5) | collective-permute-done | bytes 81952 | tf_op jit(solution)/shard_map/ppermute | solution.py:33
  17.0 0.6 collective-permute-start.8
  17.6 3.8 %collective-permute-start.13 = (bf16[40,1792]{1,0:T(8,128)(2,1)S(1)}, bf16[40,1792]{1,0:T(8,128)(2,1)S(1)}, u32[]{:S(2)}, u32[]{:S(2)}) collective-permute-start(bf16[40,1792]{1,0:T(8,128)(2,1)S(1)} %get-tuple-element.14.own_ref), channel_id=1, source_target_pairs={{0,12},{1,13},{2,14},{3,15},{4,0},{5,1},{6,2},{7,3},{8,4},{9,5},{1... | collective-permute-start | bytes 430088 | tf_op jit(solution)/shard_map/ppermute | solution.py:33
  22.0 4.1 %collective-permute-done.1.refs_3_.refs_0_ = bf16[40,1792]{1,0:T(8,128)(2,1)S(1)} collective-permute-done((bf16[40,1792]{1,0:T(8,128)(2,1)S(1)}, bf16[40,1792]{1,0:T(8,128)(2,1)S(1)}, u32[]{:S(2)}, u32[]{:S(2)}) %collective-permute-start.1) | collective-permute-done | bytes 143392 | tf_op jit(solution)/shard_map/ppermute | solution.py:33
  26.6 9.5 %collective-permute-done.12.refs_1_ = bf16[40,1792]{1,0:T(8,128)(2,1)S(1)} collective-permute-done((bf16[40,1792]{1,0:T(8,128)(2,1)S(1)}, bf16[40,1792]{1,0:T(8,128)(2,1)S(1)}, u32[]{:S(2)}, u32[]{:S(2)}) %collective-permute-start.12) | collective-permute-done | bytes 143392 | tf_op jit(solution)/shard_map/ppermute | solution.py:33
  36.2 1.6 %collective-permute-start.15 = (bf16[3,40,1792]{2,1,0:T(8,128)(2,1)S(1)}, bf16[3,40,1792]{2,1,0:T(8,128)(2,1)S(1)}, u32[]{:S(2)}, u32[]{:S(2)}) collective-permute-start(bf16[3,40,1792]{2,1,0:T(8,128)(2,1)S(1)} %pile.5.refs_0_.z_ref), channel_id=1, source_target_pairs={{0,2},{1,3},{2,0},{3,1},{4,6},{5,7},{6,4},{7,5},{8,10},{9,11},{10,... | collective-permute-start | bytes 1290248 | tf_op jit(solution)/shard_map/ppermute | solution.py:33
  37.8 0.7 collective-permute-start.2
  38.5 2.3 %rotate_out.1.refs_3_.refs_0_ = bf16[80,512]{1,0:T(8,128)(2,1)S(1)} custom-call(bf16[4,40,1024]{2,1,0:T(8,128)(2,1)S(1)} %pile.4.z_ref, bf16[4,40,1024]{2,1,0:T(8,128)(2,1)S(1)} %collective-permute-done.8.y_ref, bf16[4,40,1024]{2,1,0:T(8,128)(2,1)S(1)} %collective-permute-done.9.cz_ref, bf16[4,40,1024]{2,1,0:T(8,128)(2,1)S(1)} %collective-permute-done.10.cy_ref, ...), custom_call_target="tpu_custom_call" | custom-call | flops 671088640 | bytes 8388608 | tf_op jit(solution)/shard_map/rotate_out/pallas_call | solution.py:105
  40.8 2.6 %collective-permute-done.3.refs_2_ = bf16[40,1792]{1,0:T(8,128)(2,1)S(1)} collective-permute-done((bf16[40,1792]{1,0:T(8,128)(2,1)S(1)}, bf16[40,1792]{1,0:T(8,128)(2,1)S(1)}, u32[]{:S(2)}, u32[]{:S(2)}) %collective-permute-start.3) | collective-permute-done | bytes 143392 | tf_op jit(solution)/shard_map/ppermute | solution.py:33
  43.4 4.3 %collective-permute-done.2.refs_1_ = bf16[40,1792]{1,0:T(8,128)(2,1)S(1)} collective-permute-done((bf16[40,1792]{1,0:T(8,128)(2,1)S(1)}, bf16[40,1792]{1,0:T(8,128)(2,1)S(1)}, u32[]{:S(2)}, u32[]{:S(2)}) %collective-permute-start.2) | collective-permute-done | bytes 143392 | tf_op jit(solution)/shard_map/ppermute | solution.py:33
  48.3 2.8 %collective-permute-start.19 = (bf16[80,512]{1,0:T(8,128)(2,1)S(1)}, bf16[80,512]{1,0:T(8,128)(2,1)S(1)}, u32[]{:S(2)}, u32[]{:S(2)}) collective-permute-start(bf16[80,512]{1,0:T(8,128)(2,1)S(1)} %rotate_out.1.refs_3_.refs_0_), channel_id=1, source_target_pairs={{0,12},{1,13},{2,14},{3,15},{4,0},{5,1},{6,2},{7,3},{8,4},{9,5},{1... | collective-permute-start | bytes 245768 | tf_op jit(solution)/shard_map/ppermute | solution.py:33
  51.7 2.8 %rotate_in.2.refs_0_.refs_4_ = f32[192,40]{1,0:T(8,128)S(1)} custom-call(bf16[40,1792]{1,0:T(8,128)(2,1)S(1)} %get-tuple-element.14.own_ref, bf16[2,40,1792]{2,1,0:T(8,128)(2,1)S(1)} %collective-permute-done.refs_4_.across_ref, bf16[3,40,1792]{2,1,0:T(8,128)(2,1)S(1)} %pile.5.refs_0_.z_ref, bf16[3,40,1792]{2,1,0:T(8,128)(2,1)S(1)} %collective-permute-done.15.y_ref, ...), custom_call_target="tpu_custom_call" | custom-call | flops 220200960 | bytes 5505024 | tf_op jit(solution)/shard_map/rotate_in/pallas_call | solution.py:171
  54.6 4.0 %collective-permute-done.18.refs_2_ = bf16[80,512]{1,0:T(8,128)(2,1)S(1)} collective-permute-done((bf16[80,512]{1,0:T(8,128)(2,1)S(1)}, bf16[80,512]{1,0:T(8,128)(2,1)S(1)}, u32[]{:S(2)}, u32[]{:S(2)}) %collective-permute-start.18) | collective-permute-done | bytes 81952 | tf_op jit(solution)/shard_map/ppermute | solution.py:33
  58.6 1.6 %collective-permute-start.20 = (bf16[4,80,512]{2,1,0:T(8,128)(2,1)S(1)}, bf16[4,80,512]{2,1,0:T(8,128)(2,1)S(1)}, u32[]{:S(2)}, u32[]{:S(2)}) collective-permute-start(bf16[4,80,512]{2,1,0:T(8,128)(2,1)S(1)} %pile.7.z_ref), channel_id=1, source_target_pairs={{0,2},{1,3},{2,0},{3,1},{4,6},{5,7},{6,4},{7,5},{8,10},{9,11},{10,... | collective-permute-start | bytes 983048 | tf_op jit(solution)/shard_map/ppermute | solution.py:33
  60.2 2.8 %rotate_in.3 = (bf16[96,40]{1,0:T(8,128)(2,1)S(1)}, bf16[96,40]{1,0:T(8,128)(2,1)S(1)}) custom-call(bf16[40,1792]{1,0:T(8,128)(2,1)S(1)} %get-tuple-element.11.own_ref, bf16[2,40,1792]{2,1,0:T(8,128)(2,1)S(1)} %collective-permute-done.refs_4_.across_ref, bf16[3,40,1792]{2,1,0:T(8,128)(2,1)S(1)} %pile.6.z_ref.refs_5_, ...), custom_call_target="tpu_custom_call" | custom-call | flops 220200960 | bytes 5505024 | tf_op jit(solution)/shard_map/rotate_in/pallas_call | solution.py:171
  63.6 4.6 %collective-permute-done.20.refs_0_ = bf16[4,80,512]{2,1,0:T(8,128)(2,1)S(1)} collective-permute-done((bf16[4,80,512]{2,1,0:T(8,128)(2,1)S(1)}, bf16[4,80,512]{2,1,0:T(8,128)(2,1)S(1)}, u32[]{:S(2)}, u32[]{:S(2)}) %collective-permute-start.20) | collective-permute-done | bytes 327712 | tf_op jit(solution)/shard_map/ppermute | solution.py:33
  68.2 1.7 %combine.1._ = bf16[96,8192]{1,0:T(8,128)(2,1)} custom-call(bf16[96,40]{1,0:T(8,128)(2,1)S(1)} %get-tuple-element.15.own_ref, bf16[96,40]{1,0:T(8,128)(2,1)S(1)} %collective-permute-done.16.refs_1_.other_ref, bf16[4,80,512]{2,1,0:T(8,128)(2,1)S(1)} %pile.7.z_ref, bf16[4,80,512]{2,1,0:T(8,128)(2,1)S(1)} %after.1.y_ref, ...), custom_call_target="tpu_custom_call" | custom-call | flops 125829120 | bytes 3145728 | tf_op jit(solution)/shard_map/combine/pallas_call | solution.py:308
  69.8 1.0 %finish.1 = bf16[96,8192]{1,0:T(8,128)(2,1)} custom-call(bf16[96,40]{1,0:T(8,128)(2,1)S(1)} %get-tuple-element.15.own_ref, bf16[96,40]{1,0:T(8,128)(2,1)S(1)} %collective-permute-done.16.refs_1_.other_ref, bf16[4,80,512]{2,1,0:T(8,128)(2,1)S(1)} %collective-permute-done.21.cy_ref, bf16[96,8192]{1,0:T(8,128)(2,1)} %combine.1._), custom_call_target="tpu_custom_call", output_to_operand_aliasing={{}: (3, {})} | custom-call | flops 31457280 | bytes 655360 | tf_op jit(solution)/shard_map/finish/pallas_call | solution.py:339
  (45 shorter events, 4.3 us)
Async XLA Ops:
  0.0 17.0 %collective-permute-start.7 = (bf16[96,28672]{1,0:T(8,128)(2,1)}, bf16[96,28672]{1,0:T(8,128)(2,1)S(1)}, u32[]{:S(2)}, u32[]{:S(2)}) collective-permute-start(bf16[96,28672]{1,0:T(8,128)(2,1)} %bitcast.1), channel_id=1, source_target_pairs={{0,1},{1,0},{2,3},{3,2},{4,5},{5,4},{6,7},{7,6},{8,9},{9,8},{10,11... | collective-permute-start | bytes 16515080 | tf_op jit(solution)/shard_map/ppermute | solution.py:33
  2.7 14.3 %collective-permute-start = (bf16[2,40,1792]{2,1,0:T(8,128)(2,1)S(1)}, bf16[2,40,1792]{2,1,0:T(8,128)(2,1)S(1)}, u32[]{:S(2)}, u32[]{:S(2)}) collective-permute-start(bf16[2,40,1792]{2,1,0:T(8,128)(2,1)S(1)} %get-tuple-element.12), channel_id=1, source_target_pairs={{0,2},{1,3},{2,0},{3,1},{4,6},{5,7},{6,4},{7,5},{8,10},{9,11},{10,... | collective-permute-start | bytes 860168 | tf_op jit(solution)/shard_map/ppermute | solution.py:33
  5.2 8.6 %collective-permute-start.6 = (bf16[40,1024]{1,0:T(8,128)(2,1)S(1)}, bf16[40,1024]{1,0:T(8,128)(2,1)S(1)}, u32[]{:S(2)}, u32[]{:S(2)}) collective-permute-start(bf16[40,1024]{1,0:T(8,128)(2,1)S(1)} %get-tuple-element.13.refs_0_), channel_id=1, source_target_pairs={{0,12},{1,13},{2,14},{3,15},{4,0},{5,1},{6,2},{7,3},{8,4},{9,5},{1... | collective-permute-start | bytes 245768 | tf_op jit(solution)/shard_map/ppermute | solution.py:33
  8.9 8.1 %collective-permute-start.5 = (bf16[40,1024]{1,0:T(8,128)(2,1)S(1)}, bf16[40,1024]{1,0:T(8,128)(2,1)S(1)}, u32[]{:S(2)}, u32[]{:S(2)}) collective-permute-start(bf16[40,1024]{1,0:T(8,128)(2,1)S(1)} %get-tuple-element.13.refs_0_), channel_id=1, source_target_pairs={{0,8},{1,9},{2,10},{3,11},{4,12},{5,13},{6,14},{7,15},{8,0},{9,1},... | collective-permute-start | bytes 245768 | tf_op jit(solution)/shard_map/ppermute | solution.py:33
  8.9 8.1 %collective-permute-start.4 = (bf16[40,1024]{1,0:T(8,128)(2,1)S(1)}, bf16[40,1024]{1,0:T(8,128)(2,1)S(1)}, u32[]{:S(2)}, u32[]{:S(2)}) collective-permute-start(bf16[40,1024]{1,0:T(8,128)(2,1)S(1)} %get-tuple-element.13.refs_0_), channel_id=1, source_target_pairs={{0,4},{1,5},{2,6},{3,7},{4,8},{5,9},{6,10},{7,11},{8,12},{9,13},{1... | collective-permute-start | bytes 245768 | tf_op jit(solution)/shard_map/ppermute | solution.py:33
  17.0 9.6 %collective-permute-start.8 = (bf16[4,40,1024]{2,1,0:T(8,128)(2,1)S(1)}, bf16[4,40,1024]{2,1,0:T(8,128)(2,1)S(1)}, u32[]{:S(2)}, u32[]{:S(2)}) collective-permute-start(bf16[4,40,1024]{2,1,0:T(8,128)(2,1)S(1)} %pile.4.z_ref), channel_id=1, source_target_pairs={{0,2},{1,3},{2,0},{3,1},{4,6},{5,7},{6,4},{7,5},{8,10},{9,11},{10,... | collective-permute-start | bytes 983048 | tf_op jit(solution)/shard_map/ppermute | solution.py:33
  17.6 8.5 %collective-permute-start.1 = (bf16[40,1792]{1,0:T(8,128)(2,1)S(1)}, bf16[40,1792]{1,0:T(8,128)(2,1)S(1)}, u32[]{:S(2)}, u32[]{:S(2)}) collective-permute-start(bf16[40,1792]{1,0:T(8,128)(2,1)S(1)} %get-tuple-element.11.own_ref), channel_id=1, source_target_pairs={{0,4},{1,5},{2,6},{3,7},{4,8},{5,9},{6,10},{7,11},{8,12},{9,13},{1... | collective-permute-start | bytes 430088 | tf_op jit(solution)/shard_map/ppermute | solution.py:33
  17.6 9.0 %collective-permute-start.13 = (bf16[40,1792]{1,0:T(8,128)(2,1)S(1)}, bf16[40,1792]{1,0:T(8,128)(2,1)S(1)}, u32[]{:S(2)}, u32[]{:S(2)}) collective-permute-start(bf16[40,1792]{1,0:T(8,128)(2,1)S(1)} %get-tuple-element.14.own_ref), channel_id=1, source_target_pairs={{0,12},{1,13},{2,14},{3,15},{4,0},{5,1},{6,2},{7,3},{8,4},{9,5},{1... | collective-permute-start | bytes 430088 | tf_op jit(solution)/shard_map/ppermute | solution.py:33
  21.4 14.7 %collective-permute-start.12 = (bf16[40,1792]{1,0:T(8,128)(2,1)S(1)}, bf16[40,1792]{1,0:T(8,128)(2,1)S(1)}, u32[]{:S(2)}, u32[]{:S(2)}) collective-permute-start(bf16[40,1792]{1,0:T(8,128)(2,1)S(1)} %get-tuple-element.14.own_ref), channel_id=1, source_target_pairs={{0,8},{1,9},{2,10},{3,11},{4,12},{5,13},{6,14},{7,15},{8,0},{9,1},... | collective-permute-start | bytes 430088 | tf_op jit(solution)/shard_map/ppermute | solution.py:33
  21.5 14.7 %collective-permute-start.11 = (bf16[40,1792]{1,0:T(8,128)(2,1)S(1)}, bf16[40,1792]{1,0:T(8,128)(2,1)S(1)}, u32[]{:S(2)}, u32[]{:S(2)}) collective-permute-start(bf16[40,1792]{1,0:T(8,128)(2,1)S(1)} %get-tuple-element.14.own_ref), channel_id=1, source_target_pairs={{0,4},{1,5},{2,6},{3,7},{4,8},{5,9},{6,10},{7,11},{8,12},{9,13},{1... | collective-permute-start | bytes 430088 | tf_op jit(solution)/shard_map/ppermute | solution.py:33
  26.1 12.4 %collective-permute-start.9 = (bf16[4,40,1024]{2,1,0:T(8,128)(2,1)S(1)}, bf16[4,40,1024]{2,1,0:T(8,128)(2,1)S(1)}, u32[]{:S(2)}, u32[]{:S(2)}) collective-permute-start(bf16[4,40,1024]{2,1,0:T(8,128)(2,1)S(1)} %pile.4.z_ref), channel_id=1, source_target_pairs={{0,1},{1,0},{2,3},{3,2},{4,5},{5,4},{6,7},{7,6},{8,9},{9,8},{10,11... | collective-permute-start | bytes 983048 | tf_op jit(solution)/shard_map/ppermute | solution.py:33
  26.6 11.9 %collective-permute-start.10 = (bf16[4,40,1024]{2,1,0:T(8,128)(2,1)S(1)}, bf16[4,40,1024]{2,1,0:T(8,128)(2,1)S(1)}, u32[]{:S(2)}, u32[]{:S(2)}) collective-permute-start(bf16[4,40,1024]{2,1,0:T(8,128)(2,1)S(1)} %collective-permute-done.8.y_ref), channel_id=1, source_target_pairs={{0,1},{1,0},{2,3},{3,2},{4,5},{5,4},{6,7},{7,6},{8,9},{9,8},{10,11... | collective-permute-start | bytes 983048 | tf_op jit(solution)/shard_map/ppermute | solution.py:33
  36.2 15.6 %slice-start = ((s8[5505024]{0:T(1024)(128)(4,1)}), s8[4194304]{0:T(1024)(128)(4,1)S(1)}, s32[]{:S(2)}) async-start(s8[5505024]{0:T(1024)(128)(4,1)} %bitcast.2), calls=%async_computation | async-start | bytes 8388608
  36.2 15.5 %collective-permute-start.15 = (bf16[3,40,1792]{2,1,0:T(8,128)(2,1)S(1)}, bf16[3,40,1792]{2,1,0:T(8,128)(2,1)S(1)}, u32[]{:S(2)}, u32[]{:S(2)}) collective-permute-start(bf16[3,40,1792]{2,1,0:T(8,128)(2,1)S(1)} %pile.5.refs_0_.z_ref), channel_id=1, source_target_pairs={{0,2},{1,3},{2,0},{3,1},{4,6},{5,7},{6,4},{7,5},{8,10},{9,11},{10,... | collective-permute-start | bytes 1290248 | tf_op jit(solution)/shard_map/ppermute | solution.py:33
  37.8 5.6 %collective-permute-start.3 = (bf16[40,1792]{1,0:T(8,128)(2,1)S(1)}, bf16[40,1792]{1,0:T(8,128)(2,1)S(1)}, u32[]{:S(2)}, u32[]{:S(2)}) collective-permute-start(bf16[40,1792]{1,0:T(8,128)(2,1)S(1)} %get-tuple-element.11.own_ref), channel_id=1, source_target_pairs={{0,12},{1,13},{2,14},{3,15},{4,0},{5,1},{6,2},{7,3},{8,4},{9,5},{1... | collective-permute-start | bytes 430088 | tf_op jit(solution)/shard_map/ppermute | solution.py:33
  37.8 9.9 %collective-permute-start.2 = (bf16[40,1792]{1,0:T(8,128)(2,1)S(1)}, bf16[40,1792]{1,0:T(8,128)(2,1)S(1)}, u32[]{:S(2)}, u32[]{:S(2)}) collective-permute-start(bf16[40,1792]{1,0:T(8,128)(2,1)S(1)} %get-tuple-element.11.own_ref), channel_id=1, source_target_pairs={{0,8},{1,9},{2,10},{3,11},{4,12},{5,13},{6,14},{7,15},{8,0},{9,1},... | collective-permute-start | bytes 430088 | tf_op jit(solution)/shard_map/ppermute | solution.py:33
  47.7 12.5 %collective-permute-start.14 = (bf16[3,40,1792]{2,1,0:T(8,128)(2,1)S(1)}, bf16[3,40,1792]{2,1,0:T(8,128)(2,1)S(1)}, u32[]{:S(2)}, u32[]{:S(2)}) collective-permute-start(bf16[3,40,1792]{2,1,0:T(8,128)(2,1)S(1)} %pile.6.z_ref.refs_5_), channel_id=1, source_target_pairs={{0,2},{1,3},{2,0},{3,1},{4,6},{5,7},{6,4},{7,5},{8,10},{9,11},{10,... | collective-permute-start | bytes 1290248 | tf_op jit(solution)/shard_map/ppermute | solution.py:33
  48.3 6.2 %collective-permute-start.19 = (bf16[80,512]{1,0:T(8,128)(2,1)S(1)}, bf16[80,512]{1,0:T(8,128)(2,1)S(1)}, u32[]{:S(2)}, u32[]{:S(2)}) collective-permute-start(bf16[80,512]{1,0:T(8,128)(2,1)S(1)} %rotate_out.1.refs_3_.refs_0_), channel_id=1, source_target_pairs={{0,12},{1,13},{2,14},{3,15},{4,0},{5,1},{6,2},{7,3},{8,4},{9,5},{1... | collective-permute-start | bytes 245768 | tf_op jit(solution)/shard_map/ppermute | solution.py:33
  51.1 7.4 %collective-permute-start.18 = (bf16[80,512]{1,0:T(8,128)(2,1)S(1)}, bf16[80,512]{1,0:T(8,128)(2,1)S(1)}, u32[]{:S(2)}, u32[]{:S(2)}) collective-permute-start(bf16[80,512]{1,0:T(8,128)(2,1)S(1)} %rotate_out.1.refs_3_.refs_0_), channel_id=1, source_target_pairs={{0,8},{1,9},{2,10},{3,11},{4,12},{5,13},{6,14},{7,15},{8,0},{9,1},... | collective-permute-start | bytes 245768 | tf_op jit(solution)/shard_map/ppermute | solution.py:33
  51.1 7.4 %collective-permute-start.17 = (bf16[80,512]{1,0:T(8,128)(2,1)S(1)}, bf16[80,512]{1,0:T(8,128)(2,1)S(1)}, u32[]{:S(2)}, u32[]{:S(2)}) collective-permute-start(bf16[80,512]{1,0:T(8,128)(2,1)S(1)} %rotate_out.1.refs_3_.refs_0_), channel_id=1, source_target_pairs={{0,4},{1,5},{2,6},{3,7},{4,8},{5,9},{6,10},{7,11},{8,12},{9,13},{1... | collective-permute-start | bytes 245768 | tf_op jit(solution)/shard_map/ppermute | solution.py:33
  58.6 9.5 %collective-permute-start.20 = (bf16[4,80,512]{2,1,0:T(8,128)(2,1)S(1)}, bf16[4,80,512]{2,1,0:T(8,128)(2,1)S(1)}, u32[]{:S(2)}, u32[]{:S(2)}) collective-permute-start(bf16[4,80,512]{2,1,0:T(8,128)(2,1)S(1)} %pile.7.z_ref), channel_id=1, source_target_pairs={{0,2},{1,3},{2,0},{3,1},{4,6},{5,7},{6,4},{7,5},{8,10},{9,11},{10,... | collective-permute-start | bytes 983048 | tf_op jit(solution)/shard_map/ppermute | solution.py:33
  60.2 8.0 %collective-permute-start.22 = (bf16[4,80,512]{2,1,0:T(8,128)(2,1)S(1)}, bf16[4,80,512]{2,1,0:T(8,128)(2,1)S(1)}, u32[]{:S(2)}, u32[]{:S(2)}) collective-permute-start(bf16[4,80,512]{2,1,0:T(8,128)(2,1)S(1)} %pile.7.z_ref), channel_id=1, source_target_pairs={{0,1},{1,0},{2,3},{3,2},{4,5},{5,4},{6,7},{7,6},{8,9},{9,8},{10,11... | collective-permute-start | bytes 983048 | tf_op jit(solution)/shard_map/ppermute | solution.py:33
  63.0 5.1 %collective-permute-start.16 = (bf16[96,40]{1,0:T(8,128)(2,1)S(1)}, bf16[96,40]{1,0:T(8,128)(2,1)S(1)}, u32[]{:S(2)}, u32[]{:S(2)}) collective-permute-start(bf16[96,40]{1,0:T(8,128)(2,1)S(1)} %get-tuple-element.16), channel_id=1, source_target_pairs={{0,1},{1,0},{2,3},{3,2},{4,5},{5,4},{6,7},{7,6},{8,9},{9,8},{10,11... | collective-permute-start | bytes 23048 | tf_op jit(solution)/shard_map/ppermute | solution.py:33
  68.2 1.7 %collective-permute-start.21 = (bf16[4,80,512]{2,1,0:T(8,128)(2,1)S(1)}, bf16[4,80,512]{2,1,0:T(8,128)(2,1)S(1)}, u32[]{:S(2)}, u32[]{:S(2)}) collective-permute-start(bf16[4,80,512]{2,1,0:T(8,128)(2,1)S(1)} %after.1.y_ref), channel_id=1, source_target_pairs={{0,1},{1,0},{2,3},{3,2},{4,5},{5,4},{6,7},{7,6},{8,9},{9,8},{10,11... | collective-permute-start | bytes 983048 | tf_op jit(solution)/shard_map/ppermute | solution.py:33
  (4 other events, 20.8 us)

commit v14 on v13

--- a/solution.py
+++ b/solution.py
@@ -287,45 +287,50 @@
     return (total / block.shape[0]).astype(jnp.bfloat16)
 
 
-def combine_kernel(own_ref, other_ref, z_ref, y_ref, cz_ref, out_ref):
-    steps, _, width = z_ref.shape
+def put_all(left, out_ref, steps, pieces):
     devices = steps * CORES * PAIR
     me = lax.axis_index("wide")
-    left = both_classes(own_ref, other_ref)
-    for ref, chip_bit, core_bit in ((z_ref, 0, 0), (y_ref, 1, 0), (cz_ref, 0, 1)):
-
-        def put(step, _, ref=ref, chip_bit=chip_bit, core_bit=core_bit):
-            chip, core = origin(me, devices, step, chip_bit, core_bit)
+    for ref, first, chip_bit, core_bit in pieces:
+
+        def put(step, _, ref=ref, first=first, chip_bit=chip_bit, core_bit=core_bit):
+            chip, core = origin(me, devices, step + first, chip_bit, core_bit)
+            width = ref.shape[2]
             at = pl.multiple_of((chip * CORES + core) * width, 128)
             out_ref[:, pl.ds(at, width)] = eigenvalues(left, ref[step])
 
-        repeat(steps, put)
-
-
-def combine(own, other, z, y, cz):
-    steps, total_tokens, width = z.shape
-    features = steps * CORES * PAIR * width
+        repeat(ref.shape[0], put)
+
+
+def combine_kernel(own_ref, other_ref, near_ref, swapped_ref, z_ref, y_ref, cz_ref, out_ref):
+    left = both_classes(own_ref, other_ref)
+    pieces = [(ref.at[bit : bit + 1], 0, bit, core) for core, ref in enumerate((near_ref, swapped_ref)) for bit in range(PAIR)]
+    put_all(left, out_ref, z_ref.shape[0] + 1, pieces + [(z_ref, 1, 0, 0), (y_ref, 1, 1, 0), (cz_ref, 1, 0, 1)])
+
+
+def combine(own, other, near, swapped, z, y, cz):
+    blocks, total_tokens, width = z.shape
+    features = (blocks + 1) * CORES * PAIR * width
     return pl.pallas_call(
         combine_kernel,
         out_shape=jax.ShapeDtypeStruct((own.shape[0], features), jnp.bfloat16),
-        in_specs=[VMEM] * 5,
+        in_specs=[VMEM] * 7,
         out_specs=VMEM,
-        compiler_params=pltpu.CompilerParams(vmem_limit_bytes=room(6, steps)),
+        compiler_params=pltpu.CompilerParams(vmem_limit_bytes=room(6, blocks)),
         cost_estimate=pl.CostEstimate(
             flops=2 * own.shape[0] * total_tokens * features, bytes_accessed=4 * own.shape[0] * features, transcendentals=0
         ),
         name="combine",
-    )(own, other, z, y, cz)
+    )(own, other, near, swapped, z, y, cz)
 
 
 def finish_kernel(own_ref, other_ref, cy_ref, _, out_ref, blocks, done):
     steps, _, width = cy_ref.shape
-    devices = steps * CORES * PAIR
+    devices = (steps + 1) * CORES * PAIR
     me = lax.axis_index("wide")
     left = both_classes(own_ref, other_ref)
     copies = []
     for step in range(steps):
-        chip, core = origin(me, devices, step, 1, 1)
+        chip, core = origin(me, devices, step + 1, 1, 1)
         at = pl.multiple_of((chip * CORES + core) * width, 128)
         blocks[step] = eigenvalues(left, cy_ref[step])
         copies.append(pltpu.make_async_copy(blocks.at[step], out_ref.at[:, pl.ds(at, width)], done.at[step]))
@@ -376,31 +381,32 @@
 
     acts_z, acts_y = [], []
 
-    sent = [along_all(block) for block in own]
-
     def chunk_along(chunk, waits):
-        acts_z.append(pile(sent[chunk], waits))
+        acts_z.append(pile(along_all(own[chunk]), waits))
         acts_y.append(send(acts_z[-1], across(devices)))
 
     def part(chunk, before):
         return rotate_in(tokens, chunk, own[chunk], own_across, acts_z[chunk], acts_y[chunk], mine, theirs, before)
 
-    chunk_along(0, [sent[1][0]])
+    chunk_along(0, [])
+    [grads_y] = after([grads_y], [acts_z[0]])
     grads_cz, grads_cy = send(grads_z, swap(devices)), send(grads_y, swap(devices))
     sq_out = rotate_out(tokens, grads_z, grads_y, grads_cz, grads_cy, fetched, [acts_z[0]])
+    near = pile([sq_out, send(sq_out, across(devices))], [])
+    swapped = send(near, swap(devices))
     came = along_all(sq_out)
     for chunk in range(1, CHUNKS):
-        chunk_along(chunk, [sq_out])
+        chunk_along(chunk, [came[0]])
     total = part(0, [])
-    z = pile([sq_out] + came, [*total, acts_z[-1]])
+    z = pile(came, [*total, acts_z[-1], near])
     y = send(z, across(devices))
     for chunk in range(1, CHUNKS):
         total = part(chunk, total)
     sq_in, given = total
     other = send(given, swap(devices))
-    [y] = after([y], [other])
+    [y] = after([y], [other, swapped])
     cz, cy = send(z, swap(devices)), send(y, swap(devices))
-    return finish(sq_in, other, cy, combine(sq_in, other, z, y, cz))
+    return finish(sq_in, other, cy, combine(sq_in, other, near, swapped, z, y, cz))
 
 
 def solution(mesh):

time: 71.1 us -> 72.5 us (1.020)
  the two profiles are of different devices: /device:TPU:0 before, /device:TPU:9 now
where the time goes in v14:
time: 72.5 us; the launch traced here: 72.3 us
  waiting for transfers between devices  33.8 us (47%)
  starting transfers between devices  21.6 us (30%)
  Pallas kernels  11.5 us (16%)
  local copies, waits for them, and re-layouts  5.31 us (7%)
    ppermute x25, waiting for transfers between devices, send(): return lax.ppermute(block, 'wide', pairs)  33.8 us
    ppermute x25, starting transfers between devices, send(): return lax.ppermute(block, 'wide', pairs)  21.6 us
    pallas_call x2, Pallas kernels, rotate_in(): pl.pallas_call(functools.partial(rotate_in_kernel, tokens, chunk, len(bef...  5.62 us
    unnamed x10, local copies, waits for them, and re-layouts  5.31 us
    pallas_call x1, Pallas kernels, rotate_out(): pl.pallas_call(functools.partial(rotate_out_kernel, tokens, len(waits)),...  2.29 us
    pallas_call x1, Pallas kernels, combine(): pl.pallas_call(combine_kernel, out_shape=jax.ShapeDtypeStruct((own.shape[...  1.69 us
  transfers between devices with their start and end apart: 25, of which 9 were waited for; matrix products, arithmetic and copies ran while one was open for 0% of the time, Pallas kernels for 15%

profile of v14, /device:TPU:9, one launch (start us, length us, event | category | flops | bytes accessed | tf_op | source)
XLA Modules:
  0.0 72.3 jit_solution(9471753411314970351)
XLA Ops:
  0.7 1.0 %copy-done.1 = bf16[5,28672]{1,0:T(8,128)(2,1)S(1)} copy-done((bf16[5,28672]{1,0:T(8,128)(2,1)S(1)}, bf16[5,28672]{1,0:T(8,128)(2,1)}, u32[]{:S(2)}) %copy-start.1) | copy-done | bytes 286744
  2.9 1.3 %collective-permute-start = (bf16[2,40,1792]{2,1,0:T(8,128)(2,1)S(1)}, bf16[2,40,1792]{2,1,0:T(8,128)(2,1)S(1)}, u32[]{:S(2)}, u32[]{:S(2)}) collective-permute-start(bf16[2,40,1792]{2,1,0:T(8,128)(2,1)S(1)} %get-tuple-element.12), channel_id=1, source_target_pairs={{0,2},{1,3},{2,0},{3,1},{4,6},{5,7},{6,4},{7,5},{8,10},{9,11},{10,... | collective-permute-start | bytes 860168 | tf_op jit(solution)/shard_map/ppermute | solution.py:33
  4.2 1.3 %collective-permute-start.4 = (bf16[40,1024]{1,0:T(8,128)(2,1)S(1)}, bf16[40,1024]{1,0:T(8,128)(2,1)S(1)}, u32[]{:S(2)}, u32[]{:S(2)}) collective-permute-start(bf16[40,1024]{1,0:T(8,128)(2,1)S(1)} %get-tuple-element.13.refs_0_), channel_id=1, source_target_pairs={{0,4},{1,5},{2,6},{3,7},{4,8},{5,9},{6,10},{7,11},{8,12},{9,13},{1... | collective-permute-start | bytes 245768 | tf_op jit(solution)/shard_map/ppermute | solution.py:33
  6.5 1.5 %collective-permute-start.6 = (bf16[40,1024]{1,0:T(8,128)(2,1)S(1)}, bf16[40,1024]{1,0:T(8,128)(2,1)S(1)}, u32[]{:S(2)}, u32[]{:S(2)}) collective-permute-start(bf16[40,1024]{1,0:T(8,128)(2,1)S(1)} %get-tuple-element.13.refs_0_), channel_id=1, source_target_pairs={{0,12},{1,13},{2,14},{3,15},{4,0},{5,1},{6,2},{7,3},{8,4},{9,5},{1... | collective-permute-start | bytes 245768 | tf_op jit(solution)/shard_map/ppermute | solution.py:33
  8.0 3.4 %copy-done = bf16[8192,512]{1,0:T(8,128)(2,1)S(1)} copy-done((bf16[8192,512]{1,0:T(8,128)(2,1)S(1)}, bf16[8192,512]{1,0:T(8,128)(2,1)}, u32[]{:S(2)}) %copy-start) | copy-done | bytes 8388632
  12.2 2.5 %collective-permute-done.6.refs_3_ = bf16[40,1024]{1,0:T(8,128)(2,1)S(1)} collective-permute-done((bf16[40,1024]{1,0:T(8,128)(2,1)S(1)}, bf16[40,1024]{1,0:T(8,128)(2,1)S(1)}, u32[]{:S(2)}, u32[]{:S(2)}) %collective-permute-start.6) | collective-permute-done | bytes 81952 | tf_op jit(solution)/shard_map/ppermute | solution.py:33
  15.8 1.5 %collective-permute-start.9 = (bf16[40,1792]{1,0:T(8,128)(2,1)S(1)}, bf16[40,1792]{1,0:T(8,128)(2,1)S(1)}, u32[]{:S(2)}, u32[]{:S(2)}) collective-permute-start(bf16[40,1792]{1,0:T(8,128)(2,1)S(1)} %get-tuple-element.14.own_ref), channel_id=1, source_target_pairs={{0,4},{1,5},{2,6},{3,7},{4,8},{5,9},{6,10},{7,11},{8,12},{9,13},{1... | collective-permute-start | bytes 430088 | tf_op jit(solution)/shard_map/ppermute | solution.py:33
  17.2 7.7 %collective-permute-done.10.refs_1_ = bf16[40,1792]{1,0:T(8,128)(2,1)S(1)} collective-permute-done((bf16[40,1792]{1,0:T(8,128)(2,1)S(1)}, bf16[40,1792]{1,0:T(8,128)(2,1)S(1)}, u32[]{:S(2)}, u32[]{:S(2)}) %collective-permute-start.10) | collective-permute-done | bytes 143392 | tf_op jit(solution)/shard_map/ppermute | solution.py:33
  25.6 2.4 %collective-permute-done.9.refs_0_ = bf16[40,1792]{1,0:T(8,128)(2,1)S(1)} collective-permute-done((bf16[40,1792]{1,0:T(8,128)(2,1)S(1)}, bf16[40,1792]{1,0:T(8,128)(2,1)S(1)}, u32[]{:S(2)}, u32[]{:S(2)}) %collective-permute-start.9) | collective-permute-done | bytes 143392 | tf_op jit(solution)/shard_map/ppermute | solution.py:33
  28.0 1.7 %collective-permute-start.12 = (bf16[4,40,1024]{2,1,0:T(8,128)(2,1)S(1)}, bf16[4,40,1024]{2,1,0:T(8,128)(2,1)S(1)}, u32[]{:S(2)}, u32[]{:S(2)}) collective-permute-start(bf16[4,40,1024]{2,1,0:T(8,128)(2,1)S(1)} %pile.5.z_ref), channel_id=1, source_target_pairs={{0,1},{1,0},{2,3},{3,2},{4,5},{5,4},{6,7},{7,6},{8,9},{9,8},{10,11... | collective-permute-start | bytes 983048 | tf_op jit(solution)/shard_map/ppermute | solution.py:33
  29.8 1.2 %collective-permute-start.16 = (bf16[3,40,1792]{2,1,0:T(8,128)(2,1)S(1)}, bf16[3,40,1792]{2,1,0:T(8,128)(2,1)S(1)}, u32[]{:S(2)}, u32[]{:S(2)}) collective-permute-start(bf16[3,40,1792]{2,1,0:T(8,128)(2,1)S(1)} %pile.6.refs_1_.refs_0_.z_ref), channel_id=1, source_target_pairs={{0,2},{1,3},{2,0},{3,1},{4,6},{5,7},{6,4},{7,5},{8,10},{9,11},{10,... | collective-permute-start | bytes 1290248 | tf_op jit(solution)/shard_map/ppermute | solution.py:33
  31.0 1.1 %collective-permute-start.1 = (bf16[40,1792]{1,0:T(8,128)(2,1)S(1)}, bf16[40,1792]{1,0:T(8,128)(2,1)S(1)}, u32[]{:S(2)}, u32[]{:S(2)}) collective-permute-start(bf16[40,1792]{1,0:T(8,128)(2,1)S(1)} %get-tuple-element.11.own_ref), channel_id=1, source_target_pairs={{0,4},{1,5},{2,6},{3,7},{4,8},{5,9},{6,10},{7,11},{8,12},{9,13},{1... | collective-permute-start | bytes 430088 | tf_op jit(solution)/shard_map/ppermute | solution.py:33
  32.1 1.0 %collective-permute-start.2 = (bf16[40,1792]{1,0:T(8,128)(2,1)S(1)}, bf16[40,1792]{1,0:T(8,128)(2,1)S(1)}, u32[]{:S(2)}, u32[]{:S(2)}) collective-permute-start(bf16[40,1792]{1,0:T(8,128)(2,1)S(1)} %get-tuple-element.11.own_ref), channel_id=1, source_target_pairs={{0,8},{1,9},{2,10},{3,11},{4,12},{5,13},{6,14},{7,15},{8,0},{9,1},... | collective-permute-start | bytes 430088 | tf_op jit(solution)/shard_map/ppermute | solution.py:33
  33.3 2.3 %rotate_out.1.refs_0_ = bf16[80,512]{1,0:T(8,128)(2,1)S(1)} custom-call(bf16[4,40,1024]{2,1,0:T(8,128)(2,1)S(1)} %pile.5.z_ref, bf16[4,40,1024]{2,1,0:T(8,128)(2,1)S(1)} %after.2.y_ref, bf16[4,40,1024]{2,1,0:T(8,128)(2,1)S(1)} %collective-permute-done.12.cz_ref, bf16[4,40,1024]{2,1,0:T(8,128)(2,1)S(1)} %collective-permute-done.13.cy_ref, ...), custom_call_target="tpu_custom_call" | custom-call | flops 671088640 | bytes 8388608 | tf_op jit(solution)/shard_map/rotate_out/pallas_call | solution.py:105
  35.6 1.4 %collective-permute-start.14 = (bf16[80,512]{1,0:T(8,128)(2,1)S(1)}, bf16[80,512]{1,0:T(8,128)(2,1)S(1)}, u32[]{:S(2)}, u32[]{:S(2)}) collective-permute-start(bf16[80,512]{1,0:T(8,128)(2,1)S(1)} %rotate_out.1.refs_0_), channel_id=1, source_target_pairs={{0,4},{1,5},{2,6},{3,7},{4,8},{5,9},{6,10},{7,11},{8,12},{9,13},{1... | collective-permute-start | bytes 245768 | tf_op jit(solution)/shard_map/ppermute | solution.py:33
  36.9 6.8 %collective-permute-done.2.refs_1_ = bf16[40,1792]{1,0:T(8,128)(2,1)S(1)} collective-permute-done((bf16[40,1792]{1,0:T(8,128)(2,1)S(1)}, bf16[40,1792]{1,0:T(8,128)(2,1)S(1)}, u32[]{:S(2)}, u32[]{:S(2)}) %collective-permute-start.2) | collective-permute-done | bytes 143392 | tf_op jit(solution)/shard_map/ppermute | solution.py:33
  43.7 4.6 %collective-permute-done.3.refs_2_ = bf16[40,1792]{1,0:T(8,128)(2,1)S(1)} collective-permute-done((bf16[40,1792]{1,0:T(8,128)(2,1)S(1)}, bf16[40,1792]{1,0:T(8,128)(2,1)S(1)}, u32[]{:S(2)}, u32[]{:S(2)}) %collective-permute-start.3) | collective-permute-done | bytes 143392 | tf_op jit(solution)/shard_map/ppermute | solution.py:33
  48.6 1.2 %collective-permute-start.20 = (bf16[80,512]{1,0:T(8,128)(2,1)S(1)}, bf16[80,512]{1,0:T(8,128)(2,1)S(1)}, u32[]{:S(2)}, u32[]{:S(2)}) collective-permute-start(bf16[80,512]{1,0:T(8,128)(2,1)S(1)} %rotate_out.1.refs_0_), channel_id=1, source_target_pairs={{0,2},{1,3},{2,0},{3,1},{4,6},{5,7},{6,4},{7,5},{8,10},{9,11},{10,... | collective-permute-start | bytes 245768 | tf_op jit(solution)/shard_map/ppermute | solution.py:33
  50.3 2.8 %rotate_in.2.refs_0_.refs_3_ = f32[192,40]{1,0:T(8,128)S(1)} custom-call(bf16[40,1792]{1,0:T(8,128)(2,1)S(1)} %get-tuple-element.14.own_ref, bf16[2,40,1792]{2,1,0:T(8,128)(2,1)S(1)} %collective-permute-done.refs_4_.across_ref, bf16[3,40,1792]{2,1,0:T(8,128)(2,1)S(1)} %pile.6.refs_1_.refs_0_.z_ref, bf16[3,40,1792]{2,1,0:T(8,128)(2,1)S(1)} %collective-permute-done.16.y_ref, ...), custom_call_target="tpu_custom_call" | custom-call | flops 220200960 | bytes 5505024 | tf_op jit(solution)/shard_map/rotate_in/pallas_call | solution.py:171
  53.2 8.0 %collective-permute-done.20.refs_1_ = bf16[80,512]{1,0:T(8,128)(2,1)S(1)} collective-permute-done((bf16[80,512]{1,0:T(8,128)(2,1)S(1)}, bf16[80,512]{1,0:T(8,128)(2,1)S(1)}, u32[]{:S(2)}, u32[]{:S(2)}) %collective-permute-start.20) | collective-permute-done | bytes 81952 | tf_op jit(solution)/shard_map/ppermute | solution.py:33
  61.5 1.6 %collective-permute-start.22 = (bf16[2,80,512]{2,1,0:T(8,128)(2,1)S(1)}, bf16[2,80,512]{2,1,0:T(8,128)(2,1)S(1)}, u32[]{:S(2)}, u32[]{:S(2)}) collective-permute-start(bf16[2,80,512]{2,1,0:T(8,128)(2,1)S(1)} %pile.8.refs_5_.near_ref), channel_id=1, source_target_pairs={{0,1},{1,0},{2,3},{3,2},{4,5},{5,4},{6,7},{7,6},{8,9},{9,8},{10,11... | collective-permute-start | bytes 491528 | tf_op jit(solution)/shard_map/ppermute | solution.py:33
  63.1 2.8 %rotate_in.3 = (bf16[96,40]{1,0:T(8,128)(2,1)S(1)}, bf16[96,40]{1,0:T(8,128)(2,1)S(1)}) custom-call(bf16[40,1792]{1,0:T(8,128)(2,1)S(1)} %get-tuple-element.11.own_ref, bf16[2,40,1792]{2,1,0:T(8,128)(2,1)S(1)} %collective-permute-done.refs_4_.across_ref, bf16[3,40,1792]{2,1,0:T(8,128)(2,1)S(1)} %pile.7.z_ref.refs_4_, ...), custom_call_target="tpu_custom_call" | custom-call | flops 220200960 | bytes 5505024 | tf_op jit(solution)/shard_map/rotate_in/pallas_call | solution.py:171
  67.4 2.3 %collective-permute-start.23 = (bf16[3,80,512]{2,1,0:T(8,128)(2,1)S(1)}, bf16[3,80,512]{2,1,0:T(8,128)(2,1)S(1)}, u32[]{:S(2)}, u32[]{:S(2)}) collective-permute-start(bf16[3,80,512]{2,1,0:T(8,128)(2,1)S(1)} %after.3.y_ref), channel_id=1, source_target_pairs={{0,1},{1,0},{2,3},{3,2},{4,5},{5,4},{6,7},{7,6},{8,9},{9,8},{10,11... | collective-permute-start | bytes 737288 | tf_op jit(solution)/shard_map/ppermute | solution.py:33
  69.7 1.7 %combine.1._ = bf16[96,8192]{1,0:T(8,128)(2,1)} custom-call(bf16[96,40]{1,0:T(8,128)(2,1)S(1)} %get-tuple-element.15.own_ref, bf16[96,40]{1,0:T(8,128)(2,1)S(1)} %collective-permute-done.17.refs_1_.other_ref, bf16[2,80,512]{2,1,0:T(8,128)(2,1)S(1)} %pile.8.refs_5_.near_ref, bf16[2,80,512]{2,1,0:T(8,128)(2,1)S(1)} %collective-permute-done.22.refs_2_.swapped_ref, ...), custom_call_target="tpu_custom_call" | custom-call | flops 125829120 | bytes 3145728 | tf_op jit(solution)/shard_map/combine/pallas_call | solution.py:313
  (51 shorter events, 9.2 us)
Async XLA Ops:
  0.0 14.7 %collective-permute-start.7 = (bf16[96,28672]{1,0:T(8,128)(2,1)}, bf16[96,28672]{1,0:T(8,128)(2,1)S(1)}, u32[]{:S(2)}, u32[]{:S(2)}) collective-permute-start(bf16[96,28672]{1,0:T(8,128)(2,1)} %bitcast.1), channel_id=1, source_target_pairs={{0,1},{1,0},{2,3},{3,2},{4,5},{5,4},{6,7},{7,6},{8,9},{9,8},{10,11... | collective-permute-start | bytes 16515080 | tf_op jit(solution)/shard_map/ppermute | solution.py:33
  2.9 11.8 %collective-permute-start = (bf16[2,40,1792]{2,1,0:T(8,128)(2,1)S(1)}, bf16[2,40,1792]{2,1,0:T(8,128)(2,1)S(1)}, u32[]{:S(2)}, u32[]{:S(2)}) collective-permute-start(bf16[2,40,1792]{2,1,0:T(8,128)(2,1)S(1)} %get-tuple-element.12), channel_id=1, source_target_pairs={{0,2},{1,3},{2,0},{3,1},{4,6},{5,7},{6,4},{7,5},{8,10},{9,11},{10,... | collective-permute-start | bytes 860168 | tf_op jit(solution)/shard_map/ppermute | solution.py:33
  4.2 7.7 %collective-permute-start.4 = (bf16[40,1024]{1,0:T(8,128)(2,1)S(1)}, bf16[40,1024]{1,0:T(8,128)(2,1)S(1)}, u32[]{:S(2)}, u32[]{:S(2)}) collective-permute-start(bf16[40,1024]{1,0:T(8,128)(2,1)S(1)} %get-tuple-element.13.refs_0_), channel_id=1, source_target_pairs={{0,4},{1,5},{2,6},{3,7},{4,8},{5,9},{6,10},{7,11},{8,12},{9,13},{1... | collective-permute-start | bytes 245768 | tf_op jit(solution)/shard_map/ppermute | solution.py:33
  5.5 6.7 %collective-permute-start.5 = (bf16[40,1024]{1,0:T(8,128)(2,1)S(1)}, bf16[40,1024]{1,0:T(8,128)(2,1)S(1)}, u32[]{:S(2)}, u32[]{:S(2)}) collective-permute-start(bf16[40,1024]{1,0:T(8,128)(2,1)S(1)} %get-tuple-element.13.refs_0_), channel_id=1, source_target_pairs={{0,8},{1,9},{2,10},{3,11},{4,12},{5,13},{6,14},{7,15},{8,0},{9,1},... | collective-permute-start | bytes 245768 | tf_op jit(solution)/shard_map/ppermute | solution.py:33
  6.5 8.2 %collective-permute-start.6 = (bf16[40,1024]{1,0:T(8,128)(2,1)S(1)}, bf16[40,1024]{1,0:T(8,128)(2,1)S(1)}, u32[]{:S(2)}, u32[]{:S(2)}) collective-permute-start(bf16[40,1024]{1,0:T(8,128)(2,1)S(1)} %get-tuple-element.13.refs_0_), channel_id=1, source_target_pairs={{0,12},{1,13},{2,14},{3,15},{4,0},{5,1},{6,2},{7,3},{8,4},{9,5},{1... | collective-permute-start | bytes 245768 | tf_op jit(solution)/shard_map/ppermute | solution.py:33
  14.8 14.9 %collective-permute-start.8 = (bf16[4,40,1024]{2,1,0:T(8,128)(2,1)S(1)}, bf16[4,40,1024]{2,1,0:T(8,128)(2,1)S(1)}, u32[]{:S(2)}, u32[]{:S(2)}) collective-permute-start(bf16[4,40,1024]{2,1,0:T(8,128)(2,1)S(1)} %pile.5.z_ref), channel_id=1, source_target_pairs={{0,2},{1,3},{2,0},{3,1},{4,6},{5,7},{6,4},{7,5},{8,10},{9,11},{10,... | collective-permute-start | bytes 983048 | tf_op jit(solution)/shard_map/ppermute | solution.py:33
  15.0 9.8 %collective-permute-start.10 = (bf16[40,1792]{1,0:T(8,128)(2,1)S(1)}, bf16[40,1792]{1,0:T(8,128)(2,1)S(1)}, u32[]{:S(2)}, u32[]{:S(2)}) collective-permute-start(bf16[40,1792]{1,0:T(8,128)(2,1)S(1)} %get-tuple-element.14.own_ref), channel_id=1, source_target_pairs={{0,8},{1,9},{2,10},{3,11},{4,12},{5,13},{6,14},{7,15},{8,0},{9,1},... | collective-permute-start | bytes 430088 | tf_op jit(solution)/shard_map/ppermute | solution.py:33
  15.8 9.8 %collective-permute-start.11 = (bf16[40,1792]{1,0:T(8,128)(2,1)S(1)}, bf16[40,1792]{1,0:T(8,128)(2,1)S(1)}, u32[]{:S(2)}, u32[]{:S(2)}) collective-permute-start(bf16[40,1792]{1,0:T(8,128)(2,1)S(1)} %get-tuple-element.14.own_ref), channel_id=1, source_target_pairs={{0,12},{1,13},{2,14},{3,15},{4,0},{5,1},{6,2},{7,3},{8,4},{9,5},{1... | collective-permute-start | bytes 430088 | tf_op jit(solution)/shard_map/ppermute | solution.py:33
  15.8 12.2 %collective-permute-start.9 = (bf16[40,1792]{1,0:T(8,128)(2,1)S(1)}, bf16[40,1792]{1,0:T(8,128)(2,1)S(1)}, u32[]{:S(2)}, u32[]{:S(2)}) collective-permute-start(bf16[40,1792]{1,0:T(8,128)(2,1)S(1)} %get-tuple-element.14.own_ref), channel_id=1, source_target_pairs={{0,4},{1,5},{2,6},{3,7},{4,8},{5,9},{6,10},{7,11},{8,12},{9,13},{1... | collective-permute-start | bytes 430088 | tf_op jit(solution)/shard_map/ppermute | solution.py:33
  28.0 5.1 %collective-permute-start.12 = (bf16[4,40,1024]{2,1,0:T(8,128)(2,1)S(1)}, bf16[4,40,1024]{2,1,0:T(8,128)(2,1)S(1)}, u32[]{:S(2)}, u32[]{:S(2)}) collective-permute-start(bf16[4,40,1024]{2,1,0:T(8,128)(2,1)S(1)} %pile.5.z_ref), channel_id=1, source_target_pairs={{0,1},{1,0},{2,3},{3,2},{4,5},{5,4},{6,7},{7,6},{8,9},{9,8},{10,11... | collective-permute-start | bytes 983048 | tf_op jit(solution)/shard_map/ppermute | solution.py:33
  29.7 3.6 %collective-permute-start.13 = (bf16[4,40,1024]{2,1,0:T(8,128)(2,1)S(1)}, bf16[4,40,1024]{2,1,0:T(8,128)(2,1)S(1)}, u32[]{:S(2)}, u32[]{:S(2)}) collective-permute-start(bf16[4,40,1024]{2,1,0:T(8,128)(2,1)S(1)} %after.2.y_ref), channel_id=1, source_target_pairs={{0,1},{1,0},{2,3},{3,2},{4,5},{5,4},{6,7},{7,6},{8,9},{9,8},{10,11... | collective-permute-start | bytes 983048 | tf_op jit(solution)/shard_map/ppermute | solution.py:33
  29.8 20.5 %collective-permute-start.16 = (bf16[3,40,1792]{2,1,0:T(8,128)(2,1)S(1)}, bf16[3,40,1792]{2,1,0:T(8,128)(2,1)S(1)}, u32[]{:S(2)}, u32[]{:S(2)}) collective-permute-start(bf16[3,40,1792]{2,1,0:T(8,128)(2,1)S(1)} %pile.6.refs_1_.refs_0_.z_ref), channel_id=1, source_target_pairs={{0,2},{1,3},{2,0},{3,1},{4,6},{5,7},{6,4},{7,5},{8,10},{9,11},{10,... | collective-permute-start | bytes 1290248 | tf_op jit(solution)/shard_map/ppermute | solution.py:33
  31.0 5.9 %collective-permute-start.1 = (bf16[40,1792]{1,0:T(8,128)(2,1)S(1)}, bf16[40,1792]{1,0:T(8,128)(2,1)S(1)}, u32[]{:S(2)}, u32[]{:S(2)}) collective-permute-start(bf16[40,1792]{1,0:T(8,128)(2,1)S(1)} %get-tuple-element.11.own_ref), channel_id=1, source_target_pairs={{0,4},{1,5},{2,6},{3,7},{4,8},{5,9},{6,10},{7,11},{8,12},{9,13},{1... | collective-permute-start | bytes 430088 | tf_op jit(solution)/shard_map/ppermute | solution.py:33
  32.1 11.6 %collective-permute-start.2 = (bf16[40,1792]{1,0:T(8,128)(2,1)S(1)}, bf16[40,1792]{1,0:T(8,128)(2,1)S(1)}, u32[]{:S(2)}, u32[]{:S(2)}) collective-permute-start(bf16[40,1792]{1,0:T(8,128)(2,1)S(1)} %get-tuple-element.11.own_ref), channel_id=1, source_target_pairs={{0,8},{1,9},{2,10},{3,11},{4,12},{5,13},{6,14},{7,15},{8,0},{9,1},... | collective-permute-start | bytes 430088 | tf_op jit(solution)/shard_map/ppermute | solution.py:33
  33.1 15.2 %collective-permute-start.3 = (bf16[40,1792]{1,0:T(8,128)(2,1)S(1)}, bf16[40,1792]{1,0:T(8,128)(2,1)S(1)}, u32[]{:S(2)}, u32[]{:S(2)}) collective-permute-start(bf16[40,1792]{1,0:T(8,128)(2,1)S(1)} %get-tuple-element.11.own_ref), channel_id=1, source_target_pairs={{0,12},{1,13},{2,14},{3,15},{4,0},{5,1},{6,2},{7,3},{8,4},{9,5},{1... | collective-permute-start | bytes 430088 | tf_op jit(solution)/shard_map/ppermute | solution.py:33
  35.6 12.7 %collective-permute-start.14 = (bf16[80,512]{1,0:T(8,128)(2,1)S(1)}, bf16[80,512]{1,0:T(8,128)(2,1)S(1)}, u32[]{:S(2)}, u32[]{:S(2)}) collective-permute-start(bf16[80,512]{1,0:T(8,128)(2,1)S(1)} %rotate_out.1.refs_0_), channel_id=1, source_target_pairs={{0,4},{1,5},{2,6},{3,7},{4,8},{5,9},{6,10},{7,11},{8,12},{9,13},{1... | collective-permute-start | bytes 245768 | tf_op jit(solution)/shard_map/ppermute | solution.py:33
  48.3 14.8 %collective-permute-start.15 = (bf16[3,40,1792]{2,1,0:T(8,128)(2,1)S(1)}, bf16[3,40,1792]{2,1,0:T(8,128)(2,1)S(1)}, u32[]{:S(2)}, u32[]{:S(2)}) collective-permute-start(bf16[3,40,1792]{2,1,0:T(8,128)(2,1)S(1)} %pile.7.z_ref.refs_4_), channel_id=1, source_target_pairs={{0,2},{1,3},{2,0},{3,1},{4,6},{5,7},{6,4},{7,5},{8,10},{9,11},{10,... | collective-permute-start | bytes 1290248 | tf_op jit(solution)/shard_map/ppermute | solution.py:33
  48.6 12.5 %collective-permute-start.20 = (bf16[80,512]{1,0:T(8,128)(2,1)S(1)}, bf16[80,512]{1,0:T(8,128)(2,1)S(1)}, u32[]{:S(2)}, u32[]{:S(2)}) collective-permute-start(bf16[80,512]{1,0:T(8,128)(2,1)S(1)} %rotate_out.1.refs_0_), channel_id=1, source_target_pairs={{0,2},{1,3},{2,0},{3,1},{4,6},{5,7},{6,4},{7,5},{8,10},{9,11},{10,... | collective-permute-start | bytes 245768 | tf_op jit(solution)/shard_map/ppermute | solution.py:33
  49.9 11.3 %collective-permute-start.18 = (bf16[80,512]{1,0:T(8,128)(2,1)S(1)}, bf16[80,512]{1,0:T(8,128)(2,1)S(1)}, u32[]{:S(2)}, u32[]{:S(2)}) collective-permute-start(bf16[80,512]{1,0:T(8,128)(2,1)S(1)} %rotate_out.1.refs_0_), channel_id=1, source_target_pairs={{0,8},{1,9},{2,10},{3,11},{4,12},{5,13},{6,14},{7,15},{8,0},{9,1},... | collective-permute-start | bytes 245768 | tf_op jit(solution)/shard_map/ppermute | solution.py:33
  49.9 11.3 %collective-permute-start.19 = (bf16[80,512]{1,0:T(8,128)(2,1)S(1)}, bf16[80,512]{1,0:T(8,128)(2,1)S(1)}, u32[]{:S(2)}, u32[]{:S(2)}) collective-permute-start(bf16[80,512]{1,0:T(8,128)(2,1)S(1)} %rotate_out.1.refs_0_), channel_id=1, source_target_pairs={{0,12},{1,13},{2,14},{3,15},{4,0},{5,1},{6,2},{7,3},{8,4},{9,5},{1... | collective-permute-start | bytes 245768 | tf_op jit(solution)/shard_map/ppermute | solution.py:33
  61.2 6.2 %collective-permute-start.21 = (bf16[3,80,512]{2,1,0:T(8,128)(2,1)S(1)}, bf16[3,80,512]{2,1,0:T(8,128)(2,1)S(1)}, u32[]{:S(2)}, u32[]{:S(2)}) collective-permute-start(bf16[3,80,512]{2,1,0:T(8,128)(2,1)S(1)} %pile.9.z_ref), channel_id=1, source_target_pairs={{0,2},{1,3},{2,0},{3,1},{4,6},{5,7},{6,4},{7,5},{8,10},{9,11},{10,... | collective-permute-start | bytes 737288 | tf_op jit(solution)/shard_map/ppermute | solution.py:33
  61.5 5.0 %collective-permute-start.22 = (bf16[2,80,512]{2,1,0:T(8,128)(2,1)S(1)}, bf16[2,80,512]{2,1,0:T(8,128)(2,1)S(1)}, u32[]{:S(2)}, u32[]{:S(2)}) collective-permute-start(bf16[2,80,512]{2,1,0:T(8,128)(2,1)S(1)} %pile.8.refs_5_.near_ref), channel_id=1, source_target_pairs={{0,1},{1,0},{2,3},{3,2},{4,5},{5,4},{6,7},{7,6},{8,9},{9,8},{10,11... | collective-permute-start | bytes 491528 | tf_op jit(solution)/shard_map/ppermute | solution.py:33
  63.1 6.5 %collective-permute-start.24 = (bf16[3,80,512]{2,1,0:T(8,128)(2,1)S(1)}, bf16[3,80,512]{2,1,0:T(8,128)(2,1)S(1)}, u32[]{:S(2)}, u32[]{:S(2)}) collective-permute-start(bf16[3,80,512]{2,1,0:T(8,128)(2,1)S(1)} %pile.9.z_ref), channel_id=1, source_target_pairs={{0,1},{1,0},{2,3},{3,2},{4,5},{5,4},{6,7},{7,6},{8,9},{9,8},{10,11... | collective-permute-start | bytes 737288 | tf_op jit(solution)/shard_map/ppermute | solution.py:33
  67.4 4.0 %collective-permute-start.23 = (bf16[3,80,512]{2,1,0:T(8,128)(2,1)S(1)}, bf16[3,80,512]{2,1,0:T(8,128)(2,1)S(1)}, u32[]{:S(2)}, u32[]{:S(2)}) collective-permute-start(bf16[3,80,512]{2,1,0:T(8,128)(2,1)S(1)} %after.3.y_ref), channel_id=1, source_target_pairs={{0,1},{1,0},{2,3},{3,2},{4,5},{5,4},{6,7},{7,6},{8,9},{9,8},{10,11... | collective-permute-start | bytes 737288 | tf_op jit(solution)/shard_map/ppermute | solution.py:33
  (6 other events, 45.3 us)

commit v15 on v14

--- a/solution.py
+++ b/solution.py
@@ -396,7 +396,7 @@
     swapped = send(near, swap(devices))
     came = along_all(sq_out)
     for chunk in range(1, CHUNKS):
-        chunk_along(chunk, [came[0]])
+        chunk_along(chunk, [sq_out])
     total = part(0, [])
     z = pile(came, [*total, acts_z[-1], near])
     y = send(z, across(devices))

time: 72.5 us -> 70.7 us (0.975)
  waiting for transfers between devices: 33.8 us -> 29.6 us
  starting transfers between devices: 21.6 us -> 24 us
    ppermute x25, waiting for transfers between devices: 33.8 us -> 29.6 us  [send(): return lax.ppermute(block, 'wide', pairs)]
    ppermute x25, starting transfers between devices: 21.6 us -> 24 us  [send(): return lax.ppermute(block, 'wide', pairs)]
  transfers between devices with their start and end apart: 25 -> 25, of which waited for: 9 -> 10; matrix products, arithmetic and copies ran while one was open for 0% -> 0% of each run, Pallas kernels for 15% -> 15%
where the time goes in v15:
time: 70.7 us; the launch traced here: 70.5 us
  waiting for transfers between devices  29.6 us (42%)
  starting transfers between devices  24 us (34%)
  Pallas kernels  11.5 us (16%)
  local copies, waits for them, and re-layouts  5.31 us (8%)
    ppermute x25, waiting for transfers between devices, send(): return lax.ppermute(block, 'wide', pairs)  29.6 us
    ppermute x25, starting transfers between devices, send(): return lax.ppermute(block, 'wide', pairs)  24 us
    pallas_call x2, Pallas kernels, rotate_in(): pl.pallas_call(functools.partial(rotate_in_kernel, tokens, chunk, len(bef...  5.61 us
    unnamed x10, local copies, waits for them, and re-layouts  5.31 us
    pallas_call x1, Pallas kernels, rotate_out(): pl.pallas_call(functools.partial(rotate_out_kernel, tokens, len(waits)),...  2.29 us
    pallas_call x1, Pallas kernels, combine(): pl.pallas_call(combine_kernel, out_shape=jax.ShapeDtypeStruct((own.shape[...  1.69 us
  transfers between devices with their start and end apart: 25, of which 10 were waited for; matrix products, arithmetic and copies ran while one was open for 0% of the time, Pallas kernels for 15%

profile of v15, /device:TPU:9, one launch (start us, length us, event | category | flops | bytes accessed | tf_op | source)
XLA Modules:
  0.0 70.5 jit_solution(5503997236799450151)
XLA Ops:
  2.9 1.3 %collective-permute-start = (bf16[2,40,1792]{2,1,0:T(8,128)(2,1)S(1)}, bf16[2,40,1792]{2,1,0:T(8,128)(2,1)S(1)}, u32[]{:S(2)}, u32[]{:S(2)}) collective-permute-start(bf16[2,40,1792]{2,1,0:T(8,128)(2,1)S(1)} %get-tuple-element.12), channel_id=1, source_target_pairs={{0,2},{1,3},{2,0},{3,1},{4,6},{5,7},{6,4},{7,5},{8,10},{9,11},{10,... | collective-permute-start | bytes 860168 | tf_op jit(solution)/shard_map/ppermute | solution.py:33
  4.2 1.3 %collective-permute-start.4 = (bf16[40,1024]{1,0:T(8,128)(2,1)S(1)}, bf16[40,1024]{1,0:T(8,128)(2,1)S(1)}, u32[]{:S(2)}, u32[]{:S(2)}) collective-permute-start(bf16[40,1024]{1,0:T(8,128)(2,1)S(1)} %get-tuple-element.13.refs_0_), channel_id=1, source_target_pairs={{0,4},{1,5},{2,6},{3,7},{4,8},{5,9},{6,10},{7,11},{8,12},{9,13},{1... | collective-permute-start | bytes 245768 | tf_op jit(solution)/shard_map/ppermute | solution.py:33
  6.5 1.5 %collective-permute-start.6 = (bf16[40,1024]{1,0:T(8,128)(2,1)S(1)}, bf16[40,1024]{1,0:T(8,128)(2,1)S(1)}, u32[]{:S(2)}, u32[]{:S(2)}) collective-permute-start(bf16[40,1024]{1,0:T(8,128)(2,1)S(1)} %get-tuple-element.13.refs_0_), channel_id=1, source_target_pairs={{0,12},{1,13},{2,14},{3,15},{4,0},{5,1},{6,2},{7,3},{8,4},{9,5},{1... | collective-permute-start | bytes 245768 | tf_op jit(solution)/shard_map/ppermute | solution.py:33
  8.0 3.4 %copy-done = bf16[8192,512]{1,0:T(8,128)(2,1)S(1)} copy-done((bf16[8192,512]{1,0:T(8,128)(2,1)S(1)}, bf16[8192,512]{1,0:T(8,128)(2,1)}, u32[]{:S(2)}) %copy-start) | copy-done | bytes 8388632
  12.2 2.5 %collective-permute-done.6.refs_3_ = bf16[40,1024]{1,0:T(8,128)(2,1)S(1)} collective-permute-done((bf16[40,1024]{1,0:T(8,128)(2,1)S(1)}, bf16[40,1024]{1,0:T(8,128)(2,1)S(1)}, u32[]{:S(2)}, u32[]{:S(2)}) %collective-permute-start.6) | collective-permute-done | bytes 81952 | tf_op jit(solution)/shard_map/ppermute | solution.py:33
  15.8 1.5 %collective-permute-start.9 = (bf16[40,1792]{1,0:T(8,128)(2,1)S(1)}, bf16[40,1792]{1,0:T(8,128)(2,1)S(1)}, u32[]{:S(2)}, u32[]{:S(2)}) collective-permute-start(bf16[40,1792]{1,0:T(8,128)(2,1)S(1)} %get-tuple-element.14.own_ref), channel_id=1, source_target_pairs={{0,4},{1,5},{2,6},{3,7},{4,8},{5,9},{6,10},{7,11},{8,12},{9,13},{1... | collective-permute-start | bytes 430088 | tf_op jit(solution)/shard_map/ppermute | solution.py:33
  17.2 2.2 %collective-permute-start.12 = (bf16[4,40,1024]{2,1,0:T(8,128)(2,1)S(1)}, bf16[4,40,1024]{2,1,0:T(8,128)(2,1)S(1)}, u32[]{:S(2)}, u32[]{:S(2)}) collective-permute-start(bf16[4,40,1024]{2,1,0:T(8,128)(2,1)S(1)} %pile.5.z_ref), channel_id=1, source_target_pairs={{0,1},{1,0},{2,3},{3,2},{4,5},{5,4},{6,7},{7,6},{8,9},{9,8},{10,11... | collective-permute-start | bytes 983048 | tf_op jit(solution)/shard_map/ppermute | solution.py:33
  19.4 5.4 %collective-permute-done.10.refs_1_ = bf16[40,1792]{1,0:T(8,128)(2,1)S(1)} collective-permute-done((bf16[40,1792]{1,0:T(8,128)(2,1)S(1)}, bf16[40,1792]{1,0:T(8,128)(2,1)S(1)}, u32[]{:S(2)}, u32[]{:S(2)}) %collective-permute-start.10) | collective-permute-done | bytes 143392 | tf_op jit(solution)/shard_map/ppermute | solution.py:33
  25.6 2.4 %collective-permute-done.9.refs_0_ = bf16[40,1792]{1,0:T(8,128)(2,1)S(1)} collective-permute-done((bf16[40,1792]{1,0:T(8,128)(2,1)S(1)}, bf16[40,1792]{1,0:T(8,128)(2,1)S(1)}, u32[]{:S(2)}, u32[]{:S(2)}) %collective-permute-start.9) | collective-permute-done | bytes 143392 | tf_op jit(solution)/shard_map/ppermute | solution.py:33
  28.0 1.7 %collective-permute-start.13 = (bf16[4,40,1024]{2,1,0:T(8,128)(2,1)S(1)}, bf16[4,40,1024]{2,1,0:T(8,128)(2,1)S(1)}, u32[]{:S(2)}, u32[]{:S(2)}) collective-permute-start(bf16[4,40,1024]{2,1,0:T(8,128)(2,1)S(1)} %after.2.y_ref), channel_id=1, source_target_pairs={{0,1},{1,0},{2,3},{3,2},{4,5},{5,4},{6,7},{7,6},{8,9},{9,8},{10,11... | collective-permute-start | bytes 983048 | tf_op jit(solution)/shard_map/ppermute | solution.py:33
  29.7 1.3 %collective-permute-start.15 = (bf16[3,40,1792]{2,1,0:T(8,128)(2,1)S(1)}, bf16[3,40,1792]{2,1,0:T(8,128)(2,1)S(1)}, u32[]{:S(2)}, u32[]{:S(2)}) collective-permute-start(bf16[3,40,1792]{2,1,0:T(8,128)(2,1)S(1)} %pile.6.refs_1_.refs_0_.z_ref), channel_id=1, source_target_pairs={{0,2},{1,3},{2,0},{3,1},{4,6},{5,7},{6,4},{7,5},{8,10},{9,11},{10,... | collective-permute-start | bytes 1290248 | tf_op jit(solution)/shard_map/ppermute | solution.py:33
  31.0 1.1 %collective-permute-start.1 = (bf16[40,1792]{1,0:T(8,128)(2,1)S(1)}, bf16[40,1792]{1,0:T(8,128)(2,1)S(1)}, u32[]{:S(2)}, u32[]{:S(2)}) collective-permute-start(bf16[40,1792]{1,0:T(8,128)(2,1)S(1)} %get-tuple-element.11.own_ref), channel_id=1, source_target_pairs={{0,4},{1,5},{2,6},{3,7},{4,8},{5,9},{6,10},{7,11},{8,12},{9,13},{1... | collective-permute-start | bytes 430088 | tf_op jit(solution)/shard_map/ppermute | solution.py:33
  32.0 1.0 %collective-permute-start.2 = (bf16[40,1792]{1,0:T(8,128)(2,1)S(1)}, bf16[40,1792]{1,0:T(8,128)(2,1)S(1)}, u32[]{:S(2)}, u32[]{:S(2)}) collective-permute-start(bf16[40,1792]{1,0:T(8,128)(2,1)S(1)} %get-tuple-element.11.own_ref), channel_id=1, source_target_pairs={{0,8},{1,9},{2,10},{3,11},{4,12},{5,13},{6,14},{7,15},{8,0},{9,1},... | collective-permute-start | bytes 430088 | tf_op jit(solution)/shard_map/ppermute | solution.py:33
  33.2 2.3 %rotate_out.1.refs_3_.refs_0_ = bf16[80,512]{1,0:T(8,128)(2,1)S(1)} custom-call(bf16[4,40,1024]{2,1,0:T(8,128)(2,1)S(1)} %pile.5.z_ref, bf16[4,40,1024]{2,1,0:T(8,128)(2,1)S(1)} %after.2.y_ref, bf16[4,40,1024]{2,1,0:T(8,128)(2,1)S(1)} %collective-permute-done.12.cz_ref, bf16[4,40,1024]{2,1,0:T(8,128)(2,1)S(1)} %collective-permute-done.13.cy_ref, ...), custom_call_target="tpu_custom_call" | custom-call | flops 671088640 | bytes 8388608 | tf_op jit(solution)/shard_map/rotate_out/pallas_call | solution.py:105
  36.0 8.1 %collective-permute-done.2.refs_1_ = bf16[40,1792]{1,0:T(8,128)(2,1)S(1)} collective-permute-done((bf16[40,1792]{1,0:T(8,128)(2,1)S(1)}, bf16[40,1792]{1,0:T(8,128)(2,1)S(1)}, u32[]{:S(2)}, u32[]{:S(2)}) %collective-permute-start.2) | collective-permute-done | bytes 143392 | tf_op jit(solution)/shard_map/ppermute | solution.py:33
  44.0 2.5 %collective-permute-done.3.refs_2_ = bf16[40,1792]{1,0:T(8,128)(2,1)S(1)} collective-permute-done((bf16[40,1792]{1,0:T(8,128)(2,1)S(1)}, bf16[40,1792]{1,0:T(8,128)(2,1)S(1)}, u32[]{:S(2)}, u32[]{:S(2)}) %collective-permute-start.3) | collective-permute-done | bytes 143392 | tf_op jit(solution)/shard_map/ppermute | solution.py:33
  46.9 1.2 %collective-permute-start.20 = (bf16[80,512]{1,0:T(8,128)(2,1)S(1)}, bf16[80,512]{1,0:T(8,128)(2,1)S(1)}, u32[]{:S(2)}, u32[]{:S(2)}) collective-permute-start(bf16[80,512]{1,0:T(8,128)(2,1)S(1)} %rotate_out.1.refs_3_.refs_0_), channel_id=1, source_target_pairs={{0,2},{1,3},{2,0},{3,1},{4,6},{5,7},{6,4},{7,5},{8,10},{9,11},{10,... | collective-permute-start | bytes 245768 | tf_op jit(solution)/shard_map/ppermute | solution.py:33
  48.7 1.5 %collective-permute-start.19 = (bf16[80,512]{1,0:T(8,128)(2,1)S(1)}, bf16[80,512]{1,0:T(8,128)(2,1)S(1)}, u32[]{:S(2)}, u32[]{:S(2)}) collective-permute-start(bf16[80,512]{1,0:T(8,128)(2,1)S(1)} %rotate_out.1.refs_3_.refs_0_), channel_id=1, source_target_pairs={{0,12},{1,13},{2,14},{3,15},{4,0},{5,1},{6,2},{7,3},{8,4},{9,5},{1... | collective-permute-start | bytes 245768 | tf_op jit(solution)/shard_map/ppermute | solution.py:33
  50.2 2.8 %rotate_in.2.refs_0_.refs_3_ = f32[192,40]{1,0:T(8,128)S(1)} custom-call(bf16[40,1792]{1,0:T(8,128)(2,1)S(1)} %get-tuple-element.14.own_ref, bf16[2,40,1792]{2,1,0:T(8,128)(2,1)S(1)} %collective-permute-done.refs_4_.across_ref, bf16[3,40,1792]{2,1,0:T(8,128)(2,1)S(1)} %pile.6.refs_1_.refs_0_.z_ref, bf16[3,40,1792]{2,1,0:T(8,128)(2,1)S(1)} %collective-permute-done.15.y_ref, ...), custom_call_target="tpu_custom_call" | custom-call | flops 220200960 | bytes 5505024 | tf_op jit(solution)/shard_map/rotate_in/pallas_call | solution.py:171
  53.0 6.4 %collective-permute-done.20.refs_1_ = bf16[80,512]{1,0:T(8,128)(2,1)S(1)} collective-permute-done((bf16[80,512]{1,0:T(8,128)(2,1)S(1)}, bf16[80,512]{1,0:T(8,128)(2,1)S(1)}, u32[]{:S(2)}, u32[]{:S(2)}) %collective-permute-start.20) | collective-permute-done | bytes 81952 | tf_op jit(solution)/shard_map/ppermute | solution.py:33
  59.7 1.6 %collective-permute-start.22 = (bf16[2,80,512]{2,1,0:T(8,128)(2,1)S(1)}, bf16[2,80,512]{2,1,0:T(8,128)(2,1)S(1)}, u32[]{:S(2)}, u32[]{:S(2)}) collective-permute-start(bf16[2,80,512]{2,1,0:T(8,128)(2,1)S(1)} %pile.8.refs_5_.near_ref), channel_id=1, source_target_pairs={{0,1},{1,0},{2,3},{3,2},{4,5},{5,4},{6,7},{7,6},{8,9},{9,8},{10,11... | collective-permute-start | bytes 491528 | tf_op jit(solution)/shard_map/ppermute | solution.py:33
  61.4 2.8 %rotate_in.3 = (bf16[96,40]{1,0:T(8,128)(2,1)S(1)}, bf16[96,40]{1,0:T(8,128)(2,1)S(1)}) custom-call(bf16[40,1792]{1,0:T(8,128)(2,1)S(1)} %get-tuple-element.11.own_ref, bf16[2,40,1792]{2,1,0:T(8,128)(2,1)S(1)} %collective-permute-done.refs_4_.across_ref, bf16[3,40,1792]{2,1,0:T(8,128)(2,1)S(1)} %pile.7.z_ref.refs_4_, ...), custom_call_target="tpu_custom_call" | custom-call | flops 220200960 | bytes 5505024 | tf_op jit(solution)/shard_map/rotate_in/pallas_call | solution.py:171
  65.6 2.3 %collective-permute-start.23 = (bf16[3,80,512]{2,1,0:T(8,128)(2,1)S(1)}, bf16[3,80,512]{2,1,0:T(8,128)(2,1)S(1)}, u32[]{:S(2)}, u32[]{:S(2)}) collective-permute-start(bf16[3,80,512]{2,1,0:T(8,128)(2,1)S(1)} %after.3.y_ref), channel_id=1, source_target_pairs={{0,1},{1,0},{2,3},{3,2},{4,5},{5,4},{6,7},{7,6},{8,9},{9,8},{10,11... | collective-permute-start | bytes 737288 | tf_op jit(solution)/shard_map/ppermute | solution.py:33
  67.9 1.7 %combine.1._ = bf16[96,8192]{1,0:T(8,128)(2,1)} custom-call(bf16[96,40]{1,0:T(8,128)(2,1)S(1)} %get-tuple-element.15.own_ref, bf16[96,40]{1,0:T(8,128)(2,1)S(1)} %collective-permute-done.16.refs_1_.other_ref, bf16[2,80,512]{2,1,0:T(8,128)(2,1)S(1)} %pile.8.refs_5_.near_ref, bf16[2,80,512]{2,1,0:T(8,128)(2,1)S(1)} %collective-permute-done.22.refs_2_.swapped_ref, ...), custom_call_target="tpu_custom_call" | custom-call | flops 125829120 | bytes 3145728 | tf_op jit(solution)/shard_map/combine/pallas_call | solution.py:313
  (51 shorter events, 10.8 us)
Async XLA Ops:
  0.0 14.7 %collective-permute-start.7 = (bf16[96,28672]{1,0:T(8,128)(2,1)}, bf16[96,28672]{1,0:T(8,128)(2,1)S(1)}, u32[]{:S(2)}, u32[]{:S(2)}) collective-permute-start(bf16[96,28672]{1,0:T(8,128)(2,1)} %bitcast.1), channel_id=1, source_target_pairs={{0,1},{1,0},{2,3},{3,2},{4,5},{5,4},{6,7},{7,6},{8,9},{9,8},{10,11... | collective-permute-start | bytes 16515080 | tf_op jit(solution)/shard_map/ppermute | solution.py:33
  2.9 11.8 %collective-permute-start = (bf16[2,40,1792]{2,1,0:T(8,128)(2,1)S(1)}, bf16[2,40,1792]{2,1,0:T(8,128)(2,1)S(1)}, u32[]{:S(2)}, u32[]{:S(2)}) collective-permute-start(bf16[2,40,1792]{2,1,0:T(8,128)(2,1)S(1)} %get-tuple-element.12), channel_id=1, source_target_pairs={{0,2},{1,3},{2,0},{3,1},{4,6},{5,7},{6,4},{7,5},{8,10},{9,11},{10,... | collective-permute-start | bytes 860168 | tf_op jit(solution)/shard_map/ppermute | solution.py:33
  4.2 7.7 %collective-permute-start.4 = (bf16[40,1024]{1,0:T(8,128)(2,1)S(1)}, bf16[40,1024]{1,0:T(8,128)(2,1)S(1)}, u32[]{:S(2)}, u32[]{:S(2)}) collective-permute-start(bf16[40,1024]{1,0:T(8,128)(2,1)S(1)} %get-tuple-element.13.refs_0_), channel_id=1, source_target_pairs={{0,4},{1,5},{2,6},{3,7},{4,8},{5,9},{6,10},{7,11},{8,12},{9,13},{1... | collective-permute-start | bytes 245768 | tf_op jit(solution)/shard_map/ppermute | solution.py:33
  5.5 6.7 %collective-permute-start.5 = (bf16[40,1024]{1,0:T(8,128)(2,1)S(1)}, bf16[40,1024]{1,0:T(8,128)(2,1)S(1)}, u32[]{:S(2)}, u32[]{:S(2)}) collective-permute-start(bf16[40,1024]{1,0:T(8,128)(2,1)S(1)} %get-tuple-element.13.refs_0_), channel_id=1, source_target_pairs={{0,8},{1,9},{2,10},{3,11},{4,12},{5,13},{6,14},{7,15},{8,0},{9,1},... | collective-permute-start | bytes 245768 | tf_op jit(solution)/shard_map/ppermute | solution.py:33
  6.5 8.2 %collective-permute-start.6 = (bf16[40,1024]{1,0:T(8,128)(2,1)S(1)}, bf16[40,1024]{1,0:T(8,128)(2,1)S(1)}, u32[]{:S(2)}, u32[]{:S(2)}) collective-permute-start(bf16[40,1024]{1,0:T(8,128)(2,1)S(1)} %get-tuple-element.13.refs_0_), channel_id=1, source_target_pairs={{0,12},{1,13},{2,14},{3,15},{4,0},{5,1},{6,2},{7,3},{8,4},{9,5},{1... | collective-permute-start | bytes 245768 | tf_op jit(solution)/shard_map/ppermute | solution.py:33
  14.8 13.2 %collective-permute-start.8 = (bf16[4,40,1024]{2,1,0:T(8,128)(2,1)S(1)}, bf16[4,40,1024]{2,1,0:T(8,128)(2,1)S(1)}, u32[]{:S(2)}, u32[]{:S(2)}) collective-permute-start(bf16[4,40,1024]{2,1,0:T(8,128)(2,1)S(1)} %pile.5.z_ref), channel_id=1, source_target_pairs={{0,2},{1,3},{2,0},{3,1},{4,6},{5,7},{6,4},{7,5},{8,10},{9,11},{10,... | collective-permute-start | bytes 983048 | tf_op jit(solution)/shard_map/ppermute | solution.py:33
  15.0 9.8 %collective-permute-start.10 = (bf16[40,1792]{1,0:T(8,128)(2,1)S(1)}, bf16[40,1792]{1,0:T(8,128)(2,1)S(1)}, u32[]{:S(2)}, u32[]{:S(2)}) collective-permute-start(bf16[40,1792]{1,0:T(8,128)(2,1)S(1)} %get-tuple-element.14.own_ref), channel_id=1, source_target_pairs={{0,8},{1,9},{2,10},{3,11},{4,12},{5,13},{6,14},{7,15},{8,0},{9,1},... | collective-permute-start | bytes 430088 | tf_op jit(solution)/shard_map/ppermute | solution.py:33
  15.8 9.8 %collective-permute-start.11 = (bf16[40,1792]{1,0:T(8,128)(2,1)S(1)}, bf16[40,1792]{1,0:T(8,128)(2,1)S(1)}, u32[]{:S(2)}, u32[]{:S(2)}) collective-permute-start(bf16[40,1792]{1,0:T(8,128)(2,1)S(1)} %get-tuple-element.14.own_ref), channel_id=1, source_target_pairs={{0,12},{1,13},{2,14},{3,15},{4,0},{5,1},{6,2},{7,3},{8,4},{9,5},{1... | collective-permute-start | bytes 430088 | tf_op jit(solution)/shard_map/ppermute | solution.py:33
  15.8 12.2 %collective-permute-start.9 = (bf16[40,1792]{1,0:T(8,128)(2,1)S(1)}, bf16[40,1792]{1,0:T(8,128)(2,1)S(1)}, u32[]{:S(2)}, u32[]{:S(2)}) collective-permute-start(bf16[40,1792]{1,0:T(8,128)(2,1)S(1)} %get-tuple-element.14.own_ref), channel_id=1, source_target_pairs={{0,4},{1,5},{2,6},{3,7},{4,8},{5,9},{6,10},{7,11},{8,12},{9,13},{1... | collective-permute-start | bytes 430088 | tf_op jit(solution)/shard_map/ppermute | solution.py:33
  17.2 15.8 %collective-permute-start.12 = (bf16[4,40,1024]{2,1,0:T(8,128)(2,1)S(1)}, bf16[4,40,1024]{2,1,0:T(8,128)(2,1)S(1)}, u32[]{:S(2)}, u32[]{:S(2)}) collective-permute-start(bf16[4,40,1024]{2,1,0:T(8,128)(2,1)S(1)} %pile.5.z_ref), channel_id=1, source_target_pairs={{0,1},{1,0},{2,3},{3,2},{4,5},{5,4},{6,7},{7,6},{8,9},{9,8},{10,11... | collective-permute-start | bytes 983048 | tf_op jit(solution)/shard_map/ppermute | solution.py:33
  28.0 5.2 %collective-permute-start.13 = (bf16[4,40,1024]{2,1,0:T(8,128)(2,1)S(1)}, bf16[4,40,1024]{2,1,0:T(8,128)(2,1)S(1)}, u32[]{:S(2)}, u32[]{:S(2)}) collective-permute-start(bf16[4,40,1024]{2,1,0:T(8,128)(2,1)S(1)} %after.2.y_ref), channel_id=1, source_target_pairs={{0,1},{1,0},{2,3},{3,2},{4,5},{5,4},{6,7},{7,6},{8,9},{9,8},{10,11... | collective-permute-start | bytes 983048 | tf_op jit(solution)/shard_map/ppermute | solution.py:33
  29.7 19.0 %collective-permute-start.15 = (bf16[3,40,1792]{2,1,0:T(8,128)(2,1)S(1)}, bf16[3,40,1792]{2,1,0:T(8,128)(2,1)S(1)}, u32[]{:S(2)}, u32[]{:S(2)}) collective-permute-start(bf16[3,40,1792]{2,1,0:T(8,128)(2,1)S(1)} %pile.6.refs_1_.refs_0_.z_ref), channel_id=1, source_target_pairs={{0,2},{1,3},{2,0},{3,1},{4,6},{5,7},{6,4},{7,5},{8,10},{9,11},{10,... | collective-permute-start | bytes 1290248 | tf_op jit(solution)/shard_map/ppermute | solution.py:33
  31.0 5.0 %collective-permute-start.1 = (bf16[40,1792]{1,0:T(8,128)(2,1)S(1)}, bf16[40,1792]{1,0:T(8,128)(2,1)S(1)}, u32[]{:S(2)}, u32[]{:S(2)}) collective-permute-start(bf16[40,1792]{1,0:T(8,128)(2,1)S(1)} %get-tuple-element.11.own_ref), channel_id=1, source_target_pairs={{0,4},{1,5},{2,6},{3,7},{4,8},{5,9},{6,10},{7,11},{8,12},{9,13},{1... | collective-permute-start | bytes 430088 | tf_op jit(solution)/shard_map/ppermute | solution.py:33
  32.0 12.0 %collective-permute-start.2 = (bf16[40,1792]{1,0:T(8,128)(2,1)S(1)}, bf16[40,1792]{1,0:T(8,128)(2,1)S(1)}, u32[]{:S(2)}, u32[]{:S(2)}) collective-permute-start(bf16[40,1792]{1,0:T(8,128)(2,1)S(1)} %get-tuple-element.11.own_ref), channel_id=1, source_target_pairs={{0,8},{1,9},{2,10},{3,11},{4,12},{5,13},{6,14},{7,15},{8,0},{9,1},... | collective-permute-start | bytes 430088 | tf_op jit(solution)/shard_map/ppermute | solution.py:33
  33.1 13.5 %collective-permute-start.3 = (bf16[40,1792]{1,0:T(8,128)(2,1)S(1)}, bf16[40,1792]{1,0:T(8,128)(2,1)S(1)}, u32[]{:S(2)}, u32[]{:S(2)}) collective-permute-start(bf16[40,1792]{1,0:T(8,128)(2,1)S(1)} %get-tuple-element.11.own_ref), channel_id=1, source_target_pairs={{0,12},{1,13},{2,14},{3,15},{4,0},{5,1},{6,2},{7,3},{8,4},{9,5},{1... | collective-permute-start | bytes 430088 | tf_op jit(solution)/shard_map/ppermute | solution.py:33
  46.6 14.8 %collective-permute-start.14 = (bf16[3,40,1792]{2,1,0:T(8,128)(2,1)S(1)}, bf16[3,40,1792]{2,1,0:T(8,128)(2,1)S(1)}, u32[]{:S(2)}, u32[]{:S(2)}) collective-permute-start(bf16[3,40,1792]{2,1,0:T(8,128)(2,1)S(1)} %pile.7.z_ref.refs_4_), channel_id=1, source_target_pairs={{0,2},{1,3},{2,0},{3,1},{4,6},{5,7},{6,4},{7,5},{8,10},{9,11},{10,... | collective-permute-start | bytes 1290248 | tf_op jit(solution)/shard_map/ppermute | solution.py:33
  46.9 12.5 %collective-permute-start.20 = (bf16[80,512]{1,0:T(8,128)(2,1)S(1)}, bf16[80,512]{1,0:T(8,128)(2,1)S(1)}, u32[]{:S(2)}, u32[]{:S(2)}) collective-permute-start(bf16[80,512]{1,0:T(8,128)(2,1)S(1)} %rotate_out.1.refs_3_.refs_0_), channel_id=1, source_target_pairs={{0,2},{1,3},{2,0},{3,1},{4,6},{5,7},{6,4},{7,5},{8,10},{9,11},{10,... | collective-permute-start | bytes 245768 | tf_op jit(solution)/shard_map/ppermute | solution.py:33
  48.1 11.3 %collective-permute-start.17 = (bf16[80,512]{1,0:T(8,128)(2,1)S(1)}, bf16[80,512]{1,0:T(8,128)(2,1)S(1)}, u32[]{:S(2)}, u32[]{:S(2)}) collective-permute-start(bf16[80,512]{1,0:T(8,128)(2,1)S(1)} %rotate_out.1.refs_3_.refs_0_), channel_id=1, source_target_pairs={{0,4},{1,5},{2,6},{3,7},{4,8},{5,9},{6,10},{7,11},{8,12},{9,13},{1... | collective-permute-start | bytes 245768 | tf_op jit(solution)/shard_map/ppermute | solution.py:33
  48.1 11.3 %collective-permute-start.18 = (bf16[80,512]{1,0:T(8,128)(2,1)S(1)}, bf16[80,512]{1,0:T(8,128)(2,1)S(1)}, u32[]{:S(2)}, u32[]{:S(2)}) collective-permute-start(bf16[80,512]{1,0:T(8,128)(2,1)S(1)} %rotate_out.1.refs_3_.refs_0_), channel_id=1, source_target_pairs={{0,8},{1,9},{2,10},{3,11},{4,12},{5,13},{6,14},{7,15},{8,0},{9,1},... | collective-permute-start | bytes 245768 | tf_op jit(solution)/shard_map/ppermute | solution.py:33
  48.7 10.7 %collective-permute-start.19 = (bf16[80,512]{1,0:T(8,128)(2,1)S(1)}, bf16[80,512]{1,0:T(8,128)(2,1)S(1)}, u32[]{:S(2)}, u32[]{:S(2)}) collective-permute-start(bf16[80,512]{1,0:T(8,128)(2,1)S(1)} %rotate_out.1.refs_3_.refs_0_), channel_id=1, source_target_pairs={{0,12},{1,13},{2,14},{3,15},{4,0},{5,1},{6,2},{7,3},{8,4},{9,5},{1... | collective-permute-start | bytes 245768 | tf_op jit(solution)/shard_map/ppermute | solution.py:33
  59.4 6.2 %collective-permute-start.21 = (bf16[3,80,512]{2,1,0:T(8,128)(2,1)S(1)}, bf16[3,80,512]{2,1,0:T(8,128)(2,1)S(1)}, u32[]{:S(2)}, u32[]{:S(2)}) collective-permute-start(bf16[3,80,512]{2,1,0:T(8,128)(2,1)S(1)} %pile.9.z_ref), channel_id=1, source_target_pairs={{0,2},{1,3},{2,0},{3,1},{4,6},{5,7},{6,4},{7,5},{8,10},{9,11},{10,... | collective-permute-start | bytes 737288 | tf_op jit(solution)/shard_map/ppermute | solution.py:33
  59.7 5.0 %collective-permute-start.22 = (bf16[2,80,512]{2,1,0:T(8,128)(2,1)S(1)}, bf16[2,80,512]{2,1,0:T(8,128)(2,1)S(1)}, u32[]{:S(2)}, u32[]{:S(2)}) collective-permute-start(bf16[2,80,512]{2,1,0:T(8,128)(2,1)S(1)} %pile.8.refs_5_.near_ref), channel_id=1, source_target_pairs={{0,1},{1,0},{2,3},{3,2},{4,5},{5,4},{6,7},{7,6},{8,9},{9,8},{10,11... | collective-permute-start | bytes 491528 | tf_op jit(solution)/shard_map/ppermute | solution.py:33
  61.4 6.5 %collective-permute-start.24 = (bf16[3,80,512]{2,1,0:T(8,128)(2,1)S(1)}, bf16[3,80,512]{2,1,0:T(8,128)(2,1)S(1)}, u32[]{:S(2)}, u32[]{:S(2)}) collective-permute-start(bf16[3,80,512]{2,1,0:T(8,128)(2,1)S(1)} %pile.9.z_ref), channel_id=1, source_target_pairs={{0,1},{1,0},{2,3},{3,2},{4,5},{5,4},{6,7},{7,6},{8,9},{9,8},{10,11... | collective-permute-start | bytes 737288 | tf_op jit(solution)/shard_map/ppermute | solution.py:33
  65.6 4.0 %collective-permute-start.23 = (bf16[3,80,512]{2,1,0:T(8,128)(2,1)S(1)}, bf16[3,80,512]{2,1,0:T(8,128)(2,1)S(1)}, u32[]{:S(2)}, u32[]{:S(2)}) collective-permute-start(bf16[3,80,512]{2,1,0:T(8,128)(2,1)S(1)} %after.3.y_ref), channel_id=1, source_target_pairs={{0,1},{1,0},{2,3},{3,2},{4,5},{5,4},{6,7},{7,6},{8,9},{9,8},{10,11... | collective-permute-start | bytes 737288 | tf_op jit(solution)/shard_map/ppermute | solution.py:33
  (6 other events, 45.2 us)

commit v16 on v12

--- a/solution.py
+++ b/solution.py
@@ -201,28 +201,27 @@
             out_ref[:, tile * 128 : (tile + 1) * 128] = block
 
 
-def fold_kernel(grads_ref, acts_ref, block_ref, *refs):
-    own, every_ref, rows = refs[:-2], refs[-2], refs[-1]
-    fold_one(grads_ref, 0, [block_ref], rows)
-    for chunk, out_ref in enumerate(own):
-        fold_one(acts_ref, chunk * SUBLANES * out_ref.shape[1], [out_ref, every_ref.at[chunk]], rows)
-
-
-def folded(grads, acts):
-    height = grads.shape[0] * SUBLANES
-    width = acts.shape[1] // (CHUNKS * SUBLANES)
-    shapes = [(height, grads.shape[1] // SUBLANES)] + [(height, width)] * CHUNKS + [(CHUNKS, height, width)]
-    tiles = max(shape[-1] for shape in shapes) // 128
-    return pl.pallas_call(
-        fold_kernel,
-        out_shape=[jax.ShapeDtypeStruct(shape, acts.dtype) for shape in shapes],
-        in_specs=[VMEM] * 2,
+def fold_kernel(waits, chunks, from_ref, *refs):
+    outs, rows = refs[waits:-1], refs[-1]
+    for chunk in range(chunks):
+        width = outs[chunk].shape[1]
+        also = [outs[chunks].at[chunk]] if chunks > 1 else []
+        fold_one(from_ref, chunk * SUBLANES * width, [outs[chunk], *also], rows)
+
+
+def folded(array, chunks, waits):
+    shape = (array.shape[0] * SUBLANES, array.shape[1] // (chunks * SUBLANES))
+    shapes = [shape] * chunks + ([(chunks, *shape)] if chunks > 1 else [])
+    return pl.pallas_call(
+        functools.partial(fold_kernel, len(waits), chunks),
+        out_shape=[jax.ShapeDtypeStruct(shape, array.dtype) for shape in shapes],
+        in_specs=[VMEM] + [ANY] * len(waits),
         out_specs=[VMEM] * len(shapes),
-        scratch_shapes=[pltpu.VMEM((tiles, height, 128), jnp.float32)],
+        scratch_shapes=[pltpu.VMEM((shape[1] // 128, shape[0], 128), jnp.float32)],
         compiler_params=pltpu.CompilerParams(vmem_limit_bytes=4 * 2**20),
-        cost_estimate=pl.CostEstimate(flops=0, bytes_accessed=4 * acts.size, transcendentals=0),
+        cost_estimate=pl.CostEstimate(flops=0, bytes_accessed=4 * array.size, transcendentals=0),
         name="fold",
-    )(grads, acts)
+    )(array, *waits)
 
 
 def pile_kernel(blocks, *refs):
@@ -366,12 +365,13 @@
         y = send(z, across(devices))
         return z, y, send(z, swap(devices)), send(y, swap(devices))
 
-    block, *own, every = folded(grads, acts)
+    [block] = folded(grads, 1, [])
+    *own, every = folded(acts, CHUNKS, [block])
     fetched = fetch(basis_out, [block])
     mine = basis_in.T
     theirs = send(mine, swap(devices))
     own_across = send(every, across(devices))
-    grads_all = others(pile([block] + along_all(block), [own_across, fetched]))
+    grads_all = others(pile([block] + along_all(block), [fetched, theirs, every]))
 
     acts_z, acts_y = [], []
 
@@ -383,7 +383,7 @@
         return rotate_in(tokens, chunk, own[chunk], own_across, acts_z[chunk], acts_y[chunk], mine, theirs, before)
 
     chunk_along(0, [])
-    sq_out = rotate_out(tokens, *grads_all, fetched, [acts_z[0]])
+    sq_out = rotate_out(tokens, *grads_all, fetched, [acts_z[0], own_across])
     came = along_all(sq_out)
     for chunk in range(1, CHUNKS):
         chunk_along(chunk, [sq_out])

time: 68.1 us -> 67 us (0.984)
  starting transfers between devices: 29.9 us -> 28.1 us
  waiting for transfers between devices: 20.9 us -> 21.7 us
    ppermute x23, starting transfers between devices: 29.9 us -> 28.1 us  [send(): return lax.ppermute(block, 'wide', pairs)]
    ppermute x23, waiting for transfers between devices: 20.9 us -> 21.7 us  [send(): return lax.ppermute(block, 'wide', pairs)]
  transfers between devices with their start and end apart: 23 -> 23, of which waited for: 10 -> 8; matrix products, arithmetic and copies ran while one was open for 0% -> 0% of each run, Pallas kernels for 16% -> 16%
where the time goes in v16:
time: 67 us; the launch traced here: 66.8 us
  starting transfers between devices  28.1 us (42%)
  waiting for transfers between devices  21.7 us (32%)
  Pallas kernels  11.5 us (17%)
  local copies, waits for them, and re-layouts  5.31 us (8%)
    ppermute x23, starting transfers between devices, send(): return lax.ppermute(block, 'wide', pairs)  28.1 us
    ppermute x23, waiting for transfers between devices, send(): return lax.ppermute(block, 'wide', pairs)  21.7 us
    pallas_call x2, Pallas kernels, rotate_in(): pl.pallas_call(functools.partial(rotate_in_kernel, tokens, chunk, len(bef...  5.61 us
    unnamed x10, local copies, waits for them, and re-layouts  5.31 us
    pallas_call x1, Pallas kernels, rotate_out(): pl.pallas_call(functools.partial(rotate_out_kernel, tokens, len(waits)),...  2.29 us
    pallas_call x1, Pallas kernels, combine(): pl.pallas_call(combine_kernel, out_shape=jax.ShapeDtypeStruct((own.shape[...  1.66 us
  transfers between devices with their start and end apart: 23, of which 8 were waited for; matrix products, arithmetic and copies ran while one was open for 0% of the time, Pallas kernels for 16%

profile of v16, /device:TPU:0, one launch (start us, length us, event | category | flops | bytes accessed | tf_op | source)
XLA Modules:
  0.0 66.8 jit_solution(5350036793394008155)
XLA Ops:
  1.4 2.6 %collective-permute-start.4 = (bf16[40,1024]{1,0:T(8,128)(2,1)S(1)}, bf16[40,1024]{1,0:T(8,128)(2,1)S(1)}, u32[]{:S(2)}, u32[]{:S(2)}) collective-permute-start(bf16[40,1024]{1,0:T(8,128)(2,1)S(1)} %fold.2.refs_0_), channel_id=1, source_target_pairs={{0,4},{1,5},{2,6},{3,7},{4,8},{5,9},{6,10},{7,11},{8,12},{9,13},{1... | collective-permute-start | bytes 245768 | tf_op jit(solution)/shard_map/ppermute | solution.py:33
  4.0 2.6 %collective-permute-start.5 = (bf16[40,1024]{1,0:T(8,128)(2,1)S(1)}, bf16[40,1024]{1,0:T(8,128)(2,1)S(1)}, u32[]{:S(2)}, u32[]{:S(2)}) collective-permute-start(bf16[40,1024]{1,0:T(8,128)(2,1)S(1)} %fold.2.refs_0_), channel_id=1, source_target_pairs={{0,8},{1,9},{2,10},{3,11},{4,12},{5,13},{6,14},{7,15},{8,0},{9,1},... | collective-permute-start | bytes 245768 | tf_op jit(solution)/shard_map/ppermute | solution.py:33
  6.6 1.3 %collective-permute-start.6 = (bf16[40,1024]{1,0:T(8,128)(2,1)S(1)}, bf16[40,1024]{1,0:T(8,128)(2,1)S(1)}, u32[]{:S(2)}, u32[]{:S(2)}) collective-permute-start(bf16[40,1024]{1,0:T(8,128)(2,1)S(1)} %fold.2.refs_0_), channel_id=1, source_target_pairs={{0,12},{1,13},{2,14},{3,15},{4,0},{5,1},{6,2},{7,3},{8,4},{9,5},{1... | collective-permute-start | bytes 245768 | tf_op jit(solution)/shard_map/ppermute | solution.py:33
  8.0 1.0 %copy-done.1 = bf16[5,28672]{1,0:T(8,128)(2,1)S(1)} copy-done((bf16[5,28672]{1,0:T(8,128)(2,1)S(1)}, bf16[5,28672]{1,0:T(8,128)(2,1)}, u32[]{:S(2)}) %copy-start.1) | copy-done | bytes 286744
  9.2 3.4 %copy-done = bf16[8192,512]{1,0:T(8,128)(2,1)S(1)} copy-done((bf16[8192,512]{1,0:T(8,128)(2,1)S(1)}, bf16[8192,512]{1,0:T(8,128)(2,1)}, u32[]{:S(2)}) %copy-start) | copy-done | bytes 8388632
  13.3 1.6 %collective-permute-start.8 = (bf16[4,40,1024]{2,1,0:T(8,128)(2,1)S(1)}, bf16[4,40,1024]{2,1,0:T(8,128)(2,1)S(1)}, u32[]{:S(2)}, u32[]{:S(2)}) collective-permute-start(bf16[4,40,1024]{2,1,0:T(8,128)(2,1)S(1)} %pile.4.z_ref), channel_id=1, source_target_pairs={{0,2},{1,3},{2,0},{3,1},{4,6},{5,7},{6,4},{7,5},{8,10},{9,11},{10,... | collective-permute-start | bytes 983048 | tf_op jit(solution)/shard_map/ppermute | solution.py:33
  14.9 1.8 %collective-permute-start.11 = (bf16[40,1792]{1,0:T(8,128)(2,1)S(1)}, bf16[40,1792]{1,0:T(8,128)(2,1)S(1)}, u32[]{:S(2)}, u32[]{:S(2)}) collective-permute-start(bf16[40,1792]{1,0:T(8,128)(2,1)S(1)} %get-tuple-element.12.own_ref), channel_id=1, source_target_pairs={{0,4},{1,5},{2,6},{3,7},{4,8},{5,9},{6,10},{7,11},{8,12},{9,13},{1... | collective-permute-start | bytes 430088 | tf_op jit(solution)/shard_map/ppermute | solution.py:33
  16.7 1.6 %collective-permute-start.12 = (bf16[40,1792]{1,0:T(8,128)(2,1)S(1)}, bf16[40,1792]{1,0:T(8,128)(2,1)S(1)}, u32[]{:S(2)}, u32[]{:S(2)}) collective-permute-start(bf16[40,1792]{1,0:T(8,128)(2,1)S(1)} %get-tuple-element.12.own_ref), channel_id=1, source_target_pairs={{0,8},{1,9},{2,10},{3,11},{4,12},{5,13},{6,14},{7,15},{8,0},{9,1},... | collective-permute-start | bytes 430088 | tf_op jit(solution)/shard_map/ppermute | solution.py:33
  19.0 4.4 %collective-permute-done.11.refs_0_ = bf16[40,1792]{1,0:T(8,128)(2,1)S(1)} collective-permute-done((bf16[40,1792]{1,0:T(8,128)(2,1)S(1)}, bf16[40,1792]{1,0:T(8,128)(2,1)S(1)}, u32[]{:S(2)}, u32[]{:S(2)}) %collective-permute-start.11) | collective-permute-done | bytes 143392 | tf_op jit(solution)/shard_map/ppermute | solution.py:33
  23.9 4.0 %collective-permute-done.12.refs_1_ = bf16[40,1792]{1,0:T(8,128)(2,1)S(1)} collective-permute-done((bf16[40,1792]{1,0:T(8,128)(2,1)S(1)}, bf16[40,1792]{1,0:T(8,128)(2,1)S(1)}, u32[]{:S(2)}, u32[]{:S(2)}) %collective-permute-start.12) | collective-permute-done | bytes 143392 | tf_op jit(solution)/shard_map/ppermute | solution.py:33
  29.0 3.1 %collective-permute-start.1 = (bf16[40,1792]{1,0:T(8,128)(2,1)S(1)}, bf16[40,1792]{1,0:T(8,128)(2,1)S(1)}, u32[]{:S(2)}, u32[]{:S(2)}) collective-permute-start(bf16[40,1792]{1,0:T(8,128)(2,1)S(1)} %get-tuple-element.10.own_ref), channel_id=1, source_target_pairs={{0,4},{1,5},{2,6},{3,7},{4,8},{5,9},{6,10},{7,11},{8,12},{9,13},{1... | collective-permute-start | bytes 430088 | tf_op jit(solution)/shard_map/ppermute | solution.py:33
  32.1 1.0 %collective-permute-start.2 = (bf16[40,1792]{1,0:T(8,128)(2,1)S(1)}, bf16[40,1792]{1,0:T(8,128)(2,1)S(1)}, u32[]{:S(2)}, u32[]{:S(2)}) collective-permute-start(bf16[40,1792]{1,0:T(8,128)(2,1)S(1)} %get-tuple-element.10.own_ref), channel_id=1, source_target_pairs={{0,8},{1,9},{2,10},{3,11},{4,12},{5,13},{6,14},{7,15},{8,0},{9,1},... | collective-permute-start | bytes 430088 | tf_op jit(solution)/shard_map/ppermute | solution.py:33
  33.1 1.5 %collective-permute-start.3 = (bf16[40,1792]{1,0:T(8,128)(2,1)S(1)}, bf16[40,1792]{1,0:T(8,128)(2,1)S(1)}, u32[]{:S(2)}, u32[]{:S(2)}) collective-permute-start(bf16[40,1792]{1,0:T(8,128)(2,1)S(1)} %get-tuple-element.10.own_ref), channel_id=1, source_target_pairs={{0,12},{1,13},{2,14},{3,15},{4,0},{5,1},{6,2},{7,3},{8,4},{9,5},{1... | collective-permute-start | bytes 430088 | tf_op jit(solution)/shard_map/ppermute | solution.py:33
  34.5 2.3 %rotate_out.1.refs_3_.refs_0_ = bf16[80,512]{1,0:T(8,128)(2,1)S(1)} custom-call(bf16[4,40,1024]{2,1,0:T(8,128)(2,1)S(1)} %pile.4.z_ref, bf16[4,40,1024]{2,1,0:T(8,128)(2,1)S(1)} %collective-permute-done.8.y_ref, bf16[4,40,1024]{2,1,0:T(8,128)(2,1)S(1)} %collective-permute-done.9.cz_ref, bf16[4,40,1024]{2,1,0:T(8,128)(2,1)S(1)} %collective-permute-done.10.cy_ref, ...), custom_call_target="tpu_custom_call" | custom-call | flops 671088640 | bytes 8388608 | tf_op jit(solution)/shard_map/rotate_out/pallas_call | solution.py:105
  37.1 5.1 %collective-permute-done.2.refs_1_ = bf16[40,1792]{1,0:T(8,128)(2,1)S(1)} collective-permute-done((bf16[40,1792]{1,0:T(8,128)(2,1)S(1)}, bf16[40,1792]{1,0:T(8,128)(2,1)S(1)}, u32[]{:S(2)}, u32[]{:S(2)}) %collective-permute-start.2) | collective-permute-done | bytes 143392 | tf_op jit(solution)/shard_map/ppermute | solution.py:33
  42.2 1.6 %collective-permute-start.14 = (bf16[3,40,1792]{2,1,0:T(8,128)(2,1)S(1)}, bf16[3,40,1792]{2,1,0:T(8,128)(2,1)S(1)}, u32[]{:S(2)}, u32[]{:S(2)}) collective-permute-start(bf16[3,40,1792]{2,1,0:T(8,128)(2,1)S(1)} %pile.6.z_ref.refs_5_), channel_id=1, source_target_pairs={{0,2},{1,3},{2,0},{3,1},{4,6},{5,7},{6,4},{7,5},{8,10},{9,11},{10,... | collective-permute-start | bytes 1290248 | tf_op jit(solution)/shard_map/ppermute | solution.py:33
  43.8 3.5 %collective-permute-start.17 = (bf16[80,512]{1,0:T(8,128)(2,1)S(1)}, bf16[80,512]{1,0:T(8,128)(2,1)S(1)}, u32[]{:S(2)}, u32[]{:S(2)}) collective-permute-start(bf16[80,512]{1,0:T(8,128)(2,1)S(1)} %rotate_out.1.refs_3_.refs_0_), channel_id=1, source_target_pairs={{0,4},{1,5},{2,6},{3,7},{4,8},{5,9},{6,10},{7,11},{8,12},{9,13},{1... | collective-permute-start | bytes 245768 | tf_op jit(solution)/shard_map/ppermute | solution.py:33
  47.4 2.2 %collective-permute-start.18 = (bf16[80,512]{1,0:T(8,128)(2,1)S(1)}, bf16[80,512]{1,0:T(8,128)(2,1)S(1)}, u32[]{:S(2)}, u32[]{:S(2)}) collective-permute-start(bf16[80,512]{1,0:T(8,128)(2,1)S(1)} %rotate_out.1.refs_3_.refs_0_), channel_id=1, source_target_pairs={{0,8},{1,9},{2,10},{3,11},{4,12},{5,13},{6,14},{7,15},{8,0},{9,1},... | collective-permute-start | bytes 245768 | tf_op jit(solution)/shard_map/ppermute | solution.py:33
  49.8 2.8 %rotate_in.2.refs_0_.refs_4_ = f32[192,40]{1,0:T(8,128)S(1)} custom-call(bf16[40,1792]{1,0:T(8,128)(2,1)S(1)} %get-tuple-element.12.own_ref, bf16[2,40,1792]{2,1,0:T(8,128)(2,1)S(1)} %collective-permute-done.refs_1_.across_ref, bf16[3,40,1792]{2,1,0:T(8,128)(2,1)S(1)} %pile.5.refs_0_.z_ref, bf16[3,40,1792]{2,1,0:T(8,128)(2,1)S(1)} %collective-permute-done.15.y_ref, ...), custom_call_target="tpu_custom_call" | custom-call | flops 220200960 | bytes 5505024 | tf_op jit(solution)/shard_map/rotate_in/pallas_call | solution.py:171
  52.6 2.0 %collective-permute-done.18.refs_2_ = bf16[80,512]{1,0:T(8,128)(2,1)S(1)} collective-permute-done((bf16[80,512]{1,0:T(8,128)(2,1)S(1)}, bf16[80,512]{1,0:T(8,128)(2,1)S(1)}, u32[]{:S(2)}, u32[]{:S(2)}) %collective-permute-start.18) | collective-permute-done | bytes 81952 | tf_op jit(solution)/shard_map/ppermute | solution.py:33
  55.5 2.8 %rotate_in.3 = (bf16[96,40]{1,0:T(8,128)(2,1)S(1)}, bf16[96,40]{1,0:T(8,128)(2,1)S(1)}) custom-call(bf16[40,1792]{1,0:T(8,128)(2,1)S(1)} %get-tuple-element.10.own_ref, bf16[2,40,1792]{2,1,0:T(8,128)(2,1)S(1)} %collective-permute-done.refs_1_.across_ref, bf16[3,40,1792]{2,1,0:T(8,128)(2,1)S(1)} %pile.6.z_ref.refs_5_, ...), custom_call_target="tpu_custom_call" | custom-call | flops 220200960 | bytes 5505024 | tf_op jit(solution)/shard_map/rotate_in/pallas_call | solution.py:171
  58.9 5.2 %collective-permute-done.20.refs_0_ = bf16[4,80,512]{2,1,0:T(8,128)(2,1)S(1)} collective-permute-done((bf16[4,80,512]{2,1,0:T(8,128)(2,1)S(1)}, bf16[4,80,512]{2,1,0:T(8,128)(2,1)S(1)}, u32[]{:S(2)}, u32[]{:S(2)}) %collective-permute-start.20) | collective-permute-done | bytes 327712 | tf_op jit(solution)/shard_map/ppermute | solution.py:33
  64.1 1.7 %combine.1._ = bf16[96,8192]{1,0:T(8,128)(2,1)} custom-call(bf16[96,40]{1,0:T(8,128)(2,1)S(1)} %get-tuple-element.13.own_ref, bf16[96,40]{1,0:T(8,128)(2,1)S(1)} %collective-permute-done.16.refs_1_.other_ref, bf16[4,80,512]{2,1,0:T(8,128)(2,1)S(1)} %pile.7.z_ref, bf16[4,80,512]{2,1,0:T(8,128)(2,1)S(1)} %after.1.y_ref, ...), custom_call_target="tpu_custom_call" | custom-call | flops 125829120 | bytes 3145728 | tf_op jit(solution)/shard_map/combine/pallas_call | solution.py:307
  65.8 1.0 %finish.1 = bf16[96,8192]{1,0:T(8,128)(2,1)} custom-call(bf16[96,40]{1,0:T(8,128)(2,1)S(1)} %get-tuple-element.13.own_ref, bf16[96,40]{1,0:T(8,128)(2,1)S(1)} %collective-permute-done.16.refs_1_.other_ref, bf16[4,80,512]{2,1,0:T(8,128)(2,1)S(1)} %collective-permute-done.21.cy_ref, bf16[96,8192]{1,0:T(8,128)(2,1)} %combine.1._), custom_call_target="tpu_custom_call", output_to_operand_aliasing={{}: (3, {})} | custom-call | flops 31457280 | bytes 655360 | tf_op jit(solution)/shard_map/finish/pallas_call | solution.py:338
  (46 shorter events, 6.5 us)
Async XLA Ops:
  0.0 13.2 %collective-permute-start.7 = (bf16[96,28672]{1,0:T(8,128)(2,1)}, bf16[96,28672]{1,0:T(8,128)(2,1)S(1)}, u32[]{:S(2)}, u32[]{:S(2)}) collective-permute-start(bf16[96,28672]{1,0:T(8,128)(2,1)} %bitcast.1), channel_id=1, source_target_pairs={{0,1},{1,0},{2,3},{3,2},{4,5},{5,4},{6,7},{7,6},{8,9},{9,8},{10,11... | collective-permute-start | bytes 16515080 | tf_op jit(solution)/shard_map/ppermute | solution.py:33
  1.4 11.8 %collective-permute-start.4 = (bf16[40,1024]{1,0:T(8,128)(2,1)S(1)}, bf16[40,1024]{1,0:T(8,128)(2,1)S(1)}, u32[]{:S(2)}, u32[]{:S(2)}) collective-permute-start(bf16[40,1024]{1,0:T(8,128)(2,1)S(1)} %fold.2.refs_0_), channel_id=1, source_target_pairs={{0,4},{1,5},{2,6},{3,7},{4,8},{5,9},{6,10},{7,11},{8,12},{9,13},{1... | collective-permute-start | bytes 245768 | tf_op jit(solution)/shard_map/ppermute | solution.py:33
  4.0 9.2 %collective-permute-start.5 = (bf16[40,1024]{1,0:T(8,128)(2,1)S(1)}, bf16[40,1024]{1,0:T(8,128)(2,1)S(1)}, u32[]{:S(2)}, u32[]{:S(2)}) collective-permute-start(bf16[40,1024]{1,0:T(8,128)(2,1)S(1)} %fold.2.refs_0_), channel_id=1, source_target_pairs={{0,8},{1,9},{2,10},{3,11},{4,12},{5,13},{6,14},{7,15},{8,0},{9,1},... | collective-permute-start | bytes 245768 | tf_op jit(solution)/shard_map/ppermute | solution.py:33
  6.6 6.6 %collective-permute-start.6 = (bf16[40,1024]{1,0:T(8,128)(2,1)S(1)}, bf16[40,1024]{1,0:T(8,128)(2,1)S(1)}, u32[]{:S(2)}, u32[]{:S(2)}) collective-permute-start(bf16[40,1024]{1,0:T(8,128)(2,1)S(1)} %fold.2.refs_0_), channel_id=1, source_target_pairs={{0,12},{1,13},{2,14},{3,15},{4,0},{5,1},{6,2},{7,3},{8,4},{9,5},{1... | collective-permute-start | bytes 245768 | tf_op jit(solution)/shard_map/ppermute | solution.py:33
  13.3 10.7 %collective-permute-start.8 = (bf16[4,40,1024]{2,1,0:T(8,128)(2,1)S(1)}, bf16[4,40,1024]{2,1,0:T(8,128)(2,1)S(1)}, u32[]{:S(2)}, u32[]{:S(2)}) collective-permute-start(bf16[4,40,1024]{2,1,0:T(8,128)(2,1)S(1)} %pile.4.z_ref), channel_id=1, source_target_pairs={{0,2},{1,3},{2,0},{3,1},{4,6},{5,7},{6,4},{7,5},{8,10},{9,11},{10,... | collective-permute-start | bytes 983048 | tf_op jit(solution)/shard_map/ppermute | solution.py:33
  14.9 8.6 %collective-permute-start.11 = (bf16[40,1792]{1,0:T(8,128)(2,1)S(1)}, bf16[40,1792]{1,0:T(8,128)(2,1)S(1)}, u32[]{:S(2)}, u32[]{:S(2)}) collective-permute-start(bf16[40,1792]{1,0:T(8,128)(2,1)S(1)} %get-tuple-element.12.own_ref), channel_id=1, source_target_pairs={{0,4},{1,5},{2,6},{3,7},{4,8},{5,9},{6,10},{7,11},{8,12},{9,13},{1... | collective-permute-start | bytes 430088 | tf_op jit(solution)/shard_map/ppermute | solution.py:33
  16.7 16.4 %collective-permute-start.9 = (bf16[4,40,1024]{2,1,0:T(8,128)(2,1)S(1)}, bf16[4,40,1024]{2,1,0:T(8,128)(2,1)S(1)}, u32[]{:S(2)}, u32[]{:S(2)}) collective-permute-start(bf16[4,40,1024]{2,1,0:T(8,128)(2,1)S(1)} %pile.4.z_ref), channel_id=1, source_target_pairs={{0,1},{1,0},{2,3},{3,2},{4,5},{5,4},{6,7},{7,6},{8,9},{9,8},{10,11... | collective-permute-start | bytes 983048 | tf_op jit(solution)/shard_map/ppermute | solution.py:33
  16.7 11.2 %collective-permute-start.12 = (bf16[40,1792]{1,0:T(8,128)(2,1)S(1)}, bf16[40,1792]{1,0:T(8,128)(2,1)S(1)}, u32[]{:S(2)}, u32[]{:S(2)}) collective-permute-start(bf16[40,1792]{1,0:T(8,128)(2,1)S(1)} %get-tuple-element.12.own_ref), channel_id=1, source_target_pairs={{0,8},{1,9},{2,10},{3,11},{4,12},{5,13},{6,14},{7,15},{8,0},{9,1},... | collective-permute-start | bytes 430088 | tf_op jit(solution)/shard_map/ppermute | solution.py:33
  18.3 10.1 %collective-permute-start.13 = (bf16[40,1792]{1,0:T(8,128)(2,1)S(1)}, bf16[40,1792]{1,0:T(8,128)(2,1)S(1)}, u32[]{:S(2)}, u32[]{:S(2)}) collective-permute-start(bf16[40,1792]{1,0:T(8,128)(2,1)S(1)} %get-tuple-element.12.own_ref), channel_id=1, source_target_pairs={{0,12},{1,13},{2,14},{3,15},{4,0},{5,1},{6,2},{7,3},{8,4},{9,5},{1... | collective-permute-start | bytes 430088 | tf_op jit(solution)/shard_map/ppermute | solution.py:33
  23.4 8.7 %collective-permute-start = (bf16[2,40,1792]{2,1,0:T(8,128)(2,1)S(1)}, bf16[2,40,1792]{2,1,0:T(8,128)(2,1)S(1)}, u32[]{:S(2)}, u32[]{:S(2)}) collective-permute-start(bf16[2,40,1792]{2,1,0:T(8,128)(2,1)S(1)} %get-tuple-element.11.refs_6_), channel_id=1, source_target_pairs={{0,2},{1,3},{2,0},{3,1},{4,6},{5,7},{6,4},{7,5},{8,10},{9,11},{10,... | collective-permute-start | bytes 860168 | tf_op jit(solution)/shard_map/ppermute | solution.py:33
  23.9 10.6 %collective-permute-start.10 = (bf16[4,40,1024]{2,1,0:T(8,128)(2,1)S(1)}, bf16[4,40,1024]{2,1,0:T(8,128)(2,1)S(1)}, u32[]{:S(2)}, u32[]{:S(2)}) collective-permute-start(bf16[4,40,1024]{2,1,0:T(8,128)(2,1)S(1)} %collective-permute-done.8.y_ref), channel_id=1, source_target_pairs={{0,1},{1,0},{2,3},{3,2},{4,5},{5,4},{6,7},{7,6},{8,9},{9,8},{10,11... | collective-permute-start | bytes 983048 | tf_op jit(solution)/shard_map/ppermute | solution.py:33
  28.4 21.4 %collective-permute-start.15 = (bf16[3,40,1792]{2,1,0:T(8,128)(2,1)S(1)}, bf16[3,40,1792]{2,1,0:T(8,128)(2,1)S(1)}, u32[]{:S(2)}, u32[]{:S(2)}) collective-permute-start(bf16[3,40,1792]{2,1,0:T(8,128)(2,1)S(1)} %pile.5.refs_0_.z_ref), channel_id=1, source_target_pairs={{0,2},{1,3},{2,0},{3,1},{4,6},{5,7},{6,4},{7,5},{8,10},{9,11},{10,... | collective-permute-start | bytes 1290248 | tf_op jit(solution)/shard_map/ppermute | solution.py:33
  29.0 20.8 %slice-start.1 = ((s8[5505024]{0:T(1024)(128)(4,1)}), s8[1310720]{0:T(1024)(128)(4,1)S(1)}, s32[]{:S(2)}) async-start(s8[5505024]{0:T(1024)(128)(4,1)} %bitcast.2), calls=%async_computation.1 | async-start | bytes 2621440
  29.0 8.1 %collective-permute-start.1 = (bf16[40,1792]{1,0:T(8,128)(2,1)S(1)}, bf16[40,1792]{1,0:T(8,128)(2,1)S(1)}, u32[]{:S(2)}, u32[]{:S(2)}) collective-permute-start(bf16[40,1792]{1,0:T(8,128)(2,1)S(1)} %get-tuple-element.10.own_ref), channel_id=1, source_target_pairs={{0,4},{1,5},{2,6},{3,7},{4,8},{5,9},{6,10},{7,11},{8,12},{9,13},{1... | collective-permute-start | bytes 430088 | tf_op jit(solution)/shard_map/ppermute | solution.py:33
  32.1 10.0 %collective-permute-start.2 = (bf16[40,1792]{1,0:T(8,128)(2,1)S(1)}, bf16[40,1792]{1,0:T(8,128)(2,1)S(1)}, u32[]{:S(2)}, u32[]{:S(2)}) collective-permute-start(bf16[40,1792]{1,0:T(8,128)(2,1)S(1)} %get-tuple-element.10.own_ref), channel_id=1, source_target_pairs={{0,8},{1,9},{2,10},{3,11},{4,12},{5,13},{6,14},{7,15},{8,0},{9,1},... | collective-permute-start | bytes 430088 | tf_op jit(solution)/shard_map/ppermute | solution.py:33
  33.1 9.1 %collective-permute-start.3 = (bf16[40,1792]{1,0:T(8,128)(2,1)S(1)}, bf16[40,1792]{1,0:T(8,128)(2,1)S(1)}, u32[]{:S(2)}, u32[]{:S(2)}) collective-permute-start(bf16[40,1792]{1,0:T(8,128)(2,1)S(1)} %get-tuple-element.10.own_ref), channel_id=1, source_target_pairs={{0,12},{1,13},{2,14},{3,15},{4,0},{5,1},{6,2},{7,3},{8,4},{9,5},{1... | collective-permute-start | bytes 430088 | tf_op jit(solution)/shard_map/ppermute | solution.py:33
  42.2 13.3 %collective-permute-start.14 = (bf16[3,40,1792]{2,1,0:T(8,128)(2,1)S(1)}, bf16[3,40,1792]{2,1,0:T(8,128)(2,1)S(1)}, u32[]{:S(2)}, u32[]{:S(2)}) collective-permute-start(bf16[3,40,1792]{2,1,0:T(8,128)(2,1)S(1)} %pile.6.z_ref.refs_5_), channel_id=1, source_target_pairs={{0,2},{1,3},{2,0},{3,1},{4,6},{5,7},{6,4},{7,5},{8,10},{9,11},{10,... | collective-permute-start | bytes 1290248 | tf_op jit(solution)/shard_map/ppermute | solution.py:33
  43.8 8.7 %collective-permute-start.17 = (bf16[80,512]{1,0:T(8,128)(2,1)S(1)}, bf16[80,512]{1,0:T(8,128)(2,1)S(1)}, u32[]{:S(2)}, u32[]{:S(2)}) collective-permute-start(bf16[80,512]{1,0:T(8,128)(2,1)S(1)} %rotate_out.1.refs_3_.refs_0_), channel_id=1, source_target_pairs={{0,4},{1,5},{2,6},{3,7},{4,8},{5,9},{6,10},{7,11},{8,12},{9,13},{1... | collective-permute-start | bytes 245768 | tf_op jit(solution)/shard_map/ppermute | solution.py:33
  47.4 7.2 %collective-permute-start.18 = (bf16[80,512]{1,0:T(8,128)(2,1)S(1)}, bf16[80,512]{1,0:T(8,128)(2,1)S(1)}, u32[]{:S(2)}, u32[]{:S(2)}) collective-permute-start(bf16[80,512]{1,0:T(8,128)(2,1)S(1)} %rotate_out.1.refs_3_.refs_0_), channel_id=1, source_target_pairs={{0,8},{1,9},{2,10},{3,11},{4,12},{5,13},{6,14},{7,15},{8,0},{9,1},... | collective-permute-start | bytes 245768 | tf_op jit(solution)/shard_map/ppermute | solution.py:33
  49.6 5.4 %collective-permute-start.19 = (bf16[80,512]{1,0:T(8,128)(2,1)S(1)}, bf16[80,512]{1,0:T(8,128)(2,1)S(1)}, u32[]{:S(2)}, u32[]{:S(2)}) collective-permute-start(bf16[80,512]{1,0:T(8,128)(2,1)S(1)} %rotate_out.1.refs_3_.refs_0_), channel_id=1, source_target_pairs={{0,12},{1,13},{2,14},{3,15},{4,0},{5,1},{6,2},{7,3},{8,4},{9,5},{1... | collective-permute-start | bytes 245768 | tf_op jit(solution)/shard_map/ppermute | solution.py:33
  55.0 9.1 %collective-permute-start.20 = (bf16[4,80,512]{2,1,0:T(8,128)(2,1)S(1)}, bf16[4,80,512]{2,1,0:T(8,128)(2,1)S(1)}, u32[]{:S(2)}, u32[]{:S(2)}) collective-permute-start(bf16[4,80,512]{2,1,0:T(8,128)(2,1)S(1)} %pile.7.z_ref), channel_id=1, source_target_pairs={{0,2},{1,3},{2,0},{3,1},{4,6},{5,7},{6,4},{7,5},{8,10},{9,11},{10,... | collective-permute-start | bytes 983048 | tf_op jit(solution)/shard_map/ppermute | solution.py:33
  55.5 8.6 %collective-permute-start.22 = (bf16[4,80,512]{2,1,0:T(8,128)(2,1)S(1)}, bf16[4,80,512]{2,1,0:T(8,128)(2,1)S(1)}, u32[]{:S(2)}, u32[]{:S(2)}) collective-permute-start(bf16[4,80,512]{2,1,0:T(8,128)(2,1)S(1)} %pile.7.z_ref), channel_id=1, source_target_pairs={{0,1},{1,0},{2,3},{3,2},{4,5},{5,4},{6,7},{7,6},{8,9},{9,8},{10,11... | collective-permute-start | bytes 983048 | tf_op jit(solution)/shard_map/ppermute | solution.py:33
  58.3 5.7 %collective-permute-start.16 = (bf16[96,40]{1,0:T(8,128)(2,1)S(1)}, bf16[96,40]{1,0:T(8,128)(2,1)S(1)}, u32[]{:S(2)}, u32[]{:S(2)}) collective-permute-start(bf16[96,40]{1,0:T(8,128)(2,1)S(1)} %get-tuple-element.14), channel_id=1, source_target_pairs={{0,1},{1,0},{2,3},{3,2},{4,5},{5,4},{6,7},{7,6},{8,9},{9,8},{10,11... | collective-permute-start | bytes 23048 | tf_op jit(solution)/shard_map/ppermute | solution.py:33
  64.1 1.7 %collective-permute-start.21 = (bf16[4,80,512]{2,1,0:T(8,128)(2,1)S(1)}, bf16[4,80,512]{2,1,0:T(8,128)(2,1)S(1)}, u32[]{:S(2)}, u32[]{:S(2)}) collective-permute-start(bf16[4,80,512]{2,1,0:T(8,128)(2,1)S(1)} %after.1.y_ref), channel_id=1, source_target_pairs={{0,1},{1,0},{2,3},{3,2},{4,5},{5,4},{6,7},{7,6},{8,9},{9,8},{10,11... | collective-permute-start | bytes 983048 | tf_op jit(solution)/shard_map/ppermute | solution.py:33
  (4 other events, 26.1 us)

commit v17 on v16

--- a/solution.py
+++ b/solution.py
@@ -367,11 +367,10 @@
 
     [block] = folded(grads, 1, [])
     *own, every = folded(acts, CHUNKS, [block])
-    fetched = fetch(basis_out, [block])
     mine = basis_in.T
     theirs = send(mine, swap(devices))
     own_across = send(every, across(devices))
-    grads_all = others(pile([block] + along_all(block), [fetched, theirs, every]))
+    grads_all = others(pile([block] + along_all(block), [theirs, every]))
 
     acts_z, acts_y = [], []
 
@@ -382,7 +381,8 @@
     def part(chunk, before):
         return rotate_in(tokens, chunk, own[chunk], own_across, acts_z[chunk], acts_y[chunk], mine, theirs, before)
 
-    chunk_along(0, [])
+    fetched = fetch(basis_out, [grads_all[0]])
+    chunk_along(0, [fetched])
     sq_out = rotate_out(tokens, *grads_all, fetched, [acts_z[0], own_across])
     came = along_all(sq_out)
     for chunk in range(1, CHUNKS):

time: 67 us -> 67 us (level)
  transfers between devices with their start and end apart: 23 -> 23, of which waited for: 8 -> 10; matrix products, arithmetic and copies ran while one was open for 0% -> 0% of each run, Pallas kernels for 16% -> 16%
where the time goes in v17:
time: 67 us; the launch traced here: 66.7 us
  starting transfers between devices  28.2 us (42%)
  waiting for transfers between devices  21.6 us (32%)
  Pallas kernels  11.5 us (17%)
  local copies, waits for them, and re-layouts  5.31 us (8%)
    ppermute x23, starting transfers between devices, send(): return lax.ppermute(block, 'wide', pairs)  28.2 us
    ppermute x23, waiting for transfers between devices, send(): return lax.ppermute(block, 'wide', pairs)  21.6 us
    pallas_call x2, Pallas kernels, rotate_in(): pl.pallas_call(functools.partial(rotate_in_kernel, tokens, chunk, len(bef...  5.62 us
    unnamed x10, local copies, waits for them, and re-layouts  5.31 us
    pallas_call x1, Pallas kernels, rotate_out(): pl.pallas_call(functools.partial(rotate_out_kernel, tokens, len(waits)),...  2.3 us
    pallas_call x1, Pallas kernels, combine(): pl.pallas_call(combine_kernel, out_shape=jax.ShapeDtypeStruct((own.shape[...  1.67 us
  transfers between devices with their start and end apart: 23, of which 10 were waited for; matrix products, arithmetic and copies ran while one was open for 0% of the time, Pallas kernels for 16%

profile of v17, /device:TPU:0, one launch (start us, length us, event | category | flops | bytes accessed | tf_op | source)
XLA Modules:
  0.0 66.7 jit_solution(4483210937025037936)
XLA Ops:
  1.4 2.6 %collective-permute-start.4 = (bf16[40,1024]{1,0:T(8,128)(2,1)S(1)}, bf16[40,1024]{1,0:T(8,128)(2,1)S(1)}, u32[]{:S(2)}, u32[]{:S(2)}) collective-permute-start(bf16[40,1024]{1,0:T(8,128)(2,1)S(1)} %fold.2.refs_0_), channel_id=1, source_target_pairs={{0,4},{1,5},{2,6},{3,7},{4,8},{5,9},{6,10},{7,11},{8,12},{9,13},{1... | collective-permute-start | bytes 245768 | tf_op jit(solution)/shard_map/ppermute | solution.py:33
  4.0 2.6 %collective-permute-start.5 = (bf16[40,1024]{1,0:T(8,128)(2,1)S(1)}, bf16[40,1024]{1,0:T(8,128)(2,1)S(1)}, u32[]{:S(2)}, u32[]{:S(2)}) collective-permute-start(bf16[40,1024]{1,0:T(8,128)(2,1)S(1)} %fold.2.refs_0_), channel_id=1, source_target_pairs={{0,8},{1,9},{2,10},{3,11},{4,12},{5,13},{6,14},{7,15},{8,0},{9,1},... | collective-permute-start | bytes 245768 | tf_op jit(solution)/shard_map/ppermute | solution.py:33
  6.6 1.3 %collective-permute-start.6 = (bf16[40,1024]{1,0:T(8,128)(2,1)S(1)}, bf16[40,1024]{1,0:T(8,128)(2,1)S(1)}, u32[]{:S(2)}, u32[]{:S(2)}) collective-permute-start(bf16[40,1024]{1,0:T(8,128)(2,1)S(1)} %fold.2.refs_0_), channel_id=1, source_target_pairs={{0,12},{1,13},{2,14},{3,15},{4,0},{5,1},{6,2},{7,3},{8,4},{9,5},{1... | collective-permute-start | bytes 245768 | tf_op jit(solution)/shard_map/ppermute | solution.py:33
  8.0 1.0 %copy-done.1 = bf16[5,28672]{1,0:T(8,128)(2,1)S(1)} copy-done((bf16[5,28672]{1,0:T(8,128)(2,1)S(1)}, bf16[5,28672]{1,0:T(8,128)(2,1)}, u32[]{:S(2)}) %copy-start.1) | copy-done | bytes 286744
  9.5 3.3 %collective-permute-done.5.refs_2_ = bf16[40,1024]{1,0:T(8,128)(2,1)S(1)} collective-permute-done((bf16[40,1024]{1,0:T(8,128)(2,1)S(1)}, bf16[40,1024]{1,0:T(8,128)(2,1)S(1)}, u32[]{:S(2)}, u32[]{:S(2)}) %collective-permute-start.5) | collective-permute-done | bytes 81952 | tf_op jit(solution)/shard_map/ppermute | solution.py:33
  12.8 1.6 %collective-permute-start.8 = (bf16[4,40,1024]{2,1,0:T(8,128)(2,1)S(1)}, bf16[4,40,1024]{2,1,0:T(8,128)(2,1)S(1)}, u32[]{:S(2)}, u32[]{:S(2)}) collective-permute-start(bf16[4,40,1024]{2,1,0:T(8,128)(2,1)S(1)} %pile.4.refs_0_.z_ref), channel_id=1, source_target_pairs={{0,2},{1,3},{2,0},{3,1},{4,6},{5,7},{6,4},{7,5},{8,10},{9,11},{10,... | collective-permute-start | bytes 983048 | tf_op jit(solution)/shard_map/ppermute | solution.py:33
  14.4 2.2 %collective-permute-start.11 = (bf16[40,1792]{1,0:T(8,128)(2,1)S(1)}, bf16[40,1792]{1,0:T(8,128)(2,1)S(1)}, u32[]{:S(2)}, u32[]{:S(2)}) collective-permute-start(bf16[40,1792]{1,0:T(8,128)(2,1)S(1)} %get-tuple-element.12.own_ref), channel_id=1, source_target_pairs={{0,4},{1,5},{2,6},{3,7},{4,8},{5,9},{6,10},{7,11},{8,12},{9,13},{1... | collective-permute-start | bytes 430088 | tf_op jit(solution)/shard_map/ppermute | solution.py:33
  16.7 1.6 %collective-permute-start.12 = (bf16[40,1792]{1,0:T(8,128)(2,1)S(1)}, bf16[40,1792]{1,0:T(8,128)(2,1)S(1)}, u32[]{:S(2)}, u32[]{:S(2)}) collective-permute-start(bf16[40,1792]{1,0:T(8,128)(2,1)S(1)} %get-tuple-element.12.own_ref), channel_id=1, source_target_pairs={{0,8},{1,9},{2,10},{3,11},{4,12},{5,13},{6,14},{7,15},{8,0},{9,1},... | collective-permute-start | bytes 430088 | tf_op jit(solution)/shard_map/ppermute | solution.py:33
  19.0 3.9 %collective-permute-done.11.refs_0_ = bf16[40,1792]{1,0:T(8,128)(2,1)S(1)} collective-permute-done((bf16[40,1792]{1,0:T(8,128)(2,1)S(1)}, bf16[40,1792]{1,0:T(8,128)(2,1)S(1)}, u32[]{:S(2)}, u32[]{:S(2)}) %collective-permute-start.11) | collective-permute-done | bytes 143392 | tf_op jit(solution)/shard_map/ppermute | solution.py:33
  23.5 3.4 %copy-done = bf16[8192,512]{1,0:T(8,128)(2,1)S(1)} copy-done((bf16[8192,512]{1,0:T(8,128)(2,1)S(1)}, bf16[8192,512]{1,0:T(8,128)(2,1)}, u32[]{:S(2)}) %copy-start) | copy-done | bytes 8388632
  29.1 2.9 %collective-permute-start.1 = (bf16[40,1792]{1,0:T(8,128)(2,1)S(1)}, bf16[40,1792]{1,0:T(8,128)(2,1)S(1)}, u32[]{:S(2)}, u32[]{:S(2)}) collective-permute-start(bf16[40,1792]{1,0:T(8,128)(2,1)S(1)} %get-tuple-element.10.own_ref), channel_id=1, source_target_pairs={{0,4},{1,5},{2,6},{3,7},{4,8},{5,9},{6,10},{7,11},{8,12},{9,13},{1... | collective-permute-start | bytes 430088 | tf_op jit(solution)/shard_map/ppermute | solution.py:33
  32.0 1.1 %collective-permute-start.2 = (bf16[40,1792]{1,0:T(8,128)(2,1)S(1)}, bf16[40,1792]{1,0:T(8,128)(2,1)S(1)}, u32[]{:S(2)}, u32[]{:S(2)}) collective-permute-start(bf16[40,1792]{1,0:T(8,128)(2,1)S(1)} %get-tuple-element.10.own_ref), channel_id=1, source_target_pairs={{0,8},{1,9},{2,10},{3,11},{4,12},{5,13},{6,14},{7,15},{8,0},{9,1},... | collective-permute-start | bytes 430088 | tf_op jit(solution)/shard_map/ppermute | solution.py:33
  33.1 1.3 %collective-permute-start.3 = (bf16[40,1792]{1,0:T(8,128)(2,1)S(1)}, bf16[40,1792]{1,0:T(8,128)(2,1)S(1)}, u32[]{:S(2)}, u32[]{:S(2)}) collective-permute-start(bf16[40,1792]{1,0:T(8,128)(2,1)S(1)} %get-tuple-element.10.own_ref), channel_id=1, source_target_pairs={{0,12},{1,13},{2,14},{3,15},{4,0},{5,1},{6,2},{7,3},{8,4},{9,5},{1... | collective-permute-start | bytes 430088 | tf_op jit(solution)/shard_map/ppermute | solution.py:33
  34.4 2.3 %rotate_out.1.refs_3_.refs_0_ = bf16[80,512]{1,0:T(8,128)(2,1)S(1)} custom-call(bf16[4,40,1024]{2,1,0:T(8,128)(2,1)S(1)} %pile.4.refs_0_.z_ref, bf16[4,40,1024]{2,1,0:T(8,128)(2,1)S(1)} %collective-permute-done.8.y_ref, bf16[4,40,1024]{2,1,0:T(8,128)(2,1)S(1)} %collective-permute-done.9.cz_ref, bf16[4,40,1024]{2,1,0:T(8,128)(2,1)S(1)} %collective-permute-done.10.cy_ref, ...), custom_call_target="tpu_custom_call" | custom-call | flops 671088640 | bytes 8388608 | tf_op jit(solution)/shard_map/rotate_out/pallas_call | solution.py:105
  37.6 5.4 %collective-permute-done.2.refs_1_ = bf16[40,1792]{1,0:T(8,128)(2,1)S(1)} collective-permute-done((bf16[40,1792]{1,0:T(8,128)(2,1)S(1)}, bf16[40,1792]{1,0:T(8,128)(2,1)S(1)}, u32[]{:S(2)}, u32[]{:S(2)}) %collective-permute-start.2) | collective-permute-done | bytes 143392 | tf_op jit(solution)/shard_map/ppermute | solution.py:33
  43.8 3.5 %collective-permute-start.17 = (bf16[80,512]{1,0:T(8,128)(2,1)S(1)}, bf16[80,512]{1,0:T(8,128)(2,1)S(1)}, u32[]{:S(2)}, u32[]{:S(2)}) collective-permute-start(bf16[80,512]{1,0:T(8,128)(2,1)S(1)} %rotate_out.1.refs_3_.refs_0_), channel_id=1, source_target_pairs={{0,4},{1,5},{2,6},{3,7},{4,8},{5,9},{6,10},{7,11},{8,12},{9,13},{1... | collective-permute-start | bytes 245768 | tf_op jit(solution)/shard_map/ppermute | solution.py:33
  47.3 2.2 %collective-permute-start.18 = (bf16[80,512]{1,0:T(8,128)(2,1)S(1)}, bf16[80,512]{1,0:T(8,128)(2,1)S(1)}, u32[]{:S(2)}, u32[]{:S(2)}) collective-permute-start(bf16[80,512]{1,0:T(8,128)(2,1)S(1)} %rotate_out.1.refs_3_.refs_0_), channel_id=1, source_target_pairs={{0,8},{1,9},{2,10},{3,11},{4,12},{5,13},{6,14},{7,15},{8,0},{9,1},... | collective-permute-start | bytes 245768 | tf_op jit(solution)/shard_map/ppermute | solution.py:33
  49.7 2.8 %rotate_in.2.refs_0_.refs_4_ = f32[192,40]{1,0:T(8,128)S(1)} custom-call(bf16[40,1792]{1,0:T(8,128)(2,1)S(1)} %get-tuple-element.12.own_ref, bf16[2,40,1792]{2,1,0:T(8,128)(2,1)S(1)} %collective-permute-done.refs_1_.across_ref, bf16[3,40,1792]{2,1,0:T(8,128)(2,1)S(1)} %pile.5.refs_0_.z_ref, bf16[3,40,1792]{2,1,0:T(8,128)(2,1)S(1)} %collective-permute-done.15.y_ref, ...), custom_call_target="tpu_custom_call" | custom-call | flops 220200960 | bytes 5505024 | tf_op jit(solution)/shard_map/rotate_in/pallas_call | solution.py:171
  52.5 2.0 %collective-permute-done.18.refs_2_ = bf16[80,512]{1,0:T(8,128)(2,1)S(1)} collective-permute-done((bf16[80,512]{1,0:T(8,128)(2,1)S(1)}, bf16[80,512]{1,0:T(8,128)(2,1)S(1)}, u32[]{:S(2)}, u32[]{:S(2)}) %collective-permute-start.18) | collective-permute-done | bytes 81952 | tf_op jit(solution)/shard_map/ppermute | solution.py:33
  54.9 1.0 %collective-permute-start.20 = (bf16[4,80,512]{2,1,0:T(8,128)(2,1)S(1)}, bf16[4,80,512]{2,1,0:T(8,128)(2,1)S(1)}, u32[]{:S(2)}, u32[]{:S(2)}) collective-permute-start(bf16[4,80,512]{2,1,0:T(8,128)(2,1)S(1)} %pile.7.z_ref), channel_id=1, source_target_pairs={{0,2},{1,3},{2,0},{3,1},{4,6},{5,7},{6,4},{7,5},{8,10},{9,11},{10,... | collective-permute-start | bytes 983048 | tf_op jit(solution)/shard_map/ppermute | solution.py:33
  55.9 2.8 %rotate_in.3 = (bf16[96,40]{1,0:T(8,128)(2,1)S(1)}, bf16[96,40]{1,0:T(8,128)(2,1)S(1)}) custom-call(bf16[40,1792]{1,0:T(8,128)(2,1)S(1)} %get-tuple-element.10.own_ref, bf16[2,40,1792]{2,1,0:T(8,128)(2,1)S(1)} %collective-permute-done.refs_1_.across_ref, bf16[3,40,1792]{2,1,0:T(8,128)(2,1)S(1)} %pile.6.z_ref.refs_5_, ...), custom_call_target="tpu_custom_call" | custom-call | flops 220200960 | bytes 5505024 | tf_op jit(solution)/shard_map/rotate_in/pallas_call | solution.py:171
  59.3 4.7 %collective-permute-done.20.refs_0_ = bf16[4,80,512]{2,1,0:T(8,128)(2,1)S(1)} collective-permute-done((bf16[4,80,512]{2,1,0:T(8,128)(2,1)S(1)}, bf16[4,80,512]{2,1,0:T(8,128)(2,1)S(1)}, u32[]{:S(2)}, u32[]{:S(2)}) %collective-permute-start.20) | collective-permute-done | bytes 327712 | tf_op jit(solution)/shard_map/ppermute | solution.py:33
  64.0 1.7 %combine.1._ = bf16[96,8192]{1,0:T(8,128)(2,1)} custom-call(bf16[96,40]{1,0:T(8,128)(2,1)S(1)} %get-tuple-element.13.own_ref, bf16[96,40]{1,0:T(8,128)(2,1)S(1)} %collective-permute-done.16.refs_1_.other_ref, bf16[4,80,512]{2,1,0:T(8,128)(2,1)S(1)} %pile.7.z_ref, bf16[4,80,512]{2,1,0:T(8,128)(2,1)S(1)} %after.1.y_ref, ...), custom_call_target="tpu_custom_call" | custom-call | flops 125829120 | bytes 3145728 | tf_op jit(solution)/shard_map/combine/pallas_call | solution.py:307
  65.7 1.0 %finish.1 = bf16[96,8192]{1,0:T(8,128)(2,1)} custom-call(bf16[96,40]{1,0:T(8,128)(2,1)S(1)} %get-tuple-element.13.own_ref, bf16[96,40]{1,0:T(8,128)(2,1)S(1)} %collective-permute-done.16.refs_1_.other_ref, bf16[4,80,512]{2,1,0:T(8,128)(2,1)S(1)} %collective-permute-done.21.cy_ref, bf16[96,8192]{1,0:T(8,128)(2,1)} %combine.1._), custom_call_target="tpu_custom_call", output_to_operand_aliasing={{}: (3, {})} | custom-call | flops 31457280 | bytes 655360 | tf_op jit(solution)/shard_map/finish/pallas_call | solution.py:338
  (46 shorter events, 8.2 us)
Async XLA Ops:
  0.0 12.8 %collective-permute-start.7 = (bf16[96,28672]{1,0:T(8,128)(2,1)}, bf16[96,28672]{1,0:T(8,128)(2,1)S(1)}, u32[]{:S(2)}, u32[]{:S(2)}) collective-permute-start(bf16[96,28672]{1,0:T(8,128)(2,1)} %bitcast.1), channel_id=1, source_target_pairs={{0,1},{1,0},{2,3},{3,2},{4,5},{5,4},{6,7},{7,6},{8,9},{9,8},{10,11... | collective-permute-start | bytes 16515080 | tf_op jit(solution)/shard_map/ppermute | solution.py:33
  1.4 8.0 %collective-permute-start.4 = (bf16[40,1024]{1,0:T(8,128)(2,1)S(1)}, bf16[40,1024]{1,0:T(8,128)(2,1)S(1)}, u32[]{:S(2)}, u32[]{:S(2)}) collective-permute-start(bf16[40,1024]{1,0:T(8,128)(2,1)S(1)} %fold.2.refs_0_), channel_id=1, source_target_pairs={{0,4},{1,5},{2,6},{3,7},{4,8},{5,9},{6,10},{7,11},{8,12},{9,13},{1... | collective-permute-start | bytes 245768 | tf_op jit(solution)/shard_map/ppermute | solution.py:33
  4.0 8.7 %collective-permute-start.5 = (bf16[40,1024]{1,0:T(8,128)(2,1)S(1)}, bf16[40,1024]{1,0:T(8,128)(2,1)S(1)}, u32[]{:S(2)}, u32[]{:S(2)}) collective-permute-start(bf16[40,1024]{1,0:T(8,128)(2,1)S(1)} %fold.2.refs_0_), channel_id=1, source_target_pairs={{0,8},{1,9},{2,10},{3,11},{4,12},{5,13},{6,14},{7,15},{8,0},{9,1},... | collective-permute-start | bytes 245768 | tf_op jit(solution)/shard_map/ppermute | solution.py:33
  6.6 6.1 %collective-permute-start.6 = (bf16[40,1024]{1,0:T(8,128)(2,1)S(1)}, bf16[40,1024]{1,0:T(8,128)(2,1)S(1)}, u32[]{:S(2)}, u32[]{:S(2)}) collective-permute-start(bf16[40,1024]{1,0:T(8,128)(2,1)S(1)} %fold.2.refs_0_), channel_id=1, source_target_pairs={{0,12},{1,13},{2,14},{3,15},{4,0},{5,1},{6,2},{7,3},{8,4},{9,5},{1... | collective-permute-start | bytes 245768 | tf_op jit(solution)/shard_map/ppermute | solution.py:33
  12.8 10.7 %collective-permute-start.8 = (bf16[4,40,1024]{2,1,0:T(8,128)(2,1)S(1)}, bf16[4,40,1024]{2,1,0:T(8,128)(2,1)S(1)}, u32[]{:S(2)}, u32[]{:S(2)}) collective-permute-start(bf16[4,40,1024]{2,1,0:T(8,128)(2,1)S(1)} %pile.4.refs_0_.z_ref), channel_id=1, source_target_pairs={{0,2},{1,3},{2,0},{3,1},{4,6},{5,7},{6,4},{7,5},{8,10},{9,11},{10,... | collective-permute-start | bytes 983048 | tf_op jit(solution)/shard_map/ppermute | solution.py:33
  14.4 8.6 %collective-permute-start.11 = (bf16[40,1792]{1,0:T(8,128)(2,1)S(1)}, bf16[40,1792]{1,0:T(8,128)(2,1)S(1)}, u32[]{:S(2)}, u32[]{:S(2)}) collective-permute-start(bf16[40,1792]{1,0:T(8,128)(2,1)S(1)} %get-tuple-element.12.own_ref), channel_id=1, source_target_pairs={{0,4},{1,5},{2,6},{3,7},{4,8},{5,9},{6,10},{7,11},{8,12},{9,13},{1... | collective-permute-start | bytes 430088 | tf_op jit(solution)/shard_map/ppermute | solution.py:33
  16.7 16.4 %collective-permute-start.9 = (bf16[4,40,1024]{2,1,0:T(8,128)(2,1)S(1)}, bf16[4,40,1024]{2,1,0:T(8,128)(2,1)S(1)}, u32[]{:S(2)}, u32[]{:S(2)}) collective-permute-start(bf16[4,40,1024]{2,1,0:T(8,128)(2,1)S(1)} %pile.4.refs_0_.z_ref), channel_id=1, source_target_pairs={{0,1},{1,0},{2,3},{3,2},{4,5},{5,4},{6,7},{7,6},{8,9},{9,8},{10,11... | collective-permute-start | bytes 983048 | tf_op jit(solution)/shard_map/ppermute | solution.py:33
  16.7 11.2 %collective-permute-start.12 = (bf16[40,1792]{1,0:T(8,128)(2,1)S(1)}, bf16[40,1792]{1,0:T(8,128)(2,1)S(1)}, u32[]{:S(2)}, u32[]{:S(2)}) collective-permute-start(bf16[40,1792]{1,0:T(8,128)(2,1)S(1)} %get-tuple-element.12.own_ref), channel_id=1, source_target_pairs={{0,8},{1,9},{2,10},{3,11},{4,12},{5,13},{6,14},{7,15},{8,0},{9,1},... | collective-permute-start | bytes 430088 | tf_op jit(solution)/shard_map/ppermute | solution.py:33
  18.3 9.8 %collective-permute-start.13 = (bf16[40,1792]{1,0:T(8,128)(2,1)S(1)}, bf16[40,1792]{1,0:T(8,128)(2,1)S(1)}, u32[]{:S(2)}, u32[]{:S(2)}) collective-permute-start(bf16[40,1792]{1,0:T(8,128)(2,1)S(1)} %get-tuple-element.12.own_ref), channel_id=1, source_target_pairs={{0,12},{1,13},{2,14},{3,15},{4,0},{5,1},{6,2},{7,3},{8,4},{9,5},{1... | collective-permute-start | bytes 430088 | tf_op jit(solution)/shard_map/ppermute | solution.py:33
  23.0 9.0 %collective-permute-start = (bf16[2,40,1792]{2,1,0:T(8,128)(2,1)S(1)}, bf16[2,40,1792]{2,1,0:T(8,128)(2,1)S(1)}, u32[]{:S(2)}, u32[]{:S(2)}) collective-permute-start(bf16[2,40,1792]{2,1,0:T(8,128)(2,1)S(1)} %get-tuple-element.11.refs_5_), channel_id=1, source_target_pairs={{0,2},{1,3},{2,0},{3,1},{4,6},{5,7},{6,4},{7,5},{8,10},{9,11},{10,... | collective-permute-start | bytes 860168 | tf_op jit(solution)/shard_map/ppermute | solution.py:33
  23.5 11.0 %collective-permute-start.10 = (bf16[4,40,1024]{2,1,0:T(8,128)(2,1)S(1)}, bf16[4,40,1024]{2,1,0:T(8,128)(2,1)S(1)}, u32[]{:S(2)}, u32[]{:S(2)}) collective-permute-start(bf16[4,40,1024]{2,1,0:T(8,128)(2,1)S(1)} %collective-permute-done.8.y_ref), channel_id=1, source_target_pairs={{0,1},{1,0},{2,3},{3,2},{4,5},{5,4},{6,7},{7,6},{8,9},{9,8},{10,11... | collective-permute-start | bytes 983048 | tf_op jit(solution)/shard_map/ppermute | solution.py:33
  28.2 21.5 %collective-permute-start.15 = (bf16[3,40,1792]{2,1,0:T(8,128)(2,1)S(1)}, bf16[3,40,1792]{2,1,0:T(8,128)(2,1)S(1)}, u32[]{:S(2)}, u32[]{:S(2)}) collective-permute-start(bf16[3,40,1792]{2,1,0:T(8,128)(2,1)S(1)} %pile.5.refs_0_.z_ref), channel_id=1, source_target_pairs={{0,2},{1,3},{2,0},{3,1},{4,6},{5,7},{6,4},{7,5},{8,10},{9,11},{10,... | collective-permute-start | bytes 1290248 | tf_op jit(solution)/shard_map/ppermute | solution.py:33
  29.1 20.6 %slice-start.1 = ((s8[5505024]{0:T(1024)(128)(4,1)}), s8[1310720]{0:T(1024)(128)(4,1)S(1)}, s32[]{:S(2)}) async-start(s8[5505024]{0:T(1024)(128)(4,1)} %bitcast.2), calls=%async_computation.1 | async-start | bytes 2621440
  29.1 8.5 %collective-permute-start.1 = (bf16[40,1792]{1,0:T(8,128)(2,1)S(1)}, bf16[40,1792]{1,0:T(8,128)(2,1)S(1)}, u32[]{:S(2)}, u32[]{:S(2)}) collective-permute-start(bf16[40,1792]{1,0:T(8,128)(2,1)S(1)} %get-tuple-element.10.own_ref), channel_id=1, source_target_pairs={{0,4},{1,5},{2,6},{3,7},{4,8},{5,9},{6,10},{7,11},{8,12},{9,13},{1... | collective-permute-start | bytes 430088 | tf_op jit(solution)/shard_map/ppermute | solution.py:33
  32.0 11.1 %collective-permute-start.2 = (bf16[40,1792]{1,0:T(8,128)(2,1)S(1)}, bf16[40,1792]{1,0:T(8,128)(2,1)S(1)}, u32[]{:S(2)}, u32[]{:S(2)}) collective-permute-start(bf16[40,1792]{1,0:T(8,128)(2,1)S(1)} %get-tuple-element.10.own_ref), channel_id=1, source_target_pairs={{0,8},{1,9},{2,10},{3,11},{4,12},{5,13},{6,14},{7,15},{8,0},{9,1},... | collective-permute-start | bytes 430088 | tf_op jit(solution)/shard_map/ppermute | solution.py:33
  33.1 10.0 %collective-permute-start.3 = (bf16[40,1792]{1,0:T(8,128)(2,1)S(1)}, bf16[40,1792]{1,0:T(8,128)(2,1)S(1)}, u32[]{:S(2)}, u32[]{:S(2)}) collective-permute-start(bf16[40,1792]{1,0:T(8,128)(2,1)S(1)} %get-tuple-element.10.own_ref), channel_id=1, source_target_pairs={{0,12},{1,13},{2,14},{3,15},{4,0},{5,1},{6,2},{7,3},{8,4},{9,5},{1... | collective-permute-start | bytes 430088 | tf_op jit(solution)/shard_map/ppermute | solution.py:33
  43.1 12.8 %collective-permute-start.14 = (bf16[3,40,1792]{2,1,0:T(8,128)(2,1)S(1)}, bf16[3,40,1792]{2,1,0:T(8,128)(2,1)S(1)}, u32[]{:S(2)}, u32[]{:S(2)}) collective-permute-start(bf16[3,40,1792]{2,1,0:T(8,128)(2,1)S(1)} %pile.6.z_ref.refs_5_), channel_id=1, source_target_pairs={{0,2},{1,3},{2,0},{3,1},{4,6},{5,7},{6,4},{7,5},{8,10},{9,11},{10,... | collective-permute-start | bytes 1290248 | tf_op jit(solution)/shard_map/ppermute | solution.py:33
  43.8 8.7 %collective-permute-start.17 = (bf16[80,512]{1,0:T(8,128)(2,1)S(1)}, bf16[80,512]{1,0:T(8,128)(2,1)S(1)}, u32[]{:S(2)}, u32[]{:S(2)}) collective-permute-start(bf16[80,512]{1,0:T(8,128)(2,1)S(1)} %rotate_out.1.refs_3_.refs_0_), channel_id=1, source_target_pairs={{0,4},{1,5},{2,6},{3,7},{4,8},{5,9},{6,10},{7,11},{8,12},{9,13},{1... | collective-permute-start | bytes 245768 | tf_op jit(solution)/shard_map/ppermute | solution.py:33
  47.3 7.2 %collective-permute-start.18 = (bf16[80,512]{1,0:T(8,128)(2,1)S(1)}, bf16[80,512]{1,0:T(8,128)(2,1)S(1)}, u32[]{:S(2)}, u32[]{:S(2)}) collective-permute-start(bf16[80,512]{1,0:T(8,128)(2,1)S(1)} %rotate_out.1.refs_3_.refs_0_), channel_id=1, source_target_pairs={{0,8},{1,9},{2,10},{3,11},{4,12},{5,13},{6,14},{7,15},{8,0},{9,1},... | collective-permute-start | bytes 245768 | tf_op jit(solution)/shard_map/ppermute | solution.py:33
  49.5 5.4 %collective-permute-start.19 = (bf16[80,512]{1,0:T(8,128)(2,1)S(1)}, bf16[80,512]{1,0:T(8,128)(2,1)S(1)}, u32[]{:S(2)}, u32[]{:S(2)}) collective-permute-start(bf16[80,512]{1,0:T(8,128)(2,1)S(1)} %rotate_out.1.refs_3_.refs_0_), channel_id=1, source_target_pairs={{0,12},{1,13},{2,14},{3,15},{4,0},{5,1},{6,2},{7,3},{8,4},{9,5},{1... | collective-permute-start | bytes 245768 | tf_op jit(solution)/shard_map/ppermute | solution.py:33
  54.9 9.1 %collective-permute-start.20 = (bf16[4,80,512]{2,1,0:T(8,128)(2,1)S(1)}, bf16[4,80,512]{2,1,0:T(8,128)(2,1)S(1)}, u32[]{:S(2)}, u32[]{:S(2)}) collective-permute-start(bf16[4,80,512]{2,1,0:T(8,128)(2,1)S(1)} %pile.7.z_ref), channel_id=1, source_target_pairs={{0,2},{1,3},{2,0},{3,1},{4,6},{5,7},{6,4},{7,5},{8,10},{9,11},{10,... | collective-permute-start | bytes 983048 | tf_op jit(solution)/shard_map/ppermute | solution.py:33
  55.9 8.1 %collective-permute-start.22 = (bf16[4,80,512]{2,1,0:T(8,128)(2,1)S(1)}, bf16[4,80,512]{2,1,0:T(8,128)(2,1)S(1)}, u32[]{:S(2)}, u32[]{:S(2)}) collective-permute-start(bf16[4,80,512]{2,1,0:T(8,128)(2,1)S(1)} %pile.7.z_ref), channel_id=1, source_target_pairs={{0,1},{1,0},{2,3},{3,2},{4,5},{5,4},{6,7},{7,6},{8,9},{9,8},{10,11... | collective-permute-start | bytes 983048 | tf_op jit(solution)/shard_map/ppermute | solution.py:33
  58.7 5.3 %collective-permute-start.16 = (bf16[96,40]{1,0:T(8,128)(2,1)S(1)}, bf16[96,40]{1,0:T(8,128)(2,1)S(1)}, u32[]{:S(2)}, u32[]{:S(2)}) collective-permute-start(bf16[96,40]{1,0:T(8,128)(2,1)S(1)} %get-tuple-element.14), channel_id=1, source_target_pairs={{0,1},{1,0},{2,3},{3,2},{4,5},{5,4},{6,7},{7,6},{8,9},{9,8},{10,11... | collective-permute-start | bytes 23048 | tf_op jit(solution)/shard_map/ppermute | solution.py:33
  64.0 1.7 %collective-permute-start.21 = (bf16[4,80,512]{2,1,0:T(8,128)(2,1)S(1)}, bf16[4,80,512]{2,1,0:T(8,128)(2,1)S(1)}, u32[]{:S(2)}, u32[]{:S(2)}) collective-permute-start(bf16[4,80,512]{2,1,0:T(8,128)(2,1)S(1)} %after.1.y_ref), channel_id=1, source_target_pairs={{0,1},{1,0},{2,3},{3,2},{4,5},{5,4},{6,7},{7,6},{8,9},{9,8},{10,11... | collective-permute-start | bytes 983048 | tf_op jit(solution)/shard_map/ppermute | solution.py:33
  (4 other events, 25.9 us)

commit v18 on v17

--- a/solution.py
+++ b/solution.py
@@ -196,7 +196,7 @@
             at = start + (fold * tiles + tile) * 128
             rows[tile, pl.ds(fold, tokens, stride=SUBLANES), :] = from_ref[:, at : at + 128].astype(jnp.float32)
     for tile in range(tiles):
-        block = rows[tile].astype(jnp.bfloat16)
+        block = rows[tile, : tokens * SUBLANES, :].astype(jnp.bfloat16)
         for out_ref in out_refs:
             out_ref[:, tile * 128 : (tile + 1) * 128] = block
 
@@ -217,7 +217,7 @@
         out_shape=[jax.ShapeDtypeStruct(shape, array.dtype) for shape in shapes],
         in_specs=[VMEM] + [ANY] * len(waits),
         out_specs=[VMEM] * len(shapes),
-        scratch_shapes=[pltpu.VMEM((shape[1] // 128, shape[0], 128), jnp.float32)],
+        scratch_shapes=[pltpu.VMEM((shape[1] // 128, pl.cdiv(array.shape[0], SUBLANES) * SUBLANES**2, 128), jnp.float32)],
         compiler_params=pltpu.CompilerParams(vmem_limit_bytes=4 * 2**20),
         cost_estimate=pl.CostEstimate(flops=0, bytes_accessed=4 * array.size, transcendentals=0),
         name="fold",

time: 67 us -> 67 us (level)
  no operation moved by 1% of the time
where the time goes in v18:
time: 67 us; the launch traced here: 66.7 us
  starting transfers between devices  28.2 us (42%)
  waiting for transfers between devices  21.6 us (32%)
  Pallas kernels  11.5 us (17%)
  local copies, waits for them, and re-layouts  5.31 us (8%)
    ppermute x23, starting transfers between devices, send(): return lax.ppermute(block, 'wide', pairs)  28.2 us
    ppermute x23, waiting for transfers between devices, send(): return lax.ppermute(block, 'wide', pairs)  21.6 us
    pallas_call x2, Pallas kernels, rotate_in(): pl.pallas_call(functools.partial(rotate_in_kernel, tokens, chunk, len(bef...  5.62 us
    unnamed x10, local copies, waits for them, and re-layouts  5.31 us
    pallas_call x1, Pallas kernels, rotate_out(): pl.pallas_call(functools.partial(rotate_out_kernel, tokens, len(waits)),...  2.3 us
    pallas_call x1, Pallas kernels, combine(): pl.pallas_call(combine_kernel, out_shape=jax.ShapeDtypeStruct((own.shape[...  1.67 us
  transfers between devices with their start and end apart: 23, of which 10 were waited for; matrix products, arithmetic and copies ran while one was open for 0% of the time, Pallas kernels for 16%

profile of v18, /device:TPU:0, one launch (start us, length us, event | category | flops | bytes accessed | tf_op | source)
XLA Modules:
  0.0 66.7 jit_solution(13916216236595310735)
XLA Ops:
  1.4 2.6 %collective-permute-start.4 = (bf16[40,1024]{1,0:T(8,128)(2,1)S(1)}, bf16[40,1024]{1,0:T(8,128)(2,1)S(1)}, u32[]{:S(2)}, u32[]{:S(2)}) collective-permute-start(bf16[40,1024]{1,0:T(8,128)(2,1)S(1)} %fold.2.refs_0_), channel_id=1, source_target_pairs={{0,4},{1,5},{2,6},{3,7},{4,8},{5,9},{6,10},{7,11},{8,12},{9,13},{1... | collective-permute-start | bytes 245768 | tf_op jit(solution)/shard_map/ppermute | solution.py:33
  4.0 2.6 %collective-permute-start.5 = (bf16[40,1024]{1,0:T(8,128)(2,1)S(1)}, bf16[40,1024]{1,0:T(8,128)(2,1)S(1)}, u32[]{:S(2)}, u32[]{:S(2)}) collective-permute-start(bf16[40,1024]{1,0:T(8,128)(2,1)S(1)} %fold.2.refs_0_), channel_id=1, source_target_pairs={{0,8},{1,9},{2,10},{3,11},{4,12},{5,13},{6,14},{7,15},{8,0},{9,1},... | collective-permute-start | bytes 245768 | tf_op jit(solution)/shard_map/ppermute | solution.py:33
  6.6 1.3 %collective-permute-start.6 = (bf16[40,1024]{1,0:T(8,128)(2,1)S(1)}, bf16[40,1024]{1,0:T(8,128)(2,1)S(1)}, u32[]{:S(2)}, u32[]{:S(2)}) collective-permute-start(bf16[40,1024]{1,0:T(8,128)(2,1)S(1)} %fold.2.refs_0_), channel_id=1, source_target_pairs={{0,12},{1,13},{2,14},{3,15},{4,0},{5,1},{6,2},{7,3},{8,4},{9,5},{1... | collective-permute-start | bytes 245768 | tf_op jit(solution)/shard_map/ppermute | solution.py:33
  8.0 1.0 %copy-done.1 = bf16[5,28672]{1,0:T(8,128)(2,1)S(1)} copy-done((bf16[5,28672]{1,0:T(8,128)(2,1)S(1)}, bf16[5,28672]{1,0:T(8,128)(2,1)}, u32[]{:S(2)}) %copy-start.1) | copy-done | bytes 286744
  9.5 3.3 %collective-permute-done.5.refs_2_ = bf16[40,1024]{1,0:T(8,128)(2,1)S(1)} collective-permute-done((bf16[40,1024]{1,0:T(8,128)(2,1)S(1)}, bf16[40,1024]{1,0:T(8,128)(2,1)S(1)}, u32[]{:S(2)}, u32[]{:S(2)}) %collective-permute-start.5) | collective-permute-done | bytes 81952 | tf_op jit(solution)/shard_map/ppermute | solution.py:33
  12.8 1.6 %collective-permute-start.8 = (bf16[4,40,1024]{2,1,0:T(8,128)(2,1)S(1)}, bf16[4,40,1024]{2,1,0:T(8,128)(2,1)S(1)}, u32[]{:S(2)}, u32[]{:S(2)}) collective-permute-start(bf16[4,40,1024]{2,1,0:T(8,128)(2,1)S(1)} %pile.4.refs_0_.z_ref), channel_id=1, source_target_pairs={{0,2},{1,3},{2,0},{3,1},{4,6},{5,7},{6,4},{7,5},{8,10},{9,11},{10,... | collective-permute-start | bytes 983048 | tf_op jit(solution)/shard_map/ppermute | solution.py:33
  14.4 2.2 %collective-permute-start.11 = (bf16[40,1792]{1,0:T(8,128)(2,1)S(1)}, bf16[40,1792]{1,0:T(8,128)(2,1)S(1)}, u32[]{:S(2)}, u32[]{:S(2)}) collective-permute-start(bf16[40,1792]{1,0:T(8,128)(2,1)S(1)} %get-tuple-element.12.own_ref), channel_id=1, source_target_pairs={{0,4},{1,5},{2,6},{3,7},{4,8},{5,9},{6,10},{7,11},{8,12},{9,13},{1... | collective-permute-start | bytes 430088 | tf_op jit(solution)/shard_map/ppermute | solution.py:33
  16.7 1.6 %collective-permute-start.12 = (bf16[40,1792]{1,0:T(8,128)(2,1)S(1)}, bf16[40,1792]{1,0:T(8,128)(2,1)S(1)}, u32[]{:S(2)}, u32[]{:S(2)}) collective-permute-start(bf16[40,1792]{1,0:T(8,128)(2,1)S(1)} %get-tuple-element.12.own_ref), channel_id=1, source_target_pairs={{0,8},{1,9},{2,10},{3,11},{4,12},{5,13},{6,14},{7,15},{8,0},{9,1},... | collective-permute-start | bytes 430088 | tf_op jit(solution)/shard_map/ppermute | solution.py:33
  19.0 3.9 %collective-permute-done.11.refs_0_ = bf16[40,1792]{1,0:T(8,128)(2,1)S(1)} collective-permute-done((bf16[40,1792]{1,0:T(8,128)(2,1)S(1)}, bf16[40,1792]{1,0:T(8,128)(2,1)S(1)}, u32[]{:S(2)}, u32[]{:S(2)}) %collective-permute-start.11) | collective-permute-done | bytes 143392 | tf_op jit(solution)/shard_map/ppermute | solution.py:33
  23.5 3.4 %copy-done = bf16[8192,512]{1,0:T(8,128)(2,1)S(1)} copy-done((bf16[8192,512]{1,0:T(8,128)(2,1)S(1)}, bf16[8192,512]{1,0:T(8,128)(2,1)}, u32[]{:S(2)}) %copy-start) | copy-done | bytes 8388632
  29.1 2.9 %collective-permute-start.1 = (bf16[40,1792]{1,0:T(8,128)(2,1)S(1)}, bf16[40,1792]{1,0:T(8,128)(2,1)S(1)}, u32[]{:S(2)}, u32[]{:S(2)}) collective-permute-start(bf16[40,1792]{1,0:T(8,128)(2,1)S(1)} %get-tuple-element.10.own_ref), channel_id=1, source_target_pairs={{0,4},{1,5},{2,6},{3,7},{4,8},{5,9},{6,10},{7,11},{8,12},{9,13},{1... | collective-permute-start | bytes 430088 | tf_op jit(solution)/shard_map/ppermute | solution.py:33
  32.0 1.1 %collective-permute-start.2 = (bf16[40,1792]{1,0:T(8,128)(2,1)S(1)}, bf16[40,1792]{1,0:T(8,128)(2,1)S(1)}, u32[]{:S(2)}, u32[]{:S(2)}) collective-permute-start(bf16[40,1792]{1,0:T(8,128)(2,1)S(1)} %get-tuple-element.10.own_ref), channel_id=1, source_target_pairs={{0,8},{1,9},{2,10},{3,11},{4,12},{5,13},{6,14},{7,15},{8,0},{9,1},... | collective-permute-start | bytes 430088 | tf_op jit(solution)/shard_map/ppermute | solution.py:33
  33.1 1.3 %collective-permute-start.3 = (bf16[40,1792]{1,0:T(8,128)(2,1)S(1)}, bf16[40,1792]{1,0:T(8,128)(2,1)S(1)}, u32[]{:S(2)}, u32[]{:S(2)}) collective-permute-start(bf16[40,1792]{1,0:T(8,128)(2,1)S(1)} %get-tuple-element.10.own_ref), channel_id=1, source_target_pairs={{0,12},{1,13},{2,14},{3,15},{4,0},{5,1},{6,2},{7,3},{8,4},{9,5},{1... | collective-permute-start | bytes 430088 | tf_op jit(solution)/shard_map/ppermute | solution.py:33
  34.4 2.3 %rotate_out.1.refs_3_.refs_0_ = bf16[80,512]{1,0:T(8,128)(2,1)S(1)} custom-call(bf16[4,40,1024]{2,1,0:T(8,128)(2,1)S(1)} %pile.4.refs_0_.z_ref, bf16[4,40,1024]{2,1,0:T(8,128)(2,1)S(1)} %collective-permute-done.8.y_ref, bf16[4,40,1024]{2,1,0:T(8,128)(2,1)S(1)} %collective-permute-done.9.cz_ref, bf16[4,40,1024]{2,1,0:T(8,128)(2,1)S(1)} %collective-permute-done.10.cy_ref, ...), custom_call_target="tpu_custom_call" | custom-call | flops 671088640 | bytes 8388608 | tf_op jit(solution)/shard_map/rotate_out/pallas_call | solution.py:105
  37.6 5.4 %collective-permute-done.2.refs_1_ = bf16[40,1792]{1,0:T(8,128)(2,1)S(1)} collective-permute-done((bf16[40,1792]{1,0:T(8,128)(2,1)S(1)}, bf16[40,1792]{1,0:T(8,128)(2,1)S(1)}, u32[]{:S(2)}, u32[]{:S(2)}) %collective-permute-start.2) | collective-permute-done | bytes 143392 | tf_op jit(solution)/shard_map/ppermute | solution.py:33
  43.8 3.5 %collective-permute-start.17 = (bf16[80,512]{1,0:T(8,128)(2,1)S(1)}, bf16[80,512]{1,0:T(8,128)(2,1)S(1)}, u32[]{:S(2)}, u32[]{:S(2)}) collective-permute-start(bf16[80,512]{1,0:T(8,128)(2,1)S(1)} %rotate_out.1.refs_3_.refs_0_), channel_id=1, source_target_pairs={{0,4},{1,5},{2,6},{3,7},{4,8},{5,9},{6,10},{7,11},{8,12},{9,13},{1... | collective-permute-start | bytes 245768 | tf_op jit(solution)/shard_map/ppermute | solution.py:33
  47.3 2.2 %collective-permute-start.18 = (bf16[80,512]{1,0:T(8,128)(2,1)S(1)}, bf16[80,512]{1,0:T(8,128)(2,1)S(1)}, u32[]{:S(2)}, u32[]{:S(2)}) collective-permute-start(bf16[80,512]{1,0:T(8,128)(2,1)S(1)} %rotate_out.1.refs_3_.refs_0_), channel_id=1, source_target_pairs={{0,8},{1,9},{2,10},{3,11},{4,12},{5,13},{6,14},{7,15},{8,0},{9,1},... | collective-permute-start | bytes 245768 | tf_op jit(solution)/shard_map/ppermute | solution.py:33
  49.7 2.8 %rotate_in.2.refs_0_.refs_4_ = f32[192,40]{1,0:T(8,128)S(1)} custom-call(bf16[40,1792]{1,0:T(8,128)(2,1)S(1)} %get-tuple-element.12.own_ref, bf16[2,40,1792]{2,1,0:T(8,128)(2,1)S(1)} %collective-permute-done.refs_1_.across_ref, bf16[3,40,1792]{2,1,0:T(8,128)(2,1)S(1)} %pile.5.refs_0_.z_ref, bf16[3,40,1792]{2,1,0:T(8,128)(2,1)S(1)} %collective-permute-done.15.y_ref, ...), custom_call_target="tpu_custom_call" | custom-call | flops 220200960 | bytes 5505024 | tf_op jit(solution)/shard_map/rotate_in/pallas_call | solution.py:171
  52.5 2.0 %collective-permute-done.18.refs_2_ = bf16[80,512]{1,0:T(8,128)(2,1)S(1)} collective-permute-done((bf16[80,512]{1,0:T(8,128)(2,1)S(1)}, bf16[80,512]{1,0:T(8,128)(2,1)S(1)}, u32[]{:S(2)}, u32[]{:S(2)}) %collective-permute-start.18) | collective-permute-done | bytes 81952 | tf_op jit(solution)/shard_map/ppermute | solution.py:33
  54.9 1.0 %collective-permute-start.20 = (bf16[4,80,512]{2,1,0:T(8,128)(2,1)S(1)}, bf16[4,80,512]{2,1,0:T(8,128)(2,1)S(1)}, u32[]{:S(2)}, u32[]{:S(2)}) collective-permute-start(bf16[4,80,512]{2,1,0:T(8,128)(2,1)S(1)} %pile.7.z_ref), channel_id=1, source_target_pairs={{0,2},{1,3},{2,0},{3,1},{4,6},{5,7},{6,4},{7,5},{8,10},{9,11},{10,... | collective-permute-start | bytes 983048 | tf_op jit(solution)/shard_map/ppermute | solution.py:33
  55.9 2.8 %rotate_in.3 = (bf16[96,40]{1,0:T(8,128)(2,1)S(1)}, bf16[96,40]{1,0:T(8,128)(2,1)S(1)}) custom-call(bf16[40,1792]{1,0:T(8,128)(2,1)S(1)} %get-tuple-element.10.own_ref, bf16[2,40,1792]{2,1,0:T(8,128)(2,1)S(1)} %collective-permute-done.refs_1_.across_ref, bf16[3,40,1792]{2,1,0:T(8,128)(2,1)S(1)} %pile.6.z_ref.refs_5_, ...), custom_call_target="tpu_custom_call" | custom-call | flops 220200960 | bytes 5505024 | tf_op jit(solution)/shard_map/rotate_in/pallas_call | solution.py:171
  59.3 4.7 %collective-permute-done.20.refs_0_ = bf16[4,80,512]{2,1,0:T(8,128)(2,1)S(1)} collective-permute-done((bf16[4,80,512]{2,1,0:T(8,128)(2,1)S(1)}, bf16[4,80,512]{2,1,0:T(8,128)(2,1)S(1)}, u32[]{:S(2)}, u32[]{:S(2)}) %collective-permute-start.20) | collective-permute-done | bytes 327712 | tf_op jit(solution)/shard_map/ppermute | solution.py:33
  64.0 1.7 %combine.1._ = bf16[96,8192]{1,0:T(8,128)(2,1)} custom-call(bf16[96,40]{1,0:T(8,128)(2,1)S(1)} %get-tuple-element.13.own_ref, bf16[96,40]{1,0:T(8,128)(2,1)S(1)} %collective-permute-done.16.refs_1_.other_ref, bf16[4,80,512]{2,1,0:T(8,128)(2,1)S(1)} %pile.7.z_ref, bf16[4,80,512]{2,1,0:T(8,128)(2,1)S(1)} %after.1.y_ref, ...), custom_call_target="tpu_custom_call" | custom-call | flops 125829120 | bytes 3145728 | tf_op jit(solution)/shard_map/combine/pallas_call | solution.py:307
  65.7 1.0 %finish.1 = bf16[96,8192]{1,0:T(8,128)(2,1)} custom-call(bf16[96,40]{1,0:T(8,128)(2,1)S(1)} %get-tuple-element.13.own_ref, bf16[96,40]{1,0:T(8,128)(2,1)S(1)} %collective-permute-done.16.refs_1_.other_ref, bf16[4,80,512]{2,1,0:T(8,128)(2,1)S(1)} %collective-permute-done.21.cy_ref, bf16[96,8192]{1,0:T(8,128)(2,1)} %combine.1._), custom_call_target="tpu_custom_call", output_to_operand_aliasing={{}: (3, {})} | custom-call | flops 31457280 | bytes 655360 | tf_op jit(solution)/shard_map/finish/pallas_call | solution.py:338
  (46 shorter events, 8.2 us)
Async XLA Ops:
  0.0 12.8 %collective-permute-start.7 = (bf16[96,28672]{1,0:T(8,128)(2,1)}, bf16[96,28672]{1,0:T(8,128)(2,1)S(1)}, u32[]{:S(2)}, u32[]{:S(2)}) collective-permute-start(bf16[96,28672]{1,0:T(8,128)(2,1)} %bitcast.1), channel_id=1, source_target_pairs={{0,1},{1,0},{2,3},{3,2},{4,5},{5,4},{6,7},{7,6},{8,9},{9,8},{10,11... | collective-permute-start | bytes 16515080 | tf_op jit(solution)/shard_map/ppermute | solution.py:33
  1.4 8.0 %collective-permute-start.4 = (bf16[40,1024]{1,0:T(8,128)(2,1)S(1)}, bf16[40,1024]{1,0:T(8,128)(2,1)S(1)}, u32[]{:S(2)}, u32[]{:S(2)}) collective-permute-start(bf16[40,1024]{1,0:T(8,128)(2,1)S(1)} %fold.2.refs_0_), channel_id=1, source_target_pairs={{0,4},{1,5},{2,6},{3,7},{4,8},{5,9},{6,10},{7,11},{8,12},{9,13},{1... | collective-permute-start | bytes 245768 | tf_op jit(solution)/shard_map/ppermute | solution.py:33
  4.0 8.7 %collective-permute-start.5 = (bf16[40,1024]{1,0:T(8,128)(2,1)S(1)}, bf16[40,1024]{1,0:T(8,128)(2,1)S(1)}, u32[]{:S(2)}, u32[]{:S(2)}) collective-permute-start(bf16[40,1024]{1,0:T(8,128)(2,1)S(1)} %fold.2.refs_0_), channel_id=1, source_target_pairs={{0,8},{1,9},{2,10},{3,11},{4,12},{5,13},{6,14},{7,15},{8,0},{9,1},... | collective-permute-start | bytes 245768 | tf_op jit(solution)/shard_map/ppermute | solution.py:33
  6.6 6.1 %collective-permute-start.6 = (bf16[40,1024]{1,0:T(8,128)(2,1)S(1)}, bf16[40,1024]{1,0:T(8,128)(2,1)S(1)}, u32[]{:S(2)}, u32[]{:S(2)}) collective-permute-start(bf16[40,1024]{1,0:T(8,128)(2,1)S(1)} %fold.2.refs_0_), channel_id=1, source_target_pairs={{0,12},{1,13},{2,14},{3,15},{4,0},{5,1},{6,2},{7,3},{8,4},{9,5},{1... | collective-permute-start | bytes 245768 | tf_op jit(solution)/shard_map/ppermute | solution.py:33
  12.8 10.7 %collective-permute-start.8 = (bf16[4,40,1024]{2,1,0:T(8,128)(2,1)S(1)}, bf16[4,40,1024]{2,1,0:T(8,128)(2,1)S(1)}, u32[]{:S(2)}, u32[]{:S(2)}) collective-permute-start(bf16[4,40,1024]{2,1,0:T(8,128)(2,1)S(1)} %pile.4.refs_0_.z_ref), channel_id=1, source_target_pairs={{0,2},{1,3},{2,0},{3,1},{4,6},{5,7},{6,4},{7,5},{8,10},{9,11},{10,... | collective-permute-start | bytes 983048 | tf_op jit(solution)/shard_map/ppermute | solution.py:33
  14.4 8.6 %collective-permute-start.11 = (bf16[40,1792]{1,0:T(8,128)(2,1)S(1)}, bf16[40,1792]{1,0:T(8,128)(2,1)S(1)}, u32[]{:S(2)}, u32[]{:S(2)}) collective-permute-start(bf16[40,1792]{1,0:T(8,128)(2,1)S(1)} %get-tuple-element.12.own_ref), channel_id=1, source_target_pairs={{0,4},{1,5},{2,6},{3,7},{4,8},{5,9},{6,10},{7,11},{8,12},{9,13},{1... | collective-permute-start | bytes 430088 | tf_op jit(solution)/shard_map/ppermute | solution.py:33
  16.7 16.4 %collective-permute-start.9 = (bf16[4,40,1024]{2,1,0:T(8,128)(2,1)S(1)}, bf16[4,40,1024]{2,1,0:T(8,128)(2,1)S(1)}, u32[]{:S(2)}, u32[]{:S(2)}) collective-permute-start(bf16[4,40,1024]{2,1,0:T(8,128)(2,1)S(1)} %pile.4.refs_0_.z_ref), channel_id=1, source_target_pairs={{0,1},{1,0},{2,3},{3,2},{4,5},{5,4},{6,7},{7,6},{8,9},{9,8},{10,11... | collective-permute-start | bytes 983048 | tf_op jit(solution)/shard_map/ppermute | solution.py:33
  16.7 11.2 %collective-permute-start.12 = (bf16[40,1792]{1,0:T(8,128)(2,1)S(1)}, bf16[40,1792]{1,0:T(8,128)(2,1)S(1)}, u32[]{:S(2)}, u32[]{:S(2)}) collective-permute-start(bf16[40,1792]{1,0:T(8,128)(2,1)S(1)} %get-tuple-element.12.own_ref), channel_id=1, source_target_pairs={{0,8},{1,9},{2,10},{3,11},{4,12},{5,13},{6,14},{7,15},{8,0},{9,1},... | collective-permute-start | bytes 430088 | tf_op jit(solution)/shard_map/ppermute | solution.py:33
  18.3 9.8 %collective-permute-start.13 = (bf16[40,1792]{1,0:T(8,128)(2,1)S(1)}, bf16[40,1792]{1,0:T(8,128)(2,1)S(1)}, u32[]{:S(2)}, u32[]{:S(2)}) collective-permute-start(bf16[40,1792]{1,0:T(8,128)(2,1)S(1)} %get-tuple-element.12.own_ref), channel_id=1, source_target_pairs={{0,12},{1,13},{2,14},{3,15},{4,0},{5,1},{6,2},{7,3},{8,4},{9,5},{1... | collective-permute-start | bytes 430088 | tf_op jit(solution)/shard_map/ppermute | solution.py:33
  23.0 9.0 %collective-permute-start = (bf16[2,40,1792]{2,1,0:T(8,128)(2,1)S(1)}, bf16[2,40,1792]{2,1,0:T(8,128)(2,1)S(1)}, u32[]{:S(2)}, u32[]{:S(2)}) collective-permute-start(bf16[2,40,1792]{2,1,0:T(8,128)(2,1)S(1)} %get-tuple-element.11.refs_5_), channel_id=1, source_target_pairs={{0,2},{1,3},{2,0},{3,1},{4,6},{5,7},{6,4},{7,5},{8,10},{9,11},{10,... | collective-permute-start | bytes 860168 | tf_op jit(solution)/shard_map/ppermute | solution.py:33
  23.5 11.0 %collective-permute-start.10 = (bf16[4,40,1024]{2,1,0:T(8,128)(2,1)S(1)}, bf16[4,40,1024]{2,1,0:T(8,128)(2,1)S(1)}, u32[]{:S(2)}, u32[]{:S(2)}) collective-permute-start(bf16[4,40,1024]{2,1,0:T(8,128)(2,1)S(1)} %collective-permute-done.8.y_ref), channel_id=1, source_target_pairs={{0,1},{1,0},{2,3},{3,2},{4,5},{5,4},{6,7},{7,6},{8,9},{9,8},{10,11... | collective-permute-start | bytes 983048 | tf_op jit(solution)/shard_map/ppermute | solution.py:33
  28.2 21.5 %collective-permute-start.15 = (bf16[3,40,1792]{2,1,0:T(8,128)(2,1)S(1)}, bf16[3,40,1792]{2,1,0:T(8,128)(2,1)S(1)}, u32[]{:S(2)}, u32[]{:S(2)}) collective-permute-start(bf16[3,40,1792]{2,1,0:T(8,128)(2,1)S(1)} %pile.5.refs_0_.z_ref), channel_id=1, source_target_pairs={{0,2},{1,3},{2,0},{3,1},{4,6},{5,7},{6,4},{7,5},{8,10},{9,11},{10,... | collective-permute-start | bytes 1290248 | tf_op jit(solution)/shard_map/ppermute | solution.py:33
  29.1 20.6 %slice-start.1 = ((s8[5505024]{0:T(1024)(128)(4,1)}), s8[1310720]{0:T(1024)(128)(4,1)S(1)}, s32[]{:S(2)}) async-start(s8[5505024]{0:T(1024)(128)(4,1)} %bitcast.2), calls=%async_computation.1 | async-start | bytes 2621440
  29.1 8.5 %collective-permute-start.1 = (bf16[40,1792]{1,0:T(8,128)(2,1)S(1)}, bf16[40,1792]{1,0:T(8,128)(2,1)S(1)}, u32[]{:S(2)}, u32[]{:S(2)}) collective-permute-start(bf16[40,1792]{1,0:T(8,128)(2,1)S(1)} %get-tuple-element.10.own_ref), channel_id=1, source_target_pairs={{0,4},{1,5},{2,6},{3,7},{4,8},{5,9},{6,10},{7,11},{8,12},{9,13},{1... | collective-permute-start | bytes 430088 | tf_op jit(solution)/shard_map/ppermute | solution.py:33
  32.0 11.1 %collective-permute-start.2 = (bf16[40,1792]{1,0:T(8,128)(2,1)S(1)}, bf16[40,1792]{1,0:T(8,128)(2,1)S(1)}, u32[]{:S(2)}, u32[]{:S(2)}) collective-permute-start(bf16[40,1792]{1,0:T(8,128)(2,1)S(1)} %get-tuple-element.10.own_ref), channel_id=1, source_target_pairs={{0,8},{1,9},{2,10},{3,11},{4,12},{5,13},{6,14},{7,15},{8,0},{9,1},... | collective-permute-start | bytes 430088 | tf_op jit(solution)/shard_map/ppermute | solution.py:33
  33.1 10.0 %collective-permute-start.3 = (bf16[40,1792]{1,0:T(8,128)(2,1)S(1)}, bf16[40,1792]{1,0:T(8,128)(2,1)S(1)}, u32[]{:S(2)}, u32[]{:S(2)}) collective-permute-start(bf16[40,1792]{1,0:T(8,128)(2,1)S(1)} %get-tuple-element.10.own_ref), channel_id=1, source_target_pairs={{0,12},{1,13},{2,14},{3,15},{4,0},{5,1},{6,2},{7,3},{8,4},{9,5},{1... | collective-permute-start | bytes 430088 | tf_op jit(solution)/shard_map/ppermute | solution.py:33
  43.1 12.8 %collective-permute-start.14 = (bf16[3,40,1792]{2,1,0:T(8,128)(2,1)S(1)}, bf16[3,40,1792]{2,1,0:T(8,128)(2,1)S(1)}, u32[]{:S(2)}, u32[]{:S(2)}) collective-permute-start(bf16[3,40,1792]{2,1,0:T(8,128)(2,1)S(1)} %pile.6.z_ref.refs_5_), channel_id=1, source_target_pairs={{0,2},{1,3},{2,0},{3,1},{4,6},{5,7},{6,4},{7,5},{8,10},{9,11},{10,... | collective-permute-start | bytes 1290248 | tf_op jit(solution)/shard_map/ppermute | solution.py:33
  43.8 8.7 %collective-permute-start.17 = (bf16[80,512]{1,0:T(8,128)(2,1)S(1)}, bf16[80,512]{1,0:T(8,128)(2,1)S(1)}, u32[]{:S(2)}, u32[]{:S(2)}) collective-permute-start(bf16[80,512]{1,0:T(8,128)(2,1)S(1)} %rotate_out.1.refs_3_.refs_0_), channel_id=1, source_target_pairs={{0,4},{1,5},{2,6},{3,7},{4,8},{5,9},{6,10},{7,11},{8,12},{9,13},{1... | collective-permute-start | bytes 245768 | tf_op jit(solution)/shard_map/ppermute | solution.py:33
  47.3 7.2 %collective-permute-start.18 = (bf16[80,512]{1,0:T(8,128)(2,1)S(1)}, bf16[80,512]{1,0:T(8,128)(2,1)S(1)}, u32[]{:S(2)}, u32[]{:S(2)}) collective-permute-start(bf16[80,512]{1,0:T(8,128)(2,1)S(1)} %rotate_out.1.refs_3_.refs_0_), channel_id=1, source_target_pairs={{0,8},{1,9},{2,10},{3,11},{4,12},{5,13},{6,14},{7,15},{8,0},{9,1},... | collective-permute-start | bytes 245768 | tf_op jit(solution)/shard_map/ppermute | solution.py:33
  49.5 5.4 %collective-permute-start.19 = (bf16[80,512]{1,0:T(8,128)(2,1)S(1)}, bf16[80,512]{1,0:T(8,128)(2,1)S(1)}, u32[]{:S(2)}, u32[]{:S(2)}) collective-permute-start(bf16[80,512]{1,0:T(8,128)(2,1)S(1)} %rotate_out.1.refs_3_.refs_0_), channel_id=1, source_target_pairs={{0,12},{1,13},{2,14},{3,15},{4,0},{5,1},{6,2},{7,3},{8,4},{9,5},{1... | collective-permute-start | bytes 245768 | tf_op jit(solution)/shard_map/ppermute | solution.py:33
  54.9 9.1 %collective-permute-start.20 = (bf16[4,80,512]{2,1,0:T(8,128)(2,1)S(1)}, bf16[4,80,512]{2,1,0:T(8,128)(2,1)S(1)}, u32[]{:S(2)}, u32[]{:S(2)}) collective-permute-start(bf16[4,80,512]{2,1,0:T(8,128)(2,1)S(1)} %pile.7.z_ref), channel_id=1, source_target_pairs={{0,2},{1,3},{2,0},{3,1},{4,6},{5,7},{6,4},{7,5},{8,10},{9,11},{10,... | collective-permute-start | bytes 983048 | tf_op jit(solution)/shard_map/ppermute | solution.py:33
  55.9 8.1 %collective-permute-start.22 = (bf16[4,80,512]{2,1,0:T(8,128)(2,1)S(1)}, bf16[4,80,512]{2,1,0:T(8,128)(2,1)S(1)}, u32[]{:S(2)}, u32[]{:S(2)}) collective-permute-start(bf16[4,80,512]{2,1,0:T(8,128)(2,1)S(1)} %pile.7.z_ref), channel_id=1, source_target_pairs={{0,1},{1,0},{2,3},{3,2},{4,5},{5,4},{6,7},{7,6},{8,9},{9,8},{10,11... | collective-permute-start | bytes 983048 | tf_op jit(solution)/shard_map/ppermute | solution.py:33
  58.7 5.3 %collective-permute-start.16 = (bf16[96,40]{1,0:T(8,128)(2,1)S(1)}, bf16[96,40]{1,0:T(8,128)(2,1)S(1)}, u32[]{:S(2)}, u32[]{:S(2)}) collective-permute-start(bf16[96,40]{1,0:T(8,128)(2,1)S(1)} %get-tuple-element.14), channel_id=1, source_target_pairs={{0,1},{1,0},{2,3},{3,2},{4,5},{5,4},{6,7},{7,6},{8,9},{9,8},{10,11... | collective-permute-start | bytes 23048 | tf_op jit(solution)/shard_map/ppermute | solution.py:33
  64.0 1.7 %collective-permute-start.21 = (bf16[4,80,512]{2,1,0:T(8,128)(2,1)S(1)}, bf16[4,80,512]{2,1,0:T(8,128)(2,1)S(1)}, u32[]{:S(2)}, u32[]{:S(2)}) collective-permute-start(bf16[4,80,512]{2,1,0:T(8,128)(2,1)S(1)} %after.1.y_ref), channel_id=1, source_target_pairs={{0,1},{1,0},{2,3},{3,2},{4,5},{5,4},{6,7},{7,6},{8,9},{9,8},{10,11... | collective-permute-start | bytes 983048 | tf_op jit(solution)/shard_map/ppermute | solution.py:33
  (4 other events, 25.9 us)

commit v19 on v18

--- a/solution.py
+++ b/solution.py
@@ -10,7 +10,7 @@
 CORES = 2
 PAIR = 2
 SUBLANES = 8
-FOLDS = 2
+FOLDS = 4
 CHUNKS = 2
 VMEM = pl.BlockSpec(memory_space=pltpu.VMEM)
 ANY = pl.BlockSpec(memory_space=pl.ANY)
@@ -112,7 +112,7 @@
             pltpu.VMEM((width // 128, total * SUBLANES, 128), jnp.float32),
             pltpu.VMEM((total, columns), jnp.float32),
         ],
-        compiler_params=pltpu.CompilerParams(vmem_limit_bytes=room(10, steps)),
+        compiler_params=pltpu.CompilerParams(vmem_limit_bytes=room(14, steps)),
         cost_estimate=pl.CostEstimate(
             flops=2 * total * basis.shape[0] * columns, bytes_accessed=2 * basis.size, transcendentals=0
         ),
@@ -178,7 +178,7 @@
             pltpu.VMEM(whole.shape, jnp.float32),
             pltpu.VMEM((width // 128, chips * height, 128), jnp.float32),
         ],
-        compiler_params=pltpu.CompilerParams(vmem_limit_bytes=room(9, chips)),
+        compiler_params=pltpu.CompilerParams(vmem_limit_bytes=room(14, chips)),
         cost_estimate=pl.CostEstimate(
             flops=4 * chips * tokens * mine.shape[0] * SUBLANES * width,
             bytes_accessed=4 * mine.shape[0] * SUBLANES * width,

time: 67 us -> 67 us (level)
  waiting for transfers between devices: 21.6 us -> 22.7 us
  Pallas kernels: 11.5 us -> 10.5 us
    ppermute x23, waiting for transfers between devices: 21.6 us -> 22.7 us  [send(): return lax.ppermute(block, 'wide', pairs)]
    pallas_call x2, Pallas kernels: 5.62 us -> 4.79 us  [rotate_in(): pl.pallas_call(functools.partial(rotate_in_kernel, tokens, chunk, len(bef...]
  transfers between devices with their start and end apart: 23 -> 23, of which waited for: 10 -> 10; matrix products, arithmetic and copies ran while one was open for 0% -> 0% of each run, Pallas kernels for 16% -> 14%
where the time goes in v19:
time: 67 us; the launch traced here: 66.7 us
  starting transfers between devices  28.2 us (42%)
  waiting for transfers between devices  22.7 us (34%)
  Pallas kernels  10.5 us (16%)
  local copies, waits for them, and re-layouts  5.31 us (8%)
    ppermute x23, starting transfers between devices, send(): return lax.ppermute(block, 'wide', pairs)  28.2 us
    ppermute x23, waiting for transfers between devices, send(): return lax.ppermute(block, 'wide', pairs)  22.7 us
    unnamed x10, local copies, waits for them, and re-layouts  5.31 us
    pallas_call x2, Pallas kernels, rotate_in(): pl.pallas_call(functools.partial(rotate_in_kernel, tokens, chunk, len(bef...  4.79 us
    pallas_call x1, Pallas kernels, rotate_out(): pl.pallas_call(functools.partial(rotate_out_kernel, tokens, len(waits)),...  2.03 us
    pallas_call x1, Pallas kernels, combine(): pl.pallas_call(combine_kernel, out_shape=jax.ShapeDtypeStruct((own.shape[...  1.67 us
  transfers between devices with their start and end apart: 23, of which 10 were waited for; matrix products, arithmetic and copies ran while one was open for 0% of the time, Pallas kernels for 14%

profile of v19, /device:TPU:0, one launch (start us, length us, event | category | flops | bytes accessed | tf_op | source)
XLA Modules:
  0.0 66.7 jit_solution(5421702589186201726)
XLA Ops:
  1.4 2.6 %collective-permute-start.4 = (bf16[40,1024]{1,0:T(8,128)(2,1)S(1)}, bf16[40,1024]{1,0:T(8,128)(2,1)S(1)}, u32[]{:S(2)}, u32[]{:S(2)}) collective-permute-start(bf16[40,1024]{1,0:T(8,128)(2,1)S(1)} %fold.2.refs_0_), channel_id=1, source_target_pairs={{0,4},{1,5},{2,6},{3,7},{4,8},{5,9},{6,10},{7,11},{8,12},{9,13},{1... | collective-permute-start | bytes 245768 | tf_op jit(solution)/shard_map/ppermute | solution.py:33
  4.0 2.6 %collective-permute-start.5 = (bf16[40,1024]{1,0:T(8,128)(2,1)S(1)}, bf16[40,1024]{1,0:T(8,128)(2,1)S(1)}, u32[]{:S(2)}, u32[]{:S(2)}) collective-permute-start(bf16[40,1024]{1,0:T(8,128)(2,1)S(1)} %fold.2.refs_0_), channel_id=1, source_target_pairs={{0,8},{1,9},{2,10},{3,11},{4,12},{5,13},{6,14},{7,15},{8,0},{9,1},... | collective-permute-start | bytes 245768 | tf_op jit(solution)/shard_map/ppermute | solution.py:33
  6.6 1.3 %collective-permute-start.6 = (bf16[40,1024]{1,0:T(8,128)(2,1)S(1)}, bf16[40,1024]{1,0:T(8,128)(2,1)S(1)}, u32[]{:S(2)}, u32[]{:S(2)}) collective-permute-start(bf16[40,1024]{1,0:T(8,128)(2,1)S(1)} %fold.2.refs_0_), channel_id=1, source_target_pairs={{0,12},{1,13},{2,14},{3,15},{4,0},{5,1},{6,2},{7,3},{8,4},{9,5},{1... | collective-permute-start | bytes 245768 | tf_op jit(solution)/shard_map/ppermute | solution.py:33
  8.0 1.0 %copy-done.1 = bf16[5,28672]{1,0:T(8,128)(2,1)S(1)} copy-done((bf16[5,28672]{1,0:T(8,128)(2,1)S(1)}, bf16[5,28672]{1,0:T(8,128)(2,1)}, u32[]{:S(2)}) %copy-start.1) | copy-done | bytes 286744
  9.5 3.3 %collective-permute-done.5.refs_2_ = bf16[40,1024]{1,0:T(8,128)(2,1)S(1)} collective-permute-done((bf16[40,1024]{1,0:T(8,128)(2,1)S(1)}, bf16[40,1024]{1,0:T(8,128)(2,1)S(1)}, u32[]{:S(2)}, u32[]{:S(2)}) %collective-permute-start.5) | collective-permute-done | bytes 81952 | tf_op jit(solution)/shard_map/ppermute | solution.py:33
  12.8 1.6 %collective-permute-start.8 = (bf16[4,40,1024]{2,1,0:T(8,128)(2,1)S(1)}, bf16[4,40,1024]{2,1,0:T(8,128)(2,1)S(1)}, u32[]{:S(2)}, u32[]{:S(2)}) collective-permute-start(bf16[4,40,1024]{2,1,0:T(8,128)(2,1)S(1)} %pile.4.refs_0_.z_ref), channel_id=1, source_target_pairs={{0,2},{1,3},{2,0},{3,1},{4,6},{5,7},{6,4},{7,5},{8,10},{9,11},{10,... | collective-permute-start | bytes 983048 | tf_op jit(solution)/shard_map/ppermute | solution.py:33
  14.4 2.2 %collective-permute-start.11 = (bf16[40,1792]{1,0:T(8,128)(2,1)S(1)}, bf16[40,1792]{1,0:T(8,128)(2,1)S(1)}, u32[]{:S(2)}, u32[]{:S(2)}) collective-permute-start(bf16[40,1792]{1,0:T(8,128)(2,1)S(1)} %get-tuple-element.12.own_ref), channel_id=1, source_target_pairs={{0,4},{1,5},{2,6},{3,7},{4,8},{5,9},{6,10},{7,11},{8,12},{9,13},{1... | collective-permute-start | bytes 430088 | tf_op jit(solution)/shard_map/ppermute | solution.py:33
  16.7 1.6 %collective-permute-start.12 = (bf16[40,1792]{1,0:T(8,128)(2,1)S(1)}, bf16[40,1792]{1,0:T(8,128)(2,1)S(1)}, u32[]{:S(2)}, u32[]{:S(2)}) collective-permute-start(bf16[40,1792]{1,0:T(8,128)(2,1)S(1)} %get-tuple-element.12.own_ref), channel_id=1, source_target_pairs={{0,8},{1,9},{2,10},{3,11},{4,12},{5,13},{6,14},{7,15},{8,0},{9,1},... | collective-permute-start | bytes 430088 | tf_op jit(solution)/shard_map/ppermute | solution.py:33
  19.0 3.9 %collective-permute-done.11.refs_0_ = bf16[40,1792]{1,0:T(8,128)(2,1)S(1)} collective-permute-done((bf16[40,1792]{1,0:T(8,128)(2,1)S(1)}, bf16[40,1792]{1,0:T(8,128)(2,1)S(1)}, u32[]{:S(2)}, u32[]{:S(2)}) %collective-permute-start.11) | collective-permute-done | bytes 143392 | tf_op jit(solution)/shard_map/ppermute | solution.py:33
  23.5 3.4 %copy-done = bf16[8192,512]{1,0:T(8,128)(2,1)S(1)} copy-done((bf16[8192,512]{1,0:T(8,128)(2,1)S(1)}, bf16[8192,512]{1,0:T(8,128)(2,1)}, u32[]{:S(2)}) %copy-start) | copy-done | bytes 8388632
  29.1 2.9 %collective-permute-start.1 = (bf16[40,1792]{1,0:T(8,128)(2,1)S(1)}, bf16[40,1792]{1,0:T(8,128)(2,1)S(1)}, u32[]{:S(2)}, u32[]{:S(2)}) collective-permute-start(bf16[40,1792]{1,0:T(8,128)(2,1)S(1)} %get-tuple-element.10.own_ref), channel_id=1, source_target_pairs={{0,4},{1,5},{2,6},{3,7},{4,8},{5,9},{6,10},{7,11},{8,12},{9,13},{1... | collective-permute-start | bytes 430088 | tf_op jit(solution)/shard_map/ppermute | solution.py:33
  32.0 1.1 %collective-permute-start.2 = (bf16[40,1792]{1,0:T(8,128)(2,1)S(1)}, bf16[40,1792]{1,0:T(8,128)(2,1)S(1)}, u32[]{:S(2)}, u32[]{:S(2)}) collective-permute-start(bf16[40,1792]{1,0:T(8,128)(2,1)S(1)} %get-tuple-element.10.own_ref), channel_id=1, source_target_pairs={{0,8},{1,9},{2,10},{3,11},{4,12},{5,13},{6,14},{7,15},{8,0},{9,1},... | collective-permute-start | bytes 430088 | tf_op jit(solution)/shard_map/ppermute | solution.py:33
  33.1 1.3 %collective-permute-start.3 = (bf16[40,1792]{1,0:T(8,128)(2,1)S(1)}, bf16[40,1792]{1,0:T(8,128)(2,1)S(1)}, u32[]{:S(2)}, u32[]{:S(2)}) collective-permute-start(bf16[40,1792]{1,0:T(8,128)(2,1)S(1)} %get-tuple-element.10.own_ref), channel_id=1, source_target_pairs={{0,12},{1,13},{2,14},{3,15},{4,0},{5,1},{6,2},{7,3},{8,4},{9,5},{1... | collective-permute-start | bytes 430088 | tf_op jit(solution)/shard_map/ppermute | solution.py:33
  34.4 2.0 %rotate_out.1.refs_3_.refs_0_ = bf16[80,512]{1,0:T(8,128)(2,1)S(1)} custom-call(bf16[4,40,1024]{2,1,0:T(8,128)(2,1)S(1)} %pile.4.refs_0_.z_ref, bf16[4,40,1024]{2,1,0:T(8,128)(2,1)S(1)} %collective-permute-done.8.y_ref, bf16[4,40,1024]{2,1,0:T(8,128)(2,1)S(1)} %collective-permute-done.9.cz_ref, bf16[4,40,1024]{2,1,0:T(8,128)(2,1)S(1)} %collective-permute-done.10.cy_ref, ...), custom_call_target="tpu_custom_call" | custom-call | flops 671088640 | bytes 8388608 | tf_op jit(solution)/shard_map/rotate_out/pallas_call | solution.py:105
  36.5 1.1 %collective-permute-done.1.refs_0_ = bf16[40,1792]{1,0:T(8,128)(2,1)S(1)} collective-permute-done((bf16[40,1792]{1,0:T(8,128)(2,1)S(1)}, bf16[40,1792]{1,0:T(8,128)(2,1)S(1)}, u32[]{:S(2)}, u32[]{:S(2)}) %collective-permute-start.1) | collective-permute-done | bytes 143392 | tf_op jit(solution)/shard_map/ppermute | solution.py:33
  37.6 5.4 %collective-permute-done.2.refs_1_ = bf16[40,1792]{1,0:T(8,128)(2,1)S(1)} collective-permute-done((bf16[40,1792]{1,0:T(8,128)(2,1)S(1)}, bf16[40,1792]{1,0:T(8,128)(2,1)S(1)}, u32[]{:S(2)}, u32[]{:S(2)}) %collective-permute-start.2) | collective-permute-done | bytes 143392 | tf_op jit(solution)/shard_map/ppermute | solution.py:33
  43.8 3.5 %collective-permute-start.17 = (bf16[80,512]{1,0:T(8,128)(2,1)S(1)}, bf16[80,512]{1,0:T(8,128)(2,1)S(1)}, u32[]{:S(2)}, u32[]{:S(2)}) collective-permute-start(bf16[80,512]{1,0:T(8,128)(2,1)S(1)} %rotate_out.1.refs_3_.refs_0_), channel_id=1, source_target_pairs={{0,4},{1,5},{2,6},{3,7},{4,8},{5,9},{6,10},{7,11},{8,12},{9,13},{1... | collective-permute-start | bytes 245768 | tf_op jit(solution)/shard_map/ppermute | solution.py:33
  47.3 2.2 %collective-permute-start.18 = (bf16[80,512]{1,0:T(8,128)(2,1)S(1)}, bf16[80,512]{1,0:T(8,128)(2,1)S(1)}, u32[]{:S(2)}, u32[]{:S(2)}) collective-permute-start(bf16[80,512]{1,0:T(8,128)(2,1)S(1)} %rotate_out.1.refs_3_.refs_0_), channel_id=1, source_target_pairs={{0,8},{1,9},{2,10},{3,11},{4,12},{5,13},{6,14},{7,15},{8,0},{9,1},... | collective-permute-start | bytes 245768 | tf_op jit(solution)/shard_map/ppermute | solution.py:33
  49.7 2.4 %rotate_in.2.refs_0_.refs_4_ = f32[192,40]{1,0:T(8,128)S(1)} custom-call(bf16[40,1792]{1,0:T(8,128)(2,1)S(1)} %get-tuple-element.12.own_ref, bf16[2,40,1792]{2,1,0:T(8,128)(2,1)S(1)} %collective-permute-done.refs_1_.across_ref, bf16[3,40,1792]{2,1,0:T(8,128)(2,1)S(1)} %pile.5.refs_0_.z_ref, bf16[3,40,1792]{2,1,0:T(8,128)(2,1)S(1)} %collective-permute-done.15.y_ref, ...), custom_call_target="tpu_custom_call" | custom-call | flops 220200960 | bytes 5505024 | tf_op jit(solution)/shard_map/rotate_in/pallas_call | solution.py:171
  52.1 2.4 %collective-permute-done.18.refs_2_ = bf16[80,512]{1,0:T(8,128)(2,1)S(1)} collective-permute-done((bf16[80,512]{1,0:T(8,128)(2,1)S(1)}, bf16[80,512]{1,0:T(8,128)(2,1)S(1)}, u32[]{:S(2)}, u32[]{:S(2)}) %collective-permute-start.18) | collective-permute-done | bytes 81952 | tf_op jit(solution)/shard_map/ppermute | solution.py:33
  54.9 1.0 %collective-permute-start.20 = (bf16[4,80,512]{2,1,0:T(8,128)(2,1)S(1)}, bf16[4,80,512]{2,1,0:T(8,128)(2,1)S(1)}, u32[]{:S(2)}, u32[]{:S(2)}) collective-permute-start(bf16[4,80,512]{2,1,0:T(8,128)(2,1)S(1)} %pile.7.z_ref), channel_id=1, source_target_pairs={{0,2},{1,3},{2,0},{3,1},{4,6},{5,7},{6,4},{7,5},{8,10},{9,11},{10,... | collective-permute-start | bytes 983048 | tf_op jit(solution)/shard_map/ppermute | solution.py:33
  55.9 2.4 %rotate_in.3 = (bf16[96,40]{1,0:T(8,128)(2,1)S(1)}, bf16[96,40]{1,0:T(8,128)(2,1)S(1)}) custom-call(bf16[40,1792]{1,0:T(8,128)(2,1)S(1)} %get-tuple-element.10.own_ref, bf16[2,40,1792]{2,1,0:T(8,128)(2,1)S(1)} %collective-permute-done.refs_1_.across_ref, bf16[3,40,1792]{2,1,0:T(8,128)(2,1)S(1)} %pile.6.z_ref.refs_5_, ...), custom_call_target="tpu_custom_call" | custom-call | flops 220200960 | bytes 5505024 | tf_op jit(solution)/shard_map/rotate_in/pallas_call | solution.py:171
  58.9 5.1 %collective-permute-done.20.refs_0_ = bf16[4,80,512]{2,1,0:T(8,128)(2,1)S(1)} collective-permute-done((bf16[4,80,512]{2,1,0:T(8,128)(2,1)S(1)}, bf16[4,80,512]{2,1,0:T(8,128)(2,1)S(1)}, u32[]{:S(2)}, u32[]{:S(2)}) %collective-permute-start.20) | collective-permute-done | bytes 327712 | tf_op jit(solution)/shard_map/ppermute | solution.py:33
  64.0 1.7 %combine.1._ = bf16[96,8192]{1,0:T(8,128)(2,1)} custom-call(bf16[96,40]{1,0:T(8,128)(2,1)S(1)} %get-tuple-element.13.own_ref, bf16[96,40]{1,0:T(8,128)(2,1)S(1)} %collective-permute-done.16.refs_1_.other_ref, bf16[4,80,512]{2,1,0:T(8,128)(2,1)S(1)} %pile.7.z_ref, bf16[4,80,512]{2,1,0:T(8,128)(2,1)S(1)} %after.1.y_ref, ...), custom_call_target="tpu_custom_call" | custom-call | flops 125829120 | bytes 3145728 | tf_op jit(solution)/shard_map/combine/pallas_call | solution.py:307
  (46 shorter events, 8.3 us)
Async XLA Ops:
  0.0 12.8 %collective-permute-start.7 = (bf16[96,28672]{1,0:T(8,128)(2,1)}, bf16[96,28672]{1,0:T(8,128)(2,1)S(1)}, u32[]{:S(2)}, u32[]{:S(2)}) collective-permute-start(bf16[96,28672]{1,0:T(8,128)(2,1)} %bitcast.1), channel_id=1, source_target_pairs={{0,1},{1,0},{2,3},{3,2},{4,5},{5,4},{6,7},{7,6},{8,9},{9,8},{10,11... | collective-permute-start | bytes 16515080 | tf_op jit(solution)/shard_map/ppermute | solution.py:33
  1.4 8.0 %collective-permute-start.4 = (bf16[40,1024]{1,0:T(8,128)(2,1)S(1)}, bf16[40,1024]{1,0:T(8,128)(2,1)S(1)}, u32[]{:S(2)}, u32[]{:S(2)}) collective-permute-start(bf16[40,1024]{1,0:T(8,128)(2,1)S(1)} %fold.2.refs_0_), channel_id=1, source_target_pairs={{0,4},{1,5},{2,6},{3,7},{4,8},{5,9},{6,10},{7,11},{8,12},{9,13},{1... | collective-permute-start | bytes 245768 | tf_op jit(solution)/shard_map/ppermute | solution.py:33
  4.0 8.7 %collective-permute-start.5 = (bf16[40,1024]{1,0:T(8,128)(2,1)S(1)}, bf16[40,1024]{1,0:T(8,128)(2,1)S(1)}, u32[]{:S(2)}, u32[]{:S(2)}) collective-permute-start(bf16[40,1024]{1,0:T(8,128)(2,1)S(1)} %fold.2.refs_0_), channel_id=1, source_target_pairs={{0,8},{1,9},{2,10},{3,11},{4,12},{5,13},{6,14},{7,15},{8,0},{9,1},... | collective-permute-start | bytes 245768 | tf_op jit(solution)/shard_map/ppermute | solution.py:33
  6.6 6.1 %collective-permute-start.6 = (bf16[40,1024]{1,0:T(8,128)(2,1)S(1)}, bf16[40,1024]{1,0:T(8,128)(2,1)S(1)}, u32[]{:S(2)}, u32[]{:S(2)}) collective-permute-start(bf16[40,1024]{1,0:T(8,128)(2,1)S(1)} %fold.2.refs_0_), channel_id=1, source_target_pairs={{0,12},{1,13},{2,14},{3,15},{4,0},{5,1},{6,2},{7,3},{8,4},{9,5},{1... | collective-permute-start | bytes 245768 | tf_op jit(solution)/shard_map/ppermute | solution.py:33
  12.8 10.7 %collective-permute-start.8 = (bf16[4,40,1024]{2,1,0:T(8,128)(2,1)S(1)}, bf16[4,40,1024]{2,1,0:T(8,128)(2,1)S(1)}, u32[]{:S(2)}, u32[]{:S(2)}) collective-permute-start(bf16[4,40,1024]{2,1,0:T(8,128)(2,1)S(1)} %pile.4.refs_0_.z_ref), channel_id=1, source_target_pairs={{0,2},{1,3},{2,0},{3,1},{4,6},{5,7},{6,4},{7,5},{8,10},{9,11},{10,... | collective-permute-start | bytes 983048 | tf_op jit(solution)/shard_map/ppermute | solution.py:33
  14.4 8.6 %collective-permute-start.11 = (bf16[40,1792]{1,0:T(8,128)(2,1)S(1)}, bf16[40,1792]{1,0:T(8,128)(2,1)S(1)}, u32[]{:S(2)}, u32[]{:S(2)}) collective-permute-start(bf16[40,1792]{1,0:T(8,128)(2,1)S(1)} %get-tuple-element.12.own_ref), channel_id=1, source_target_pairs={{0,4},{1,5},{2,6},{3,7},{4,8},{5,9},{6,10},{7,11},{8,12},{9,13},{1... | collective-permute-start | bytes 430088 | tf_op jit(solution)/shard_map/ppermute | solution.py:33
  16.7 16.4 %collective-permute-start.9 = (bf16[4,40,1024]{2,1,0:T(8,128)(2,1)S(1)}, bf16[4,40,1024]{2,1,0:T(8,128)(2,1)S(1)}, u32[]{:S(2)}, u32[]{:S(2)}) collective-permute-start(bf16[4,40,1024]{2,1,0:T(8,128)(2,1)S(1)} %pile.4.refs_0_.z_ref), channel_id=1, source_target_pairs={{0,1},{1,0},{2,3},{3,2},{4,5},{5,4},{6,7},{7,6},{8,9},{9,8},{10,11... | collective-permute-start | bytes 983048 | tf_op jit(solution)/shard_map/ppermute | solution.py:33
  16.7 11.2 %collective-permute-start.12 = (bf16[40,1792]{1,0:T(8,128)(2,1)S(1)}, bf16[40,1792]{1,0:T(8,128)(2,1)S(1)}, u32[]{:S(2)}, u32[]{:S(2)}) collective-permute-start(bf16[40,1792]{1,0:T(8,128)(2,1)S(1)} %get-tuple-element.12.own_ref), channel_id=1, source_target_pairs={{0,8},{1,9},{2,10},{3,11},{4,12},{5,13},{6,14},{7,15},{8,0},{9,1},... | collective-permute-start | bytes 430088 | tf_op jit(solution)/shard_map/ppermute | solution.py:33
  18.3 9.8 %collective-permute-start.13 = (bf16[40,1792]{1,0:T(8,128)(2,1)S(1)}, bf16[40,1792]{1,0:T(8,128)(2,1)S(1)}, u32[]{:S(2)}, u32[]{:S(2)}) collective-permute-start(bf16[40,1792]{1,0:T(8,128)(2,1)S(1)} %get-tuple-element.12.own_ref), channel_id=1, source_target_pairs={{0,12},{1,13},{2,14},{3,15},{4,0},{5,1},{6,2},{7,3},{8,4},{9,5},{1... | collective-permute-start | bytes 430088 | tf_op jit(solution)/shard_map/ppermute | solution.py:33
  23.0 9.0 %collective-permute-start = (bf16[2,40,1792]{2,1,0:T(8,128)(2,1)S(1)}, bf16[2,40,1792]{2,1,0:T(8,128)(2,1)S(1)}, u32[]{:S(2)}, u32[]{:S(2)}) collective-permute-start(bf16[2,40,1792]{2,1,0:T(8,128)(2,1)S(1)} %get-tuple-element.11.refs_5_), channel_id=1, source_target_pairs={{0,2},{1,3},{2,0},{3,1},{4,6},{5,7},{6,4},{7,5},{8,10},{9,11},{10,... | collective-permute-start | bytes 860168 | tf_op jit(solution)/shard_map/ppermute | solution.py:33
  23.5 11.0 %collective-permute-start.10 = (bf16[4,40,1024]{2,1,0:T(8,128)(2,1)S(1)}, bf16[4,40,1024]{2,1,0:T(8,128)(2,1)S(1)}, u32[]{:S(2)}, u32[]{:S(2)}) collective-permute-start(bf16[4,40,1024]{2,1,0:T(8,128)(2,1)S(1)} %collective-permute-done.8.y_ref), channel_id=1, source_target_pairs={{0,1},{1,0},{2,3},{3,2},{4,5},{5,4},{6,7},{7,6},{8,9},{9,8},{10,11... | collective-permute-start | bytes 983048 | tf_op jit(solution)/shard_map/ppermute | solution.py:33
  28.2 21.5 %collective-permute-start.15 = (bf16[3,40,1792]{2,1,0:T(8,128)(2,1)S(1)}, bf16[3,40,1792]{2,1,0:T(8,128)(2,1)S(1)}, u32[]{:S(2)}, u32[]{:S(2)}) collective-permute-start(bf16[3,40,1792]{2,1,0:T(8,128)(2,1)S(1)} %pile.5.refs_0_.z_ref), channel_id=1, source_target_pairs={{0,2},{1,3},{2,0},{3,1},{4,6},{5,7},{6,4},{7,5},{8,10},{9,11},{10,... | collective-permute-start | bytes 1290248 | tf_op jit(solution)/shard_map/ppermute | solution.py:33
  29.1 20.6 %slice-start.1 = ((s8[5505024]{0:T(1024)(128)(4,1)}), s8[1310720]{0:T(1024)(128)(4,1)S(1)}, s32[]{:S(2)}) async-start(s8[5505024]{0:T(1024)(128)(4,1)} %bitcast.2), calls=%async_computation.1 | async-start | bytes 2621440
  29.1 8.5 %collective-permute-start.1 = (bf16[40,1792]{1,0:T(8,128)(2,1)S(1)}, bf16[40,1792]{1,0:T(8,128)(2,1)S(1)}, u32[]{:S(2)}, u32[]{:S(2)}) collective-permute-start(bf16[40,1792]{1,0:T(8,128)(2,1)S(1)} %get-tuple-element.10.own_ref), channel_id=1, source_target_pairs={{0,4},{1,5},{2,6},{3,7},{4,8},{5,9},{6,10},{7,11},{8,12},{9,13},{1... | collective-permute-start | bytes 430088 | tf_op jit(solution)/shard_map/ppermute | solution.py:33
  32.0 11.1 %collective-permute-start.2 = (bf16[40,1792]{1,0:T(8,128)(2,1)S(1)}, bf16[40,1792]{1,0:T(8,128)(2,1)S(1)}, u32[]{:S(2)}, u32[]{:S(2)}) collective-permute-start(bf16[40,1792]{1,0:T(8,128)(2,1)S(1)} %get-tuple-element.10.own_ref), channel_id=1, source_target_pairs={{0,8},{1,9},{2,10},{3,11},{4,12},{5,13},{6,14},{7,15},{8,0},{9,1},... | collective-permute-start | bytes 430088 | tf_op jit(solution)/shard_map/ppermute | solution.py:33
  33.1 10.0 %collective-permute-start.3 = (bf16[40,1792]{1,0:T(8,128)(2,1)S(1)}, bf16[40,1792]{1,0:T(8,128)(2,1)S(1)}, u32[]{:S(2)}, u32[]{:S(2)}) collective-permute-start(bf16[40,1792]{1,0:T(8,128)(2,1)S(1)} %get-tuple-element.10.own_ref), channel_id=1, source_target_pairs={{0,12},{1,13},{2,14},{3,15},{4,0},{5,1},{6,2},{7,3},{8,4},{9,5},{1... | collective-permute-start | bytes 430088 | tf_op jit(solution)/shard_map/ppermute | solution.py:33
  43.1 12.8 %collective-permute-start.14 = (bf16[3,40,1792]{2,1,0:T(8,128)(2,1)S(1)}, bf16[3,40,1792]{2,1,0:T(8,128)(2,1)S(1)}, u32[]{:S(2)}, u32[]{:S(2)}) collective-permute-start(bf16[3,40,1792]{2,1,0:T(8,128)(2,1)S(1)} %pile.6.z_ref.refs_5_), channel_id=1, source_target_pairs={{0,2},{1,3},{2,0},{3,1},{4,6},{5,7},{6,4},{7,5},{8,10},{9,11},{10,... | collective-permute-start | bytes 1290248 | tf_op jit(solution)/shard_map/ppermute | solution.py:33
  43.8 8.3 %collective-permute-start.17 = (bf16[80,512]{1,0:T(8,128)(2,1)S(1)}, bf16[80,512]{1,0:T(8,128)(2,1)S(1)}, u32[]{:S(2)}, u32[]{:S(2)}) collective-permute-start(bf16[80,512]{1,0:T(8,128)(2,1)S(1)} %rotate_out.1.refs_3_.refs_0_), channel_id=1, source_target_pairs={{0,4},{1,5},{2,6},{3,7},{4,8},{5,9},{6,10},{7,11},{8,12},{9,13},{1... | collective-permute-start | bytes 245768 | tf_op jit(solution)/shard_map/ppermute | solution.py:33
  47.3 7.2 %collective-permute-start.18 = (bf16[80,512]{1,0:T(8,128)(2,1)S(1)}, bf16[80,512]{1,0:T(8,128)(2,1)S(1)}, u32[]{:S(2)}, u32[]{:S(2)}) collective-permute-start(bf16[80,512]{1,0:T(8,128)(2,1)S(1)} %rotate_out.1.refs_3_.refs_0_), channel_id=1, source_target_pairs={{0,8},{1,9},{2,10},{3,11},{4,12},{5,13},{6,14},{7,15},{8,0},{9,1},... | collective-permute-start | bytes 245768 | tf_op jit(solution)/shard_map/ppermute | solution.py:33
  49.5 5.4 %collective-permute-start.19 = (bf16[80,512]{1,0:T(8,128)(2,1)S(1)}, bf16[80,512]{1,0:T(8,128)(2,1)S(1)}, u32[]{:S(2)}, u32[]{:S(2)}) collective-permute-start(bf16[80,512]{1,0:T(8,128)(2,1)S(1)} %rotate_out.1.refs_3_.refs_0_), channel_id=1, source_target_pairs={{0,12},{1,13},{2,14},{3,15},{4,0},{5,1},{6,2},{7,3},{8,4},{9,5},{1... | collective-permute-start | bytes 245768 | tf_op jit(solution)/shard_map/ppermute | solution.py:33
  54.9 9.1 %collective-permute-start.20 = (bf16[4,80,512]{2,1,0:T(8,128)(2,1)S(1)}, bf16[4,80,512]{2,1,0:T(8,128)(2,1)S(1)}, u32[]{:S(2)}, u32[]{:S(2)}) collective-permute-start(bf16[4,80,512]{2,1,0:T(8,128)(2,1)S(1)} %pile.7.z_ref), channel_id=1, source_target_pairs={{0,2},{1,3},{2,0},{3,1},{4,6},{5,7},{6,4},{7,5},{8,10},{9,11},{10,... | collective-permute-start | bytes 983048 | tf_op jit(solution)/shard_map/ppermute | solution.py:33
  55.9 8.1 %collective-permute-start.22 = (bf16[4,80,512]{2,1,0:T(8,128)(2,1)S(1)}, bf16[4,80,512]{2,1,0:T(8,128)(2,1)S(1)}, u32[]{:S(2)}, u32[]{:S(2)}) collective-permute-start(bf16[4,80,512]{2,1,0:T(8,128)(2,1)S(1)} %pile.7.z_ref), channel_id=1, source_target_pairs={{0,1},{1,0},{2,3},{3,2},{4,5},{5,4},{6,7},{7,6},{8,9},{9,8},{10,11... | collective-permute-start | bytes 983048 | tf_op jit(solution)/shard_map/ppermute | solution.py:33
  58.3 5.7 %collective-permute-start.16 = (bf16[96,40]{1,0:T(8,128)(2,1)S(1)}, bf16[96,40]{1,0:T(8,128)(2,1)S(1)}, u32[]{:S(2)}, u32[]{:S(2)}) collective-permute-start(bf16[96,40]{1,0:T(8,128)(2,1)S(1)} %get-tuple-element.14), channel_id=1, source_target_pairs={{0,1},{1,0},{2,3},{3,2},{4,5},{5,4},{6,7},{7,6},{8,9},{9,8},{10,11... | collective-permute-start | bytes 23048 | tf_op jit(solution)/shard_map/ppermute | solution.py:33
  64.0 1.7 %collective-permute-start.21 = (bf16[4,80,512]{2,1,0:T(8,128)(2,1)S(1)}, bf16[4,80,512]{2,1,0:T(8,128)(2,1)S(1)}, u32[]{:S(2)}, u32[]{:S(2)}) collective-permute-start(bf16[4,80,512]{2,1,0:T(8,128)(2,1)S(1)} %after.1.y_ref), channel_id=1, source_target_pairs={{0,1},{1,0},{2,3},{3,2},{4,5},{5,4},{6,7},{7,6},{8,9},{9,8},{10,11... | collective-permute-start | bytes 983048 | tf_op jit(solution)/shard_map/ppermute | solution.py:33
  (4 other events, 25.9 us)
